TPU v7x, 128 devices: a whole 4x4x4 slice. The times are simulated.
128 devices in a mesh: gx: 8 (over y, core), gy: 16 (over z, x).
Axes of the slice: x: 4, y: 4, z: 4, core: 2. Of those that a mesh axis runs over, the one named last changes fastest.
Arguments:
- ensemble: float32 [80, 4, 256, 4096], P(None, None, 'gx', 'gy'), may hold values from -6 to 6
- obs_value: float32 [4, 2048], replicated, may hold values from -6 to 6
- obs_variance: float32 [4, 2048], replicated, may hold values from 0.25 to 2
- obs_owner: int32 [4, 2048], replicated, may hold values from 0 to 127, as said below
- obs_cell: int32 [4, 2048], replicated, may hold values from 0 to 8191
- obs_reach: int32 [4, 2048, 8], replicated, may hold values 0 or 1
- batch_order: int32 [4], replicated, may hold values from 0 to 3, each once
Outputs:
- posterior: float32 [80, 4, 256, 4096], P(None, None, 'gx', 'gy')
- innovation: float32 [4, 2048], replicated
Inputs may be any that keep to these rules, and one draw needn't show every extreme that they name: `obs_owner`: In every batch no tile owns more than 64 observations, and some tile owns exactly 64.
All inputs are finite; a program needn't handle non-finite values.
Results may differ from a plain program's by a relative error of at most 0.00017.
Values sent between devices are 32-bit elements; how exact they have to be, the bound alone decides.
No kernel may reach another device: no remote copies, remote signals or barrier semaphores. Data moves between devices by JAX's collectives and lax.ppermute only.
A program may use at most 128 MiB of HBM per device.

v0:
```python
import jax
import jax.numpy as jnp
from jax import lax
from jax.sharding import PartitionSpec as P

OWN_CAP = 64


EPS = 1e-05


def with_halo(block, sides, width):
    for axis, dim in sides:
        count = lax.axis_size(axis)
        forward = [(i, i + 1) for i in range(count - 1)]
        backward = [(target, source) for source, target in forward]
        low = lax.ppermute(
            lax.slice_in_dim(block, block.shape[dim] - width, None, axis=dim), axis, forward
        )
        high = lax.ppermute(lax.slice_in_dim(block, 0, width, axis=dim), axis, backward)
        block = jnp.concatenate([low, block, high], axis=dim)
    return block


def increments(prior, value, variance):
    members = prior.shape[0]
    center = jnp.mean(prior, axis=0)
    deviation = prior - center[None, :]
    spread = jnp.sum(deviation * deviation, axis=0) / (members - 1)
    total = spread + variance
    normed = (value - center) / jnp.sqrt(total)
    shift = (spread / total * (value - center))[None, :] + (jnp.sqrt(variance / total) - 1.0)[
        None, :
    ] * deviation
    scaled = deviation / ((members - 1) * (spread + EPS))[None, :]
    return (scaled, shift, normed)


def tile_weight(reach, step_x, step_y):
    inside = (jnp.abs(step_x) <= 1) & (jnp.abs(step_y) <= 1)
    offset = (step_x + 1) * 3 + (step_y + 1)
    column = jnp.where(offset < 4, offset, offset - 1)
    picked = jnp.zeros(reach.shape[:-1], jnp.float32)
    for index in range(8):
        picked = picked + jnp.where(column == index, reach[..., index], 0.0)
    reached = jnp.where(offset == 4, 1.0, picked)
    distance = jnp.abs(step_x) + jnp.abs(step_y)
    taper = jnp.where(distance == 0, 1.0, jnp.where(distance == 1, 0.5, 0.25))
    return jnp.where(inside, taper * reached, 0.0)


def local(ensemble, obs_value, obs_variance, obs_owner, obs_cell, obs_reach, batch_order):
    members = ensemble.shape[0]
    width_y = lax.axis_size("gy")
    my_x = lax.axis_index("gx")
    my_y = lax.axis_index("gy")
    myself = my_x * width_y + my_y
    batches = obs_value.shape[0]
    count_obs = obs_value.shape[1]
    capacity = OWN_CAP
    positions = jnp.arange(count_obs, dtype=jnp.int32)
    state = ensemble
    innovation = jnp.zeros((batches, count_obs), jnp.float32)
    for step in range(batches):
        batch = batch_order[step]
        value = lax.dynamic_index_in_dim(obs_value, batch, 0, keepdims=False)
        variance = lax.dynamic_index_in_dim(obs_variance, batch, 0, keepdims=False)
        owner = lax.dynamic_index_in_dim(obs_owner, batch, 0, keepdims=False)
        cell = lax.dynamic_index_in_dim(obs_cell, batch, 0, keepdims=False)
        reach = lax.dynamic_index_in_dim(obs_reach, batch, 0, keepdims=False)
        owned = owner == myself
        order_key = jnp.where(owned, positions, count_obs + positions)
        picked = jnp.argsort(order_key)[:capacity]
        valid = owned[picked]
        cells = jnp.where(valid, cell[picked], 0)
        surface = state[:, 0].reshape(members, -1)
        prior = jnp.take(surface, cells, axis=1)
        scaled, shift, normed = increments(prior, value[picked], variance[picked])
        scaled = jnp.where(valid[None, :], scaled, 0.0)
        shift = jnp.where(valid[None, :], shift, 0.0)
        reach_rows = jnp.where(valid[:, None], reach[picked].astype(jnp.float32), 0.0)
        packed = jnp.concatenate([scaled.T, shift.T, reach_rows], axis=1)
        innovation = innovation.at[batch, picked].add(jnp.where(valid, normed, 0.0))
        block = with_halo(packed[None, None], (("gx", 0), ("gy", 1)), 1)
        offsets = 1 - jnp.arange(3, dtype=jnp.int32)
        weight = tile_weight(
            block[:, :, :, 2 * members :], offsets[:, None, None], offsets[None, :, None]
        )
        gain = jnp.einsum(
            "abjm,abjn->mn",
            block[:, :, :, :members] * weight[..., None],
            block[:, :, :, members : 2 * members],
            precision=lax.Precision.HIGHEST,
        )
        center = jnp.mean(state, axis=0)
        anomaly = (state - center[None]).reshape(members, -1)
        update = jnp.dot(gain.T, anomaly, precision=lax.Precision.HIGHEST)
        state = state + update.reshape(state.shape)
    innovation = lax.psum(innovation, ("gx", "gy"))
    return (state, innovation)


def solution(mesh):
    placed = (P(None, None, "gx", "gy"), P(), P(), P(), P(), P(), P())
    return jax.shard_map(
        local,
        mesh=mesh,
        in_specs=placed,
        out_specs=(P(None, None, "gx", "gy"), P()),
        check_vma=False,
    )
```

profile of v0, /device:TPU:1, one launch (start us, length us, event | category | flops | bytes accessed | tf_op | source)
XLA Modules:
  0.0 434.0 jit_solution(13329420337702167750)
XLA Ops:
  0.6 1.5 fusion.88
  9.8 1.0 compare_reduce_fusion
  10.9 5.0 %sort.60 = (s32[2048]{0:T(1024)}, s32[2048]{0:T(1024)S(1)}) sort(s32[2048]{0:T(1024)S(1)} %iota_select_fusion.2, s32[2048]{0:T(1024)S(1)} %iota.140), dimensions={0}, to_apply=%region_4.6 | sort | flops 22528 | bytes 32768 | tf_op jit(solution)/shard_map/jit(argsort)/sort | solution.py:73
  15.9 5.0 %sort.59 = (s32[2048]{0:T(1024)}, s32[2048]{0:T(1024)S(1)}) sort(s32[2048]{0:T(1024)S(1)} %fusion.75, s32[2048]{0:T(1024)S(1)} %iota.136), dimensions={0}, to_apply=%region_0.1 | sort | flops 22528 | bytes 32768 | tf_op jit(solution)/shard_map/jit(argsort)/sort | solution.py:73
  21.8 0.9 constant_dynamic-slice_fusion.3
  23.5 1.0 constant_dynamic-slice_fusion.1
  26.1 1.0 constant_dynamic-slice_fusion
  27.0 1.3 copy.17
  28.3 1.8 gather_fusion.4
  30.3 3.1 copy.16
  33.4 2.8 gather_fusion.20
  36.8 3.3 collective-permute-start.1
  40.1 3.2 collective-permute-start
  43.6 5.0 %sort.62 = (s32[2048]{0:T(1024)}, s32[2048]{0:T(1024)S(1)}) sort(s32[2048]{0:T(1024)S(1)} %iota_select_fusion, s32[2048]{0:T(1024)S(1)} %iota.144), dimensions={0}, to_apply=%region_12.14 | sort | flops 22528 | bytes 32768 | tf_op jit(solution)/shard_map/jit(argsort)/sort | solution.py:73
  48.6 5.0 %sort.61 = (s32[2048]{0:T(1024)}, s32[2048]{0:T(1024)S(1)}) sort(s32[2048]{0:T(1024)S(1)} %iota_select_fusion.1, s32[2048]{0:T(1024)S(1)} %iota.142), dimensions={0}, to_apply=%region_8.10 | sort | flops 22528 | bytes 32768 | tf_op jit(solution)/shard_map/jit(argsort)/sort | solution.py:73
  58.4 4.7 %reduce_sum.110 = f32[4,32,256]{2,1,0:T(8,128)S(1)} reduce(f32[80,4,32,256]{3,2,1,0:T(8,128)} %param.9, f32[]{:T(128)} %constant.116.clone.1), dimensions={0}, to_apply=%region_3.5 | reduce | flops 2588672 | bytes 10616836 | tf_op jit(solution)/shard_map/reduce_sum | solution.py:95
  66.3 10.5 %fusion.92 = f32[4,32,256,80]{2,1,0,3:T(8,128)} fusion(f32[80,4,32,256]{3,2,1,0:T(8,128)} %param.9, f32[4,32,256]{2,1,0:T(8,128)S(1)} %broadcast_multiply_fusion.3), kind=kLoop, calls=%fused_computation.288 | loop fusion | flops 2621440 | bytes 21102592 | tf_op jit(solution)/shard_map/dot_general | solution.py:97
  77.0 1.3 collective-permute-start.3
  78.3 4.2 collective-permute-start.2
  87.1 3.7 scatter_fusion
  91.0 0.9 fusion.64
  91.9 0.9 fusion.58
  92.7 28.8 %fusion.89 = (f32[4,32,256]{2,1,0:T(8,128)S(1)}, f32[80,4,32,256]{3,0,2,1:T(8,128)S(1)}) fusion(f32[80,80,1,1]{0,1,3,2:T(8,128)S(1)} %fusion.58, f32[4,32,256,80]{2,1,0,3:T(8,128)} %fusion.92, f32[80,4,32,256]{3,2,1,0:T(8,128)} %param.9), kind=kOutput, calls=%fused_computation.285 | convolution fusion | flops 2521792512 | bytes 31613952 | tf_op jit(solution)/shard_map/dot_general | solution.py:97
  121.6 4.1 copy-done.1
  125.8 3.4 copy.44
  129.2 2.8 gather_fusion.21
  132.6 1.9 collective-permute-start.5
  134.5 3.6 collective-permute-start.4
  138.2 1.3 collective-permute-done.4
  139.5 1.3 collective-permute-start.7
  140.8 4.0 collective-permute-start.6
  144.8 9.7 %broadcast_subtract_fusion.2 = f32[80,4,32,256]{3,0,2,1:T(8,128)} fusion(f32[80,4,32,256]{3,0,2,1:T(8,128)} %copy-done.1, f32[4,32,256]{2,1,0:T(8,128)S(1)} %broadcast_multiply_fusion.2), kind=kLoop, calls=%fused_computation.39 | loop fusion | flops 2621440 | bytes 21102592 | tf_op jit(solution)/shard_map/sub | solution.py:96
  154.5 13.9 %copy.53 = f32[10,8,128,256]{3,2,1,0:T(8,128)} copy(f32[10,8,128,256]{3,1,0,2:T(8,128)} %bitcast.188) | data formatting | bytes 20971520
  168.4 3.9 scatter_fusion.1
  172.4 0.9 fusion.51
  174.2 22.2 %fusion.90 = (f32[4,32,256]{2,1,0:T(8,128)S(1)}, f32[80,4,32,256]{3,0,2,1:T(8,128)S(1)}) fusion(f32[80,4,32,256]{3,0,2,1:T(8,128)} %copy-done.1, f32[80,80,1,1]{0,1,3,2:T(8,128)S(1)} %fusion.45, f32[4,32,256,80]{2,1,0,3:T(8,128)} %bitcast.186), kind=kOutput, calls=%fused_computation.286 | convolution fusion | flops 2521792512 | bytes 31613952 | tf_op jit(solution)/shard_map/dot_general | solution.py:97
  196.3 4.1 copy-done.2
  200.6 3.4 copy.45
  204.0 2.8 gather_fusion.22
  207.4 1.9 collective-permute-start.9
  209.3 4.8 %collective-permute-start.8 = (f32[1,1,64,168]{3,2,1,0:T(8,128)S(1)}, f32[1,1,64,168]{3,2,1,0:T(8,128)S(1)}, u32[]{:S(2)}, u32[]{:S(2)}) collective-permute-start(f32[1,1,64,168]{3,2,1,0:T(8,128)S(1)} %maximum_bitcast_fusion.2), channel_id=1, source_target_pairs={{0,16},{16,32},{32,48},{48,64},{64,80},{80,96},{96,112},{1,17},{17... | collective-permute-start | bytes 129032 | tf_op jit(solution)/shard_map/ppermute | solution.py:17
  214.2 1.3 collective-permute-done.8
  215.5 1.3 collective-permute-start.11
  216.8 4.2 collective-permute-start.10
  221.0 9.7 %broadcast_subtract_fusion.1 = f32[80,4,32,256]{3,0,2,1:T(8,128)} fusion(f32[80,4,32,256]{3,0,2,1:T(8,128)} %copy-done.2, f32[4,32,256]{2,1,0:T(8,128)S(1)} %broadcast_multiply_fusion.1), kind=kLoop, calls=%fused_computation.38 | loop fusion | flops 2621440 | bytes 21102592 | tf_op jit(solution)/shard_map/sub | solution.py:96
  230.7 13.9 %copy.55 = f32[10,8,128,256]{3,2,1,0:T(8,128)} copy(f32[10,8,128,256]{3,1,0,2:T(8,128)} %bitcast.189) | data formatting | bytes 20971520
  244.6 4.1 scatter_fusion.2
  248.8 0.9 fusion.38
  250.6 22.2 %fusion.91 = (f32[4,32,256]{2,1,0:T(8,128)S(1)}, f32[80,4,32,256]{3,0,2,1:T(8,128)S(1)}) fusion(f32[80,4,32,256]{3,0,2,1:T(8,128)} %copy-done.2, f32[80,80,1,1]{0,1,3,2:T(8,128)S(1)} %fusion.32, f32[4,32,256,80]{2,1,0,3:T(8,128)} %bitcast.187), kind=kOutput, calls=%fused_computation.287 | convolution fusion | flops 2521792512 | bytes 31613952 | tf_op jit(solution)/shard_map/dot_general | solution.py:97
  272.7 4.1 copy-done
  277.0 3.4 copy.46
  280.4 2.8 gather_fusion.23
  283.8 1.9 collective-permute-start.13
  285.7 4.8 %collective-permute-start.12 = (f32[1,1,64,168]{3,2,1,0:T(8,128)S(1)}, f32[1,1,64,168]{3,2,1,0:T(8,128)S(1)}, u32[]{:S(2)}, u32[]{:S(2)}) collective-permute-start(f32[1,1,64,168]{3,2,1,0:T(8,128)S(1)} %maximum_bitcast_fusion.3), channel_id=1, source_target_pairs={{0,16},{16,32},{32,48},{48,64},{64,80},{80,96},{96,112},{1,17},{17... | collective-permute-start | bytes 129032 | tf_op jit(solution)/shard_map/ppermute | solution.py:17
  290.6 1.3 collective-permute-done.12
  291.9 1.3 collective-permute-start.15
  293.2 4.7 %collective-permute-start.14 = (f32[3,1,64,168]{3,2,1,0:T(8,128)S(1)}, f32[3,1,64,168]{3,2,1,0:T(8,128)S(1)}, u32[]{:S(2)}, u32[]{:S(2)}) collective-permute-start(f32[3,1,64,168]{3,2,1,0:T(8,128)S(1)} %pad_maximum_fusion.7), channel_id=1, source_target_pairs={{0,1},{1,2},{2,3},{3,4},{4,5},{5,6},{6,7},{7,8},{8,9},{9,10},{10,1... | collective-permute-start | bytes 387080 | tf_op jit(solution)/shard_map/ppermute | solution.py:17
  297.9 9.7 %broadcast_subtract_fusion = f32[80,4,32,256]{3,0,2,1:T(8,128)} fusion(f32[80,4,32,256]{3,0,2,1:T(8,128)} %copy-done, f32[4,32,256]{2,1,0:T(8,128)S(1)} %broadcast_multiply_fusion), kind=kLoop, calls=%fused_computation.37 | loop fusion | flops 2621440 | bytes 21102592 | tf_op jit(solution)/shard_map/sub | solution.py:96
  307.6 13.9 %copy.57 = f32[10,8,128,256]{3,2,1,0:T(8,128)} copy(f32[10,8,128,256]{3,1,0,2:T(8,128)} %bitcast.190) | data formatting | bytes 20971520
  321.4 3.7 scatter_fusion.3
  325.2 75.1 %psum.7 = f32[4,2048]{1,0:T(4,128)} all-reduce(f32[4,2048]{1,0:T(4,128)S(1)} %scatter_fusion.3), channel_id=1, replica_groups=mesh['gx'=8,'gy'=16] {'gx','gy'}, use_global_device_ids=true, to_apply=%region_20.22 | all-reduce | flops 8192 | bytes 65536 | tf_op jit(solution)/shard_map/psum | solution.py:99
  400.3 0.9 fusion.25
  402.1 21.3 %fusion.16 = f32[80,4,32,256]{3,0,2,1:T(8,128)S(1)} fusion(f32[80,4,32,256]{3,0,2,1:T(8,128)} %copy-done, f32[80,80,1,1]{0,1,3,2:T(8,128)S(1)} %fusion.19, f32[4,32,256,80]{2,1,0,3:T(8,128)} %bitcast.185), kind=kOutput, calls=%fused_computation.43 | convolution fusion | flops 2519203840 | bytes 31482880 | tf_op jit(solution)/shard_map/dot_general | solution.py:97
  423.4 10.2 %copy.35 = f32[80,4,32,256]{3,2,1,0:T(8,128)} copy(f32[80,4,32,256]{3,0,2,1:T(8,128)S(1)} %fusion.16) | data formatting | bytes 20971520
  (117 shorter events, 21.8 us)
Async XLA Ops:
  0.6 29.6 %slice-start = ((f32[80,4,32,256]{3,2,1,0:T(8,128)}), f32[80,1,32,256]{3,2,1,0:T(8,128)S(1)}, s32[]{:S(2)}) async-start(f32[80,4,32,256]{3,2,1,0:T(8,128)} %param.9), calls=%async_computation | async-start | bytes 5242880 | tf_op jit(solution)/shard_map/slice | solution.py:76
  36.8 40.1 %collective-permute-start.1 = (f32[1,1,64,168]{3,2,1,0:T(8,128)S(1)}, f32[1,1,64,168]{3,2,1,0:T(8,128)S(1)}, u32[]{:S(2)}, u32[]{:S(2)}) collective-permute-start(f32[1,1,64,168]{3,2,1,0:T(8,128)S(1)} %maximum_bitcast_fusion), channel_id=1, source_target_pairs={{16,0},{32,16},{48,32},{64,48},{80,64},{96,80},{112,96},{17,1},{33... | collective-permute-start | bytes 129032 | tf_op jit(solution)/shard_map/ppermute | solution.py:20
  40.1 36.8 %collective-permute-start = (f32[1,1,64,168]{3,2,1,0:T(8,128)S(1)}, f32[1,1,64,168]{3,2,1,0:T(8,128)S(1)}, u32[]{:S(2)}, u32[]{:S(2)}) collective-permute-start(f32[1,1,64,168]{3,2,1,0:T(8,128)S(1)} %maximum_bitcast_fusion), channel_id=1, source_target_pairs={{0,16},{16,32},{32,48},{48,64},{64,80},{80,96},{96,112},{1,17},{17... | collective-permute-start | bytes 129032 | tf_op jit(solution)/shard_map/ppermute | solution.py:17
  77.0 13.9 %collective-permute-start.3 = (f32[3,1,64,168]{3,2,1,0:T(8,128)S(1)}, f32[3,1,64,168]{3,2,1,0:T(8,128)S(1)}, u32[]{:S(2)}, u32[]{:S(2)}) collective-permute-start(f32[3,1,64,168]{3,2,1,0:T(8,128)S(1)} %pad_maximum_fusion.4), channel_id=1, source_target_pairs={{1,0},{2,1},{3,2},{4,3},{5,4},{6,5},{7,6},{8,7},{9,8},{10,9},{11,1... | collective-permute-start | bytes 387080 | tf_op jit(solution)/shard_map/ppermute | solution.py:20
  78.3 12.6 %collective-permute-start.2 = (f32[3,1,64,168]{3,2,1,0:T(8,128)S(1)}, f32[3,1,64,168]{3,2,1,0:T(8,128)S(1)}, u32[]{:S(2)}, u32[]{:S(2)}) collective-permute-start(f32[3,1,64,168]{3,2,1,0:T(8,128)S(1)} %pad_maximum_fusion.4), channel_id=1, source_target_pairs={{0,1},{1,2},{2,3},{3,4},{4,5},{5,6},{6,7},{7,8},{8,9},{9,10},{10,1... | collective-permute-start | bytes 387080 | tf_op jit(solution)/shard_map/ppermute | solution.py:17
  121.5 4.1 copy-start.1
  132.6 5.6 %collective-permute-start.5 = (f32[1,1,64,168]{3,2,1,0:T(8,128)S(1)}, f32[1,1,64,168]{3,2,1,0:T(8,128)S(1)}, u32[]{:S(2)}, u32[]{:S(2)}) collective-permute-start(f32[1,1,64,168]{3,2,1,0:T(8,128)S(1)} %maximum_bitcast_fusion.1), channel_id=1, source_target_pairs={{16,0},{32,16},{48,32},{64,48},{80,64},{96,80},{112,96},{17,1},{33... | collective-permute-start | bytes 129032 | tf_op jit(solution)/shard_map/ppermute | solution.py:20
  134.5 5.0 %collective-permute-start.4 = (f32[1,1,64,168]{3,2,1,0:T(8,128)S(1)}, f32[1,1,64,168]{3,2,1,0:T(8,128)S(1)}, u32[]{:S(2)}, u32[]{:S(2)}) collective-permute-start(f32[1,1,64,168]{3,2,1,0:T(8,128)S(1)} %maximum_bitcast_fusion.1), channel_id=1, source_target_pairs={{0,16},{16,32},{32,48},{48,64},{64,80},{80,96},{96,112},{1,17},{17... | collective-permute-start | bytes 129032 | tf_op jit(solution)/shard_map/ppermute | solution.py:17
  139.5 32.8 %collective-permute-start.7 = (f32[3,1,64,168]{3,2,1,0:T(8,128)S(1)}, f32[3,1,64,168]{3,2,1,0:T(8,128)S(1)}, u32[]{:S(2)}, u32[]{:S(2)}) collective-permute-start(f32[3,1,64,168]{3,2,1,0:T(8,128)S(1)} %pad_maximum_fusion.5), channel_id=1, source_target_pairs={{1,0},{2,1},{3,2},{4,3},{5,4},{6,5},{7,6},{8,7},{9,8},{10,9},{11,1... | collective-permute-start | bytes 387080 | tf_op jit(solution)/shard_map/ppermute | solution.py:20
  140.8 31.5 %collective-permute-start.6 = (f32[3,1,64,168]{3,2,1,0:T(8,128)S(1)}, f32[3,1,64,168]{3,2,1,0:T(8,128)S(1)}, u32[]{:S(2)}, u32[]{:S(2)}) collective-permute-start(f32[3,1,64,168]{3,2,1,0:T(8,128)S(1)} %pad_maximum_fusion.5), channel_id=1, source_target_pairs={{0,1},{1,2},{2,3},{3,4},{4,5},{5,6},{6,7},{7,8},{8,9},{9,10},{10,1... | collective-permute-start | bytes 387080 | tf_op jit(solution)/shard_map/ppermute | solution.py:17
  196.3 4.1 copy-start.2
  207.4 6.8 %collective-permute-start.9 = (f32[1,1,64,168]{3,2,1,0:T(8,128)S(1)}, f32[1,1,64,168]{3,2,1,0:T(8,128)S(1)}, u32[]{:S(2)}, u32[]{:S(2)}) collective-permute-start(f32[1,1,64,168]{3,2,1,0:T(8,128)S(1)} %maximum_bitcast_fusion.2), channel_id=1, source_target_pairs={{16,0},{32,16},{48,32},{64,48},{80,64},{96,80},{112,96},{17,1},{33... | collective-permute-start | bytes 129032 | tf_op jit(solution)/shard_map/ppermute | solution.py:20
  209.3 6.1 %collective-permute-start.8 = (f32[1,1,64,168]{3,2,1,0:T(8,128)S(1)}, f32[1,1,64,168]{3,2,1,0:T(8,128)S(1)}, u32[]{:S(2)}, u32[]{:S(2)}) collective-permute-start(f32[1,1,64,168]{3,2,1,0:T(8,128)S(1)} %maximum_bitcast_fusion.2), channel_id=1, source_target_pairs={{0,16},{16,32},{32,48},{48,64},{64,80},{80,96},{96,112},{1,17},{17... | collective-permute-start | bytes 129032 | tf_op jit(solution)/shard_map/ppermute | solution.py:17
  215.5 33.2 %collective-permute-start.11 = (f32[3,1,64,168]{3,2,1,0:T(8,128)S(1)}, f32[3,1,64,168]{3,2,1,0:T(8,128)S(1)}, u32[]{:S(2)}, u32[]{:S(2)}) collective-permute-start(f32[3,1,64,168]{3,2,1,0:T(8,128)S(1)} %pad_maximum_fusion.6), channel_id=1, source_target_pairs={{1,0},{2,1},{3,2},{4,3},{5,4},{6,5},{7,6},{8,7},{9,8},{10,9},{11,1... | collective-permute-start | bytes 387080 | tf_op jit(solution)/shard_map/ppermute | solution.py:20
  216.8 31.9 %collective-permute-start.10 = (f32[3,1,64,168]{3,2,1,0:T(8,128)S(1)}, f32[3,1,64,168]{3,2,1,0:T(8,128)S(1)}, u32[]{:S(2)}, u32[]{:S(2)}) collective-permute-start(f32[3,1,64,168]{3,2,1,0:T(8,128)S(1)} %pad_maximum_fusion.6), channel_id=1, source_target_pairs={{0,1},{1,2},{2,3},{3,4},{4,5},{5,6},{6,7},{7,8},{8,9},{9,10},{10,1... | collective-permute-start | bytes 387080 | tf_op jit(solution)/shard_map/ppermute | solution.py:17
  272.7 4.1 copy-start
  283.8 6.8 %collective-permute-start.13 = (f32[1,1,64,168]{3,2,1,0:T(8,128)S(1)}, f32[1,1,64,168]{3,2,1,0:T(8,128)S(1)}, u32[]{:S(2)}, u32[]{:S(2)}) collective-permute-start(f32[1,1,64,168]{3,2,1,0:T(8,128)S(1)} %maximum_bitcast_fusion.3), channel_id=1, source_target_pairs={{16,0},{32,16},{48,32},{64,48},{80,64},{96,80},{112,96},{17,1},{33... | collective-permute-start | bytes 129032 | tf_op jit(solution)/shard_map/ppermute | solution.py:20
  285.7 6.1 %collective-permute-start.12 = (f32[1,1,64,168]{3,2,1,0:T(8,128)S(1)}, f32[1,1,64,168]{3,2,1,0:T(8,128)S(1)}, u32[]{:S(2)}, u32[]{:S(2)}) collective-permute-start(f32[1,1,64,168]{3,2,1,0:T(8,128)S(1)} %maximum_bitcast_fusion.3), channel_id=1, source_target_pairs={{0,16},{16,32},{32,48},{48,64},{64,80},{80,96},{96,112},{1,17},{17... | collective-permute-start | bytes 129032 | tf_op jit(solution)/shard_map/ppermute | solution.py:17
  291.9 108.4 %collective-permute-start.15 = (f32[3,1,64,168]{3,2,1,0:T(8,128)S(1)}, f32[3,1,64,168]{3,2,1,0:T(8,128)S(1)}, u32[]{:S(2)}, u32[]{:S(2)}) collective-permute-start(f32[3,1,64,168]{3,2,1,0:T(8,128)S(1)} %pad_maximum_fusion.7), channel_id=1, source_target_pairs={{1,0},{2,1},{3,2},{4,3},{5,4},{6,5},{7,6},{8,7},{9,8},{10,9},{11,1... | collective-permute-start | bytes 387080 | tf_op jit(solution)/shard_map/ppermute | solution.py:20
  293.2 107.1 %collective-permute-start.14 = (f32[3,1,64,168]{3,2,1,0:T(8,128)S(1)}, f32[3,1,64,168]{3,2,1,0:T(8,128)S(1)}, u32[]{:S(2)}, u32[]{:S(2)}) collective-permute-start(f32[3,1,64,168]{3,2,1,0:T(8,128)S(1)} %pad_maximum_fusion.7), channel_id=1, source_target_pairs={{0,1},{1,2},{2,3},{3,4},{4,5},{5,6},{6,7},{7,8},{8,9},{9,10},{10,1... | collective-permute-start | bytes 387080 | tf_op jit(solution)/shard_map/ppermute | solution.py:17
where the time goes:
time: 443 us; the launch traced here: 434 us
  local copies, waits for them, and re-layouts  112 us (25%)
  matrix products  97.8 us (22%)
  other arithmetic  88.1 us (20%)
  blocking collectives  75.1 us (17%)
  starting transfers between devices  47.8 us (11%)
  between operations  9.49 us (2%)
    dot_general x4, matrix products, local(): update = jnp.dot(gain.T, anomaly, precision=lax.Precision.HIGHEST)  94.4 us
    psum x1, blocking collectives, local(): innovation = lax.psum(innovation, ('gx', 'gy'))  75.1 us
    unnamed x10, local copies, waits for them, and re-layouts  64 us
    ppermute x8, starting transfers between devices, with_halo(): lax.ppermute(lax.slice_in_dim(block, block.shape[dim] - width, None, axis...  33.6 us
    sub x3, other arithmetic, local(): anomaly = (state - center[None]).reshape(members, -1)  29.1 us
    sort x4, other arithmetic, local(): picked = jnp.argsort(order_key)[:capacity]  20.2 us
    scatter-add x4, other arithmetic, local(): innovation = innovation.at[batch, picked].add(jnp.where(valid, normed, 0.0))  15.5 us
    ppermute x8, starting transfers between devices, with_halo(): lax.ppermute(lax.slice_in_dim(block, 0, width, axis=dim), axis, backward)  14.3 us
  transfers between devices with their start and end apart: 16, of which 3 were waited for; matrix products, arithmetic and copies ran while one was open for 29% of the time, Pallas kernels for 0%

commit v1 on v0

v1 whole, which is shorter than its diff:
```python
import functools

import jax
import jax.numpy as jnp
from jax import lax
from jax.experimental import pallas as pl
from jax.experimental.pallas import tpu as pltpu
from jax.sharding import PartitionSpec as P

M = 80
LEV = 4
NB = 4
TX = 32
TY = 256
CAP = 64
OBS = 2048
TILES = 128
EPS = 1e-05
F32 = jnp.float32
BF16 = jnp.bfloat16
HIGH = lax.Precision.HIGHEST

ROW_A = M
ROW_C = M + 1
ROW_W = M + 2
ROWS = 96
TAPER = (0.25, 0.5, 0.25, 0.5, 1.0, 0.5, 0.25, 0.5, 0.25)


def split2(x):
    high = x.astype(BF16)
    return high, (x - high.astype(F32)).astype(BF16)


def split3(x):
    high = x.astype(BF16)
    rest = x - high.astype(F32)
    mid = rest.astype(BF16)
    return high, mid, (rest - mid.astype(F32)).astype(BF16)


def iota(shape, dim):
    return lax.broadcasted_iota(jnp.int32, shape, dim)


def dot(a, b, **kw):
    return jnp.dot(a, b, preferred_element_type=F32, **kw)


def dot_t(a, b, **kw):
    return lax.dot_general(a, b, (((1,), (1,)), ((), ())), preferred_element_type=F32, **kw)


def pack(rows):
    return jnp.concatenate([rows[: ROWS // 2], rows[ROWS // 2 :]], axis=1)


def unpack(packed):
    return jnp.concatenate([packed[:, :CAP], packed[:, CAP:]], axis=0)


def make_payload(prior, meta):
    valid = meta[0:1] > 0.5
    value = meta[1:2]
    variance = jnp.where(valid, meta[2:3], 1.0)
    center = jnp.sum(prior, axis=0, keepdims=True) / M
    deviation = prior - center
    spread = jnp.sum(deviation * deviation, axis=0, keepdims=True) / (M - 1)
    total = spread + variance
    miss = value - center
    normed = jnp.where(valid, miss / jnp.sqrt(total), 0.0)
    a = spread / total * miss
    c = jnp.sqrt(variance / total) - 1.0
    d = jnp.where(valid, 1.0 / ((M - 1) * (spread + EPS)), 0.0)
    rows = [deviation, a, c]
    for i in range(9):
        if i == 4:
            rows.append(d)
        else:
            at = 3 + (i if i < 4 else i - 1)
            rows.append(d * (meta[at : at + 1] * TAPER[i]))
    rows.append(jnp.zeros((ROWS - M - 11, CAP), F32))
    return pack(jnp.concatenate(rows, axis=0)), normed


def init_kernel(order, value, variance, owner, cell, reach, x_hbm, z_out, meta_out, pay_out, nv_out, surface, sem):
    load = pltpu.make_async_copy(x_hbm.at[:, 0], surface, sem)
    load.start()
    my_x = lax.axis_index("gx")
    me = my_x * lax.axis_size("gy") + lax.axis_index("gy")
    flip = lax.rem(my_x, 2) == 1
    owned = jnp.concatenate([owner[pl.ds(order[k], 1), :] for k in range(NB)], axis=0) == me
    ownf = jnp.where(owned, 1.0, 0.0)
    chunks = OBS // 128
    own64 = jnp.concatenate([ownf[:, 128 * c : 128 * c + 128] for c in range(chunks)], axis=0).astype(BF16)
    upper = jnp.where(iota((128, 128), 0) < iota((128, 128), 1), 1.0, 0.0).astype(BF16)
    rows = NB * chunks
    r0, r1 = iota((rows, rows), 0), iota((rows, rows), 1)
    before = jnp.where((r1 < r0) & (((r0 - r1) & (NB - 1)) == 0), 1.0, 0.0).astype(BF16)
    base = dot(dot(before, own64).astype(BF16), jnp.ones((128, 128), BF16))
    rank64 = dot(own64, upper) + base
    rank = jnp.concatenate([rank64[NB * c : NB * c + NB] for c in range(chunks)], axis=1)
    rank = jnp.where(owned, rank, -1.0)
    slots = iota((CAP, OBS), 0).astype(F32)
    metas = []
    for k in range(NB):
        b = order[k]
        hot = jnp.where(rank[k : k + 1] == slots, 1.0, 0.0).astype(BF16)
        where = cell[pl.ds(b, 1), :]
        vh, vm, vl = split3(value[pl.ds(b, 1), :])
        rh, rm, rl = split3(variance[pl.ds(b, 1), :])
        parts = [
            reach[b].astype(F32),
            lax.shift_right_logical(where, 8).astype(F32),
            (where & 255).astype(F32),
            vh.astype(F32), vm.astype(F32), vl.astype(F32),
            rh.astype(F32), rm.astype(F32), rl.astype(F32),
            jnp.ones((1, OBS), F32),
            jnp.zeros((15, OBS), F32),
        ]
        metas.append(dot_t(jnp.concatenate(parts, axis=0).astype(BF16), hot))
    for k in range(NB):
        got = metas[k]
        rows = [got[16:17], got[10:11] + got[11:12] + got[12:13], got[13:14] + got[14:15] + got[15:16]]
        for i in range(8):
            rows.append(jnp.where(flip, got[7 - i : 8 - i], got[i : i + 1]))
        rows.append(jnp.zeros((5, CAP), F32))
        meta_out[k] = jnp.concatenate(rows, axis=0)
    cell_x = jnp.concatenate([g[8:9] for g in metas], axis=1)
    cell_y = jnp.concatenate([g[9:10] for g in metas], axis=1)
    hot_y = jnp.where(cell_y == iota((TY, NB * CAP), 0).astype(F32), 1.0, 0.0).astype(BF16)
    hot_x = jnp.where(cell_x == iota((TX, NB * CAP), 0).astype(F32), 1.0, 0.0)
    load.wait()
    group = 16
    for g in range(M // group):
        h, m, l = split3(surface[group * g : group * g + group].reshape(group * TX, TY))
        picked = dot(h, hot_y) + dot(m, hot_y) + dot(l, hot_y)
        z_out[group * g : group * g + group, : NB * CAP] = jnp.sum(
            picked.reshape(group, TX, NB * CAP) * hot_x[None], axis=1
        )
    z_out[:, NB * CAP :] = jnp.where(iota((M, 128), 0) == iota((M, 128), 1), 1.0, 0.0)
    pay, normed = make_payload(z_out[:, :CAP], meta_out[0])
    pay_out[...] = pay
    nv_out[...] = normed


def right_side(rows):
    return rows[ROW_A : ROW_A + 1] + rows[ROW_C : ROW_C + 1] * rows[:M]


def left_side(rows, direction, side):
    at = ROW_W + 3 * direction + side
    return rows[:M] * rows[at : at + 1]


def gain_of(terms):
    left = jnp.concatenate([left_side(rows, d, s) for rows, _, d, s in terms], axis=1)
    right = jnp.concatenate([r for _, r, _, _ in terms], axis=1)
    return dot_t(right, left, precision=HIGH)


def send_kernel(own, outer, sib, sib_outer, out):
    own, outer, sib, sib_outer = (unpack(r[...]) for r in (own, outer, sib, sib_outer))
    r_own, r_outer, r_sib, r_so = (right_side(r) for r in (own, outer, sib, sib_outer))
    out[0] = gain_of([(own, r_own, 1, 0), (outer, r_outer, 0, 2), (sib, r_sib, 2, 2)])
    out[1] = gain_of([(sib, r_sib, 1, 2), (own, r_own, 2, 0), (sib_outer, r_so, 0, 0)])


def same_kernel(own, outer, sib, out):
    own, outer, sib = (unpack(r[...]) for r in (own, outer, sib))
    r_own, r_outer, r_sib = (right_side(r) for r in (own, outer, sib))
    out[...] = gain_of([(own, r_own, 1, 1), (outer, r_outer, 0, 1), (sib, r_sib, 2, 1)])


def advance(z, gain):
    anomaly = z - jnp.sum(z, axis=0, keepdims=True) / M
    return z + dot(gain, anomaly, precision=HIGH)


def step_kernel(k, q0, h, g, z, meta, z_out, pay_out, nv_out):
    gain = q0[...] + h[1] + g[...]
    new = advance(z[...], gain)
    z_out[...] = new
    pay, normed = make_payload(new[:, CAP * k : CAP * k + CAP], meta[k])
    pay_out[...] = pay
    nv_out[...] = normed


def final_kernel(q0, h, g, z, x, out, mix):
    @pl.when(pl.program_id(0) == 0)
    def _():
        gain = q0[...] + h[1] + g[...]
        t = z[:, NB * CAP :]
        t = advance(t, gain)[:, :M]
        d = t - jnp.where(iota((M, M), 0) == iota((M, M), 1), 1.0, 0.0)
        dh, dl = split2(d)
        mix[...] = jnp.concatenate([dh, dh, dl], axis=1)

    w = mix[...]
    for t in range(TX // 8):
        block = x[:, 0, 8 * t : 8 * t + 8, :]
        turned = jnp.swapaxes(block, 0, 1)
        updates = []
        for i in range(8):
            h_, l_ = split2(turned[i])
            updates.append(dot(w, jnp.concatenate([h_, l_, h_], axis=0))[None])
        out[:, 0, 8 * t : 8 * t + 8, :] = block + jnp.swapaxes(jnp.concatenate(updates, axis=0), 0, 1)


def rank_kernel(owner, out):
    chunks = OBS // 128
    upper = jnp.where(iota((128, 128), 0) < iota((128, 128), 1), 1.0, 0.0).astype(BF16)
    tiles = iota((TILES, 128), 0)
    for b in range(NB):
        base = jnp.zeros((TILES, 1), F32)
        for c in range(chunks):
            at = slice(128 * c, 128 * c + 128)
            hot = jnp.where(owner[b : b + 1, at] == tiles, 1.0, 0.0)
            rank = dot(hot.astype(BF16), upper) + base
            out[b : b + 1, at] = jnp.sum(hot * rank, axis=0, keepdims=True)
            base = base + jnp.sum(hot, axis=1, keepdims=True)


def place_kernel(order, owner, rank, nv, out):
    turned = nv[...].T
    tiles = iota((TILES, OBS), 0)
    slots = iota((CAP, OBS), 0).astype(F32)
    for k in range(NB):
        b = order[k]
        hot = jnp.where(owner[pl.ds(b, 1), :] == tiles, 1.0, 0.0).astype(BF16)
        h, m, l = split3(turned[CAP * k : CAP * k + CAP])
        got = dot(h, hot) + dot(m, hot) + dot(l, hot)
        mine = rank[pl.ds(b, 1), :] == slots
        out[pl.ds(b, 1), :] = jnp.sum(jnp.where(mine, got, 0.0), axis=0, keepdims=True)


VMEM = pl.BlockSpec(memory_space=pltpu.VMEM)
SMEM = pl.BlockSpec(memory_space=pltpu.SMEM)
ANY = pl.BlockSpec(memory_space=pl.ANY)


def shape(*dims):
    return jax.ShapeDtypeStruct(dims, F32)


def swap(count, first):
    pairs = []
    for i in range(first, count - 1, 2):
        pairs += [(i, i + 1), (i + 1, i)]
    return pairs


def diagonal(width, height):
    pairs = []
    for x in range(0, width, 2):
        for k in range(1, height):
            low, high = x * height + k, (x + 1) * height + k - 1
            pairs += [(low, high), (high, low)]
    return pairs


def local(ensemble, obs_value, obs_variance, obs_owner, obs_cell, obs_reach, batch_order):
    params = pltpu.CompilerParams(vmem_limit_bytes=48 * 2**20)
    call = functools.partial(pl.pallas_call, compiler_params=params)
    width, height = lax.axis_size("gx"), lax.axis_size("gy")
    core, outward, diag = swap(width, 0), swap(width, 1), diagonal(width, height)
    z, meta, pay, nv = call(
        init_kernel,
        out_shape=(shape(M, NB * CAP + 128), shape(NB, 16, CAP), shape(ROWS // 2, 128), shape(1, CAP)),
        in_specs=[SMEM, VMEM, VMEM, VMEM, VMEM, VMEM, ANY],
        out_specs=(VMEM,) * 4,
        scratch_shapes=[pltpu.VMEM((M, TX, TY), F32), pltpu.SemaphoreType.DMA],
        name="init",
    )(batch_order, obs_value, obs_variance, obs_owner, obs_cell, jnp.swapaxes(obs_reach, 1, 2), ensemble)
    rank = call(rank_kernel, out_shape=shape(NB, OBS), in_specs=[VMEM], out_specs=VMEM, name="rank")(obs_owner)
    normed = [nv]
    for k in range(NB):
        outer = lax.ppermute(pay, "gx", outward)
        sib = lax.ppermute(pay, "gx", core)
        sib_outer = lax.ppermute(outer, "gx", core)
        send = call(send_kernel, out_shape=shape(2, M, M), in_specs=[VMEM] * 4, out_specs=VMEM, name="send")(
            pay, outer, sib, sib_outer
        )
        h = lax.ppermute(send, ("gx", "gy"), diag)
        q0 = call(same_kernel, out_shape=shape(M, M), in_specs=[VMEM] * 3, out_specs=VMEM, name="same")(pay, outer, sib)
        g = lax.ppermute(h[0], "gx", core)
        if k + 1 < NB:
            z, pay, nv = call(
                functools.partial(step_kernel, k + 1),
                out_shape=(shape(M, NB * CAP + 128), shape(ROWS // 2, 128), shape(1, CAP)),
                in_specs=[VMEM] * 5,
                out_specs=(VMEM,) * 3,
                name="step",
            )(q0, h, g, z, meta)
            normed.append(nv)
    small = lambda *dims: pl.BlockSpec(dims, lambda i: (0,) * len(dims))
    slab = pl.BlockSpec((M, 1, TX, TY), lambda i: (0, i, 0, 0))
    state = call(
        final_kernel,
        out_shape=shape(M, LEV, TX, TY),
        grid=(LEV,),
        in_specs=[small(M, M), small(2, M, M), small(M, M), small(M, NB * CAP + 128), slab],
        out_specs=slab,
        scratch_shapes=[pltpu.VMEM((M, 3 * M), BF16)],
        name="final",
    )(q0, h, g, z, ensemble)
    mine = jnp.concatenate(normed, axis=1)
    everyone = lax.all_to_all(jnp.broadcast_to(mine, (TILES, NB * CAP)), ("gx", "gy"), 0, 0, tiled=True)
    innovation = call(
        place_kernel,
        out_shape=shape(NB, OBS),
        in_specs=[SMEM, VMEM, VMEM, VMEM],
        out_specs=VMEM,
        name="place",
    )(batch_order, obs_owner, rank, everyone)
    return state, innovation


def solution(mesh):
    placed = (P(None, None, "gx", "gy"), P(), P(), P(), P(), P(), P())
    return jax.shard_map(
        local,
        mesh=mesh,
        in_specs=placed,
        out_specs=(P(None, None, "gx", "gy"), P()),
        check_vma=False,
    )
```

time: 443 us -> 98.1 us (0.22); the launches traced: 434 us -> 97.4 us
  local copies, waits for them, and re-layouts: 112 us -> 5.39 us
  matrix products: 97.8 us -> 0 us
  other arithmetic: 88.1 us -> 0.08 us
  blocking collectives: 75.1 us -> 0 us
  Pallas kernels: 0 us -> 24 us
  waiting for transfers between devices: 3.86 us -> 21.3 us
  between operations: 9.49 us -> 0.89 us
    dot_general x8 -> x0, matrix products: 97.8 us -> none  [the longest x4 94.4 us: local(): update = jnp.dot(gain.T, anomaly, precision=lax.Precision.HIGHEST)]
    psum x1 -> x0, blocking collectives: 75.1 us -> none  [local(): innovation = lax.psum(innovation, ('gx', 'gy'))]
    unnamed x10 -> x17, local copies, waits for them, and re-layouts: 64 us -> 4.65 us
    sub x3 -> x0, other arithmetic: 29.1 us -> none  [local(): anomaly = (state - center[None]).reshape(members, -1)]
    gather x24 -> x0, local copies, waits for them, and re-layouts: 27.2 us -> none  [the longest x4 11.1 us: local(): prior = jnp.take(surface, cells, axis=1)]
    pallas_call x0 -> x15, Pallas kernels: none -> 24 us  [the longest x1 11.3 us: local(): call(final_kernel, out_shape=shape(M, LEV, TX, TY), grid=(LEV,), in_specs...]
    sort x4 -> x0, other arithmetic: 20.2 us -> none  [local(): picked = jnp.argsort(order_key)[:capacity]]
    ppermute x16 -> x20, starting transfers between devices: 47.8 us -> 30.2 us  [the longest x4 14.9 us: local(): outer = lax.ppermute(pay, 'gx', outward)]
  transfers between devices with their start and end apart: 16 -> 21, of which waited for: 3 -> 14; matrix products, arithmetic and copies ran while one was open for 29% -> 1% of each run, Pallas kernels for 0% -> 15%
where the time goes in v1:
time: 98.1 us; the launch traced here: 97.4 us
  starting transfers between devices  45.7 us (47%)
  Pallas kernels  24 us (24%)
  waiting for transfers between devices  21.3 us (22%)
  local copies, waits for them, and re-layouts  5.39 us (5%)
    all_to_all x1, starting transfers between devices, local(): lax.all_to_all(jnp.broadcast_to(mine, (TILES, NB * CAP)), ('gx', 'gy'), 0...  15.6 us
    ppermute x4, starting transfers between devices, local(): outer = lax.ppermute(pay, 'gx', outward)  14.9 us
    ppermute x4, starting transfers between devices, local(): h = lax.ppermute(send, ('gx', 'gy'), diag)  13.5 us
    pallas_call x1, Pallas kernels, local(): call(final_kernel, out_shape=shape(M, LEV, TX, TY), grid=(LEV,), in_specs...  11.3 us
    ppermute x4, waiting for transfers between devices, local(): h = lax.ppermute(send, ('gx', 'gy'), diag)  7.77 us
    ppermute x4, waiting for transfers between devices, local(): outer = lax.ppermute(pay, 'gx', outward)  6.18 us
    ppermute x4, waiting for transfers between devices, local(): sib_outer = lax.ppermute(outer, 'gx', core)  4.76 us
    unnamed x17, local copies, waits for them, and re-layouts  4.65 us
  transfers between devices with their start and end apart: 21, of which 14 were waited for; matrix products, arithmetic and copies ran while one was open for 1% of the time, Pallas kernels for 15%

profile of v1, /device:TPU:1, one launch (start us, length us, event | category | flops | bytes accessed | tf_op | source)
XLA Modules:
  0.0 97.4 jit_solution(13781932973502032875)
XLA Ops:
  0.6 0.7 copy-done
  1.4 0.9 copy-done.2
  2.3 0.8 copy-done.3
  3.1 0.8 copy-done.4
  3.9 0.8 copy-done.5
  4.6 0.7 copy-done.6
  5.3 4.4 %init.1 = (f32[80,384]{1,0:T(8,128)S(1)}, f32[4,16,64]{2,1,0:T(8,128)S(1)}, f32[48,128]{1,0:T(8,128)S(1)}, f32[1,64]{1,0:T(1,128)S(1)}) custom-call(s32[4]{0:T(128)S(1)} %copy-done.6, f32[4,2048]{1,0:T(4,128)S(1)} %copy-done.3, f32[4,2048]{1,0:T(4,128)S(1)} %copy-done.4, s32[4,2048]{1,0:T(4,128)S(1)} %copy-done, s32[4,2048]{1,0:T(4,128)S(1)} %copy-done.5, ...), custom_call_target="tpu_custom_call" | custom-call | tf_op jit(solution)/shard_map/init/pallas_call | solution.py:267
  9.7 4.6 %collective-permute-start = (f32[48,128]{1,0:T(8,128)S(1)}, f32[48,128]{1,0:T(8,128)S(1)}, u32[]{:S(2)}, u32[]{:S(2)}) collective-permute-start(f32[48,128]{1,0:T(8,128)S(1)} %get-tuple-element.15.own), channel_id=1, source_target_pairs={{16,32},{32,16},{48,64},{64,48},{80,96},{96,80},{17,33},{33,17},{4... | collective-permute-start | bytes 73736 | tf_op jit(solution)/shard_map/ppermute | solution.py:278
  14.3 0.1 collective-permute-start.1
  14.4 1.4 %collective-permute-done.outer = f32[48,128]{1,0:T(8,128)S(1)} collective-permute-done((f32[48,128]{1,0:T(8,128)S(1)}, f32[48,128]{1,0:T(8,128)S(1)}, u32[]{:S(2)}, u32[]{:S(2)}) %collective-permute-start) | collective-permute-done | bytes 24608 | tf_op jit(solution)/shard_map/ppermute | solution.py:278
  15.8 0.0 collective-permute-start.2
  15.8 0.0 collective-permute-done.1.sib
  15.8 1.2 %collective-permute-done.2.sib_outer = f32[48,128]{1,0:T(8,128)S(1)} collective-permute-done((f32[48,128]{1,0:T(8,128)S(1)}, f32[48,128]{1,0:T(8,128)S(1)}, u32[]{:S(2)}, u32[]{:S(2)}) %collective-permute-start.2) | collective-permute-done | bytes 24608 | tf_op jit(solution)/shard_map/ppermute | solution.py:280
  17.0 0.4 send.4
  17.4 3.2 %collective-permute-start.3 = (f32[2,80,80]{2,1,0:T(8,128)S(1)}, f32[2,80,80]{2,1,0:T(8,128)S(1)}, u32[]{:S(2)}, u32[]{:S(2)}) collective-permute-start(f32[2,80,80]{2,1,0:T(8,128)S(1)} %send.4), channel_id=1, source_target_pairs={{1,16},{16,1},{2,17},{17,2},{3,18},{18,3},{4,19},{19,4},{5,20},{20... | collective-permute-start | bytes 153608 | tf_op jit(solution)/shard_map/ppermute | solution.py:284
  20.6 2.6 %collective-permute-done.3.h = f32[2,80,80]{2,1,0:T(8,128)S(1)} collective-permute-done((f32[2,80,80]{2,1,0:T(8,128)S(1)}, f32[2,80,80]{2,1,0:T(8,128)S(1)}, u32[]{:S(2)}, u32[]{:S(2)}) %collective-permute-start.3) | collective-permute-done | bytes 51232 | tf_op jit(solution)/shard_map/ppermute | solution.py:284
  23.2 0.0 collective-permute-start.4
  23.2 0.4 same.4.q0
  23.6 0.9 collective-permute-done.4.g
  24.4 0.5 step.3
  24.9 3.5 %collective-permute-start.5 = (f32[48,128]{1,0:T(8,128)S(1)}, f32[48,128]{1,0:T(8,128)S(1)}, u32[]{:S(2)}, u32[]{:S(2)}) collective-permute-start(f32[48,128]{1,0:T(8,128)S(1)} %get-tuple-element.18.own), channel_id=1, source_target_pairs={{16,32},{32,16},{48,64},{64,48},{80,96},{96,80},{17,33},{33,17},{4... | collective-permute-start | bytes 73736 | tf_op jit(solution)/shard_map/ppermute | solution.py:278
  28.3 0.1 collective-permute-start.6
  28.4 1.6 %collective-permute-done.5.outer = f32[48,128]{1,0:T(8,128)S(1)} collective-permute-done((f32[48,128]{1,0:T(8,128)S(1)}, f32[48,128]{1,0:T(8,128)S(1)}, u32[]{:S(2)}, u32[]{:S(2)}) %collective-permute-start.5) | collective-permute-done | bytes 24608 | tf_op jit(solution)/shard_map/ppermute | solution.py:278
  30.0 0.0 collective-permute-start.7
  30.0 0.0 collective-permute-done.6.sib
  30.0 1.2 %collective-permute-done.7.sib_outer = f32[48,128]{1,0:T(8,128)S(1)} collective-permute-done((f32[48,128]{1,0:T(8,128)S(1)}, f32[48,128]{1,0:T(8,128)S(1)}, u32[]{:S(2)}, u32[]{:S(2)}) %collective-permute-start.7) | collective-permute-done | bytes 24608 | tf_op jit(solution)/shard_map/ppermute | solution.py:280
  31.2 0.4 send.5
  31.7 3.2 %collective-permute-start.8 = (f32[2,80,80]{2,1,0:T(8,128)S(1)}, f32[2,80,80]{2,1,0:T(8,128)S(1)}, u32[]{:S(2)}, u32[]{:S(2)}) collective-permute-start(f32[2,80,80]{2,1,0:T(8,128)S(1)} %send.5), channel_id=1, source_target_pairs={{1,16},{16,1},{2,17},{17,2},{3,18},{18,3},{4,19},{19,4},{5,20},{20... | collective-permute-start | bytes 153608 | tf_op jit(solution)/shard_map/ppermute | solution.py:284
  34.8 2.6 %collective-permute-done.8.h = f32[2,80,80]{2,1,0:T(8,128)S(1)} collective-permute-done((f32[2,80,80]{2,1,0:T(8,128)S(1)}, f32[2,80,80]{2,1,0:T(8,128)S(1)}, u32[]{:S(2)}, u32[]{:S(2)}) %collective-permute-start.8) | collective-permute-done | bytes 51232 | tf_op jit(solution)/shard_map/ppermute | solution.py:284
  37.4 0.0 collective-permute-start.9
  37.4 0.4 same.5.q0
  37.8 0.9 collective-permute-done.9.g
  38.6 0.4 step.4
  39.0 3.4 %collective-permute-start.10 = (f32[48,128]{1,0:T(8,128)S(1)}, f32[48,128]{1,0:T(8,128)S(1)}, u32[]{:S(2)}, u32[]{:S(2)}) collective-permute-start(f32[48,128]{1,0:T(8,128)S(1)} %get-tuple-element.20.own), channel_id=1, source_target_pairs={{16,32},{32,16},{48,64},{64,48},{80,96},{96,80},{17,33},{33,17},{4... | collective-permute-start | bytes 73736 | tf_op jit(solution)/shard_map/ppermute | solution.py:278
  42.5 0.1 collective-permute-start.11
  42.6 1.6 %collective-permute-done.10.outer = f32[48,128]{1,0:T(8,128)S(1)} collective-permute-done((f32[48,128]{1,0:T(8,128)S(1)}, f32[48,128]{1,0:T(8,128)S(1)}, u32[]{:S(2)}, u32[]{:S(2)}) %collective-permute-start.10) | collective-permute-done | bytes 24608 | tf_op jit(solution)/shard_map/ppermute | solution.py:278
  44.2 0.0 collective-permute-start.12
  44.2 0.0 collective-permute-done.11.sib
  44.2 1.2 %collective-permute-done.12.sib_outer = f32[48,128]{1,0:T(8,128)S(1)} collective-permute-done((f32[48,128]{1,0:T(8,128)S(1)}, f32[48,128]{1,0:T(8,128)S(1)}, u32[]{:S(2)}, u32[]{:S(2)}) %collective-permute-start.12) | collective-permute-done | bytes 24608 | tf_op jit(solution)/shard_map/ppermute | solution.py:280
  45.4 0.4 send.6
  45.8 3.2 %collective-permute-start.13 = (f32[2,80,80]{2,1,0:T(8,128)S(1)}, f32[2,80,80]{2,1,0:T(8,128)S(1)}, u32[]{:S(2)}, u32[]{:S(2)}) collective-permute-start(f32[2,80,80]{2,1,0:T(8,128)S(1)} %send.6), channel_id=1, source_target_pairs={{1,16},{16,1},{2,17},{17,2},{3,18},{18,3},{4,19},{19,4},{5,20},{20... | collective-permute-start | bytes 153608 | tf_op jit(solution)/shard_map/ppermute | solution.py:284
  49.0 2.6 %collective-permute-done.13.h = f32[2,80,80]{2,1,0:T(8,128)S(1)} collective-permute-done((f32[2,80,80]{2,1,0:T(8,128)S(1)}, f32[2,80,80]{2,1,0:T(8,128)S(1)}, u32[]{:S(2)}, u32[]{:S(2)}) %collective-permute-start.13) | collective-permute-done | bytes 51232 | tf_op jit(solution)/shard_map/ppermute | solution.py:284
  51.6 0.0 collective-permute-start.14
  51.6 0.4 same.6.q0
  51.9 0.9 collective-permute-done.14.g
  52.8 0.5 step.5
  53.2 3.5 %collective-permute-start.15 = (f32[48,128]{1,0:T(8,128)S(1)}, f32[48,128]{1,0:T(8,128)S(1)}, u32[]{:S(2)}, u32[]{:S(2)}) collective-permute-start(f32[48,128]{1,0:T(8,128)S(1)} %get-tuple-element.22.own), channel_id=1, source_target_pairs={{16,32},{32,16},{48,64},{64,48},{80,96},{96,80},{17,33},{33,17},{4... | collective-permute-start | bytes 73736 | tf_op jit(solution)/shard_map/ppermute | solution.py:278
  56.7 0.1 collective-permute-start.16
  56.8 1.6 %collective-permute-done.15.outer = f32[48,128]{1,0:T(8,128)S(1)} collective-permute-done((f32[48,128]{1,0:T(8,128)S(1)}, f32[48,128]{1,0:T(8,128)S(1)}, u32[]{:S(2)}, u32[]{:S(2)}) %collective-permute-start.15) | collective-permute-done | bytes 24608 | tf_op jit(solution)/shard_map/ppermute | solution.py:278
  58.4 0.0 collective-permute-start.17
  58.4 0.0 collective-permute-done.16.sib
  58.4 1.2 %collective-permute-done.17.sib_outer = f32[48,128]{1,0:T(8,128)S(1)} collective-permute-done((f32[48,128]{1,0:T(8,128)S(1)}, f32[48,128]{1,0:T(8,128)S(1)}, u32[]{:S(2)}, u32[]{:S(2)}) %collective-permute-start.17) | collective-permute-done | bytes 24608 | tf_op jit(solution)/shard_map/ppermute | solution.py:280
  59.6 0.4 send.7
  60.0 4.0 %collective-permute-start.18 = (f32[2,80,80]{2,1,0:T(8,128)S(1)}, f32[2,80,80]{2,1,0:T(8,128)S(1)}, u32[]{:S(2)}, u32[]{:S(2)}) collective-permute-start(f32[2,80,80]{2,1,0:T(8,128)S(1)} %send.7), channel_id=1, source_target_pairs={{1,16},{16,1},{2,17},{17,2},{3,18},{18,3},{4,19},{19,4},{5,20},{20... | collective-permute-start | bytes 153608 | tf_op jit(solution)/shard_map/ppermute | solution.py:284
  64.1 0.1 pad_maximum_fusion
  64.1 0.7 broadcast_in_dim.2
  64.9 15.6 %all-to-all-start = ((f32[128,1,256]{2,1,0:T(1,128)}), f32[128,1,256]{2,1,0:T(1,128)S(1)}, u32[]{:S(2)}, u32[]{:S(2)}) async-start(f32[128,1,256]{2,1,0:T(1,128)} %broadcast_in_dim.2), calls=%async_computation | async-start | bytes 262144 | tf_op jit(solution)/shard_map/all_to_all | solution.py:308
  80.5 1.3 %collective-permute-start.19 = (f32[80,80]{1,0:T(8,128)S(1)}, f32[80,80]{1,0:T(8,128)S(1)}, u32[]{:S(2)}, u32[]{:S(2)}) collective-permute-start(f32[80,80]{1,0:T(8,128)S(1)} %slice_bitcast_fusion), channel_id=1, source_target_pairs={{0,16},{16,0},{32,48},{48,32},{64,80},{80,64},{96,112},{112,96},{1... | collective-permute-start | bytes 76808 | tf_op jit(solution)/shard_map/ppermute | solution.py:286
  81.8 1.5 %rank.1 = f32[4,2048]{1,0:T(4,128)S(1)} custom-call(s32[4,2048]{1,0:T(4,128)S(1)} %copy-done.1), custom_call_target="tpu_custom_call" | custom-call | tf_op jit(solution)/shard_map/rank/pallas_call | solution.py:275
  83.2 0.4 same.7.q0
  83.6 0.0 collective-permute-done.19.g
  83.6 0.0 copy-start.7
  83.6 11.3 %final.1 = f32[80,4,32,256]{3,2,1,0:T(8,128)} custom-call(f32[80,80]{1,0:T(8,128)S(1)} %same.7.q0, f32[2,80,80]{2,1,0:T(8,128)S(1)} %collective-permute-done.18.h, f32[80,80]{1,0:T(8,128)S(1)} %collective-permute-done.19.g, f32[80,384]{1,0:T(8,128)S(1)} %get-tuple-element.23.z, f32[80,4,32,256]{3,2,1,0:T(8,128)} %x.1), custom_call_target="tpu_custom_call" | custom-call | tf_op jit(solution)/shard_map/final/pallas_call | solution.py:298
  95.0 2.4 %place.1 = f32[4,2048]{1,0:T(4,128)} custom-call(s32[4]{0:T(128)S(1)} %copy-done.7, s32[4,2048]{1,0:T(4,128)S(1)} %copy-done.1, f32[4,2048]{1,0:T(4,128)S(1)} %rank.1, f32[128,256]{1,0:T(8,128)S(1)} %bitcast.13), custom_call_target="tpu_custom_call" | custom-call | tf_op jit(solution)/shard_map/place/pallas_call | solution.py:309
  (16 shorter events, 0.0 us)
Async XLA Ops:
  0.6 0.8 copy-start
  1.4 0.9 copy-start.2
  2.3 0.8 copy-start.3
  3.1 0.8 copy-start.4
  3.9 0.8 copy-start.5
  4.6 0.7 copy-start.6
  5.3 76.5 %copy-start.1 = (s32[4,2048]{1,0:T(4,128)S(1)}, s32[4,2048]{1,0:T(4,128)}, u32[]{:S(2)}) copy-start(s32[4,2048]{1,0:T(4,128)} %owner.5) | copy-start | bytes 98308
  9.7 6.1 %collective-permute-start = (f32[48,128]{1,0:T(8,128)S(1)}, f32[48,128]{1,0:T(8,128)S(1)}, u32[]{:S(2)}, u32[]{:S(2)}) collective-permute-start(f32[48,128]{1,0:T(8,128)S(1)} %get-tuple-element.15.own), channel_id=1, source_target_pairs={{16,32},{32,16},{48,64},{64,48},{80,96},{96,80},{17,33},{33,17},{4... | collective-permute-start | bytes 73736 | tf_op jit(solution)/shard_map/ppermute | solution.py:278
  14.3 1.5 %collective-permute-start.1 = (f32[48,128]{1,0:T(8,128)S(1)}, f32[48,128]{1,0:T(8,128)S(1)}, u32[]{:S(2)}, u32[]{:S(2)}) collective-permute-start(f32[48,128]{1,0:T(8,128)S(1)} %get-tuple-element.15.own), channel_id=1, source_target_pairs={{0,16},{16,0},{32,48},{48,32},{64,80},{80,64},{96,112},{112,96},{1... | collective-permute-start | bytes 73736 | tf_op jit(solution)/shard_map/ppermute | solution.py:279
  15.8 1.2 %collective-permute-start.2 = (f32[48,128]{1,0:T(8,128)S(1)}, f32[48,128]{1,0:T(8,128)S(1)}, u32[]{:S(2)}, u32[]{:S(2)}) collective-permute-start(f32[48,128]{1,0:T(8,128)S(1)} %collective-permute-done.outer), channel_id=1, source_target_pairs={{0,16},{16,0},{32,48},{48,32},{64,80},{80,64},{96,112},{112,96},{1... | collective-permute-start | bytes 73736 | tf_op jit(solution)/shard_map/ppermute | solution.py:280
  17.4 5.8 %collective-permute-start.3 = (f32[2,80,80]{2,1,0:T(8,128)S(1)}, f32[2,80,80]{2,1,0:T(8,128)S(1)}, u32[]{:S(2)}, u32[]{:S(2)}) collective-permute-start(f32[2,80,80]{2,1,0:T(8,128)S(1)} %send.4), channel_id=1, source_target_pairs={{1,16},{16,1},{2,17},{17,2},{3,18},{18,3},{4,19},{19,4},{5,20},{20... | collective-permute-start | bytes 153608 | tf_op jit(solution)/shard_map/ppermute | solution.py:284
  23.2 1.2 %collective-permute-start.4 = (f32[80,80]{1,0:T(8,128)S(1)}, f32[80,80]{1,0:T(8,128)S(1)}, u32[]{:S(2)}, u32[]{:S(2)}) collective-permute-start(f32[80,80]{1,0:T(8,128)S(1)} %slice_bitcast_fusion.3), channel_id=1, source_target_pairs={{0,16},{16,0},{32,48},{48,32},{64,80},{80,64},{96,112},{112,96},{1... | collective-permute-start | bytes 76808 | tf_op jit(solution)/shard_map/ppermute | solution.py:286
  24.9 5.1 %collective-permute-start.5 = (f32[48,128]{1,0:T(8,128)S(1)}, f32[48,128]{1,0:T(8,128)S(1)}, u32[]{:S(2)}, u32[]{:S(2)}) collective-permute-start(f32[48,128]{1,0:T(8,128)S(1)} %get-tuple-element.18.own), channel_id=1, source_target_pairs={{16,32},{32,16},{48,64},{64,48},{80,96},{96,80},{17,33},{33,17},{4... | collective-permute-start | bytes 73736 | tf_op jit(solution)/shard_map/ppermute | solution.py:278
  28.3 1.7 %collective-permute-start.6 = (f32[48,128]{1,0:T(8,128)S(1)}, f32[48,128]{1,0:T(8,128)S(1)}, u32[]{:S(2)}, u32[]{:S(2)}) collective-permute-start(f32[48,128]{1,0:T(8,128)S(1)} %get-tuple-element.18.own), channel_id=1, source_target_pairs={{0,16},{16,0},{32,48},{48,32},{64,80},{80,64},{96,112},{112,96},{1... | collective-permute-start | bytes 73736 | tf_op jit(solution)/shard_map/ppermute | solution.py:279
  30.0 1.2 %collective-permute-start.7 = (f32[48,128]{1,0:T(8,128)S(1)}, f32[48,128]{1,0:T(8,128)S(1)}, u32[]{:S(2)}, u32[]{:S(2)}) collective-permute-start(f32[48,128]{1,0:T(8,128)S(1)} %collective-permute-done.5.outer), channel_id=1, source_target_pairs={{0,16},{16,0},{32,48},{48,32},{64,80},{80,64},{96,112},{112,96},{1... | collective-permute-start | bytes 73736 | tf_op jit(solution)/shard_map/ppermute | solution.py:280
  31.7 5.8 %collective-permute-start.8 = (f32[2,80,80]{2,1,0:T(8,128)S(1)}, f32[2,80,80]{2,1,0:T(8,128)S(1)}, u32[]{:S(2)}, u32[]{:S(2)}) collective-permute-start(f32[2,80,80]{2,1,0:T(8,128)S(1)} %send.5), channel_id=1, source_target_pairs={{1,16},{16,1},{2,17},{17,2},{3,18},{18,3},{4,19},{19,4},{5,20},{20... | collective-permute-start | bytes 153608 | tf_op jit(solution)/shard_map/ppermute | solution.py:284
  37.4 1.2 %collective-permute-start.9 = (f32[80,80]{1,0:T(8,128)S(1)}, f32[80,80]{1,0:T(8,128)S(1)}, u32[]{:S(2)}, u32[]{:S(2)}) collective-permute-start(f32[80,80]{1,0:T(8,128)S(1)} %slice_bitcast_fusion.2), channel_id=1, source_target_pairs={{0,16},{16,0},{32,48},{48,32},{64,80},{80,64},{96,112},{112,96},{1... | collective-permute-start | bytes 76808 | tf_op jit(solution)/shard_map/ppermute | solution.py:286
  39.0 5.1 %collective-permute-start.10 = (f32[48,128]{1,0:T(8,128)S(1)}, f32[48,128]{1,0:T(8,128)S(1)}, u32[]{:S(2)}, u32[]{:S(2)}) collective-permute-start(f32[48,128]{1,0:T(8,128)S(1)} %get-tuple-element.20.own), channel_id=1, source_target_pairs={{16,32},{32,16},{48,64},{64,48},{80,96},{96,80},{17,33},{33,17},{4... | collective-permute-start | bytes 73736 | tf_op jit(solution)/shard_map/ppermute | solution.py:278
  42.5 1.7 %collective-permute-start.11 = (f32[48,128]{1,0:T(8,128)S(1)}, f32[48,128]{1,0:T(8,128)S(1)}, u32[]{:S(2)}, u32[]{:S(2)}) collective-permute-start(f32[48,128]{1,0:T(8,128)S(1)} %get-tuple-element.20.own), channel_id=1, source_target_pairs={{0,16},{16,0},{32,48},{48,32},{64,80},{80,64},{96,112},{112,96},{1... | collective-permute-start | bytes 73736 | tf_op jit(solution)/shard_map/ppermute | solution.py:279
  44.2 1.2 %collective-permute-start.12 = (f32[48,128]{1,0:T(8,128)S(1)}, f32[48,128]{1,0:T(8,128)S(1)}, u32[]{:S(2)}, u32[]{:S(2)}) collective-permute-start(f32[48,128]{1,0:T(8,128)S(1)} %collective-permute-done.10.outer), channel_id=1, source_target_pairs={{0,16},{16,0},{32,48},{48,32},{64,80},{80,64},{96,112},{112,96},{1... | collective-permute-start | bytes 73736 | tf_op jit(solution)/shard_map/ppermute | solution.py:280
  45.8 5.8 %collective-permute-start.13 = (f32[2,80,80]{2,1,0:T(8,128)S(1)}, f32[2,80,80]{2,1,0:T(8,128)S(1)}, u32[]{:S(2)}, u32[]{:S(2)}) collective-permute-start(f32[2,80,80]{2,1,0:T(8,128)S(1)} %send.6), channel_id=1, source_target_pairs={{1,16},{16,1},{2,17},{17,2},{3,18},{18,3},{4,19},{19,4},{5,20},{20... | collective-permute-start | bytes 153608 | tf_op jit(solution)/shard_map/ppermute | solution.py:284
  51.6 1.2 %collective-permute-start.14 = (f32[80,80]{1,0:T(8,128)S(1)}, f32[80,80]{1,0:T(8,128)S(1)}, u32[]{:S(2)}, u32[]{:S(2)}) collective-permute-start(f32[80,80]{1,0:T(8,128)S(1)} %slice_bitcast_fusion.1), channel_id=1, source_target_pairs={{0,16},{16,0},{32,48},{48,32},{64,80},{80,64},{96,112},{112,96},{1... | collective-permute-start | bytes 76808 | tf_op jit(solution)/shard_map/ppermute | solution.py:286
  53.2 5.1 %collective-permute-start.15 = (f32[48,128]{1,0:T(8,128)S(1)}, f32[48,128]{1,0:T(8,128)S(1)}, u32[]{:S(2)}, u32[]{:S(2)}) collective-permute-start(f32[48,128]{1,0:T(8,128)S(1)} %get-tuple-element.22.own), channel_id=1, source_target_pairs={{16,32},{32,16},{48,64},{64,48},{80,96},{96,80},{17,33},{33,17},{4... | collective-permute-start | bytes 73736 | tf_op jit(solution)/shard_map/ppermute | solution.py:278
  56.7 1.7 %collective-permute-start.16 = (f32[48,128]{1,0:T(8,128)S(1)}, f32[48,128]{1,0:T(8,128)S(1)}, u32[]{:S(2)}, u32[]{:S(2)}) collective-permute-start(f32[48,128]{1,0:T(8,128)S(1)} %get-tuple-element.22.own), channel_id=1, source_target_pairs={{0,16},{16,0},{32,48},{48,32},{64,80},{80,64},{96,112},{112,96},{1... | collective-permute-start | bytes 73736 | tf_op jit(solution)/shard_map/ppermute | solution.py:279
  58.4 1.2 %collective-permute-start.17 = (f32[48,128]{1,0:T(8,128)S(1)}, f32[48,128]{1,0:T(8,128)S(1)}, u32[]{:S(2)}, u32[]{:S(2)}) collective-permute-start(f32[48,128]{1,0:T(8,128)S(1)} %collective-permute-done.15.outer), channel_id=1, source_target_pairs={{0,16},{16,0},{32,48},{48,32},{64,80},{80,64},{96,112},{112,96},{1... | collective-permute-start | bytes 73736 | tf_op jit(solution)/shard_map/ppermute | solution.py:280
  60.0 20.4 %collective-permute-start.18 = (f32[2,80,80]{2,1,0:T(8,128)S(1)}, f32[2,80,80]{2,1,0:T(8,128)S(1)}, u32[]{:S(2)}, u32[]{:S(2)}) collective-permute-start(f32[2,80,80]{2,1,0:T(8,128)S(1)} %send.7), channel_id=1, source_target_pairs={{1,16},{16,1},{2,17},{17,2},{3,18},{18,3},{4,19},{19,4},{5,20},{20... | collective-permute-start | bytes 153608 | tf_op jit(solution)/shard_map/ppermute | solution.py:284
  64.9 30.1 %all-to-all-start = ((f32[128,1,256]{2,1,0:T(1,128)}), f32[128,1,256]{2,1,0:T(1,128)S(1)}, u32[]{:S(2)}, u32[]{:S(2)}) async-start(f32[128,1,256]{2,1,0:T(1,128)} %broadcast_in_dim.2), calls=%async_computation | async-start | bytes 262144 | tf_op jit(solution)/shard_map/all_to_all | solution.py:308
  80.5 3.2 %collective-permute-start.19 = (f32[80,80]{1,0:T(8,128)S(1)}, f32[80,80]{1,0:T(8,128)S(1)}, u32[]{:S(2)}, u32[]{:S(2)}) collective-permute-start(f32[80,80]{1,0:T(8,128)S(1)} %slice_bitcast_fusion), channel_id=1, source_target_pairs={{0,16},{16,0},{32,48},{48,32},{64,80},{80,64},{96,112},{112,96},{1... | collective-permute-start | bytes 76808 | tf_op jit(solution)/shard_map/ppermute | solution.py:286
  83.6 11.4 %copy-start.7 = (s32[4]{0:T(128)S(1)}, s32[4]{0:T(128)}, u32[]{:S(2)}) copy-start(s32[4]{0:T(128)} %order.3) | copy-start | bytes 52

commit v2 on v1

v2 whole, which is shorter than its diff:
```python
import functools

import jax
import jax.numpy as jnp
from jax import lax
from jax.experimental import pallas as pl
from jax.experimental.pallas import tpu as pltpu
from jax.sharding import PartitionSpec as P

M = 80
LEV = 4
NB = 4
TX = 32
TY = 256
CAP = 64
OBS = 2048
TILES = 128
EPS = 1e-05
F32 = jnp.float32
BF16 = jnp.bfloat16
HIGH = lax.Precision.HIGHEST

ROW_A = M
ROW_C = M + 1
ROW_W = M + 2
ROWS = 96
TAPER = (0.25, 0.5, 0.25, 0.5, 1.0, 0.5, 0.25, 0.5, 0.25)


def split2(x):
    high = x.astype(BF16)
    return high, (x - high.astype(F32)).astype(BF16)


def split3(x):
    high = x.astype(BF16)
    rest = x - high.astype(F32)
    mid = rest.astype(BF16)
    return high, mid, (rest - mid.astype(F32)).astype(BF16)


def iota(shape, dim):
    return lax.broadcasted_iota(jnp.int32, shape, dim)


def dot(a, b, **kw):
    return jnp.dot(a, b, preferred_element_type=F32, **kw)


def dot_t(a, b, **kw):
    return lax.dot_general(a, b, (((1,), (1,)), ((), ())), preferred_element_type=F32, **kw)


def pack(rows):
    return jnp.concatenate([rows[: ROWS // 2], rows[ROWS // 2 :]], axis=1)


def unpack(packed):
    return jnp.concatenate([packed[:, :CAP], packed[:, CAP:]], axis=0)


def make_payload(prior, meta):
    valid = meta[0:1] > 0.5
    value = meta[1:2]
    variance = jnp.where(valid, meta[2:3], 1.0)
    center = jnp.sum(prior, axis=0, keepdims=True) / M
    deviation = prior - center
    spread = jnp.sum(deviation * deviation, axis=0, keepdims=True) / (M - 1)
    total = spread + variance
    miss = value - center
    normed = jnp.where(valid, miss / jnp.sqrt(total), 0.0)
    a = spread / total * miss
    c = jnp.sqrt(variance / total) - 1.0
    d = jnp.where(valid, 1.0 / ((M - 1) * (spread + EPS)), 0.0)
    rows = [deviation, a, c]
    for i in range(9):
        if i == 4:
            rows.append(d)
        else:
            at = 3 + (i if i < 4 else i - 1)
            rows.append(d * (meta[at : at + 1] * TAPER[i]))
    rows.append(jnp.zeros((ROWS - M - 11, CAP), F32))
    return pack(jnp.concatenate(rows, axis=0)), normed


def init_kernel(order_hbm, value_hbm, variance_hbm, owner_hbm, cell_hbm, reach_hbm, x_hbm, out,
                order, value, variance, owner, cell, reach, surface, sems):
    small = [
        pltpu.make_async_copy(source, target, sems.at[i])
        for i, (source, target) in enumerate([
            (order_hbm, order), (owner_hbm, owner), (cell_hbm, cell),
            (value_hbm, value), (variance_hbm, variance), (reach_hbm, reach),
        ])
    ]
    load = pltpu.make_async_copy(x_hbm.at[:, 0], surface, sems.at[6])
    for copy in small:
        copy.start()
    load.start()
    me = lax.axis_index("gx") * lax.axis_size("gy") + lax.axis_index("gy")
    small[0].wait()
    small[1].wait()
    owned = jnp.concatenate([owner[pl.ds(order[k], 1), :] for k in range(NB)], axis=0) == me
    ownf = jnp.where(owned, 1.0, 0.0)
    chunks = OBS // 128
    own64 = jnp.concatenate([ownf[:, 128 * c : 128 * c + 128] for c in range(chunks)], axis=0).astype(BF16)
    upper = jnp.where(iota((128, 128), 0) < iota((128, 128), 1), 1.0, 0.0).astype(BF16)
    rows = NB * chunks
    r0, r1 = iota((rows, rows), 0), iota((rows, rows), 1)
    before = jnp.where((r1 < r0) & (((r0 - r1) & (NB - 1)) == 0), 1.0, 0.0).astype(BF16)
    base = dot(dot(before, own64).astype(BF16), jnp.ones((128, 128), BF16))
    rank64 = dot(own64, upper) + base
    rank = jnp.concatenate([rank64[NB * c : NB * c + NB] for c in range(chunks)], axis=1)
    rank = jnp.where(owned, rank, -1.0)
    slots = iota((CAP, OBS), 0).astype(F32)
    for copy in small[2:]:
        copy.wait()
    metas = []
    for k in range(NB):
        b = order[k]
        hot = jnp.where(rank[k : k + 1] == slots, 1.0, 0.0).astype(BF16)
        where = cell[pl.ds(b, 1), :]
        vh, vm, vl = split3(value[pl.ds(b, 1), :])
        rh, rm, rl = split3(variance[pl.ds(b, 1), :])
        parts = [
            reach[b].astype(F32),
            lax.shift_right_logical(where, 8).astype(F32),
            (where & 255).astype(F32),
            vh.astype(F32), vm.astype(F32), vl.astype(F32),
            rh.astype(F32), rm.astype(F32), rl.astype(F32),
            jnp.ones((1, OBS), F32),
            jnp.zeros((15, OBS), F32),
        ]
        metas.append(dot_t(jnp.concatenate(parts, axis=0).astype(BF16), hot))
    got = jnp.concatenate(metas, axis=1)
    out[M:] = jnp.concatenate(
        [
            got[16:17],
            got[10:11] + got[11:12] + got[12:13],
            got[13:14] + got[14:15] + got[15:16],
            got[:8],
            jnp.zeros((5, NB * CAP), F32),
        ],
        axis=0,
    )
    hot_y = jnp.where(got[9:10] == iota((TY, NB * CAP), 0).astype(F32), 1.0, 0.0).astype(BF16)
    hot_x = jnp.where(got[8:9] == iota((TX, NB * CAP), 0).astype(F32), 1.0, 0.0)
    load.wait()
    group = 16
    for g in range(M // group):
        h, m, l = split3(surface[group * g : group * g + group].reshape(group * TX, TY))
        picked = dot(h, hot_y) + dot(m, hot_y) + dot(l, hot_y)
        out[group * g : group * g + group] = jnp.sum(
            picked.reshape(group, TX, NB * CAP) * hot_x[None], axis=1
        )


def core_of():
    return lax.rem(lax.axis_index("gx"), 2)


def upward(index):
    return lax.rem(index + core_of(), 2) == 0


def emit(k, z, pay_out, edge_out, nv_out):
    pays, news = [], []
    for t in range(2):
        at = slice(CAP * k, CAP * k + CAP)
        pay, normed = make_payload(z[t][:M, at], z[t][M:, at])
        pay_out[t] = pay
        pays.append(pay)
        news.append(normed)
    edge_out[...] = jnp.where(upward(lax.axis_index("gx") // 2), pays[1], pays[0])
    nv_out[...] = jnp.where(core_of() == 0, news[0], news[1])


def start_kernel(own, sib, z_out, pay_out, edge_out, nv_out):
    first = core_of() == 0
    mine, other = own[...], sib[...]
    z = [jnp.where(first, mine, other), jnp.where(first, other, mine)]
    unit = jnp.where(iota((ROWS, 128), 0) == iota((ROWS, 128), 1), 1.0, 0.0)
    unit = jnp.where(iota((ROWS, 128), 0) < M, unit, 0.0)
    for t in range(2):
        z_out[t, :, : NB * CAP] = z[t]
        z_out[t, :, NB * CAP :] = unit
    emit(0, z, pay_out, edge_out, nv_out)


def right_side(rows):
    return rows[ROW_A : ROW_A + 1] + rows[ROW_C : ROW_C + 1] * rows[:M]


def gains(pay, far, sib_far, weight):
    up = upward(lax.axis_index("gx") // 2)
    far, sib_far = far[...], sib_far[...]
    blocks = [jnp.where(up, sib_far, far), pay[0], pay[1], jnp.where(up, far, sib_far)]
    blocks = [unpack(b) for b in blocks]
    rights = [right_side(b) for b in blocks]
    results = []
    for t in range(2):
        left = jnp.concatenate([blocks[t + i][:M] * weight(blocks[t + i], 1 - i) for i in range(3)], axis=1)
        right = jnp.concatenate(rights[t : t + 3], axis=1)
        results.append(dot_t(right, left, precision=HIGH))
    return results


def factor(rows, dx, dy):
    at = ROW_W + 3 * (dx + 1) + dy + 1
    return rows[at : at + 1]


def send_kernel(pay, far, sib_far, out):
    up = upward(lax.axis_index("gy"))
    both = gains(pay, far, sib_far, lambda rows, dx: jnp.where(up, factor(rows, dx, 1), factor(rows, dx, -1)))
    for t in range(2):
        out[t] = both[t]


def same_kernel(k, order, owner, pay, far, sib_far, out, rank_out):
    both = gains(pay, far, sib_far, lambda rows, dx: factor(rows, dx, 0))
    for t in range(2):
        out[t] = both[t]
    row = owner[pl.ds(order[k], 1), :]
    upper = jnp.where(iota((128, 128), 0) < iota((128, 128), 1), 1.0, 0.0).astype(BF16)
    tiles = iota((TILES, 128), 0)
    base = jnp.zeros((TILES, 1), F32)
    for c in range(OBS // 128):
        at = slice(128 * c, 128 * c + 128)
        hot = jnp.where(row[:, at] == tiles, 1.0, 0.0)
        rank = dot(hot.astype(BF16), upper) + base
        rank_out[:, at] = jnp.sum(hot * rank, axis=0, keepdims=True)
        base = base + jnp.sum(hot, axis=1, keepdims=True)


def advance(z, gain):
    anomaly = z - jnp.sum(z, axis=0, keepdims=True) / M
    return z + dot(gain, anomaly, precision=HIGH)


def step_kernel(k, q0, h, g, z, z_out, pay_out, edge_out, nv_out):
    new = []
    for t in range(2):
        moved = advance(z[t, :M], q0[t] + h[t] + g[t])
        z_out[t, :M] = moved
        z_out[t, M:] = z[t, M:]
        new.append(jnp.concatenate([moved, z[t, M:]], axis=0))
    emit(k, new, pay_out, edge_out, nv_out)


def final_kernel(q0, h, g, z, x, out, mix):
    @pl.when(pl.program_id(0) == 0)
    def _():
        c = core_of()
        t = advance(z[c, :M, NB * CAP :], q0[c] + h[c] + g[c])[:, :M]
        d = t - jnp.where(iota((M, M), 0) == iota((M, M), 1), 1.0, 0.0)
        dh, dl = split2(d)
        mix[...] = jnp.concatenate([dh, dh, dl], axis=1)

    w = mix[...]
    for t in range(TX // 8):
        block = x[:, 0, 8 * t : 8 * t + 8, :]
        turned = jnp.swapaxes(block, 0, 1)
        updates = []
        for i in range(8):
            h_, l_ = split2(turned[i])
            updates.append(dot(w, jnp.concatenate([h_, l_, h_], axis=0))[None])
        out[:, 0, 8 * t : 8 * t + 8, :] = block + jnp.swapaxes(jnp.concatenate(updates, axis=0), 0, 1)


def place_kernel(order, owner, nv, r0, r1, r2, r3, out):
    turned = nv[...].T
    slots = iota((CAP, 128), 0).astype(F32)
    for k, rank in enumerate((r0, r1, r2, r3)):
        b = order[k]
        table = turned[CAP * k : CAP * k + CAP]
        row = owner[pl.ds(b, 1), :]
        pieces = []
        for c in range(OBS // 128):
            at = slice(128 * c, 128 * c + 128)
            got = jnp.take_along_axis(table, jnp.broadcast_to(row[:, at], (CAP, 128)), axis=1)
            got = jnp.where(rank[:, at] == slots, got, 0.0)
            pieces.append(jnp.sum(got, axis=0, keepdims=True))
        out[pl.ds(b, 1), :] = jnp.concatenate(pieces, axis=1)


VMEM = pl.BlockSpec(memory_space=pltpu.VMEM)
SMEM = pl.BlockSpec(memory_space=pltpu.SMEM)
HBM = pl.BlockSpec(memory_space=pltpu.HBM)


def shape(*dims):
    return jax.ShapeDtypeStruct(dims, F32)


def swaps(pairs):
    return pairs + [(high, low) for low, high in pairs]


def local(ensemble, obs_value, obs_variance, obs_owner, obs_cell, obs_reach, batch_order):
    params = pltpu.CompilerParams(vmem_limit_bytes=48 * 2**20)
    call = functools.partial(pl.pallas_call, compiler_params=params)
    width, height = lax.axis_size("gx"), lax.axis_size("gy")
    both = ("gx", "gy")
    core = swaps([(x, x + 1) for x in range(0, width, 2)])
    side_x = swaps([(2 * y + c, 2 * y + 2 + c) for c in range(2) for y in range(c, width // 2 - 1, 2)])
    side_y = swaps([
        (x * height + k, x * height + k + 1) for x in range(width) for k in range(x % 2, height - 1, 2)
    ])
    pay_shapes = (shape(2, ROWS // 2, 128), shape(ROWS // 2, 128), shape(1, CAP))
    z_shape = shape(2, ROWS, NB * CAP + 128)
    row = pltpu.VMEM((NB, OBS), F32)
    row_i = pltpu.VMEM((NB, OBS), jnp.int32)
    own = call(
        init_kernel,
        out_shape=shape(ROWS, NB * CAP),
        in_specs=[HBM] * 7,
        out_specs=VMEM,
        scratch_shapes=[
            pltpu.SMEM((NB,), jnp.int32), row, row, row_i, row_i,
            pltpu.VMEM((NB, 8, OBS), jnp.int32), pltpu.VMEM((M, TX, TY), F32), pltpu.SemaphoreType.DMA((7,)),
        ],
        name="init",
    )(batch_order, obs_value, obs_variance, obs_owner, obs_cell, jnp.swapaxes(obs_reach, 1, 2), ensemble)
    z, pay, edge, nv = call(
        start_kernel,
        out_shape=(z_shape,) + pay_shapes,
        in_specs=[VMEM] * 2,
        out_specs=(VMEM,) * 4,
        name="start",
    )(own, lax.ppermute(own, "gx", core))
    normed, ranks = [nv], []
    for k in range(NB):
        far = lax.ppermute(edge, "gx", side_x)
        sib_far = lax.ppermute(far, "gx", core)
        send = call(send_kernel, out_shape=shape(2, M, M), in_specs=[VMEM] * 3, out_specs=VMEM, name="send")(
            pay, far, sib_far
        )
        h = lax.ppermute(send, both, side_y)
        q0, rank = call(
            functools.partial(same_kernel, k),
            out_shape=(shape(2, M, M), shape(1, OBS)),
            in_specs=[SMEM] + [VMEM] * 4,
            out_specs=(VMEM, VMEM),
            name="same",
        )(batch_order, obs_owner, pay, far, sib_far)
        ranks.append(rank)
        g = lax.ppermute(h, "gx", core)
        if k + 1 < NB:
            z, pay, edge, nv = call(
                functools.partial(step_kernel, k + 1),
                out_shape=(z_shape,) + pay_shapes,
                in_specs=[VMEM] * 4,
                out_specs=(VMEM,) * 4,
                name="step",
            )(q0, h, g, z)
            normed.append(nv)
    small = lambda *dims: pl.BlockSpec(dims, lambda i: (0,) * len(dims))
    slab = pl.BlockSpec((M, 1, TX, TY), lambda i: (0, i, 0, 0))
    state = call(
        final_kernel,
        out_shape=shape(M, LEV, TX, TY),
        grid=(LEV,),
        in_specs=[small(2, M, M)] * 3 + [small(2, ROWS, NB * CAP + 128), slab],
        out_specs=slab,
        scratch_shapes=[pltpu.VMEM((M, 3 * M), BF16)],
        name="final",
    )(q0, h, g, z, ensemble)
    mine = jnp.concatenate(normed, axis=1)
    everyone = lax.all_to_all(jnp.broadcast_to(mine, (TILES, NB * CAP)), both, 0, 0, tiled=True)
    innovation = call(
        place_kernel,
        out_shape=shape(NB, OBS),
        in_specs=[SMEM] + [VMEM] * 6,
        out_specs=VMEM,
        name="place",
    )(batch_order, obs_owner, everyone, *ranks)
    return state, innovation


def solution(mesh):
    placed = (P(None, None, "gx", "gy"), P(), P(), P(), P(), P(), P())
    return jax.shard_map(
        local,
        mesh=mesh,
        in_specs=placed,
        out_specs=(P(None, None, "gx", "gy"), P()),
        check_vma=False,
    )
```

time: 98.1 us -> 99.1 us (1.010)
  starting transfers between devices: 45.7 us -> 62.9 us
  waiting for transfers between devices: 21.3 us -> 4.38 us
    ppermute x20 -> x17, starting transfers between devices: 30.2 us -> 47.5 us  [the longest x4 24 us: local(): g = lax.ppermute(h, 'gx', core)]
    ppermute x20 -> x17, waiting for transfers between devices: 21.3 us -> 4.37 us  [the longest x4 3.4 us: local(): sib_far = lax.ppermute(far, 'gx', core)]
  transfers between devices with their start and end apart: 21 -> 18, of which waited for: 14 -> 5; matrix products, arithmetic and copies ran while one was open for 1% -> 1% of each run, Pallas kernels for 15% -> 7%
where the time goes in v2:
time: 99.1 us; the launch traced here: 98.4 us
  starting transfers between devices  62.9 us (63%)
  Pallas kernels  24.7 us (25%)
  local copies, waits for them, and re-layouts  5.38 us (5%)
  waiting for transfers between devices  4.38 us (4%)
    ppermute x4, starting transfers between devices, local(): g = lax.ppermute(h, 'gx', core)  24 us
    ppermute x4, starting transfers between devices, local(): sib_far = lax.ppermute(far, 'gx', core)  16.8 us
    all_to_all x1, starting transfers between devices, local(): lax.all_to_all(jnp.broadcast_to(mine, (TILES, NB * CAP)), both, 0, 0, til...  15.4 us
    pallas_call x1, Pallas kernels, local(): call(final_kernel, out_shape=shape(M, LEV, TX, TY), grid=(LEV,), in_specs...  11.3 us
    pallas_call x4, Pallas kernels, local(): call(functools.partial(same_kernel, k), out_shape=(shape(2, M, M), shape(...  4.69 us
    unnamed x17, local copies, waits for them, and re-layouts  4.65 us
    ppermute x4, waiting for transfers between devices, local(): sib_far = lax.ppermute(far, 'gx', core)  3.4 us
    pallas_call x1, Pallas kernels, local(): call(init_kernel, out_shape=shape(ROWS, NB * CAP), in_specs=[HBM] * 7, ou...  3.27 us
  transfers between devices with their start and end apart: 18, of which 5 were waited for; matrix products, arithmetic and copies ran while one was open for 1% of the time, Pallas kernels for 7%

profile of v2, /device:TPU:1, one launch (start us, length us, event | category | flops | bytes accessed | tf_op | source)
XLA Modules:
  0.0 98.4 jit_solution(10141800380200031327)
XLA Ops:
  0.6 0.0 copy-start.7
  0.6 0.0 copy-start
  0.7 0.8 copy-done
  1.4 0.0 copy-start.2
  1.4 0.9 copy-done.2
  2.4 0.8 copy-done.3
  3.1 0.8 copy-done.4
  3.9 0.8 copy-done.5
  4.6 0.7 copy-done.6
  5.3 3.3 %init.1.own = f32[96,256]{1,0:T(8,128)S(1)} custom-call(s32[4]{0:T(128)S(1)} %copy-done.6, f32[4,2048]{1,0:T(4,128)S(1)} %copy-done.3, f32[4,2048]{1,0:T(4,128)S(1)} %copy-done.4, s32[4,2048]{1,0:T(4,128)S(1)} %copy-done, s32[4,2048]{1,0:T(4,128)S(1)} %copy-done.5, s32[4,8,2048]{2,1,0:T(8,128)S(1)} %bitcast.6, f32[80,4,32,256]{3,2,1,0:T(8,128)} %x.1), custom_call_target="tpu_custom_call" | custom-call | tf_op jit(solution)/shard_map/init/pallas_call | solution.py:313
  8.6 1.5 %collective-permute-start = (f32[96,256]{1,0:T(8,128)S(1)}, f32[96,256]{1,0:T(8,128)S(1)}, u32[]{:S(2)}, u32[]{:S(2)}) collective-permute-start(f32[96,256]{1,0:T(8,128)S(1)} %init.1.own), channel_id=1, source_target_pairs={{0,16},{32,48},{64,80},{96,112},{16,0},{48,32},{80,64},{112,96},{1... | collective-permute-start | bytes 294920 | tf_op jit(solution)/shard_map/ppermute | solution.py:330
  10.1 0.9 collective-permute-done.sib
  11.0 0.2 start.1
  11.2 0.7 collective-permute-start.1
  11.8 0.0 collective-permute-done.1.far
  11.8 5.4 %collective-permute-start.2 = (f32[48,128]{1,0:T(8,128)S(1)}, f32[48,128]{1,0:T(8,128)S(1)}, u32[]{:S(2)}, u32[]{:S(2)}) collective-permute-start(f32[48,128]{1,0:T(8,128)S(1)} %collective-permute-done.1.far), channel_id=1, source_target_pairs={{0,16},{32,48},{64,80},{96,112},{16,0},{48,32},{80,64},{112,96},{1... | collective-permute-start | bytes 73736 | tf_op jit(solution)/shard_map/ppermute | solution.py:334
  17.2 0.8 collective-permute-done.2.sib_far
  18.1 0.4 send.4
  18.5 0.7 collective-permute-start.3
  19.2 0.0 collective-permute-done.3.h
  19.2 6.0 %collective-permute-start.4 = (f32[2,80,80]{2,1,0:T(8,128)S(1)}, f32[2,80,80]{2,1,0:T(8,128)S(1)}, u32[]{:S(2)}, u32[]{:S(2)}) collective-permute-start(f32[2,80,80]{2,1,0:T(8,128)S(1)} %collective-permute-done.3.h), channel_id=1, source_target_pairs={{0,16},{32,48},{64,80},{96,112},{16,0},{48,32},{80,64},{112,96},{1... | collective-permute-start | bytes 153608 | tf_op jit(solution)/shard_map/ppermute | solution.py:347
  25.2 0.0 copy-done.7
  25.2 0.0 copy-done.1
  25.2 1.2 %same.4 = (f32[2,80,80]{2,1,0:T(8,128)S(1)}, f32[1,2048]{1,0:T(1,128)S(1)}) custom-call(s32[4]{0:T(128)S(1)} %copy-done.7, s32[4,2048]{1,0:T(4,128)S(1)} %copy-done.1, f32[2,48,128]{2,1,0:T(8,128)S(1)} %get-tuple-element.26.pay, f32[48,128]{1,0:T(8,128)S(1)} %collective-permute-done.1.far, f32[48,128]{1,0:T(8,128)S(1)} %collective-permute-done.2.sib_far), custom_call_target="tpu_custom_call" | custom-call | tf_op jit(solution)/shard_map/same/pallas_call | solution.py:339
  26.4 0.0 collective-permute-done.4.g
  26.4 0.5 step.3
  26.9 0.7 collective-permute-start.5
  27.5 0.0 collective-permute-done.5.far
  27.5 5.1 %collective-permute-start.6 = (f32[48,128]{1,0:T(8,128)S(1)}, f32[48,128]{1,0:T(8,128)S(1)}, u32[]{:S(2)}, u32[]{:S(2)}) collective-permute-start(f32[48,128]{1,0:T(8,128)S(1)} %collective-permute-done.5.far), channel_id=1, source_target_pairs={{0,16},{32,48},{64,80},{96,112},{16,0},{48,32},{80,64},{112,96},{1... | collective-permute-start | bytes 73736 | tf_op jit(solution)/shard_map/ppermute | solution.py:334
  32.7 0.8 collective-permute-done.6.sib_far
  33.5 0.4 send.5
  33.9 0.7 collective-permute-start.7
  34.6 0.0 collective-permute-done.7.h
  34.6 6.0 %collective-permute-start.8 = (f32[2,80,80]{2,1,0:T(8,128)S(1)}, f32[2,80,80]{2,1,0:T(8,128)S(1)}, u32[]{:S(2)}, u32[]{:S(2)}) collective-permute-start(f32[2,80,80]{2,1,0:T(8,128)S(1)} %collective-permute-done.7.h), channel_id=1, source_target_pairs={{0,16},{32,48},{64,80},{96,112},{16,0},{48,32},{80,64},{112,96},{1... | collective-permute-start | bytes 153608 | tf_op jit(solution)/shard_map/ppermute | solution.py:347
  40.6 1.2 %same.5 = (f32[2,80,80]{2,1,0:T(8,128)S(1)}, f32[1,2048]{1,0:T(1,128)S(1)}) custom-call(s32[4]{0:T(128)S(1)} %copy-done.7, s32[4,2048]{1,0:T(4,128)S(1)} %copy-done.1, f32[2,48,128]{2,1,0:T(8,128)S(1)} %get-tuple-element.30.pay, f32[48,128]{1,0:T(8,128)S(1)} %collective-permute-done.5.far, f32[48,128]{1,0:T(8,128)S(1)} %collective-permute-done.6.sib_far), custom_call_target="tpu_custom_call" | custom-call | tf_op jit(solution)/shard_map/same/pallas_call | solution.py:339
  41.8 0.0 collective-permute-done.8.g
  41.8 0.5 step.4
  42.3 0.7 collective-permute-start.9
  43.0 0.0 collective-permute-done.9.far
  43.0 5.1 %collective-permute-start.10 = (f32[48,128]{1,0:T(8,128)S(1)}, f32[48,128]{1,0:T(8,128)S(1)}, u32[]{:S(2)}, u32[]{:S(2)}) collective-permute-start(f32[48,128]{1,0:T(8,128)S(1)} %collective-permute-done.9.far), channel_id=1, source_target_pairs={{0,16},{32,48},{64,80},{96,112},{16,0},{48,32},{80,64},{112,96},{1... | collective-permute-start | bytes 73736 | tf_op jit(solution)/shard_map/ppermute | solution.py:334
  48.1 0.8 collective-permute-done.10.sib_far
  49.0 0.4 send.6
  49.4 0.7 collective-permute-start.11
  50.1 0.0 collective-permute-done.11.h
  50.1 6.0 %collective-permute-start.12 = (f32[2,80,80]{2,1,0:T(8,128)S(1)}, f32[2,80,80]{2,1,0:T(8,128)S(1)}, u32[]{:S(2)}, u32[]{:S(2)}) collective-permute-start(f32[2,80,80]{2,1,0:T(8,128)S(1)} %collective-permute-done.11.h), channel_id=1, source_target_pairs={{0,16},{32,48},{64,80},{96,112},{16,0},{48,32},{80,64},{112,96},{1... | collective-permute-start | bytes 153608 | tf_op jit(solution)/shard_map/ppermute | solution.py:347
  56.1 1.2 %same.6 = (f32[2,80,80]{2,1,0:T(8,128)S(1)}, f32[1,2048]{1,0:T(1,128)S(1)}) custom-call(s32[4]{0:T(128)S(1)} %copy-done.7, s32[4,2048]{1,0:T(4,128)S(1)} %copy-done.1, f32[2,48,128]{2,1,0:T(8,128)S(1)} %get-tuple-element.34.pay, f32[48,128]{1,0:T(8,128)S(1)} %collective-permute-done.9.far, f32[48,128]{1,0:T(8,128)S(1)} %collective-permute-done.10.sib_far), custom_call_target="tpu_custom_call" | custom-call | tf_op jit(solution)/shard_map/same/pallas_call | solution.py:339
  57.3 0.0 collective-permute-done.12.g
  57.3 0.5 step.5
  57.7 0.7 collective-permute-start.13
  58.4 0.1 pad_maximum_fusion
  58.5 0.7 broadcast_in_dim.2
  59.2 15.4 %all-to-all-start = ((f32[128,1,256]{2,1,0:T(1,128)}), f32[128,1,256]{2,1,0:T(1,128)S(1)}, u32[]{:S(2)}, u32[]{:S(2)}) async-start(f32[128,1,256]{2,1,0:T(1,128)} %broadcast_in_dim.2), calls=%async_computation | async-start | bytes 262144 | tf_op jit(solution)/shard_map/all_to_all | solution.py:369
  74.6 0.0 collective-permute-done.13.far
  74.6 1.1 %collective-permute-start.14 = (f32[48,128]{1,0:T(8,128)S(1)}, f32[48,128]{1,0:T(8,128)S(1)}, u32[]{:S(2)}, u32[]{:S(2)}) collective-permute-start(f32[48,128]{1,0:T(8,128)S(1)} %collective-permute-done.13.far), channel_id=1, source_target_pairs={{0,16},{32,48},{64,80},{96,112},{16,0},{48,32},{80,64},{112,96},{1... | collective-permute-start | bytes 73736 | tf_op jit(solution)/shard_map/ppermute | solution.py:334
  75.8 0.8 collective-permute-done.14.sib_far
  76.6 0.4 send.7
  77.1 0.7 collective-permute-start.15
  77.7 0.0 collective-permute-done.15.h
  77.7 6.0 %collective-permute-start.16 = (f32[2,80,80]{2,1,0:T(8,128)S(1)}, f32[2,80,80]{2,1,0:T(8,128)S(1)}, u32[]{:S(2)}, u32[]{:S(2)}) collective-permute-start(f32[2,80,80]{2,1,0:T(8,128)S(1)} %collective-permute-done.15.h), channel_id=1, source_target_pairs={{0,16},{32,48},{64,80},{96,112},{16,0},{48,32},{80,64},{112,96},{1... | collective-permute-start | bytes 153608 | tf_op jit(solution)/shard_map/ppermute | solution.py:347
  83.7 1.2 %same.7 = (f32[2,80,80]{2,1,0:T(8,128)S(1)}, f32[1,2048]{1,0:T(1,128)S(1)}) custom-call(s32[4]{0:T(128)S(1)} %copy-done.7, s32[4,2048]{1,0:T(4,128)S(1)} %copy-done.1, f32[2,48,128]{2,1,0:T(8,128)S(1)} %get-tuple-element.38.pay, f32[48,128]{1,0:T(8,128)S(1)} %collective-permute-done.13.far, f32[48,128]{1,0:T(8,128)S(1)} %collective-permute-done.14.sib_far), custom_call_target="tpu_custom_call" | custom-call | tf_op jit(solution)/shard_map/same/pallas_call | solution.py:339
  84.9 0.0 all-to-all-done
  84.9 2.1 %place.1 = f32[4,2048]{1,0:T(4,128)} custom-call(s32[4]{0:T(128)S(1)} %copy-done.7, s32[4,2048]{1,0:T(4,128)S(1)} %copy-done.1, f32[128,256]{1,0:T(8,128)S(1)} %bitcast.5, f32[1,2048]{1,0:T(1,128)S(1)} %get-tuple-element.46.r0, f32[1,2048]{1,0:T(1,128)S(1)} %get-tuple-element.47.r1, f32[1,2048]{1,0:T(1,128)S(1)} %get-tuple-element.48.r2, ...), custom_call_target="tpu_custom_call" | custom-call | tf_op jit(solution)/shard_map/place/pallas_call | solution.py:370
  87.1 0.0 collective-permute-done.16.g
  87.1 11.3 %final.1 = f32[80,4,32,256]{3,2,1,0:T(8,128)} custom-call(f32[2,80,80]{2,1,0:T(8,128)S(1)} %get-tuple-element.40.q0, f32[2,80,80]{2,1,0:T(8,128)S(1)} %collective-permute-done.15.h, f32[2,80,80]{2,1,0:T(8,128)S(1)} %collective-permute-done.16.g, f32[2,96,384]{2,1,0:T(8,128)S(1)} %get-tuple-element.41.z, f32[80,4,32,256]{3,2,1,0:T(8,128)} %x.1), custom_call_target="tpu_custom_call" | custom-call | tf_op jit(solution)/shard_map/final/pallas_call | solution.py:359
  (6 shorter events, 0.0 us)
Async XLA Ops:
  0.6 24.6 %copy-start.7 = (s32[4]{0:T(128)S(1)}, s32[4]{0:T(128)}, u32[]{:S(2)}) copy-start(s32[4]{0:T(128)} %order.9) | copy-start | bytes 52
  0.6 0.8 copy-start
  1.4 0.9 copy-start.2
  2.4 0.8 copy-start.3
  3.1 0.8 copy-start.4
  3.9 0.8 copy-start.5
  4.6 0.7 copy-start.6
  5.3 19.9 %copy-start.1 = (s32[4,2048]{1,0:T(4,128)S(1)}, s32[4,2048]{1,0:T(4,128)}, u32[]{:S(2)}) copy-start(s32[4,2048]{1,0:T(4,128)} %owner.9) | copy-start | bytes 98308
  8.6 2.4 %collective-permute-start = (f32[96,256]{1,0:T(8,128)S(1)}, f32[96,256]{1,0:T(8,128)S(1)}, u32[]{:S(2)}, u32[]{:S(2)}) collective-permute-start(f32[96,256]{1,0:T(8,128)S(1)} %init.1.own), channel_id=1, source_target_pairs={{0,16},{32,48},{64,80},{96,112},{16,0},{48,32},{80,64},{112,96},{1... | collective-permute-start | bytes 294920 | tf_op jit(solution)/shard_map/ppermute | solution.py:330
  11.2 0.7 collective-permute-start.1
  11.8 6.2 %collective-permute-start.2 = (f32[48,128]{1,0:T(8,128)S(1)}, f32[48,128]{1,0:T(8,128)S(1)}, u32[]{:S(2)}, u32[]{:S(2)}) collective-permute-start(f32[48,128]{1,0:T(8,128)S(1)} %collective-permute-done.1.far), channel_id=1, source_target_pairs={{0,16},{32,48},{64,80},{96,112},{16,0},{48,32},{80,64},{112,96},{1... | collective-permute-start | bytes 73736 | tf_op jit(solution)/shard_map/ppermute | solution.py:334
  18.5 0.7 collective-permute-start.3
  19.2 7.2 %collective-permute-start.4 = (f32[2,80,80]{2,1,0:T(8,128)S(1)}, f32[2,80,80]{2,1,0:T(8,128)S(1)}, u32[]{:S(2)}, u32[]{:S(2)}) collective-permute-start(f32[2,80,80]{2,1,0:T(8,128)S(1)} %collective-permute-done.3.h), channel_id=1, source_target_pairs={{0,16},{32,48},{64,80},{96,112},{16,0},{48,32},{80,64},{112,96},{1... | collective-permute-start | bytes 153608 | tf_op jit(solution)/shard_map/ppermute | solution.py:347
  26.9 0.7 collective-permute-start.5
  27.5 6.0 %collective-permute-start.6 = (f32[48,128]{1,0:T(8,128)S(1)}, f32[48,128]{1,0:T(8,128)S(1)}, u32[]{:S(2)}, u32[]{:S(2)}) collective-permute-start(f32[48,128]{1,0:T(8,128)S(1)} %collective-permute-done.5.far), channel_id=1, source_target_pairs={{0,16},{32,48},{64,80},{96,112},{16,0},{48,32},{80,64},{112,96},{1... | collective-permute-start | bytes 73736 | tf_op jit(solution)/shard_map/ppermute | solution.py:334
  33.9 0.7 collective-permute-start.7
  34.6 7.2 %collective-permute-start.8 = (f32[2,80,80]{2,1,0:T(8,128)S(1)}, f32[2,80,80]{2,1,0:T(8,128)S(1)}, u32[]{:S(2)}, u32[]{:S(2)}) collective-permute-start(f32[2,80,80]{2,1,0:T(8,128)S(1)} %collective-permute-done.7.h), channel_id=1, source_target_pairs={{0,16},{32,48},{64,80},{96,112},{16,0},{48,32},{80,64},{112,96},{1... | collective-permute-start | bytes 153608 | tf_op jit(solution)/shard_map/ppermute | solution.py:347
  42.3 0.7 collective-permute-start.9
  43.0 6.0 %collective-permute-start.10 = (f32[48,128]{1,0:T(8,128)S(1)}, f32[48,128]{1,0:T(8,128)S(1)}, u32[]{:S(2)}, u32[]{:S(2)}) collective-permute-start(f32[48,128]{1,0:T(8,128)S(1)} %collective-permute-done.9.far), channel_id=1, source_target_pairs={{0,16},{32,48},{64,80},{96,112},{16,0},{48,32},{80,64},{112,96},{1... | collective-permute-start | bytes 73736 | tf_op jit(solution)/shard_map/ppermute | solution.py:334
  49.4 0.7 collective-permute-start.11
  50.1 7.2 %collective-permute-start.12 = (f32[2,80,80]{2,1,0:T(8,128)S(1)}, f32[2,80,80]{2,1,0:T(8,128)S(1)}, u32[]{:S(2)}, u32[]{:S(2)}) collective-permute-start(f32[2,80,80]{2,1,0:T(8,128)S(1)} %collective-permute-done.11.h), channel_id=1, source_target_pairs={{0,16},{32,48},{64,80},{96,112},{16,0},{48,32},{80,64},{112,96},{1... | collective-permute-start | bytes 153608 | tf_op jit(solution)/shard_map/ppermute | solution.py:347
  57.7 16.9 %collective-permute-start.13 = (f32[48,128]{1,0:T(8,128)S(1)}, f32[48,128]{1,0:T(8,128)S(1)}, u32[]{:S(2)}, u32[]{:S(2)}) collective-permute-start(f32[48,128]{1,0:T(8,128)S(1)} %get-tuple-element.39), channel_id=1, source_target_pairs={{0,32},{64,96},{48,80},{32,0},{96,64},{80,48},{1,33},{65,97},{49,8... | collective-permute-start | bytes 73736 | tf_op jit(solution)/shard_map/ppermute | solution.py:333
  59.2 25.7 %all-to-all-start = ((f32[128,1,256]{2,1,0:T(1,128)}), f32[128,1,256]{2,1,0:T(1,128)S(1)}, u32[]{:S(2)}, u32[]{:S(2)}) async-start(f32[128,1,256]{2,1,0:T(1,128)} %broadcast_in_dim.2), calls=%async_computation | async-start | bytes 262144 | tf_op jit(solution)/shard_map/all_to_all | solution.py:369
  74.6 2.0 %collective-permute-start.14 = (f32[48,128]{1,0:T(8,128)S(1)}, f32[48,128]{1,0:T(8,128)S(1)}, u32[]{:S(2)}, u32[]{:S(2)}) collective-permute-start(f32[48,128]{1,0:T(8,128)S(1)} %collective-permute-done.13.far), channel_id=1, source_target_pairs={{0,16},{32,48},{64,80},{96,112},{16,0},{48,32},{80,64},{112,96},{1... | collective-permute-start | bytes 73736 | tf_op jit(solution)/shard_map/ppermute | solution.py:334
  77.1 0.7 collective-permute-start.15
  77.7 9.3 %collective-permute-start.16 = (f32[2,80,80]{2,1,0:T(8,128)S(1)}, f32[2,80,80]{2,1,0:T(8,128)S(1)}, u32[]{:S(2)}, u32[]{:S(2)}) collective-permute-start(f32[2,80,80]{2,1,0:T(8,128)S(1)} %collective-permute-done.15.h), channel_id=1, source_target_pairs={{0,16},{32,48},{64,80},{96,112},{16,0},{48,32},{80,64},{112,96},{1... | collective-permute-start | bytes 153608 | tf_op jit(solution)/shard_map/ppermute | solution.py:347

commit v3 on v2

--- a/solution.py
+++ b/solution.py
@@ -158,6 +158,10 @@
     return lax.rem(lax.axis_index("gx"), 2)
 
 
+def edge(index, count):
+    return (index == 0) | (index == count - 1)
+
+
 def upward(index):
     return lax.rem(index + core_of(), 2) == 0
 
@@ -191,8 +195,12 @@
 
 
 def gains(pay, far, sib_far, weight):
-    up = upward(lax.axis_index("gx") // 2)
-    far, sib_far = far[...], sib_far[...]
+    y, chips = lax.axis_index("gx") // 2, lax.axis_size("gx") // 2
+    up = upward(y)
+    first = core_of() == 0
+    ends = edge(y, chips)
+    far = jnp.where(ends & jnp.logical_not(first), 0.0, far[...])
+    sib_far = jnp.where(ends & first, 0.0, sib_far[...])
     blocks = [jnp.where(up, sib_far, far), pay[0], pay[1], jnp.where(up, far, sib_far)]
     blocks = [unpack(b) for b in blocks]
     rights = [right_side(b) for b in blocks]
@@ -237,10 +245,16 @@
     return z + dot(gain, anomaly, precision=HIGH)
 
 
+def whole_gain(t, q0, h, g):
+    first = core_of() == 0
+    ends = edge(lax.axis_index("gy"), lax.axis_size("gy"))
+    return q0[t] + jnp.where(ends & jnp.logical_not(first), 0.0, h[t]) + jnp.where(ends & first, 0.0, g[t])
+
+
 def step_kernel(k, q0, h, g, z, z_out, pay_out, edge_out, nv_out):
     new = []
     for t in range(2):
-        moved = advance(z[t, :M], q0[t] + h[t] + g[t])
+        moved = advance(z[t, :M], whole_gain(t, q0, h, g))
         z_out[t, :M] = moved
         z_out[t, M:] = z[t, M:]
         new.append(jnp.concatenate([moved, z[t, M:]], axis=0))
@@ -251,7 +265,7 @@
     @pl.when(pl.program_id(0) == 0)
     def _():
         c = core_of()
-        t = advance(z[c, :M, NB * CAP :], q0[c] + h[c] + g[c])[:, :M]
+        t = advance(z[c, :M, NB * CAP :], whole_gain(c, q0, h, g))[:, :M]
         d = t - jnp.where(iota((M, M), 0) == iota((M, M), 1), 1.0, 0.0)
         dh, dl = split2(d)
         mix[...] = jnp.concatenate([dh, dh, dl], axis=1)
@@ -302,9 +316,10 @@
     width, height = lax.axis_size("gx"), lax.axis_size("gy")
     both = ("gx", "gy")
     core = swaps([(x, x + 1) for x in range(0, width, 2)])
-    side_x = swaps([(2 * y + c, 2 * y + 2 + c) for c in range(2) for y in range(c, width // 2 - 1, 2)])
+    chips = width // 2
+    side_x = swaps([(2 * y + c, 2 * ((y + 1) % chips) + c) for c in range(2) for y in range(c, chips, 2)])
     side_y = swaps([
-        (x * height + k, x * height + k + 1) for x in range(width) for k in range(x % 2, height - 1, 2)
+        (x * height + k, x * height + (k + 1) % height) for x in range(width) for k in range(x % 2, height, 2)
     ])
     pay_shapes = (shape(2, ROWS // 2, 128), shape(ROWS // 2, 128), shape(1, CAP))
     z_shape = shape(2, ROWS, NB * CAP + 128)
@@ -320,7 +335,12 @@
             pltpu.VMEM((NB, 8, OBS), jnp.int32), pltpu.VMEM((M, TX, TY), F32), pltpu.SemaphoreType.DMA((7,)),
         ],
         name="init",
-    )(batch_order, obs_value, obs_variance, obs_owner, obs_cell, jnp.swapaxes(obs_reach, 1, 2), ensemble)
+    )(*(
+        pltpu.with_memory_space_constraint(value, pltpu.HBM)
+        for value in (
+            batch_order, obs_value, obs_variance, obs_owner, obs_cell, jnp.swapaxes(obs_reach, 1, 2), ensemble
+        )
+    ))
     z, pay, edge, nv = call(
         start_kernel,
         out_shape=(z_shape,) + pay_shapes,
@@ -344,6 +364,7 @@
             name="same",
         )(batch_order, obs_owner, pay, far, sib_far)
         ranks.append(rank)
+        h, q0 = lax.optimization_barrier((h, q0))
         g = lax.ppermute(h, "gx", core)
         if k + 1 < NB:
             z, pay, edge, nv = call(

time: 99.1 us -> 84.5 us (0.85)
  starting transfers between devices: 62.9 us -> 41.8 us
  waiting for transfers between devices: 4.38 us -> 16.2 us
  local copies, waits for them, and re-layouts: 5.38 us -> 0.75 us
    ppermute x4, starting transfers between devices: 24 us -> 0.01 us  [local(): g = lax.ppermute(h, 'gx', core)]
    ppermute x4, starting transfers between devices: 2.66 us -> 20.5 us  [local(): h = lax.ppermute(send, both, side_y)]
    ppermute x4, starting transfers between devices: 16.8 us -> 1.5 us  [local(): sib_far = lax.ppermute(far, 'gx', core)]
    ppermute x4, starting transfers between devices: 2.62 us -> 11 us  [local(): far = lax.ppermute(edge, 'gx', side_x)]
    all_to_all x1, starting transfers between devices: 15.4 us -> 7.26 us  [local(): lax.all_to_all(jnp.broadcast_to(mine, (TILES, NB * CAP)), both, 0, 0, til...]
    unnamed x17 -> x5, local copies, waits for them, and re-layouts: 4.65 us -> 0.02 us
    ppermute x4, waiting for transfers between devices: 0.01 us -> 3.83 us  [local(): g = lax.ppermute(h, 'gx', core)]
    ppermute x4, waiting for transfers between devices: 0.01 us -> 3.65 us  [local(): far = lax.ppermute(edge, 'gx', side_x)]
  transfers between devices with their start and end apart: 18 -> 18, of which waited for: 5 -> 16; matrix products, arithmetic and copies ran while one was open for 1% -> 1% of each run, Pallas kernels for 7% -> 8%
where the time goes in v3:
time: 84.5 us; the launch traced here: 84.3 us
  starting transfers between devices  41.8 us (49%)
  Pallas kernels  24.7 us (29%)
  waiting for transfers between devices  16.2 us (19%)
    ppermute x4, starting transfers between devices, local(): h = lax.ppermute(send, both, side_y)  20.5 us
    pallas_call x1, Pallas kernels, local(): call(final_kernel, out_shape=shape(M, LEV, TX, TY), grid=(LEV,), in_specs...  11.3 us
    ppermute x4, starting transfers between devices, local(): far = lax.ppermute(edge, 'gx', side_x)  11 us
    all_to_all x1, starting transfers between devices, local(): lax.all_to_all(jnp.broadcast_to(mine, (TILES, NB * CAP)), both, 0, 0, til...  7.26 us
    pallas_call x4, Pallas kernels, local(): call(functools.partial(same_kernel, k), out_shape=(shape(2, M, M), shape(...  4.7 us
    ppermute x4, waiting for transfers between devices, local(): sib_far = lax.ppermute(far, 'gx', core)  4.09 us
    ppermute x4, waiting for transfers between devices, local(): g = lax.ppermute(h, 'gx', core)  3.83 us
    ppermute x4, waiting for transfers between devices, local(): far = lax.ppermute(edge, 'gx', side_x)  3.65 us
  transfers between devices with their start and end apart: 18, of which 16 were waited for; matrix products, arithmetic and copies ran while one was open for 1% of the time, Pallas kernels for 8%

profile of v3, /device:TPU:1, one launch (start us, length us, event | category | flops | bytes accessed | tf_op | source)
XLA Modules:
  0.0 84.3 jit_solution(15160373476397818271)
XLA Ops:
  0.6 0.0 copy-start.1
  0.6 0.0 copy-start
  0.7 3.3 %init.1.own = f32[96,256]{1,0:T(8,128)S(1)} custom-call(s32[4]{0:T(128)} %order.9, f32[4,2048]{1,0:T(4,128)} %value_hbm.1, f32[4,2048]{1,0:T(4,128)} %variance_hbm.1, s32[4,2048]{1,0:T(4,128)} %owner.9, s32[4,2048]{1,0:T(4,128)} %cell_hbm.1, s32[4,8,2048]{2,1,0:T(8,128)} %bitcast.6, f32[80,4,32,256]{3,2,1,0:T(8,128)} %x.1), custom_call_target="tpu_custom_call" | custom-call | tf_op jit(solution)/shard_map/init/pallas_call | solution.py:328
  3.9 1.5 %collective-permute-start = (f32[96,256]{1,0:T(8,128)S(1)}, f32[96,256]{1,0:T(8,128)S(1)}, u32[]{:S(2)}, u32[]{:S(2)}) collective-permute-start(f32[96,256]{1,0:T(8,128)S(1)} %init.1.own), channel_id=1, source_target_pairs={{0,16},{32,48},{64,80},{96,112},{16,0},{48,32},{80,64},{112,96},{1... | collective-permute-start | bytes 294920 | tf_op jit(solution)/shard_map/ppermute | solution.py:350
  5.4 0.9 %collective-permute-done.sib = f32[96,256]{1,0:T(8,128)S(1)} collective-permute-done((f32[96,256]{1,0:T(8,128)S(1)}, f32[96,256]{1,0:T(8,128)S(1)}, u32[]{:S(2)}, u32[]{:S(2)}) %collective-permute-start) | collective-permute-done | bytes 98336 | tf_op jit(solution)/shard_map/ppermute | solution.py:350
  6.4 0.2 start.1
  6.5 2.9 %collective-permute-start.1 = (f32[48,128]{1,0:T(8,128)S(1)}, f32[48,128]{1,0:T(8,128)S(1)}, u32[]{:S(2)}, u32[]{:S(2)}) collective-permute-start(f32[48,128]{1,0:T(8,128)S(1)} %get-tuple-element.35), channel_id=1, source_target_pairs={{0,32},{64,96},{48,80},{112,16},{32,0},{96,64},{80,48},{16,112},{1... | collective-permute-start | bytes 73736 | tf_op jit(solution)/shard_map/ppermute | solution.py:353
  9.4 1.2 %collective-permute-done.1.far = f32[48,128]{1,0:T(8,128)S(1)} collective-permute-done((f32[48,128]{1,0:T(8,128)S(1)}, f32[48,128]{1,0:T(8,128)S(1)}, u32[]{:S(2)}, u32[]{:S(2)}) %collective-permute-start.1) | collective-permute-done | bytes 24608 | tf_op jit(solution)/shard_map/ppermute | solution.py:353
  10.6 0.2 collective-permute-start.2
  10.8 1.0 %collective-permute-done.2.sib_far = f32[48,128]{1,0:T(8,128)S(1)} collective-permute-done((f32[48,128]{1,0:T(8,128)S(1)}, f32[48,128]{1,0:T(8,128)S(1)}, u32[]{:S(2)}, u32[]{:S(2)}) %collective-permute-start.2) | collective-permute-done | bytes 24608 | tf_op jit(solution)/shard_map/ppermute | solution.py:354
  11.8 0.4 send.4
  12.2 6.0 %collective-permute-start.3 = (f32[2,80,80]{2,1,0:T(8,128)S(1)}, f32[2,80,80]{2,1,0:T(8,128)S(1)}, u32[]{:S(2)}, u32[]{:S(2)}) collective-permute-start(f32[2,80,80]{2,1,0:T(8,128)S(1)} %send.4), channel_id=1, source_target_pairs={{0,1},{2,3},{4,5},{6,7},{8,9},{10,11},{12,13},{14,15},{17,18},{19,... | collective-permute-start | bytes 153608 | tf_op jit(solution)/shard_map/ppermute | solution.py:358
  18.3 0.0 copy-done.1
  18.3 0.0 copy-done
  18.3 1.2 %same.4 = (f32[2,80,80]{2,1,0:T(8,128)S(1)}, f32[1,2048]{1,0:T(1,128)S(1)}) custom-call(s32[4]{0:T(128)S(1)} %copy-done.1, s32[4,2048]{1,0:T(4,128)S(1)} %copy-done, f32[2,48,128]{2,1,0:T(8,128)S(1)} %get-tuple-element.34.pay, f32[48,128]{1,0:T(8,128)S(1)} %collective-permute-done.1.far, f32[48,128]{1,0:T(8,128)S(1)} %collective-permute-done.2.sib_far), custom_call_target="tpu_custom_call" | custom-call | tf_op jit(solution)/shard_map/same/pallas_call | solution.py:359
  19.5 0.6 collective-permute-done.3.h
  20.1 0.0 collective-permute-start.4
  20.1 1.3 %collective-permute-done.4.g = f32[2,80,80]{2,1,0:T(8,128)S(1)} collective-permute-done((f32[2,80,80]{2,1,0:T(8,128)S(1)}, f32[2,80,80]{2,1,0:T(8,128)S(1)}, u32[]{:S(2)}, u32[]{:S(2)}) %collective-permute-start.4) | collective-permute-done | bytes 51232 | tf_op jit(solution)/shard_map/ppermute | solution.py:368
  21.4 0.5 step.3
  21.9 2.7 %collective-permute-start.5 = (f32[48,128]{1,0:T(8,128)S(1)}, f32[48,128]{1,0:T(8,128)S(1)}, u32[]{:S(2)}, u32[]{:S(2)}) collective-permute-start(f32[48,128]{1,0:T(8,128)S(1)} %get-tuple-element.41), channel_id=1, source_target_pairs={{0,32},{64,96},{48,80},{112,16},{32,0},{96,64},{80,48},{16,112},{1... | collective-permute-start | bytes 73736 | tf_op jit(solution)/shard_map/ppermute | solution.py:353
  24.6 1.2 %collective-permute-done.5.far = f32[48,128]{1,0:T(8,128)S(1)} collective-permute-done((f32[48,128]{1,0:T(8,128)S(1)}, f32[48,128]{1,0:T(8,128)S(1)}, u32[]{:S(2)}, u32[]{:S(2)}) %collective-permute-start.5) | collective-permute-done | bytes 24608 | tf_op jit(solution)/shard_map/ppermute | solution.py:353
  25.8 0.1 collective-permute-start.6
  25.9 1.1 %collective-permute-done.6.sib_far = f32[48,128]{1,0:T(8,128)S(1)} collective-permute-done((f32[48,128]{1,0:T(8,128)S(1)}, f32[48,128]{1,0:T(8,128)S(1)}, u32[]{:S(2)}, u32[]{:S(2)}) %collective-permute-start.6) | collective-permute-done | bytes 24608 | tf_op jit(solution)/shard_map/ppermute | solution.py:354
  27.0 0.4 send.5
  27.4 4.9 %collective-permute-start.7 = (f32[2,80,80]{2,1,0:T(8,128)S(1)}, f32[2,80,80]{2,1,0:T(8,128)S(1)}, u32[]{:S(2)}, u32[]{:S(2)}) collective-permute-start(f32[2,80,80]{2,1,0:T(8,128)S(1)} %send.5), channel_id=1, source_target_pairs={{0,1},{2,3},{4,5},{6,7},{8,9},{10,11},{12,13},{14,15},{17,18},{19,... | collective-permute-start | bytes 153608 | tf_op jit(solution)/shard_map/ppermute | solution.py:358
  32.3 1.2 %same.5 = (f32[2,80,80]{2,1,0:T(8,128)S(1)}, f32[1,2048]{1,0:T(1,128)S(1)}) custom-call(s32[4]{0:T(128)S(1)} %copy-done.1, s32[4,2048]{1,0:T(4,128)S(1)} %copy-done, f32[2,48,128]{2,1,0:T(8,128)S(1)} %get-tuple-element.40.pay, f32[48,128]{1,0:T(8,128)S(1)} %collective-permute-done.5.far, f32[48,128]{1,0:T(8,128)S(1)} %collective-permute-done.6.sib_far), custom_call_target="tpu_custom_call" | custom-call | tf_op jit(solution)/shard_map/same/pallas_call | solution.py:359
  33.5 0.6 collective-permute-done.7.h
  34.1 0.0 collective-permute-start.8
  34.1 1.3 %collective-permute-done.8.g = f32[2,80,80]{2,1,0:T(8,128)S(1)} collective-permute-done((f32[2,80,80]{2,1,0:T(8,128)S(1)}, f32[2,80,80]{2,1,0:T(8,128)S(1)}, u32[]{:S(2)}, u32[]{:S(2)}) %collective-permute-start.8) | collective-permute-done | bytes 51232 | tf_op jit(solution)/shard_map/ppermute | solution.py:368
  35.4 0.5 step.4
  35.9 2.7 %collective-permute-start.9 = (f32[48,128]{1,0:T(8,128)S(1)}, f32[48,128]{1,0:T(8,128)S(1)}, u32[]{:S(2)}, u32[]{:S(2)}) collective-permute-start(f32[48,128]{1,0:T(8,128)S(1)} %get-tuple-element.47), channel_id=1, source_target_pairs={{0,32},{64,96},{48,80},{112,16},{32,0},{96,64},{80,48},{16,112},{1... | collective-permute-start | bytes 73736 | tf_op jit(solution)/shard_map/ppermute | solution.py:353
  38.6 1.2 %collective-permute-done.9.far = f32[48,128]{1,0:T(8,128)S(1)} collective-permute-done((f32[48,128]{1,0:T(8,128)S(1)}, f32[48,128]{1,0:T(8,128)S(1)}, u32[]{:S(2)}, u32[]{:S(2)}) %collective-permute-start.9) | collective-permute-done | bytes 24608 | tf_op jit(solution)/shard_map/ppermute | solution.py:353
  39.8 0.1 collective-permute-start.10
  39.9 1.1 %collective-permute-done.10.sib_far = f32[48,128]{1,0:T(8,128)S(1)} collective-permute-done((f32[48,128]{1,0:T(8,128)S(1)}, f32[48,128]{1,0:T(8,128)S(1)}, u32[]{:S(2)}, u32[]{:S(2)}) %collective-permute-start.10) | collective-permute-done | bytes 24608 | tf_op jit(solution)/shard_map/ppermute | solution.py:354
  41.0 0.4 send.6
  41.4 4.9 %collective-permute-start.11 = (f32[2,80,80]{2,1,0:T(8,128)S(1)}, f32[2,80,80]{2,1,0:T(8,128)S(1)}, u32[]{:S(2)}, u32[]{:S(2)}) collective-permute-start(f32[2,80,80]{2,1,0:T(8,128)S(1)} %send.6), channel_id=1, source_target_pairs={{0,1},{2,3},{4,5},{6,7},{8,9},{10,11},{12,13},{14,15},{17,18},{19,... | collective-permute-start | bytes 153608 | tf_op jit(solution)/shard_map/ppermute | solution.py:358
  46.3 1.2 %same.6 = (f32[2,80,80]{2,1,0:T(8,128)S(1)}, f32[1,2048]{1,0:T(1,128)S(1)}) custom-call(s32[4]{0:T(128)S(1)} %copy-done.1, s32[4,2048]{1,0:T(4,128)S(1)} %copy-done, f32[2,48,128]{2,1,0:T(8,128)S(1)} %get-tuple-element.46.pay, f32[48,128]{1,0:T(8,128)S(1)} %collective-permute-done.9.far, f32[48,128]{1,0:T(8,128)S(1)} %collective-permute-done.10.sib_far), custom_call_target="tpu_custom_call" | custom-call | tf_op jit(solution)/shard_map/same/pallas_call | solution.py:359
  47.5 0.6 collective-permute-done.11.h
  48.1 0.0 collective-permute-start.12
  48.1 1.3 %collective-permute-done.12.g = f32[2,80,80]{2,1,0:T(8,128)S(1)} collective-permute-done((f32[2,80,80]{2,1,0:T(8,128)S(1)}, f32[2,80,80]{2,1,0:T(8,128)S(1)}, u32[]{:S(2)}, u32[]{:S(2)}) %collective-permute-start.12) | collective-permute-done | bytes 51232 | tf_op jit(solution)/shard_map/ppermute | solution.py:368
  49.4 0.5 step.5
  49.9 2.7 %collective-permute-start.13 = (f32[48,128]{1,0:T(8,128)S(1)}, f32[48,128]{1,0:T(8,128)S(1)}, u32[]{:S(2)}, u32[]{:S(2)}) collective-permute-start(f32[48,128]{1,0:T(8,128)S(1)} %get-tuple-element.53), channel_id=1, source_target_pairs={{0,32},{64,96},{48,80},{112,16},{32,0},{96,64},{80,48},{16,112},{1... | collective-permute-start | bytes 73736 | tf_op jit(solution)/shard_map/ppermute | solution.py:353
  52.6 0.1 pad_maximum_fusion
  52.6 0.7 broadcast_in_dim.2
  53.4 7.3 %all-to-all-start = ((f32[128,1,256]{2,1,0:T(1,128)}), f32[128,1,256]{2,1,0:T(1,128)S(1)}, u32[]{:S(2)}, u32[]{:S(2)}) async-start(f32[128,1,256]{2,1,0:T(1,128)} %broadcast_in_dim.2), calls=%async_computation | async-start | bytes 262144 | tf_op jit(solution)/shard_map/all_to_all | solution.py:390
  60.6 0.0 collective-permute-done.13.far
  60.6 1.1 %collective-permute-start.14 = (f32[48,128]{1,0:T(8,128)S(1)}, f32[48,128]{1,0:T(8,128)S(1)}, u32[]{:S(2)}, u32[]{:S(2)}) collective-permute-start(f32[48,128]{1,0:T(8,128)S(1)} %collective-permute-done.13.far), channel_id=1, source_target_pairs={{0,16},{32,48},{64,80},{96,112},{16,0},{48,32},{80,64},{112,96},{1... | collective-permute-start | bytes 73736 | tf_op jit(solution)/shard_map/ppermute | solution.py:354
  61.8 0.8 %collective-permute-done.14.sib_far = f32[48,128]{1,0:T(8,128)S(1)} collective-permute-done((f32[48,128]{1,0:T(8,128)S(1)}, f32[48,128]{1,0:T(8,128)S(1)}, u32[]{:S(2)}, u32[]{:S(2)}) %collective-permute-start.14) | collective-permute-done | bytes 24608 | tf_op jit(solution)/shard_map/ppermute | solution.py:354
  62.6 0.4 send.7
  63.1 4.8 %collective-permute-start.15 = (f32[2,80,80]{2,1,0:T(8,128)S(1)}, f32[2,80,80]{2,1,0:T(8,128)S(1)}, u32[]{:S(2)}, u32[]{:S(2)}) collective-permute-start(f32[2,80,80]{2,1,0:T(8,128)S(1)} %send.7), channel_id=1, source_target_pairs={{0,1},{2,3},{4,5},{6,7},{8,9},{10,11},{12,13},{14,15},{17,18},{19,... | collective-permute-start | bytes 153608 | tf_op jit(solution)/shard_map/ppermute | solution.py:358
  67.9 1.2 %same.7 = (f32[2,80,80]{2,1,0:T(8,128)S(1)}, f32[1,2048]{1,0:T(1,128)S(1)}) custom-call(s32[4]{0:T(128)S(1)} %copy-done.1, s32[4,2048]{1,0:T(4,128)S(1)} %copy-done, f32[2,48,128]{2,1,0:T(8,128)S(1)} %get-tuple-element.52.pay, f32[48,128]{1,0:T(8,128)S(1)} %collective-permute-done.13.far, f32[48,128]{1,0:T(8,128)S(1)} %collective-permute-done.14.sib_far), custom_call_target="tpu_custom_call" | custom-call | tf_op jit(solution)/shard_map/same/pallas_call | solution.py:359
  69.0 1.0 %collective-permute-done.15.h = f32[2,80,80]{2,1,0:T(8,128)S(1)} collective-permute-done((f32[2,80,80]{2,1,0:T(8,128)S(1)}, f32[2,80,80]{2,1,0:T(8,128)S(1)}, u32[]{:S(2)}, u32[]{:S(2)}) %collective-permute-start.15) | collective-permute-done | bytes 51232 | tf_op jit(solution)/shard_map/ppermute | solution.py:358
  70.1 0.0 collective-permute-start.16
  70.1 0.8 all-to-all-done
  70.8 2.1 %place.1 = f32[4,2048]{1,0:T(4,128)} custom-call(s32[4]{0:T(128)S(1)} %copy-done.1, s32[4,2048]{1,0:T(4,128)S(1)} %copy-done, f32[128,256]{1,0:T(8,128)S(1)} %bitcast.5, f32[1,2048]{1,0:T(1,128)S(1)} %get-tuple-element.62.r0, f32[1,2048]{1,0:T(1,128)S(1)} %get-tuple-element.63.r1, f32[1,2048]{1,0:T(1,128)S(1)} %get-tuple-element.64.r2, ...), custom_call_target="tpu_custom_call" | custom-call | tf_op jit(solution)/shard_map/place/pallas_call | solution.py:391
  73.0 0.0 collective-permute-done.16.g
  73.0 11.3 %final.1 = f32[80,4,32,256]{3,2,1,0:T(8,128)} custom-call(f32[2,80,80]{2,1,0:T(8,128)S(1)} %get-tuple-element.55.q0, f32[2,80,80]{2,1,0:T(8,128)S(1)} %collective-permute-done.15.h, f32[2,80,80]{2,1,0:T(8,128)S(1)} %collective-permute-done.16.g, f32[2,96,384]{2,1,0:T(8,128)S(1)} %get-tuple-element.57.z, f32[80,4,32,256]{3,2,1,0:T(8,128)} %x.1), custom_call_target="tpu_custom_call" | custom-call | tf_op jit(solution)/shard_map/final/pallas_call | solution.py:380
  (1 shorter events, 0.0 us)
Async XLA Ops:
  0.6 17.6 %copy-start.1 = (s32[4]{0:T(128)S(1)}, s32[4]{0:T(128)}, u32[]{:S(2)}) copy-start(s32[4]{0:T(128)} %order.9) | copy-start | bytes 52
  0.6 17.6 %copy-start = (s32[4,2048]{1,0:T(4,128)S(1)}, s32[4,2048]{1,0:T(4,128)}, u32[]{:S(2)}) copy-start(s32[4,2048]{1,0:T(4,128)} %owner.9) | copy-start | bytes 98308
  3.9 2.5 %collective-permute-start = (f32[96,256]{1,0:T(8,128)S(1)}, f32[96,256]{1,0:T(8,128)S(1)}, u32[]{:S(2)}, u32[]{:S(2)}) collective-permute-start(f32[96,256]{1,0:T(8,128)S(1)} %init.1.own), channel_id=1, source_target_pairs={{0,16},{32,48},{64,80},{96,112},{16,0},{48,32},{80,64},{112,96},{1... | collective-permute-start | bytes 294920 | tf_op jit(solution)/shard_map/ppermute | solution.py:350
  6.5 4.1 %collective-permute-start.1 = (f32[48,128]{1,0:T(8,128)S(1)}, f32[48,128]{1,0:T(8,128)S(1)}, u32[]{:S(2)}, u32[]{:S(2)}) collective-permute-start(f32[48,128]{1,0:T(8,128)S(1)} %get-tuple-element.35), channel_id=1, source_target_pairs={{0,32},{64,96},{48,80},{112,16},{32,0},{96,64},{80,48},{16,112},{1... | collective-permute-start | bytes 73736 | tf_op jit(solution)/shard_map/ppermute | solution.py:353
  10.6 1.2 %collective-permute-start.2 = (f32[48,128]{1,0:T(8,128)S(1)}, f32[48,128]{1,0:T(8,128)S(1)}, u32[]{:S(2)}, u32[]{:S(2)}) collective-permute-start(f32[48,128]{1,0:T(8,128)S(1)} %collective-permute-done.1.far), channel_id=1, source_target_pairs={{0,16},{32,48},{64,80},{96,112},{16,0},{48,32},{80,64},{112,96},{1... | collective-permute-start | bytes 73736 | tf_op jit(solution)/shard_map/ppermute | solution.py:354
  12.2 7.9 %collective-permute-start.3 = (f32[2,80,80]{2,1,0:T(8,128)S(1)}, f32[2,80,80]{2,1,0:T(8,128)S(1)}, u32[]{:S(2)}, u32[]{:S(2)}) collective-permute-start(f32[2,80,80]{2,1,0:T(8,128)S(1)} %send.4), channel_id=1, source_target_pairs={{0,1},{2,3},{4,5},{6,7},{8,9},{10,11},{12,13},{14,15},{17,18},{19,... | collective-permute-start | bytes 153608 | tf_op jit(solution)/shard_map/ppermute | solution.py:358
  20.1 1.3 %collective-permute-start.4 = (f32[2,80,80]{2,1,0:T(8,128)S(1)}, f32[2,80,80]{2,1,0:T(8,128)S(1)}, u32[]{:S(2)}, u32[]{:S(2)}) collective-permute-start(f32[2,80,80]{2,1,0:T(8,128)S(1)} %collective-permute-done.3.h), channel_id=1, source_target_pairs={{0,16},{32,48},{64,80},{96,112},{16,0},{48,32},{80,64},{112,96},{1... | collective-permute-start | bytes 153608 | tf_op jit(solution)/shard_map/ppermute | solution.py:368
  21.9 3.9 %collective-permute-start.5 = (f32[48,128]{1,0:T(8,128)S(1)}, f32[48,128]{1,0:T(8,128)S(1)}, u32[]{:S(2)}, u32[]{:S(2)}) collective-permute-start(f32[48,128]{1,0:T(8,128)S(1)} %get-tuple-element.41), channel_id=1, source_target_pairs={{0,32},{64,96},{48,80},{112,16},{32,0},{96,64},{80,48},{16,112},{1... | collective-permute-start | bytes 73736 | tf_op jit(solution)/shard_map/ppermute | solution.py:353
  25.8 1.2 %collective-permute-start.6 = (f32[48,128]{1,0:T(8,128)S(1)}, f32[48,128]{1,0:T(8,128)S(1)}, u32[]{:S(2)}, u32[]{:S(2)}) collective-permute-start(f32[48,128]{1,0:T(8,128)S(1)} %collective-permute-done.5.far), channel_id=1, source_target_pairs={{0,16},{32,48},{64,80},{96,112},{16,0},{48,32},{80,64},{112,96},{1... | collective-permute-start | bytes 73736 | tf_op jit(solution)/shard_map/ppermute | solution.py:354
  27.4 6.7 %collective-permute-start.7 = (f32[2,80,80]{2,1,0:T(8,128)S(1)}, f32[2,80,80]{2,1,0:T(8,128)S(1)}, u32[]{:S(2)}, u32[]{:S(2)}) collective-permute-start(f32[2,80,80]{2,1,0:T(8,128)S(1)} %send.5), channel_id=1, source_target_pairs={{0,1},{2,3},{4,5},{6,7},{8,9},{10,11},{12,13},{14,15},{17,18},{19,... | collective-permute-start | bytes 153608 | tf_op jit(solution)/shard_map/ppermute | solution.py:358
  34.1 1.3 %collective-permute-start.8 = (f32[2,80,80]{2,1,0:T(8,128)S(1)}, f32[2,80,80]{2,1,0:T(8,128)S(1)}, u32[]{:S(2)}, u32[]{:S(2)}) collective-permute-start(f32[2,80,80]{2,1,0:T(8,128)S(1)} %collective-permute-done.7.h), channel_id=1, source_target_pairs={{0,16},{32,48},{64,80},{96,112},{16,0},{48,32},{80,64},{112,96},{1... | collective-permute-start | bytes 153608 | tf_op jit(solution)/shard_map/ppermute | solution.py:368
  35.9 3.9 %collective-permute-start.9 = (f32[48,128]{1,0:T(8,128)S(1)}, f32[48,128]{1,0:T(8,128)S(1)}, u32[]{:S(2)}, u32[]{:S(2)}) collective-permute-start(f32[48,128]{1,0:T(8,128)S(1)} %get-tuple-element.47), channel_id=1, source_target_pairs={{0,32},{64,96},{48,80},{112,16},{32,0},{96,64},{80,48},{16,112},{1... | collective-permute-start | bytes 73736 | tf_op jit(solution)/shard_map/ppermute | solution.py:353
  39.8 1.2 %collective-permute-start.10 = (f32[48,128]{1,0:T(8,128)S(1)}, f32[48,128]{1,0:T(8,128)S(1)}, u32[]{:S(2)}, u32[]{:S(2)}) collective-permute-start(f32[48,128]{1,0:T(8,128)S(1)} %collective-permute-done.9.far), channel_id=1, source_target_pairs={{0,16},{32,48},{64,80},{96,112},{16,0},{48,32},{80,64},{112,96},{1... | collective-permute-start | bytes 73736 | tf_op jit(solution)/shard_map/ppermute | solution.py:354
  41.4 6.7 %collective-permute-start.11 = (f32[2,80,80]{2,1,0:T(8,128)S(1)}, f32[2,80,80]{2,1,0:T(8,128)S(1)}, u32[]{:S(2)}, u32[]{:S(2)}) collective-permute-start(f32[2,80,80]{2,1,0:T(8,128)S(1)} %send.6), channel_id=1, source_target_pairs={{0,1},{2,3},{4,5},{6,7},{8,9},{10,11},{12,13},{14,15},{17,18},{19,... | collective-permute-start | bytes 153608 | tf_op jit(solution)/shard_map/ppermute | solution.py:358
  48.1 1.3 %collective-permute-start.12 = (f32[2,80,80]{2,1,0:T(8,128)S(1)}, f32[2,80,80]{2,1,0:T(8,128)S(1)}, u32[]{:S(2)}, u32[]{:S(2)}) collective-permute-start(f32[2,80,80]{2,1,0:T(8,128)S(1)} %collective-permute-done.11.h), channel_id=1, source_target_pairs={{0,16},{32,48},{64,80},{96,112},{16,0},{48,32},{80,64},{112,96},{1... | collective-permute-start | bytes 153608 | tf_op jit(solution)/shard_map/ppermute | solution.py:368
  49.9 10.8 %collective-permute-start.13 = (f32[48,128]{1,0:T(8,128)S(1)}, f32[48,128]{1,0:T(8,128)S(1)}, u32[]{:S(2)}, u32[]{:S(2)}) collective-permute-start(f32[48,128]{1,0:T(8,128)S(1)} %get-tuple-element.53), channel_id=1, source_target_pairs={{0,32},{64,96},{48,80},{112,16},{32,0},{96,64},{80,48},{16,112},{1... | collective-permute-start | bytes 73736 | tf_op jit(solution)/shard_map/ppermute | solution.py:353
  53.4 17.5 %all-to-all-start = ((f32[128,1,256]{2,1,0:T(1,128)}), f32[128,1,256]{2,1,0:T(1,128)S(1)}, u32[]{:S(2)}, u32[]{:S(2)}) async-start(f32[128,1,256]{2,1,0:T(1,128)} %broadcast_in_dim.2), calls=%async_computation | async-start | bytes 262144 | tf_op jit(solution)/shard_map/all_to_all | solution.py:390
  60.6 2.0 %collective-permute-start.14 = (f32[48,128]{1,0:T(8,128)S(1)}, f32[48,128]{1,0:T(8,128)S(1)}, u32[]{:S(2)}, u32[]{:S(2)}) collective-permute-start(f32[48,128]{1,0:T(8,128)S(1)} %collective-permute-done.13.far), channel_id=1, source_target_pairs={{0,16},{32,48},{64,80},{96,112},{16,0},{48,32},{80,64},{112,96},{1... | collective-permute-start | bytes 73736 | tf_op jit(solution)/shard_map/ppermute | solution.py:354
  63.1 7.0 %collective-permute-start.15 = (f32[2,80,80]{2,1,0:T(8,128)S(1)}, f32[2,80,80]{2,1,0:T(8,128)S(1)}, u32[]{:S(2)}, u32[]{:S(2)}) collective-permute-start(f32[2,80,80]{2,1,0:T(8,128)S(1)} %send.7), channel_id=1, source_target_pairs={{0,1},{2,3},{4,5},{6,7},{8,9},{10,11},{12,13},{14,15},{17,18},{19,... | collective-permute-start | bytes 153608 | tf_op jit(solution)/shard_map/ppermute | solution.py:358
  70.1 2.9 %collective-permute-start.16 = (f32[2,80,80]{2,1,0:T(8,128)S(1)}, f32[2,80,80]{2,1,0:T(8,128)S(1)}, u32[]{:S(2)}, u32[]{:S(2)}) collective-permute-start(f32[2,80,80]{2,1,0:T(8,128)S(1)} %collective-permute-done.15.h), channel_id=1, source_target_pairs={{0,16},{32,48},{64,80},{96,112},{16,0},{48,32},{80,64},{112,96},{1... | collective-permute-start | bytes 153608 | tf_op jit(solution)/shard_map/ppermute | solution.py:368

commit v4 on v3

--- a/solution.py
+++ b/solution.py
@@ -19,10 +19,13 @@
 F32 = jnp.float32
 BF16 = jnp.bfloat16
 HIGH = lax.Precision.HIGHEST
+SLAB = 16
+PARTS = TX // SLAB
 
 ROW_A = M
 ROW_C = M + 1
 ROW_W = M + 2
+ROW_N = M + 11
 ROWS = 96
 TAPER = (0.25, 0.5, 0.25, 0.5, 1.0, 0.5, 0.25, 0.5, 0.25)
 
@@ -166,19 +169,28 @@
     return lax.rem(index + core_of(), 2) == 0
 
 
-def emit(k, z, pay_out, edge_out, nv_out):
-    pays, news = [], []
-    for t in range(2):
-        at = slice(CAP * k, CAP * k + CAP)
+def emit(k, z, z_out, pay_out, edge_out, nv_out=None):
+    pays = []
+    at = slice(CAP * k, CAP * k + CAP)
+    news = []
+    for t in range(2):
         pay, normed = make_payload(z[t][:M, at], z[t][M:, at])
         pay_out[t] = pay
+        z_out[t, ROW_N : ROW_N + 1, at] = normed
         pays.append(pay)
         news.append(normed)
     edge_out[...] = jnp.where(upward(lax.axis_index("gx") // 2), pays[1], pays[0])
-    nv_out[...] = jnp.where(core_of() == 0, news[0], news[1])
-
-
-def start_kernel(own, sib, z_out, pay_out, edge_out, nv_out):
+    if nv_out is not None:
+        first = core_of() == 0
+        past = slice(0, CAP * k)
+        row = jnp.concatenate([
+            jnp.where(first, z[0][ROW_N : ROW_N + 1, past], z[1][ROW_N : ROW_N + 1, past]),
+            jnp.where(first, news[0], news[1]),
+        ], axis=1)
+        nv_out[...] = jnp.broadcast_to(row[None], nv_out.shape)
+
+
+def start_kernel(own, sib, z_out, pay_out, edge_out):
     first = core_of() == 0
     mine, other = own[...], sib[...]
     z = [jnp.where(first, mine, other), jnp.where(first, other, mine)]
@@ -187,7 +199,7 @@
     for t in range(2):
         z_out[t, :, : NB * CAP] = z[t]
         z_out[t, :, NB * CAP :] = unit
-    emit(0, z, pay_out, edge_out, nv_out)
+    emit(0, z, z_out, pay_out, edge_out)
 
 
 def right_side(rows):
@@ -251,18 +263,20 @@
     return q0[t] + jnp.where(ends & jnp.logical_not(first), 0.0, h[t]) + jnp.where(ends & first, 0.0, g[t])
 
 
-def step_kernel(k, q0, h, g, z, z_out, pay_out, edge_out, nv_out):
+def step_kernel(k, q0, h, g, z, z_out, pay_out, edge_out, nv_out=None):
     new = []
     for t in range(2):
         moved = advance(z[t, :M], whole_gain(t, q0, h, g))
         z_out[t, :M] = moved
         z_out[t, M:] = z[t, M:]
         new.append(jnp.concatenate([moved, z[t, M:]], axis=0))
-    emit(k, new, pay_out, edge_out, nv_out)
+    emit(k, new, z_out, pay_out, edge_out, nv_out)
 
 
 def final_kernel(q0, h, g, z, x, out, mix):
-    @pl.when(pl.program_id(0) == 0)
+    step = pl.program_id(0)
+
+    @pl.when(step == 0)
     def _():
         c = core_of()
         t = advance(z[c, :M, NB * CAP :], whole_gain(c, q0, h, g))[:, :M]
@@ -271,8 +285,9 @@
         mix[...] = jnp.concatenate([dh, dh, dl], axis=1)
 
     w = mix[...]
-    for t in range(TX // 8):
-        block = x[:, 0, 8 * t : 8 * t + 8, :]
+    level, start = step // PARTS, lax.rem(step, PARTS) * SLAB
+    for t in range(SLAB // 8):
+        block = x[:, level, pl.ds(pl.multiple_of(start + 8 * t, 8), 8), :]
         turned = jnp.swapaxes(block, 0, 1)
         updates = []
         for i in range(8):
@@ -311,7 +326,7 @@
 
 
 def local(ensemble, obs_value, obs_variance, obs_owner, obs_cell, obs_reach, batch_order):
-    params = pltpu.CompilerParams(vmem_limit_bytes=48 * 2**20)
+    params = pltpu.CompilerParams(vmem_limit_bytes=24 * 2**20)
     call = functools.partial(pl.pallas_call, compiler_params=params)
     width, height = lax.axis_size("gx"), lax.axis_size("gy")
     both = ("gx", "gy")
@@ -319,9 +334,9 @@
     chips = width // 2
     side_x = swaps([(2 * y + c, 2 * ((y + 1) % chips) + c) for c in range(2) for y in range(c, chips, 2)])
     side_y = swaps([
-        (x * height + k, x * height + (k + 1) % height) for x in range(width) for k in range(x % 2, height, 2)
-    ])
-    pay_shapes = (shape(2, ROWS // 2, 128), shape(ROWS // 2, 128), shape(1, CAP))
+        (x * height + k, x * height + k + 1) for x in range(width) for k in range(x % 2, height - 1, 2)
+    ] + [(x * height + k, (x + 2) * height + k) for x in range(1, width, 4) for k in (0, height - 1)])
+    pay_shapes = (shape(2, ROWS // 2, 128), shape(ROWS // 2, 128))
     z_shape = shape(2, ROWS, NB * CAP + 128)
     row = pltpu.VMEM((NB, OBS), F32)
     row_i = pltpu.VMEM((NB, OBS), jnp.int32)
@@ -341,16 +356,20 @@
             batch_order, obs_value, obs_variance, obs_owner, obs_cell, jnp.swapaxes(obs_reach, 1, 2), ensemble
         )
     ))
-    z, pay, edge, nv = call(
+    z, pay, edge = call(
         start_kernel,
         out_shape=(z_shape,) + pay_shapes,
         in_specs=[VMEM] * 2,
-        out_specs=(VMEM,) * 4,
+        out_specs=(VMEM,) * 3,
         name="start",
     )(own, lax.ppermute(own, "gx", core))
-    normed, ranks = [nv], []
+    ranks = []
     for k in range(NB):
+        last = k + 1 == NB
         far = lax.ppermute(edge, "gx", side_x)
+        if last:
+            everyone = lax.all_to_all(nv, both, 0, 0, tiled=True).reshape(TILES, NB * CAP)
+            far, everyone = lax.optimization_barrier((far, everyone))
         sib_far = lax.ppermute(far, "gx", core)
         send = call(send_kernel, out_shape=shape(2, M, M), in_specs=[VMEM] * 3, out_specs=VMEM, name="send")(
             pay, far, sib_far
@@ -364,37 +383,38 @@
             name="same",
         )(batch_order, obs_owner, pay, far, sib_far)
         ranks.append(rank)
-        h, q0 = lax.optimization_barrier((h, q0))
+        if last:
+            innovation = call(
+                place_kernel,
+                out_shape=shape(NB, OBS),
+                in_specs=[SMEM] + [VMEM] * 6,
+                out_specs=VMEM,
+                name="place",
+            )(batch_order, obs_owner, everyone, *ranks)
+            h, q0, innovation = lax.optimization_barrier((h, q0, innovation))
+        else:
+            h, q0 = lax.optimization_barrier((h, q0))
         g = lax.ppermute(h, "gx", core)
-        if k + 1 < NB:
-            z, pay, edge, nv = call(
+        if not last:
+            wide = (shape(TILES, 1, NB * CAP),) if k + 2 == NB else ()
+            z, pay, edge, *rest = call(
                 functools.partial(step_kernel, k + 1),
-                out_shape=(z_shape,) + pay_shapes,
+                out_shape=(z_shape,) + pay_shapes + wide,
                 in_specs=[VMEM] * 4,
-                out_specs=(VMEM,) * 4,
+                out_specs=(VMEM,) * (3 + len(wide)),
                 name="step",
             )(q0, h, g, z)
-            normed.append(nv)
-    small = lambda *dims: pl.BlockSpec(dims, lambda i: (0,) * len(dims))
-    slab = pl.BlockSpec((M, 1, TX, TY), lambda i: (0, i, 0, 0))
+            if rest:
+                nv = rest[0]
     state = call(
         final_kernel,
         out_shape=shape(M, LEV, TX, TY),
-        grid=(LEV,),
-        in_specs=[small(2, M, M)] * 3 + [small(2, ROWS, NB * CAP + 128), slab],
-        out_specs=slab,
+        grid=(LEV * PARTS,),
+        in_specs=[VMEM] * 5,
+        out_specs=pl.BlockSpec((M, 1, SLAB, TY), lambda i: (0, i // PARTS, i % PARTS, 0)),
         scratch_shapes=[pltpu.VMEM((M, 3 * M), BF16)],
         name="final",
-    )(q0, h, g, z, ensemble)
-    mine = jnp.concatenate(normed, axis=1)
-    everyone = lax.all_to_all(jnp.broadcast_to(mine, (TILES, NB * CAP)), both, 0, 0, tiled=True)
-    innovation = call(
-        place_kernel,
-        out_shape=shape(NB, OBS),
-        in_specs=[SMEM] + [VMEM] * 6,
-        out_specs=VMEM,
-        name="place",
-    )(batch_order, obs_owner, everyone, *ranks)
+    )(q0, h, g, z, pltpu.with_memory_space_constraint(ensemble, pltpu.VMEM))
     return state, innovation
 
 

time: 84.5 us -> 86 us (1.018)
  waiting for transfers between devices: 16.2 us -> 23.4 us
  starting transfers between devices: 41.8 us -> 35.1 us
  local copies, waits for them, and re-layouts: 0.75 us -> 4 us
  Pallas kernels: 24.7 us -> 22.6 us
    ppermute x4, starting transfers between devices: 20.5 us -> 4.39 us  [local(): h = lax.ppermute(send, both, side_y)]
    all_to_all x1, waiting for transfers between devices: 0.77 us -> 7.47 us  [local(): lax.all_to_all(nv, both, 0, 0, tiled=True).reshape(TILES, NB * CAP)]
    all_to_all x1, starting transfers between devices: 7.26 us -> 12.7 us  [local(): lax.all_to_all(nv, both, 0, 0, tiled=True).reshape(TILES, NB * CAP)]
    ppermute x4, starting transfers between devices: 0.01 us -> 4.2 us  [local(): g = lax.ppermute(h, 'gx', core)]
    unnamed x5 -> x7, local copies, waits for them, and re-layouts: 0.02 us -> 4 us
    pallas_call x1, Pallas kernels: 11.3 us -> 8.6 us  [local(): call(final_kernel, out_shape=shape(M, LEV, TX, TY), grid=(LEV * PARTS,),...]
  transfers between devices with their start and end apart: 18 -> 18, of which waited for: 16 -> 16; matrix products, arithmetic and copies ran while one was open for 1% -> 0% of each run, Pallas kernels for 8% -> 8%
where the time goes in v4:
time: 86 us; the launch traced here: 85.8 us
  starting transfers between devices  35.1 us (41%)
  waiting for transfers between devices  23.4 us (27%)
  Pallas kernels  22.6 us (26%)
  local copies, waits for them, and re-layouts  4 us (5%)
    all_to_all x1, starting transfers between devices, local(): lax.all_to_all(nv, both, 0, 0, tiled=True).reshape(TILES, NB * CAP)  12.7 us
    ppermute x4, starting transfers between devices, local(): far = lax.ppermute(edge, 'gx', side_x)  11.3 us
    pallas_call x1, Pallas kernels, local(): call(final_kernel, out_shape=shape(M, LEV, TX, TY), grid=(LEV * PARTS,),...  8.6 us
    all_to_all x1, waiting for transfers between devices, local(): lax.all_to_all(nv, both, 0, 0, tiled=True).reshape(TILES, NB * CAP)  7.47 us
    pallas_call x4, Pallas kernels, local(): call(functools.partial(same_kernel, k), out_shape=(shape(2, M, M), shape(...  4.7 us
    ppermute x4, starting transfers between devices, local(): h = lax.ppermute(send, both, side_y)  4.39 us
    ppermute x4, starting transfers between devices, local(): g = lax.ppermute(h, 'gx', core)  4.2 us
    unnamed x7, local copies, waits for them, and re-layouts  4 us
  transfers between devices with their start and end apart: 18, of which 16 were waited for; matrix products, arithmetic and copies ran while one was open for 0% of the time, Pallas kernels for 8%

profile of v4, /device:TPU:1, one launch (start us, length us, event | category | flops | bytes accessed | tf_op | source)
XLA Modules:
  0.0 85.8 jit_solution(7774376619661749794)
XLA Ops:
  0.6 0.0 copy-start.2
  0.6 0.0 copy-start.1
  0.7 3.3 %init.1.own = f32[96,256]{1,0:T(8,128)S(1)} custom-call(s32[4]{0:T(128)} %order.9, f32[4,2048]{1,0:T(4,128)} %value_hbm.1, f32[4,2048]{1,0:T(4,128)} %variance_hbm.1, s32[4,2048]{1,0:T(4,128)} %owner.9, s32[4,2048]{1,0:T(4,128)} %cell_hbm.1, s32[4,8,2048]{2,1,0:T(8,128)} %bitcast.5, f32[80,4,32,256]{3,2,1,0:T(8,128)} %x.1), custom_call_target="tpu_custom_call" | custom-call | tf_op jit(solution)/shard_map/init/pallas_call | solution.py:343
  3.9 1.5 %collective-permute-start = (f32[96,256]{1,0:T(8,128)S(1)}, f32[96,256]{1,0:T(8,128)S(1)}, u32[]{:S(2)}, u32[]{:S(2)}) collective-permute-start(f32[96,256]{1,0:T(8,128)S(1)} %init.1.own), channel_id=1, source_target_pairs={{0,16},{32,48},{64,80},{96,112},{16,0},{48,32},{80,64},{112,96},{1... | collective-permute-start | bytes 294920 | tf_op jit(solution)/shard_map/ppermute | solution.py:365
  5.4 0.9 %collective-permute-done.sib = f32[96,256]{1,0:T(8,128)S(1)} collective-permute-done((f32[96,256]{1,0:T(8,128)S(1)}, f32[96,256]{1,0:T(8,128)S(1)}, u32[]{:S(2)}, u32[]{:S(2)}) %collective-permute-start) | collective-permute-done | bytes 98336 | tf_op jit(solution)/shard_map/ppermute | solution.py:365
  6.4 0.2 start.1
  6.5 2.9 %collective-permute-start.1 = (f32[48,128]{1,0:T(8,128)S(1)}, f32[48,128]{1,0:T(8,128)S(1)}, u32[]{:S(2)}, u32[]{:S(2)}) collective-permute-start(f32[48,128]{1,0:T(8,128)S(1)} %get-tuple-element.35), channel_id=1, source_target_pairs={{0,32},{64,96},{48,80},{112,16},{32,0},{96,64},{80,48},{16,112},{1... | collective-permute-start | bytes 73736 | tf_op jit(solution)/shard_map/ppermute | solution.py:369
  9.4 1.2 %collective-permute-done.1.far = f32[48,128]{1,0:T(8,128)S(1)} collective-permute-done((f32[48,128]{1,0:T(8,128)S(1)}, f32[48,128]{1,0:T(8,128)S(1)}, u32[]{:S(2)}, u32[]{:S(2)}) %collective-permute-start.1) | collective-permute-done | bytes 24608 | tf_op jit(solution)/shard_map/ppermute | solution.py:369
  10.6 0.2 collective-permute-start.2
  10.8 1.0 %collective-permute-done.2.sib_far = f32[48,128]{1,0:T(8,128)S(1)} collective-permute-done((f32[48,128]{1,0:T(8,128)S(1)}, f32[48,128]{1,0:T(8,128)S(1)}, u32[]{:S(2)}, u32[]{:S(2)}) %collective-permute-start.2) | collective-permute-done | bytes 24608 | tf_op jit(solution)/shard_map/ppermute | solution.py:373
  11.8 0.4 send.4
  12.2 1.3 %collective-permute-start.3 = (f32[2,80,80]{2,1,0:T(8,128)S(1)}, f32[2,80,80]{2,1,0:T(8,128)S(1)}, u32[]{:S(2)}, u32[]{:S(2)}) collective-permute-start(f32[2,80,80]{2,1,0:T(8,128)S(1)} %send.4), channel_id=1, source_target_pairs={{0,1},{2,3},{4,5},{6,7},{8,9},{10,11},{12,13},{14,15},{17,18},{19,... | collective-permute-start | bytes 153608 | tf_op jit(solution)/shard_map/ppermute | solution.py:377
  13.5 0.0 copy-done.2
  13.5 0.0 copy-done.1
  13.5 1.2 %same.4 = (f32[2,80,80]{2,1,0:T(8,128)S(1)}, f32[1,2048]{1,0:T(1,128)S(1)}) custom-call(s32[4]{0:T(128)S(1)} %copy-done.2, s32[4,2048]{1,0:T(4,128)S(1)} %copy-done.1, f32[2,48,128]{2,1,0:T(8,128)S(1)} %get-tuple-element.34.pay, f32[48,128]{1,0:T(8,128)S(1)} %collective-permute-done.1.far, f32[48,128]{1,0:T(8,128)S(1)} %collective-permute-done.2.sib_far), custom_call_target="tpu_custom_call" | custom-call | tf_op jit(solution)/shard_map/same/pallas_call | solution.py:378
  14.7 1.2 %collective-permute-done.3.h = f32[2,80,80]{2,1,0:T(8,128)S(1)} collective-permute-done((f32[2,80,80]{2,1,0:T(8,128)S(1)}, f32[2,80,80]{2,1,0:T(8,128)S(1)}, u32[]{:S(2)}, u32[]{:S(2)}) %collective-permute-start.3) | collective-permute-done | bytes 51232 | tf_op jit(solution)/shard_map/ppermute | solution.py:377
  15.9 1.0 %collective-permute-start.4 = (f32[2,80,80]{2,1,0:T(8,128)S(1)}, f32[2,80,80]{2,1,0:T(8,128)S(1)}, u32[]{:S(2)}, u32[]{:S(2)}) collective-permute-start(f32[2,80,80]{2,1,0:T(8,128)S(1)} %collective-permute-done.3.h), channel_id=1, source_target_pairs={{0,16},{32,48},{64,80},{96,112},{16,0},{48,32},{80,64},{112,96},{1... | collective-permute-start | bytes 153608 | tf_op jit(solution)/shard_map/ppermute | solution.py:397
  16.9 0.9 %collective-permute-done.4.g = f32[2,80,80]{2,1,0:T(8,128)S(1)} collective-permute-done((f32[2,80,80]{2,1,0:T(8,128)S(1)}, f32[2,80,80]{2,1,0:T(8,128)S(1)}, u32[]{:S(2)}, u32[]{:S(2)}) %collective-permute-start.4) | collective-permute-done | bytes 51232 | tf_op jit(solution)/shard_map/ppermute | solution.py:397
  17.9 0.4 step.3
  18.3 2.9 %collective-permute-start.5 = (f32[48,128]{1,0:T(8,128)S(1)}, f32[48,128]{1,0:T(8,128)S(1)}, u32[]{:S(2)}, u32[]{:S(2)}) collective-permute-start(f32[48,128]{1,0:T(8,128)S(1)} %get-tuple-element.41), channel_id=1, source_target_pairs={{0,32},{64,96},{48,80},{112,16},{32,0},{96,64},{80,48},{16,112},{1... | collective-permute-start | bytes 73736 | tf_op jit(solution)/shard_map/ppermute | solution.py:369
  21.2 1.2 %collective-permute-done.5.far = f32[48,128]{1,0:T(8,128)S(1)} collective-permute-done((f32[48,128]{1,0:T(8,128)S(1)}, f32[48,128]{1,0:T(8,128)S(1)}, u32[]{:S(2)}, u32[]{:S(2)}) %collective-permute-start.5) | collective-permute-done | bytes 24608 | tf_op jit(solution)/shard_map/ppermute | solution.py:369
  22.4 0.2 collective-permute-start.6
  22.5 1.0 %collective-permute-done.6.sib_far = f32[48,128]{1,0:T(8,128)S(1)} collective-permute-done((f32[48,128]{1,0:T(8,128)S(1)}, f32[48,128]{1,0:T(8,128)S(1)}, u32[]{:S(2)}, u32[]{:S(2)}) %collective-permute-start.6) | collective-permute-done | bytes 24608 | tf_op jit(solution)/shard_map/ppermute | solution.py:373
  23.6 0.4 send.5
  24.0 1.3 %collective-permute-start.7 = (f32[2,80,80]{2,1,0:T(8,128)S(1)}, f32[2,80,80]{2,1,0:T(8,128)S(1)}, u32[]{:S(2)}, u32[]{:S(2)}) collective-permute-start(f32[2,80,80]{2,1,0:T(8,128)S(1)} %send.5), channel_id=1, source_target_pairs={{0,1},{2,3},{4,5},{6,7},{8,9},{10,11},{12,13},{14,15},{17,18},{19,... | collective-permute-start | bytes 153608 | tf_op jit(solution)/shard_map/ppermute | solution.py:377
  25.3 1.2 %same.5 = (f32[2,80,80]{2,1,0:T(8,128)S(1)}, f32[1,2048]{1,0:T(1,128)S(1)}) custom-call(s32[4]{0:T(128)S(1)} %copy-done.2, s32[4,2048]{1,0:T(4,128)S(1)} %copy-done.1, f32[2,48,128]{2,1,0:T(8,128)S(1)} %get-tuple-element.40.pay, f32[48,128]{1,0:T(8,128)S(1)} %collective-permute-done.5.far, f32[48,128]{1,0:T(8,128)S(1)} %collective-permute-done.6.sib_far), custom_call_target="tpu_custom_call" | custom-call | tf_op jit(solution)/shard_map/same/pallas_call | solution.py:378
  26.4 1.2 %collective-permute-done.7.h = f32[2,80,80]{2,1,0:T(8,128)S(1)} collective-permute-done((f32[2,80,80]{2,1,0:T(8,128)S(1)}, f32[2,80,80]{2,1,0:T(8,128)S(1)}, u32[]{:S(2)}, u32[]{:S(2)}) %collective-permute-start.7) | collective-permute-done | bytes 51232 | tf_op jit(solution)/shard_map/ppermute | solution.py:377
  27.7 1.0 %collective-permute-start.8 = (f32[2,80,80]{2,1,0:T(8,128)S(1)}, f32[2,80,80]{2,1,0:T(8,128)S(1)}, u32[]{:S(2)}, u32[]{:S(2)}) collective-permute-start(f32[2,80,80]{2,1,0:T(8,128)S(1)} %collective-permute-done.7.h), channel_id=1, source_target_pairs={{0,16},{32,48},{64,80},{96,112},{16,0},{48,32},{80,64},{112,96},{1... | collective-permute-start | bytes 153608 | tf_op jit(solution)/shard_map/ppermute | solution.py:397
  28.7 0.9 %collective-permute-done.8.g = f32[2,80,80]{2,1,0:T(8,128)S(1)} collective-permute-done((f32[2,80,80]{2,1,0:T(8,128)S(1)}, f32[2,80,80]{2,1,0:T(8,128)S(1)}, u32[]{:S(2)}, u32[]{:S(2)}) %collective-permute-start.8) | collective-permute-done | bytes 51232 | tf_op jit(solution)/shard_map/ppermute | solution.py:397
  29.6 0.5 step.4
  30.1 2.8 %collective-permute-start.9 = (f32[48,128]{1,0:T(8,128)S(1)}, f32[48,128]{1,0:T(8,128)S(1)}, u32[]{:S(2)}, u32[]{:S(2)}) collective-permute-start(f32[48,128]{1,0:T(8,128)S(1)} %get-tuple-element.47), channel_id=1, source_target_pairs={{0,32},{64,96},{48,80},{112,16},{32,0},{96,64},{80,48},{16,112},{1... | collective-permute-start | bytes 73736 | tf_op jit(solution)/shard_map/ppermute | solution.py:369
  32.9 1.2 %collective-permute-done.9.far = f32[48,128]{1,0:T(8,128)S(1)} collective-permute-done((f32[48,128]{1,0:T(8,128)S(1)}, f32[48,128]{1,0:T(8,128)S(1)}, u32[]{:S(2)}, u32[]{:S(2)}) %collective-permute-start.9) | collective-permute-done | bytes 24608 | tf_op jit(solution)/shard_map/ppermute | solution.py:369
  34.2 0.2 collective-permute-start.10
  34.3 1.0 %collective-permute-done.10.sib_far = f32[48,128]{1,0:T(8,128)S(1)} collective-permute-done((f32[48,128]{1,0:T(8,128)S(1)}, f32[48,128]{1,0:T(8,128)S(1)}, u32[]{:S(2)}, u32[]{:S(2)}) %collective-permute-start.10) | collective-permute-done | bytes 24608 | tf_op jit(solution)/shard_map/ppermute | solution.py:373
  35.3 0.4 send.6
  35.8 1.3 %collective-permute-start.11 = (f32[2,80,80]{2,1,0:T(8,128)S(1)}, f32[2,80,80]{2,1,0:T(8,128)S(1)}, u32[]{:S(2)}, u32[]{:S(2)}) collective-permute-start(f32[2,80,80]{2,1,0:T(8,128)S(1)} %send.6), channel_id=1, source_target_pairs={{0,1},{2,3},{4,5},{6,7},{8,9},{10,11},{12,13},{14,15},{17,18},{19,... | collective-permute-start | bytes 153608 | tf_op jit(solution)/shard_map/ppermute | solution.py:377
  37.0 1.2 %same.6 = (f32[2,80,80]{2,1,0:T(8,128)S(1)}, f32[1,2048]{1,0:T(1,128)S(1)}) custom-call(s32[4]{0:T(128)S(1)} %copy-done.2, s32[4,2048]{1,0:T(4,128)S(1)} %copy-done.1, f32[2,48,128]{2,1,0:T(8,128)S(1)} %get-tuple-element.46.pay, f32[48,128]{1,0:T(8,128)S(1)} %collective-permute-done.9.far, f32[48,128]{1,0:T(8,128)S(1)} %collective-permute-done.10.sib_far), custom_call_target="tpu_custom_call" | custom-call | tf_op jit(solution)/shard_map/same/pallas_call | solution.py:378
  38.2 1.2 %collective-permute-done.11.h = f32[2,80,80]{2,1,0:T(8,128)S(1)} collective-permute-done((f32[2,80,80]{2,1,0:T(8,128)S(1)}, f32[2,80,80]{2,1,0:T(8,128)S(1)}, u32[]{:S(2)}, u32[]{:S(2)}) %collective-permute-start.11) | collective-permute-done | bytes 51232 | tf_op jit(solution)/shard_map/ppermute | solution.py:377
  39.4 1.0 %collective-permute-start.12 = (f32[2,80,80]{2,1,0:T(8,128)S(1)}, f32[2,80,80]{2,1,0:T(8,128)S(1)}, u32[]{:S(2)}, u32[]{:S(2)}) collective-permute-start(f32[2,80,80]{2,1,0:T(8,128)S(1)} %collective-permute-done.11.h), channel_id=1, source_target_pairs={{0,16},{32,48},{64,80},{96,112},{16,0},{48,32},{80,64},{112,96},{1... | collective-permute-start | bytes 153608 | tf_op jit(solution)/shard_map/ppermute | solution.py:397
  40.5 0.9 %collective-permute-done.12.g = f32[2,80,80]{2,1,0:T(8,128)S(1)} collective-permute-done((f32[2,80,80]{2,1,0:T(8,128)S(1)}, f32[2,80,80]{2,1,0:T(8,128)S(1)}, u32[]{:S(2)}, u32[]{:S(2)}) %collective-permute-start.12) | collective-permute-done | bytes 51232 | tf_op jit(solution)/shard_map/ppermute | solution.py:397
  41.4 1.1 %step.5 = (f32[2,96,384]{2,1,0:T(8,128)S(1)}, f32[2,48,128]{2,1,0:T(8,128)S(1)}, f32[48,128]{1,0:T(8,128)S(1)}, f32[128,1,256]{2,1,0:T(1,128)}) custom-call(f32[2,80,80]{2,1,0:T(8,128)S(1)} %get-tuple-element.49.q0, f32[2,80,80]{2,1,0:T(8,128)S(1)} %collective-permute-done.11.h, f32[2,80,80]{2,1,0:T(8,128)S(1)} %collective-permute-done.12.g, ...), custom_call_target="tpu_custom_call" | custom-call | tf_op jit(solution)/shard_map/step/pallas_call | solution.py:400
  42.5 12.7 %all-to-all-start = ((f32[128,1,256]{2,1,0:T(1,128)}), f32[128,1,256]{2,1,0:T(1,128)S(1)}, u32[]{:S(2)}, u32[]{:S(2)}) async-start(f32[128,1,256]{2,1,0:T(1,128)} %get-tuple-element.54), calls=%async_computation | async-start | bytes 262144 | tf_op jit(solution)/shard_map/all_to_all | solution.py:371
  55.2 2.7 %collective-permute-start.13 = (f32[48,128]{1,0:T(8,128)S(1)}, f32[48,128]{1,0:T(8,128)S(1)}, u32[]{:S(2)}, u32[]{:S(2)}) collective-permute-start(f32[48,128]{1,0:T(8,128)S(1)} %get-tuple-element.53), channel_id=1, source_target_pairs={{0,32},{64,96},{48,80},{112,16},{32,0},{96,64},{80,48},{16,112},{1... | collective-permute-start | bytes 73736 | tf_op jit(solution)/shard_map/ppermute | solution.py:369
  57.9 7.5 %all-to-all-done = f32[128,1,256]{2,1,0:T(1,128)S(1)} async-done(((f32[128,1,256]{2,1,0:T(1,128)}), f32[128,1,256]{2,1,0:T(1,128)S(1)}, u32[]{:S(2)}, u32[]{:S(2)}) %all-to-all-start) | async-done | bytes 131104 | tf_op jit(solution)/shard_map/all_to_all | solution.py:371
  65.4 0.0 collective-permute-done.13.far
  65.4 0.5 collective-permute-start.14
  65.9 0.8 collective-permute-done.14.sib_far
  66.8 0.4 send.7
  67.2 0.6 collective-permute-start.15
  67.8 1.2 %same.7 = (f32[2,80,80]{2,1,0:T(8,128)S(1)}, f32[1,2048]{1,0:T(1,128)S(1)}) custom-call(s32[4]{0:T(128)S(1)} %copy-done.2, s32[4,2048]{1,0:T(4,128)S(1)} %copy-done.1, f32[2,48,128]{2,1,0:T(8,128)S(1)} %get-tuple-element.52.pay, f32[48,128]{1,0:T(8,128)S(1)} %collective-permute-done.13.far, f32[48,128]{1,0:T(8,128)S(1)} %collective-permute-done.14.sib_far), custom_call_target="tpu_custom_call" | custom-call | tf_op jit(solution)/shard_map/same/pallas_call | solution.py:378
  69.0 2.1 %place.1 = f32[4,2048]{1,0:T(4,128)} custom-call(s32[4]{0:T(128)S(1)} %copy-done.2, s32[4,2048]{1,0:T(4,128)S(1)} %copy-done.1, f32[128,256]{1,0:T(8,128)S(1)} %bitcast.4, f32[1,2048]{1,0:T(1,128)S(1)} %get-tuple-element.58.r0, f32[1,2048]{1,0:T(1,128)S(1)} %get-tuple-element.59.r1, f32[1,2048]{1,0:T(1,128)S(1)} %get-tuple-element.60.r2, ...), custom_call_target="tpu_custom_call" | custom-call | tf_op jit(solution)/shard_map/place/pallas_call | solution.py:387
  71.1 0.0 collective-permute-done.15.h
  71.1 1.1 %collective-permute-start.16 = (f32[2,80,80]{2,1,0:T(8,128)S(1)}, f32[2,80,80]{2,1,0:T(8,128)S(1)}, u32[]{:S(2)}, u32[]{:S(2)}) collective-permute-start(f32[2,80,80]{2,1,0:T(8,128)S(1)} %collective-permute-done.15.h), channel_id=1, source_target_pairs={{0,16},{32,48},{64,80},{96,112},{16,0},{48,32},{80,64},{112,96},{1... | collective-permute-start | bytes 153608 | tf_op jit(solution)/shard_map/ppermute | solution.py:397
  72.3 0.9 %collective-permute-done.16.g = f32[2,80,80]{2,1,0:T(8,128)S(1)} collective-permute-done((f32[2,80,80]{2,1,0:T(8,128)S(1)}, f32[2,80,80]{2,1,0:T(8,128)S(1)}, u32[]{:S(2)}, u32[]{:S(2)}) %collective-permute-start.16) | collective-permute-done | bytes 51232 | tf_op jit(solution)/shard_map/ppermute | solution.py:397
  73.2 0.0 copy-start
  73.2 4.0 %copy-done = f32[80,4,32,256]{3,2,1,0:T(8,128)S(1)} copy-done((f32[80,4,32,256]{3,2,1,0:T(8,128)S(1)}, f32[80,4,32,256]{3,2,1,0:T(8,128)}, u32[]{:S(2)}) %copy-start) | copy-done | bytes 10485784
  77.2 8.6 %final.1 = f32[80,4,32,256]{3,2,1,0:T(8,128)} custom-call(f32[2,80,80]{2,1,0:T(8,128)S(1)} %get-tuple-element.62.q0, f32[2,80,80]{2,1,0:T(8,128)S(1)} %collective-permute-done.15.h, f32[2,80,80]{2,1,0:T(8,128)S(1)} %collective-permute-done.16.g, f32[2,96,384]{2,1,0:T(8,128)S(1)} %get-tuple-element.64.z, f32[80,4,32,256]{3,2,1,0:T(8,128)S(1)} %copy-done), custom_call_target="tpu_custom_call" | custom-call | tf_op jit(solution)/shard_map/final/pallas_call | solution.py:409
  (1 shorter events, 0.0 us)
Async XLA Ops:
  0.6 12.9 %copy-start.2 = (s32[4]{0:T(128)S(1)}, s32[4]{0:T(128)}, u32[]{:S(2)}) copy-start(s32[4]{0:T(128)} %order.9) | copy-start | bytes 52
  0.6 12.9 %copy-start.1 = (s32[4,2048]{1,0:T(4,128)S(1)}, s32[4,2048]{1,0:T(4,128)}, u32[]{:S(2)}) copy-start(s32[4,2048]{1,0:T(4,128)} %owner.9) | copy-start | bytes 98308
  3.9 2.5 %collective-permute-start = (f32[96,256]{1,0:T(8,128)S(1)}, f32[96,256]{1,0:T(8,128)S(1)}, u32[]{:S(2)}, u32[]{:S(2)}) collective-permute-start(f32[96,256]{1,0:T(8,128)S(1)} %init.1.own), channel_id=1, source_target_pairs={{0,16},{32,48},{64,80},{96,112},{16,0},{48,32},{80,64},{112,96},{1... | collective-permute-start | bytes 294920 | tf_op jit(solution)/shard_map/ppermute | solution.py:365
  6.5 4.1 %collective-permute-start.1 = (f32[48,128]{1,0:T(8,128)S(1)}, f32[48,128]{1,0:T(8,128)S(1)}, u32[]{:S(2)}, u32[]{:S(2)}) collective-permute-start(f32[48,128]{1,0:T(8,128)S(1)} %get-tuple-element.35), channel_id=1, source_target_pairs={{0,32},{64,96},{48,80},{112,16},{32,0},{96,64},{80,48},{16,112},{1... | collective-permute-start | bytes 73736 | tf_op jit(solution)/shard_map/ppermute | solution.py:369
  10.6 1.2 %collective-permute-start.2 = (f32[48,128]{1,0:T(8,128)S(1)}, f32[48,128]{1,0:T(8,128)S(1)}, u32[]{:S(2)}, u32[]{:S(2)}) collective-permute-start(f32[48,128]{1,0:T(8,128)S(1)} %collective-permute-done.1.far), channel_id=1, source_target_pairs={{0,16},{32,48},{64,80},{96,112},{16,0},{48,32},{80,64},{112,96},{1... | collective-permute-start | bytes 73736 | tf_op jit(solution)/shard_map/ppermute | solution.py:373
  12.2 3.7 %collective-permute-start.3 = (f32[2,80,80]{2,1,0:T(8,128)S(1)}, f32[2,80,80]{2,1,0:T(8,128)S(1)}, u32[]{:S(2)}, u32[]{:S(2)}) collective-permute-start(f32[2,80,80]{2,1,0:T(8,128)S(1)} %send.4), channel_id=1, source_target_pairs={{0,1},{2,3},{4,5},{6,7},{8,9},{10,11},{12,13},{14,15},{17,18},{19,... | collective-permute-start | bytes 153608 | tf_op jit(solution)/shard_map/ppermute | solution.py:377
  15.9 1.9 %collective-permute-start.4 = (f32[2,80,80]{2,1,0:T(8,128)S(1)}, f32[2,80,80]{2,1,0:T(8,128)S(1)}, u32[]{:S(2)}, u32[]{:S(2)}) collective-permute-start(f32[2,80,80]{2,1,0:T(8,128)S(1)} %collective-permute-done.3.h), channel_id=1, source_target_pairs={{0,16},{32,48},{64,80},{96,112},{16,0},{48,32},{80,64},{112,96},{1... | collective-permute-start | bytes 153608 | tf_op jit(solution)/shard_map/ppermute | solution.py:397
  18.3 4.1 %collective-permute-start.5 = (f32[48,128]{1,0:T(8,128)S(1)}, f32[48,128]{1,0:T(8,128)S(1)}, u32[]{:S(2)}, u32[]{:S(2)}) collective-permute-start(f32[48,128]{1,0:T(8,128)S(1)} %get-tuple-element.41), channel_id=1, source_target_pairs={{0,32},{64,96},{48,80},{112,16},{32,0},{96,64},{80,48},{16,112},{1... | collective-permute-start | bytes 73736 | tf_op jit(solution)/shard_map/ppermute | solution.py:369
  22.4 1.2 %collective-permute-start.6 = (f32[48,128]{1,0:T(8,128)S(1)}, f32[48,128]{1,0:T(8,128)S(1)}, u32[]{:S(2)}, u32[]{:S(2)}) collective-permute-start(f32[48,128]{1,0:T(8,128)S(1)} %collective-permute-done.5.far), channel_id=1, source_target_pairs={{0,16},{32,48},{64,80},{96,112},{16,0},{48,32},{80,64},{112,96},{1... | collective-permute-start | bytes 73736 | tf_op jit(solution)/shard_map/ppermute | solution.py:373
  24.0 3.7 %collective-permute-start.7 = (f32[2,80,80]{2,1,0:T(8,128)S(1)}, f32[2,80,80]{2,1,0:T(8,128)S(1)}, u32[]{:S(2)}, u32[]{:S(2)}) collective-permute-start(f32[2,80,80]{2,1,0:T(8,128)S(1)} %send.5), channel_id=1, source_target_pairs={{0,1},{2,3},{4,5},{6,7},{8,9},{10,11},{12,13},{14,15},{17,18},{19,... | collective-permute-start | bytes 153608 | tf_op jit(solution)/shard_map/ppermute | solution.py:377
  27.7 1.9 %collective-permute-start.8 = (f32[2,80,80]{2,1,0:T(8,128)S(1)}, f32[2,80,80]{2,1,0:T(8,128)S(1)}, u32[]{:S(2)}, u32[]{:S(2)}) collective-permute-start(f32[2,80,80]{2,1,0:T(8,128)S(1)} %collective-permute-done.7.h), channel_id=1, source_target_pairs={{0,16},{32,48},{64,80},{96,112},{16,0},{48,32},{80,64},{112,96},{1... | collective-permute-start | bytes 153608 | tf_op jit(solution)/shard_map/ppermute | solution.py:397
  30.1 4.1 %collective-permute-start.9 = (f32[48,128]{1,0:T(8,128)S(1)}, f32[48,128]{1,0:T(8,128)S(1)}, u32[]{:S(2)}, u32[]{:S(2)}) collective-permute-start(f32[48,128]{1,0:T(8,128)S(1)} %get-tuple-element.47), channel_id=1, source_target_pairs={{0,32},{64,96},{48,80},{112,16},{32,0},{96,64},{80,48},{16,112},{1... | collective-permute-start | bytes 73736 | tf_op jit(solution)/shard_map/ppermute | solution.py:369
  34.2 1.2 %collective-permute-start.10 = (f32[48,128]{1,0:T(8,128)S(1)}, f32[48,128]{1,0:T(8,128)S(1)}, u32[]{:S(2)}, u32[]{:S(2)}) collective-permute-start(f32[48,128]{1,0:T(8,128)S(1)} %collective-permute-done.9.far), channel_id=1, source_target_pairs={{0,16},{32,48},{64,80},{96,112},{16,0},{48,32},{80,64},{112,96},{1... | collective-permute-start | bytes 73736 | tf_op jit(solution)/shard_map/ppermute | solution.py:373
  35.8 3.7 %collective-permute-start.11 = (f32[2,80,80]{2,1,0:T(8,128)S(1)}, f32[2,80,80]{2,1,0:T(8,128)S(1)}, u32[]{:S(2)}, u32[]{:S(2)}) collective-permute-start(f32[2,80,80]{2,1,0:T(8,128)S(1)} %send.6), channel_id=1, source_target_pairs={{0,1},{2,3},{4,5},{6,7},{8,9},{10,11},{12,13},{14,15},{17,18},{19,... | collective-permute-start | bytes 153608 | tf_op jit(solution)/shard_map/ppermute | solution.py:377
  39.4 1.9 %collective-permute-start.12 = (f32[2,80,80]{2,1,0:T(8,128)S(1)}, f32[2,80,80]{2,1,0:T(8,128)S(1)}, u32[]{:S(2)}, u32[]{:S(2)}) collective-permute-start(f32[2,80,80]{2,1,0:T(8,128)S(1)} %collective-permute-done.11.h), channel_id=1, source_target_pairs={{0,16},{32,48},{64,80},{96,112},{16,0},{48,32},{80,64},{112,96},{1... | collective-permute-start | bytes 153608 | tf_op jit(solution)/shard_map/ppermute | solution.py:397
  42.5 22.9 %all-to-all-start = ((f32[128,1,256]{2,1,0:T(1,128)}), f32[128,1,256]{2,1,0:T(1,128)S(1)}, u32[]{:S(2)}, u32[]{:S(2)}) async-start(f32[128,1,256]{2,1,0:T(1,128)} %get-tuple-element.54), calls=%async_computation | async-start | bytes 262144 | tf_op jit(solution)/shard_map/all_to_all | solution.py:371
  55.2 10.2 %collective-permute-start.13 = (f32[48,128]{1,0:T(8,128)S(1)}, f32[48,128]{1,0:T(8,128)S(1)}, u32[]{:S(2)}, u32[]{:S(2)}) collective-permute-start(f32[48,128]{1,0:T(8,128)S(1)} %get-tuple-element.53), channel_id=1, source_target_pairs={{0,32},{64,96},{48,80},{112,16},{32,0},{96,64},{80,48},{16,112},{1... | collective-permute-start | bytes 73736 | tf_op jit(solution)/shard_map/ppermute | solution.py:369
  65.4 1.4 %collective-permute-start.14 = (f32[48,128]{1,0:T(8,128)S(1)}, f32[48,128]{1,0:T(8,128)S(1)}, u32[]{:S(2)}, u32[]{:S(2)}) collective-permute-start(f32[48,128]{1,0:T(8,128)S(1)} %collective-permute-done.13.far), channel_id=1, source_target_pairs={{0,16},{32,48},{64,80},{96,112},{16,0},{48,32},{80,64},{112,96},{1... | collective-permute-start | bytes 73736 | tf_op jit(solution)/shard_map/ppermute | solution.py:373
  67.2 3.9 %collective-permute-start.15 = (f32[2,80,80]{2,1,0:T(8,128)S(1)}, f32[2,80,80]{2,1,0:T(8,128)S(1)}, u32[]{:S(2)}, u32[]{:S(2)}) collective-permute-start(f32[2,80,80]{2,1,0:T(8,128)S(1)} %send.7), channel_id=1, source_target_pairs={{0,1},{2,3},{4,5},{6,7},{8,9},{10,11},{12,13},{14,15},{17,18},{19,... | collective-permute-start | bytes 153608 | tf_op jit(solution)/shard_map/ppermute | solution.py:377
  71.1 2.1 %collective-permute-start.16 = (f32[2,80,80]{2,1,0:T(8,128)S(1)}, f32[2,80,80]{2,1,0:T(8,128)S(1)}, u32[]{:S(2)}, u32[]{:S(2)}) collective-permute-start(f32[2,80,80]{2,1,0:T(8,128)S(1)} %collective-permute-done.15.h), channel_id=1, source_target_pairs={{0,16},{32,48},{64,80},{96,112},{16,0},{48,32},{80,64},{112,96},{1... | collective-permute-start | bytes 153608 | tf_op jit(solution)/shard_map/ppermute | solution.py:397
  73.2 4.0 %copy-start = (f32[80,4,32,256]{3,2,1,0:T(8,128)S(1)}, f32[80,4,32,256]{3,2,1,0:T(8,128)}, u32[]{:S(2)}) copy-start(f32[80,4,32,256]{3,2,1,0:T(8,128)} %x.1) | copy-start | bytes 31457284

commit v5 on v4

--- a/solution.py
+++ b/solution.py
@@ -21,6 +21,7 @@
 HIGH = lax.Precision.HIGHEST
 SLAB = 16
 PARTS = TX // SLAB
+SLABS = LEV * PARTS
 
 ROW_A = M
 ROW_C = M + 1
@@ -183,11 +184,8 @@
     if nv_out is not None:
         first = core_of() == 0
         past = slice(0, CAP * k)
-        row = jnp.concatenate([
-            jnp.where(first, z[0][ROW_N : ROW_N + 1, past], z[1][ROW_N : ROW_N + 1, past]),
-            jnp.where(first, news[0], news[1]),
-        ], axis=1)
-        nv_out[...] = jnp.broadcast_to(row[None], nv_out.shape)
+        nv_out[:, past] = jnp.where(first, z[0][ROW_N : ROW_N + 1, past], z[1][ROW_N : ROW_N + 1, past])
+        nv_out[:, at] = jnp.where(first, news[0], news[1])
 
 
 def start_kernel(own, sib, z_out, pay_out, edge_out):
@@ -273,43 +271,42 @@
     emit(k, new, z_out, pay_out, edge_out, nv_out)
 
 
-def final_kernel(q0, h, g, z, x, out, mix):
-    step = pl.program_id(0)
-
-    @pl.when(step == 0)
-    def _():
-        c = core_of()
-        t = advance(z[c, :M, NB * CAP :], whole_gain(c, q0, h, g))[:, :M]
-        d = t - jnp.where(iota((M, M), 0) == iota((M, M), 1), 1.0, 0.0)
-        dh, dl = split2(d)
-        mix[...] = jnp.concatenate([dh, dh, dl], axis=1)
-
-    w = mix[...]
-    level, start = step // PARTS, lax.rem(step, PARTS) * SLAB
-    for t in range(SLAB // 8):
-        block = x[:, level, pl.ds(pl.multiple_of(start + 8 * t, 8), 8), :]
-        turned = jnp.swapaxes(block, 0, 1)
-        updates = []
-        for i in range(8):
-            h_, l_ = split2(turned[i])
-            updates.append(dot(w, jnp.concatenate([h_, l_, h_], axis=0))[None])
-        out[:, 0, 8 * t : 8 * t + 8, :] = block + jnp.swapaxes(jnp.concatenate(updates, axis=0), 0, 1)
+def final_kernel(q0, h, g, z, x, out, come, go, come_sems, go_sems):
+    def part(ref, i):
+        return ref.at[:, i // PARTS, pl.ds((i % PARTS) * SLAB, SLAB), :]
+
+    loads = [pltpu.make_async_copy(part(x, i), come.at[i], come_sems.at[i]) for i in range(SLABS)]
+    stores = [pltpu.make_async_copy(go.at[i], part(out, i), go_sems.at[i]) for i in range(SLABS)]
+    for load in loads:
+        load.start()
+    c = core_of()
+    t = advance(z[c, :M, NB * CAP :], whole_gain(c, q0, h, g))[:, :M]
+    th, tl = split2(t)
+    w = jnp.concatenate([th, th, tl], axis=1)
+    for i in range(SLABS):
+        loads[i].wait()
+        for j in range(0, SLAB, 8):
+            turned = jnp.swapaxes(come[i, :, j : j + 8, :], 0, 1)
+            rows = []
+            for r in range(8):
+                xh, xl = split2(turned[r])
+                rows.append(dot(w, jnp.concatenate([xh, xl, xh], axis=0))[None])
+            go[i, :, j : j + 8, :] = jnp.swapaxes(jnp.concatenate(rows, axis=0), 0, 1)
+        stores[i].start()
+    for store in stores:
+        store.wait()
 
 
 def place_kernel(order, owner, nv, r0, r1, r2, r3, out):
-    turned = nv[...].T
-    slots = iota((CAP, 128), 0).astype(F32)
+    high, low = split2(nv[...].T)
+    tiles = iota((TILES, OBS), 0)
+    slots = iota((CAP, OBS), 0).astype(F32)
     for k, rank in enumerate((r0, r1, r2, r3)):
         b = order[k]
-        table = turned[CAP * k : CAP * k + CAP]
-        row = owner[pl.ds(b, 1), :]
-        pieces = []
-        for c in range(OBS // 128):
-            at = slice(128 * c, 128 * c + 128)
-            got = jnp.take_along_axis(table, jnp.broadcast_to(row[:, at], (CAP, 128)), axis=1)
-            got = jnp.where(rank[:, at] == slots, got, 0.0)
-            pieces.append(jnp.sum(got, axis=0, keepdims=True))
-        out[pl.ds(b, 1), :] = jnp.concatenate(pieces, axis=1)
+        at = slice(CAP * k, CAP * k + CAP)
+        hot = jnp.where(owner[pl.ds(b, 1), :] == tiles, 1.0, 0.0).astype(BF16)
+        got = dot(jnp.concatenate([high[at], low[at]], axis=1), jnp.concatenate([hot, hot], axis=0))
+        out[pl.ds(b, 1), :] = jnp.sum(jnp.where(rank[...] == slots, got, 0.0), axis=0, keepdims=True)
 
 
 VMEM = pl.BlockSpec(memory_space=pltpu.VMEM)
@@ -326,7 +323,7 @@
 
 
 def local(ensemble, obs_value, obs_variance, obs_owner, obs_cell, obs_reach, batch_order):
-    params = pltpu.CompilerParams(vmem_limit_bytes=24 * 2**20)
+    params = pltpu.CompilerParams(vmem_limit_bytes=32 * 2**20)
     call = functools.partial(pl.pallas_call, compiler_params=params)
     width, height = lax.axis_size("gx"), lax.axis_size("gy")
     both = ("gx", "gy")
@@ -368,8 +365,8 @@
         last = k + 1 == NB
         far = lax.ppermute(edge, "gx", side_x)
         if last:
-            everyone = lax.all_to_all(nv, both, 0, 0, tiled=True).reshape(TILES, NB * CAP)
-            far, everyone = lax.optimization_barrier((far, everyone))
+            spread = jnp.broadcast_to(nv, (TILES, NB * CAP))
+            everyone = lax.all_to_all(spread, both, 0, 0, tiled=True)
         sib_far = lax.ppermute(far, "gx", core)
         send = call(send_kernel, out_shape=shape(2, M, M), in_specs=[VMEM] * 3, out_specs=VMEM, name="send")(
             pay, far, sib_far
@@ -383,20 +380,10 @@
             name="same",
         )(batch_order, obs_owner, pay, far, sib_far)
         ranks.append(rank)
-        if last:
-            innovation = call(
-                place_kernel,
-                out_shape=shape(NB, OBS),
-                in_specs=[SMEM] + [VMEM] * 6,
-                out_specs=VMEM,
-                name="place",
-            )(batch_order, obs_owner, everyone, *ranks)
-            h, q0, innovation = lax.optimization_barrier((h, q0, innovation))
-        else:
-            h, q0 = lax.optimization_barrier((h, q0))
+        h, q0 = lax.optimization_barrier((h, q0))
         g = lax.ppermute(h, "gx", core)
         if not last:
-            wide = (shape(TILES, 1, NB * CAP),) if k + 2 == NB else ()
+            wide = (shape(1, NB * CAP),) if k + 2 == NB else ()
             z, pay, edge, *rest = call(
                 functools.partial(step_kernel, k + 1),
                 out_shape=(z_shape,) + pay_shapes + wide,
@@ -406,15 +393,23 @@
             )(q0, h, g, z)
             if rest:
                 nv = rest[0]
+    slabs = pltpu.VMEM((SLABS, M, SLAB, TY), F32)
     state = call(
         final_kernel,
         out_shape=shape(M, LEV, TX, TY),
-        grid=(LEV * PARTS,),
-        in_specs=[VMEM] * 5,
-        out_specs=pl.BlockSpec((M, 1, SLAB, TY), lambda i: (0, i // PARTS, i % PARTS, 0)),
-        scratch_shapes=[pltpu.VMEM((M, 3 * M), BF16)],
+        in_specs=[VMEM] * 4 + [HBM],
+        out_specs=HBM,
+        scratch_shapes=[slabs, slabs, pltpu.SemaphoreType.DMA((SLABS,)), pltpu.SemaphoreType.DMA((SLABS,))],
         name="final",
-    )(q0, h, g, z, pltpu.with_memory_space_constraint(ensemble, pltpu.VMEM))
+    )(q0, h, g, z, pltpu.with_memory_space_constraint(ensemble, pltpu.HBM))
+    state, everyone = lax.optimization_barrier((state, everyone))
+    innovation = call(
+        place_kernel,
+        out_shape=shape(NB, OBS),
+        in_specs=[SMEM] + [VMEM] * 6,
+        out_specs=VMEM,
+        name="place",
+    )(batch_order, obs_owner, everyone, *ranks)
     return state, innovation
 
 

time: 86 us -> 78.3 us (0.910)
  waiting for transfers between devices: 23.4 us -> 19.8 us
  local copies, waits for them, and re-layouts: 4 us -> 0.74 us
    all_to_all x1, waiting for transfers between devices: 7.47 us -> 2.9 us  [local(): everyone = lax.all_to_all(spread, both, 0, 0, tiled=True)]
    unnamed x7 -> x5, local copies, waits for them, and re-layouts: 4 us -> 0.02 us
    ppermute x4, waiting for transfers between devices: 3.67 us -> 5.59 us  [local(): h = lax.ppermute(send, both, side_y)]
    all_to_all x1, starting transfers between devices: 12.7 us -> 11.3 us  [local(): everyone = lax.all_to_all(spread, both, 0, 0, tiled=True)]
    ppermute x4, waiting for transfers between devices: 3.69 us -> 2.77 us  [local(): g = lax.ppermute(h, 'gx', core)]
  transfers between devices with their start and end apart: 18 -> 18, of which waited for: 16 -> 16; matrix products, arithmetic and copies ran while one was open for 0% -> 1% of each run, Pallas kernels for 8% -> 6%
where the time goes in v5:
time: 78.3 us; the launch traced here: 78.1 us
  starting transfers between devices  34.5 us (44%)
  Pallas kernels  22.3 us (28%)
  waiting for transfers between devices  19.8 us (25%)
    ppermute x4, starting transfers between devices, local(): far = lax.ppermute(edge, 'gx', side_x)  11.4 us
    all_to_all x1, starting transfers between devices, local(): everyone = lax.all_to_all(spread, both, 0, 0, tiled=True)  11.3 us
    pallas_call x1, Pallas kernels, local(): call(final_kernel, out_shape=shape(M, LEV, TX, TY), in_specs=[VMEM] * 4 +...  8.68 us
    ppermute x4, waiting for transfers between devices, local(): h = lax.ppermute(send, both, side_y)  5.59 us
    pallas_call x4, Pallas kernels, local(): call(functools.partial(same_kernel, k), out_shape=(shape(2, M, M), shape(...  4.7 us
    ppermute x4, starting transfers between devices, local(): h = lax.ppermute(send, both, side_y)  4.54 us
    ppermute x4, starting transfers between devices, local(): g = lax.ppermute(h, 'gx', core)  4.05 us
    ppermute x4, waiting for transfers between devices, local(): sib_far = lax.ppermute(far, 'gx', core)  3.94 us
  transfers between devices with their start and end apart: 18, of which 16 were waited for; matrix products, arithmetic and copies ran while one was open for 1% of the time, Pallas kernels for 6%

profile of v5, /device:TPU:1, one launch (start us, length us, event | category | flops | bytes accessed | tf_op | source)
XLA Modules:
  0.0 78.1 jit_solution(11885376925270510880)
XLA Ops:
  0.6 0.0 copy-start
  0.6 0.0 copy-start.1
  0.7 3.3 %init.1.own = f32[96,256]{1,0:T(8,128)S(1)} custom-call(s32[4]{0:T(128)} %order.9, f32[4,2048]{1,0:T(4,128)} %value_hbm.1, f32[4,2048]{1,0:T(4,128)} %variance_hbm.1, s32[4,2048]{1,0:T(4,128)} %owner.9, s32[4,2048]{1,0:T(4,128)} %cell_hbm.1, s32[4,8,2048]{2,1,0:T(8,128)} %bitcast.7, f32[80,4,32,256]{3,2,1,0:T(8,128)} %x.1), custom_call_target="tpu_custom_call" | custom-call | tf_op jit(solution)/shard_map/init/pallas_call | solution.py:340
  3.9 1.5 %collective-permute-start = (f32[96,256]{1,0:T(8,128)S(1)}, f32[96,256]{1,0:T(8,128)S(1)}, u32[]{:S(2)}, u32[]{:S(2)}) collective-permute-start(f32[96,256]{1,0:T(8,128)S(1)} %init.1.own), channel_id=1, source_target_pairs={{0,16},{32,48},{64,80},{96,112},{16,0},{48,32},{80,64},{112,96},{1... | collective-permute-start | bytes 294920 | tf_op jit(solution)/shard_map/ppermute | solution.py:362
  5.4 0.9 %collective-permute-done.sib = f32[96,256]{1,0:T(8,128)S(1)} collective-permute-done((f32[96,256]{1,0:T(8,128)S(1)}, f32[96,256]{1,0:T(8,128)S(1)}, u32[]{:S(2)}, u32[]{:S(2)}) %collective-permute-start) | collective-permute-done | bytes 98336 | tf_op jit(solution)/shard_map/ppermute | solution.py:362
  6.4 0.2 start.1
  6.5 2.9 %collective-permute-start.1 = (f32[48,128]{1,0:T(8,128)S(1)}, f32[48,128]{1,0:T(8,128)S(1)}, u32[]{:S(2)}, u32[]{:S(2)}) collective-permute-start(f32[48,128]{1,0:T(8,128)S(1)} %get-tuple-element.34), channel_id=1, source_target_pairs={{0,32},{64,96},{48,80},{112,16},{32,0},{96,64},{80,48},{16,112},{1... | collective-permute-start | bytes 73736 | tf_op jit(solution)/shard_map/ppermute | solution.py:366
  9.4 1.2 %collective-permute-done.1.far = f32[48,128]{1,0:T(8,128)S(1)} collective-permute-done((f32[48,128]{1,0:T(8,128)S(1)}, f32[48,128]{1,0:T(8,128)S(1)}, u32[]{:S(2)}, u32[]{:S(2)}) %collective-permute-start.1) | collective-permute-done | bytes 24608 | tf_op jit(solution)/shard_map/ppermute | solution.py:366
  10.6 0.2 collective-permute-start.2
  10.8 1.0 %collective-permute-done.2.sib_far = f32[48,128]{1,0:T(8,128)S(1)} collective-permute-done((f32[48,128]{1,0:T(8,128)S(1)}, f32[48,128]{1,0:T(8,128)S(1)}, u32[]{:S(2)}, u32[]{:S(2)}) %collective-permute-start.2) | collective-permute-done | bytes 24608 | tf_op jit(solution)/shard_map/ppermute | solution.py:370
  11.8 0.4 send.4
  12.2 1.3 %collective-permute-start.3 = (f32[2,80,80]{2,1,0:T(8,128)S(1)}, f32[2,80,80]{2,1,0:T(8,128)S(1)}, u32[]{:S(2)}, u32[]{:S(2)}) collective-permute-start(f32[2,80,80]{2,1,0:T(8,128)S(1)} %send.4), channel_id=1, source_target_pairs={{0,1},{2,3},{4,5},{6,7},{8,9},{10,11},{12,13},{14,15},{17,18},{19,... | collective-permute-start | bytes 153608 | tf_op jit(solution)/shard_map/ppermute | solution.py:374
  13.5 0.0 copy-done
  13.5 0.0 copy-done.1
  13.5 1.2 %same.4 = (f32[2,80,80]{2,1,0:T(8,128)S(1)}, f32[1,2048]{1,0:T(1,128)S(1)}) custom-call(s32[4]{0:T(128)S(1)} %copy-done.1, s32[4,2048]{1,0:T(4,128)S(1)} %copy-done, f32[2,48,128]{2,1,0:T(8,128)S(1)} %get-tuple-element.33.pay, f32[48,128]{1,0:T(8,128)S(1)} %collective-permute-done.1.far, f32[48,128]{1,0:T(8,128)S(1)} %collective-permute-done.2.sib_far), custom_call_target="tpu_custom_call" | custom-call | tf_op jit(solution)/shard_map/same/pallas_call | solution.py:375
  14.7 1.2 %collective-permute-done.3.h = f32[2,80,80]{2,1,0:T(8,128)S(1)} collective-permute-done((f32[2,80,80]{2,1,0:T(8,128)S(1)}, f32[2,80,80]{2,1,0:T(8,128)S(1)}, u32[]{:S(2)}, u32[]{:S(2)}) %collective-permute-start.3) | collective-permute-done | bytes 51232 | tf_op jit(solution)/shard_map/ppermute | solution.py:374
  15.9 1.0 %collective-permute-start.4 = (f32[2,80,80]{2,1,0:T(8,128)S(1)}, f32[2,80,80]{2,1,0:T(8,128)S(1)}, u32[]{:S(2)}, u32[]{:S(2)}) collective-permute-start(f32[2,80,80]{2,1,0:T(8,128)S(1)} %collective-permute-done.3.h), channel_id=1, source_target_pairs={{0,16},{32,48},{64,80},{96,112},{16,0},{48,32},{80,64},{112,96},{1... | collective-permute-start | bytes 153608 | tf_op jit(solution)/shard_map/ppermute | solution.py:384
  16.9 0.9 %collective-permute-done.4.g = f32[2,80,80]{2,1,0:T(8,128)S(1)} collective-permute-done((f32[2,80,80]{2,1,0:T(8,128)S(1)}, f32[2,80,80]{2,1,0:T(8,128)S(1)}, u32[]{:S(2)}, u32[]{:S(2)}) %collective-permute-start.4) | collective-permute-done | bytes 51232 | tf_op jit(solution)/shard_map/ppermute | solution.py:384
  17.9 0.4 step.3
  18.3 2.9 %collective-permute-start.5 = (f32[48,128]{1,0:T(8,128)S(1)}, f32[48,128]{1,0:T(8,128)S(1)}, u32[]{:S(2)}, u32[]{:S(2)}) collective-permute-start(f32[48,128]{1,0:T(8,128)S(1)} %get-tuple-element.40), channel_id=1, source_target_pairs={{0,32},{64,96},{48,80},{112,16},{32,0},{96,64},{80,48},{16,112},{1... | collective-permute-start | bytes 73736 | tf_op jit(solution)/shard_map/ppermute | solution.py:366
  21.2 1.2 %collective-permute-done.5.far = f32[48,128]{1,0:T(8,128)S(1)} collective-permute-done((f32[48,128]{1,0:T(8,128)S(1)}, f32[48,128]{1,0:T(8,128)S(1)}, u32[]{:S(2)}, u32[]{:S(2)}) %collective-permute-start.5) | collective-permute-done | bytes 24608 | tf_op jit(solution)/shard_map/ppermute | solution.py:366
  22.4 0.2 collective-permute-start.6
  22.5 1.0 %collective-permute-done.6.sib_far = f32[48,128]{1,0:T(8,128)S(1)} collective-permute-done((f32[48,128]{1,0:T(8,128)S(1)}, f32[48,128]{1,0:T(8,128)S(1)}, u32[]{:S(2)}, u32[]{:S(2)}) %collective-permute-start.6) | collective-permute-done | bytes 24608 | tf_op jit(solution)/shard_map/ppermute | solution.py:370
  23.6 0.4 send.5
  24.0 1.3 %collective-permute-start.7 = (f32[2,80,80]{2,1,0:T(8,128)S(1)}, f32[2,80,80]{2,1,0:T(8,128)S(1)}, u32[]{:S(2)}, u32[]{:S(2)}) collective-permute-start(f32[2,80,80]{2,1,0:T(8,128)S(1)} %send.5), channel_id=1, source_target_pairs={{0,1},{2,3},{4,5},{6,7},{8,9},{10,11},{12,13},{14,15},{17,18},{19,... | collective-permute-start | bytes 153608 | tf_op jit(solution)/shard_map/ppermute | solution.py:374
  25.3 1.2 %same.5 = (f32[2,80,80]{2,1,0:T(8,128)S(1)}, f32[1,2048]{1,0:T(1,128)S(1)}) custom-call(s32[4]{0:T(128)S(1)} %copy-done.1, s32[4,2048]{1,0:T(4,128)S(1)} %copy-done, f32[2,48,128]{2,1,0:T(8,128)S(1)} %get-tuple-element.39.pay, f32[48,128]{1,0:T(8,128)S(1)} %collective-permute-done.5.far, f32[48,128]{1,0:T(8,128)S(1)} %collective-permute-done.6.sib_far), custom_call_target="tpu_custom_call" | custom-call | tf_op jit(solution)/shard_map/same/pallas_call | solution.py:375
  26.4 1.2 %collective-permute-done.7.h = f32[2,80,80]{2,1,0:T(8,128)S(1)} collective-permute-done((f32[2,80,80]{2,1,0:T(8,128)S(1)}, f32[2,80,80]{2,1,0:T(8,128)S(1)}, u32[]{:S(2)}, u32[]{:S(2)}) %collective-permute-start.7) | collective-permute-done | bytes 51232 | tf_op jit(solution)/shard_map/ppermute | solution.py:374
  27.7 1.0 %collective-permute-start.8 = (f32[2,80,80]{2,1,0:T(8,128)S(1)}, f32[2,80,80]{2,1,0:T(8,128)S(1)}, u32[]{:S(2)}, u32[]{:S(2)}) collective-permute-start(f32[2,80,80]{2,1,0:T(8,128)S(1)} %collective-permute-done.7.h), channel_id=1, source_target_pairs={{0,16},{32,48},{64,80},{96,112},{16,0},{48,32},{80,64},{112,96},{1... | collective-permute-start | bytes 153608 | tf_op jit(solution)/shard_map/ppermute | solution.py:384
  28.7 0.9 %collective-permute-done.8.g = f32[2,80,80]{2,1,0:T(8,128)S(1)} collective-permute-done((f32[2,80,80]{2,1,0:T(8,128)S(1)}, f32[2,80,80]{2,1,0:T(8,128)S(1)}, u32[]{:S(2)}, u32[]{:S(2)}) %collective-permute-start.8) | collective-permute-done | bytes 51232 | tf_op jit(solution)/shard_map/ppermute | solution.py:384
  29.6 0.5 step.4
  30.1 2.8 %collective-permute-start.9 = (f32[48,128]{1,0:T(8,128)S(1)}, f32[48,128]{1,0:T(8,128)S(1)}, u32[]{:S(2)}, u32[]{:S(2)}) collective-permute-start(f32[48,128]{1,0:T(8,128)S(1)} %get-tuple-element.46), channel_id=1, source_target_pairs={{0,32},{64,96},{48,80},{112,16},{32,0},{96,64},{80,48},{16,112},{1... | collective-permute-start | bytes 73736 | tf_op jit(solution)/shard_map/ppermute | solution.py:366
  32.9 1.2 %collective-permute-done.9.far = f32[48,128]{1,0:T(8,128)S(1)} collective-permute-done((f32[48,128]{1,0:T(8,128)S(1)}, f32[48,128]{1,0:T(8,128)S(1)}, u32[]{:S(2)}, u32[]{:S(2)}) %collective-permute-start.9) | collective-permute-done | bytes 24608 | tf_op jit(solution)/shard_map/ppermute | solution.py:366
  34.2 0.2 collective-permute-start.10
  34.3 1.0 %collective-permute-done.10.sib_far = f32[48,128]{1,0:T(8,128)S(1)} collective-permute-done((f32[48,128]{1,0:T(8,128)S(1)}, f32[48,128]{1,0:T(8,128)S(1)}, u32[]{:S(2)}, u32[]{:S(2)}) %collective-permute-start.10) | collective-permute-done | bytes 24608 | tf_op jit(solution)/shard_map/ppermute | solution.py:370
  35.3 0.4 send.6
  35.8 1.3 %collective-permute-start.11 = (f32[2,80,80]{2,1,0:T(8,128)S(1)}, f32[2,80,80]{2,1,0:T(8,128)S(1)}, u32[]{:S(2)}, u32[]{:S(2)}) collective-permute-start(f32[2,80,80]{2,1,0:T(8,128)S(1)} %send.6), channel_id=1, source_target_pairs={{0,1},{2,3},{4,5},{6,7},{8,9},{10,11},{12,13},{14,15},{17,18},{19,... | collective-permute-start | bytes 153608 | tf_op jit(solution)/shard_map/ppermute | solution.py:374
  37.0 1.2 %same.6 = (f32[2,80,80]{2,1,0:T(8,128)S(1)}, f32[1,2048]{1,0:T(1,128)S(1)}) custom-call(s32[4]{0:T(128)S(1)} %copy-done.1, s32[4,2048]{1,0:T(4,128)S(1)} %copy-done, f32[2,48,128]{2,1,0:T(8,128)S(1)} %get-tuple-element.45.pay, f32[48,128]{1,0:T(8,128)S(1)} %collective-permute-done.9.far, f32[48,128]{1,0:T(8,128)S(1)} %collective-permute-done.10.sib_far), custom_call_target="tpu_custom_call" | custom-call | tf_op jit(solution)/shard_map/same/pallas_call | solution.py:375
  38.2 1.2 %collective-permute-done.11.h = f32[2,80,80]{2,1,0:T(8,128)S(1)} collective-permute-done((f32[2,80,80]{2,1,0:T(8,128)S(1)}, f32[2,80,80]{2,1,0:T(8,128)S(1)}, u32[]{:S(2)}, u32[]{:S(2)}) %collective-permute-start.11) | collective-permute-done | bytes 51232 | tf_op jit(solution)/shard_map/ppermute | solution.py:374
  39.4 1.0 %collective-permute-start.12 = (f32[2,80,80]{2,1,0:T(8,128)S(1)}, f32[2,80,80]{2,1,0:T(8,128)S(1)}, u32[]{:S(2)}, u32[]{:S(2)}) collective-permute-start(f32[2,80,80]{2,1,0:T(8,128)S(1)} %collective-permute-done.11.h), channel_id=1, source_target_pairs={{0,16},{32,48},{64,80},{96,112},{16,0},{48,32},{80,64},{112,96},{1... | collective-permute-start | bytes 153608 | tf_op jit(solution)/shard_map/ppermute | solution.py:384
  40.5 0.9 %collective-permute-done.12.g = f32[2,80,80]{2,1,0:T(8,128)S(1)} collective-permute-done((f32[2,80,80]{2,1,0:T(8,128)S(1)}, f32[2,80,80]{2,1,0:T(8,128)S(1)}, u32[]{:S(2)}, u32[]{:S(2)}) %collective-permute-start.12) | collective-permute-done | bytes 51232 | tf_op jit(solution)/shard_map/ppermute | solution.py:384
  41.4 0.4 step.5
  41.8 2.9 %collective-permute-start.13 = (f32[48,128]{1,0:T(8,128)S(1)}, f32[48,128]{1,0:T(8,128)S(1)}, u32[]{:S(2)}, u32[]{:S(2)}) collective-permute-start(f32[48,128]{1,0:T(8,128)S(1)} %get-tuple-element.52), channel_id=1, source_target_pairs={{0,32},{64,96},{48,80},{112,16},{32,0},{96,64},{80,48},{16,112},{1... | collective-permute-start | bytes 73736 | tf_op jit(solution)/shard_map/ppermute | solution.py:366
  44.7 0.7 broadcast_in_dim.2
  45.4 11.3 %all-to-all-start = ((f32[128,1,256]{2,1,0:T(1,128)}), f32[128,1,256]{2,1,0:T(1,128)S(1)}, u32[]{:S(2)}, u32[]{:S(2)}) async-start(f32[128,1,256]{2,1,0:T(1,128)} %broadcast_in_dim.2), calls=%async_computation | async-start | bytes 262144 | tf_op jit(solution)/shard_map/all_to_all | solution.py:369
  56.8 0.0 collective-permute-done.13.far
  56.8 1.1 %collective-permute-start.14 = (f32[48,128]{1,0:T(8,128)S(1)}, f32[48,128]{1,0:T(8,128)S(1)}, u32[]{:S(2)}, u32[]{:S(2)}) collective-permute-start(f32[48,128]{1,0:T(8,128)S(1)} %collective-permute-done.13.far), channel_id=1, source_target_pairs={{0,16},{32,48},{64,80},{96,112},{16,0},{48,32},{80,64},{112,96},{1... | collective-permute-start | bytes 73736 | tf_op jit(solution)/shard_map/ppermute | solution.py:370
  57.9 0.8 %collective-permute-done.14.sib_far = f32[48,128]{1,0:T(8,128)S(1)} collective-permute-done((f32[48,128]{1,0:T(8,128)S(1)}, f32[48,128]{1,0:T(8,128)S(1)}, u32[]{:S(2)}, u32[]{:S(2)}) %collective-permute-start.14) | collective-permute-done | bytes 24608 | tf_op jit(solution)/shard_map/ppermute | solution.py:370
  58.8 0.4 send.7
  59.2 0.8 collective-permute-start.15
  60.0 1.2 %same.7 = (f32[2,80,80]{2,1,0:T(8,128)S(1)}, f32[1,2048]{1,0:T(1,128)S(1)}) custom-call(s32[4]{0:T(128)S(1)} %copy-done.1, s32[4,2048]{1,0:T(4,128)S(1)} %copy-done, f32[2,48,128]{2,1,0:T(8,128)S(1)} %get-tuple-element.51.pay, f32[48,128]{1,0:T(8,128)S(1)} %collective-permute-done.13.far, f32[48,128]{1,0:T(8,128)S(1)} %collective-permute-done.14.sib_far), custom_call_target="tpu_custom_call" | custom-call | tf_op jit(solution)/shard_map/same/pallas_call | solution.py:375
  61.1 1.9 %collective-permute-done.15.h = f32[2,80,80]{2,1,0:T(8,128)S(1)} collective-permute-done((f32[2,80,80]{2,1,0:T(8,128)S(1)}, f32[2,80,80]{2,1,0:T(8,128)S(1)}, u32[]{:S(2)}, u32[]{:S(2)}) %collective-permute-start.15) | collective-permute-done | bytes 51232 | tf_op jit(solution)/shard_map/ppermute | solution.py:374
  63.1 1.0 %collective-permute-start.16 = (f32[2,80,80]{2,1,0:T(8,128)S(1)}, f32[2,80,80]{2,1,0:T(8,128)S(1)}, u32[]{:S(2)}, u32[]{:S(2)}) collective-permute-start(f32[2,80,80]{2,1,0:T(8,128)S(1)} %collective-permute-done.15.h), channel_id=1, source_target_pairs={{0,16},{32,48},{64,80},{96,112},{16,0},{48,32},{80,64},{112,96},{1... | collective-permute-start | bytes 153608 | tf_op jit(solution)/shard_map/ppermute | solution.py:384
  64.1 2.9 %all-to-all-done = f32[128,1,256]{2,1,0:T(1,128)S(1)} async-done(((f32[128,1,256]{2,1,0:T(1,128)}), f32[128,1,256]{2,1,0:T(1,128)S(1)}, u32[]{:S(2)}, u32[]{:S(2)}) %all-to-all-start) | async-done | bytes 131104 | tf_op jit(solution)/shard_map/all_to_all | solution.py:369
  67.0 0.0 collective-permute-done.16.g
  67.0 8.7 %final.1 = f32[80,4,32,256]{3,2,1,0:T(8,128)} custom-call(f32[2,80,80]{2,1,0:T(8,128)S(1)} %get-tuple-element.54.q0, f32[2,80,80]{2,1,0:T(8,128)S(1)} %collective-permute-done.15.h, f32[2,80,80]{2,1,0:T(8,128)S(1)} %collective-permute-done.16.g, f32[2,96,384]{2,1,0:T(8,128)S(1)} %get-tuple-element.56.z, f32[80,4,32,256]{3,2,1,0:T(8,128)} %x.1), custom_call_target="tpu_custom_call" | custom-call | tf_op jit(solution)/shard_map/final/pallas_call | solution.py:397
  75.7 2.4 %place.1 = f32[4,2048]{1,0:T(4,128)} custom-call(s32[4]{0:T(128)S(1)} %copy-done.1, s32[4,2048]{1,0:T(4,128)S(1)} %copy-done, f32[128,256]{1,0:T(8,128)S(1)} %bitcast.5, f32[1,2048]{1,0:T(1,128)S(1)} %get-tuple-element.60.r0, f32[1,2048]{1,0:T(1,128)S(1)} %get-tuple-element.61.r1, f32[1,2048]{1,0:T(1,128)S(1)} %get-tuple-element.62.r2, ...), custom_call_target="tpu_custom_call" | custom-call | tf_op jit(solution)/shard_map/place/pallas_call | solution.py:406
  (1 shorter events, 0.0 us)
Async XLA Ops:
  0.6 12.9 %copy-start = (s32[4,2048]{1,0:T(4,128)S(1)}, s32[4,2048]{1,0:T(4,128)}, u32[]{:S(2)}) copy-start(s32[4,2048]{1,0:T(4,128)} %owner.9) | copy-start | bytes 98308
  0.6 12.9 %copy-start.1 = (s32[4]{0:T(128)S(1)}, s32[4]{0:T(128)}, u32[]{:S(2)}) copy-start(s32[4]{0:T(128)} %order.9) | copy-start | bytes 52
  3.9 2.5 %collective-permute-start = (f32[96,256]{1,0:T(8,128)S(1)}, f32[96,256]{1,0:T(8,128)S(1)}, u32[]{:S(2)}, u32[]{:S(2)}) collective-permute-start(f32[96,256]{1,0:T(8,128)S(1)} %init.1.own), channel_id=1, source_target_pairs={{0,16},{32,48},{64,80},{96,112},{16,0},{48,32},{80,64},{112,96},{1... | collective-permute-start | bytes 294920 | tf_op jit(solution)/shard_map/ppermute | solution.py:362
  6.5 4.1 %collective-permute-start.1 = (f32[48,128]{1,0:T(8,128)S(1)}, f32[48,128]{1,0:T(8,128)S(1)}, u32[]{:S(2)}, u32[]{:S(2)}) collective-permute-start(f32[48,128]{1,0:T(8,128)S(1)} %get-tuple-element.34), channel_id=1, source_target_pairs={{0,32},{64,96},{48,80},{112,16},{32,0},{96,64},{80,48},{16,112},{1... | collective-permute-start | bytes 73736 | tf_op jit(solution)/shard_map/ppermute | solution.py:366
  10.6 1.2 %collective-permute-start.2 = (f32[48,128]{1,0:T(8,128)S(1)}, f32[48,128]{1,0:T(8,128)S(1)}, u32[]{:S(2)}, u32[]{:S(2)}) collective-permute-start(f32[48,128]{1,0:T(8,128)S(1)} %collective-permute-done.1.far), channel_id=1, source_target_pairs={{0,16},{32,48},{64,80},{96,112},{16,0},{48,32},{80,64},{112,96},{1... | collective-permute-start | bytes 73736 | tf_op jit(solution)/shard_map/ppermute | solution.py:370
  12.2 3.7 %collective-permute-start.3 = (f32[2,80,80]{2,1,0:T(8,128)S(1)}, f32[2,80,80]{2,1,0:T(8,128)S(1)}, u32[]{:S(2)}, u32[]{:S(2)}) collective-permute-start(f32[2,80,80]{2,1,0:T(8,128)S(1)} %send.4), channel_id=1, source_target_pairs={{0,1},{2,3},{4,5},{6,7},{8,9},{10,11},{12,13},{14,15},{17,18},{19,... | collective-permute-start | bytes 153608 | tf_op jit(solution)/shard_map/ppermute | solution.py:374
  15.9 1.9 %collective-permute-start.4 = (f32[2,80,80]{2,1,0:T(8,128)S(1)}, f32[2,80,80]{2,1,0:T(8,128)S(1)}, u32[]{:S(2)}, u32[]{:S(2)}) collective-permute-start(f32[2,80,80]{2,1,0:T(8,128)S(1)} %collective-permute-done.3.h), channel_id=1, source_target_pairs={{0,16},{32,48},{64,80},{96,112},{16,0},{48,32},{80,64},{112,96},{1... | collective-permute-start | bytes 153608 | tf_op jit(solution)/shard_map/ppermute | solution.py:384
  18.3 4.1 %collective-permute-start.5 = (f32[48,128]{1,0:T(8,128)S(1)}, f32[48,128]{1,0:T(8,128)S(1)}, u32[]{:S(2)}, u32[]{:S(2)}) collective-permute-start(f32[48,128]{1,0:T(8,128)S(1)} %get-tuple-element.40), channel_id=1, source_target_pairs={{0,32},{64,96},{48,80},{112,16},{32,0},{96,64},{80,48},{16,112},{1... | collective-permute-start | bytes 73736 | tf_op jit(solution)/shard_map/ppermute | solution.py:366
  22.4 1.2 %collective-permute-start.6 = (f32[48,128]{1,0:T(8,128)S(1)}, f32[48,128]{1,0:T(8,128)S(1)}, u32[]{:S(2)}, u32[]{:S(2)}) collective-permute-start(f32[48,128]{1,0:T(8,128)S(1)} %collective-permute-done.5.far), channel_id=1, source_target_pairs={{0,16},{32,48},{64,80},{96,112},{16,0},{48,32},{80,64},{112,96},{1... | collective-permute-start | bytes 73736 | tf_op jit(solution)/shard_map/ppermute | solution.py:370
  24.0 3.7 %collective-permute-start.7 = (f32[2,80,80]{2,1,0:T(8,128)S(1)}, f32[2,80,80]{2,1,0:T(8,128)S(1)}, u32[]{:S(2)}, u32[]{:S(2)}) collective-permute-start(f32[2,80,80]{2,1,0:T(8,128)S(1)} %send.5), channel_id=1, source_target_pairs={{0,1},{2,3},{4,5},{6,7},{8,9},{10,11},{12,13},{14,15},{17,18},{19,... | collective-permute-start | bytes 153608 | tf_op jit(solution)/shard_map/ppermute | solution.py:374
  27.7 1.9 %collective-permute-start.8 = (f32[2,80,80]{2,1,0:T(8,128)S(1)}, f32[2,80,80]{2,1,0:T(8,128)S(1)}, u32[]{:S(2)}, u32[]{:S(2)}) collective-permute-start(f32[2,80,80]{2,1,0:T(8,128)S(1)} %collective-permute-done.7.h), channel_id=1, source_target_pairs={{0,16},{32,48},{64,80},{96,112},{16,0},{48,32},{80,64},{112,96},{1... | collective-permute-start | bytes 153608 | tf_op jit(solution)/shard_map/ppermute | solution.py:384
  30.1 4.1 %collective-permute-start.9 = (f32[48,128]{1,0:T(8,128)S(1)}, f32[48,128]{1,0:T(8,128)S(1)}, u32[]{:S(2)}, u32[]{:S(2)}) collective-permute-start(f32[48,128]{1,0:T(8,128)S(1)} %get-tuple-element.46), channel_id=1, source_target_pairs={{0,32},{64,96},{48,80},{112,16},{32,0},{96,64},{80,48},{16,112},{1... | collective-permute-start | bytes 73736 | tf_op jit(solution)/shard_map/ppermute | solution.py:366
  34.2 1.2 %collective-permute-start.10 = (f32[48,128]{1,0:T(8,128)S(1)}, f32[48,128]{1,0:T(8,128)S(1)}, u32[]{:S(2)}, u32[]{:S(2)}) collective-permute-start(f32[48,128]{1,0:T(8,128)S(1)} %collective-permute-done.9.far), channel_id=1, source_target_pairs={{0,16},{32,48},{64,80},{96,112},{16,0},{48,32},{80,64},{112,96},{1... | collective-permute-start | bytes 73736 | tf_op jit(solution)/shard_map/ppermute | solution.py:370
  35.8 3.7 %collective-permute-start.11 = (f32[2,80,80]{2,1,0:T(8,128)S(1)}, f32[2,80,80]{2,1,0:T(8,128)S(1)}, u32[]{:S(2)}, u32[]{:S(2)}) collective-permute-start(f32[2,80,80]{2,1,0:T(8,128)S(1)} %send.6), channel_id=1, source_target_pairs={{0,1},{2,3},{4,5},{6,7},{8,9},{10,11},{12,13},{14,15},{17,18},{19,... | collective-permute-start | bytes 153608 | tf_op jit(solution)/shard_map/ppermute | solution.py:374
  39.4 1.9 %collective-permute-start.12 = (f32[2,80,80]{2,1,0:T(8,128)S(1)}, f32[2,80,80]{2,1,0:T(8,128)S(1)}, u32[]{:S(2)}, u32[]{:S(2)}) collective-permute-start(f32[2,80,80]{2,1,0:T(8,128)S(1)} %collective-permute-done.11.h), channel_id=1, source_target_pairs={{0,16},{32,48},{64,80},{96,112},{16,0},{48,32},{80,64},{112,96},{1... | collective-permute-start | bytes 153608 | tf_op jit(solution)/shard_map/ppermute | solution.py:384
  41.8 14.9 %collective-permute-start.13 = (f32[48,128]{1,0:T(8,128)S(1)}, f32[48,128]{1,0:T(8,128)S(1)}, u32[]{:S(2)}, u32[]{:S(2)}) collective-permute-start(f32[48,128]{1,0:T(8,128)S(1)} %get-tuple-element.52), channel_id=1, source_target_pairs={{0,32},{64,96},{48,80},{112,16},{32,0},{96,64},{80,48},{16,112},{1... | collective-permute-start | bytes 73736 | tf_op jit(solution)/shard_map/ppermute | solution.py:366
  45.4 21.5 %all-to-all-start = ((f32[128,1,256]{2,1,0:T(1,128)}), f32[128,1,256]{2,1,0:T(1,128)S(1)}, u32[]{:S(2)}, u32[]{:S(2)}) async-start(f32[128,1,256]{2,1,0:T(1,128)} %broadcast_in_dim.2), calls=%async_computation | async-start | bytes 262144 | tf_op jit(solution)/shard_map/all_to_all | solution.py:369
  56.8 2.0 %collective-permute-start.14 = (f32[48,128]{1,0:T(8,128)S(1)}, f32[48,128]{1,0:T(8,128)S(1)}, u32[]{:S(2)}, u32[]{:S(2)}) collective-permute-start(f32[48,128]{1,0:T(8,128)S(1)} %collective-permute-done.13.far), channel_id=1, source_target_pairs={{0,16},{32,48},{64,80},{96,112},{16,0},{48,32},{80,64},{112,96},{1... | collective-permute-start | bytes 73736 | tf_op jit(solution)/shard_map/ppermute | solution.py:370
  59.2 3.9 %collective-permute-start.15 = (f32[2,80,80]{2,1,0:T(8,128)S(1)}, f32[2,80,80]{2,1,0:T(8,128)S(1)}, u32[]{:S(2)}, u32[]{:S(2)}) collective-permute-start(f32[2,80,80]{2,1,0:T(8,128)S(1)} %send.7), channel_id=1, source_target_pairs={{0,1},{2,3},{4,5},{6,7},{8,9},{10,11},{12,13},{14,15},{17,18},{19,... | collective-permute-start | bytes 153608 | tf_op jit(solution)/shard_map/ppermute | solution.py:374
  63.1 3.9 %collective-permute-start.16 = (f32[2,80,80]{2,1,0:T(8,128)S(1)}, f32[2,80,80]{2,1,0:T(8,128)S(1)}, u32[]{:S(2)}, u32[]{:S(2)}) collective-permute-start(f32[2,80,80]{2,1,0:T(8,128)S(1)} %collective-permute-done.15.h), channel_id=1, source_target_pairs={{0,16},{32,48},{64,80},{96,112},{16,0},{48,32},{80,64},{112,96},{1... | collective-permute-start | bytes 153608 | tf_op jit(solution)/shard_map/ppermute | solution.py:384

commit v6 on v5

--- a/solution.py
+++ b/solution.py
@@ -170,7 +170,7 @@
     return lax.rem(index + core_of(), 2) == 0
 
 
-def emit(k, z, z_out, pay_out, edge_out, nv_out=None):
+def emit(k, z, z_out, pay_out, edge_out, news_out=None):
     pays = []
     at = slice(CAP * k, CAP * k + CAP)
     news = []
@@ -180,12 +180,16 @@
         z_out[t, ROW_N : ROW_N + 1, at] = normed
         pays.append(pay)
         news.append(normed)
-    edge_out[...] = jnp.where(upward(lax.axis_index("gx") // 2), pays[1], pays[0])
-    if nv_out is not None:
-        first = core_of() == 0
-        past = slice(0, CAP * k)
-        nv_out[:, past] = jnp.where(first, z[0][ROW_N : ROW_N + 1, past], z[1][ROW_N : ROW_N + 1, past])
-        nv_out[:, at] = jnp.where(first, news[0], news[1])
+    edge_out[: ROWS // 2] = jnp.where(upward(lax.axis_index("gx") // 2), pays[1], pays[0])
+    if news_out is not None:
+        rows = [
+            jnp.concatenate([z[t][ROW_N : ROW_N + 1, CAP * i : CAP * i + CAP] for t in range(2)], axis=1) for i in range(k)
+        ]
+        rows.append(jnp.concatenate(news, axis=1))
+        rows.append(jnp.zeros((8 - NB, 2 * CAP), F32))
+        block = jnp.concatenate(rows, axis=0)
+        edge_out[ROWS // 2 :] = block
+        news_out[...] = block
 
 
 def start_kernel(own, sib, z_out, pay_out, edge_out):
@@ -209,8 +213,8 @@
     up = upward(y)
     first = core_of() == 0
     ends = edge(y, chips)
-    far = jnp.where(ends & jnp.logical_not(first), 0.0, far[...])
-    sib_far = jnp.where(ends & first, 0.0, sib_far[...])
+    far = jnp.where(ends & jnp.logical_not(first), 0.0, far[: ROWS // 2])
+    sib_far = jnp.where(ends & first, 0.0, sib_far[: ROWS // 2])
     blocks = [jnp.where(up, sib_far, far), pay[0], pay[1], jnp.where(up, far, sib_far)]
     blocks = [unpack(b) for b in blocks]
     rights = [right_side(b) for b in blocks]
@@ -250,6 +254,17 @@
         base = base + jnp.sum(hot, axis=1, keepdims=True)
 
 
+def same_last_kernel(k, order, owner, pay, far, sib_far, news, across, out, rank_out, column):
+    first = core_of() == 0
+    at = slice(ROWS // 2, ROWS // 2 + NB)
+    mine, other = far[at], sib_far[at]
+    column[0:NB] = news[:NB]
+    column[NB : 2 * NB] = jnp.where(first, mine, other)
+    column[2 * NB : 3 * NB] = across[:NB]
+    column[3 * NB :] = jnp.where(first, other, mine)
+    same_kernel(k, order, owner, pay, far, sib_far, out, rank_out)
+
+
 def advance(z, gain):
     anomaly = z - jnp.sum(z, axis=0, keepdims=True) / M
     return z + dot(gain, anomaly, precision=HIGH)
@@ -261,14 +276,14 @@
     return q0[t] + jnp.where(ends & jnp.logical_not(first), 0.0, h[t]) + jnp.where(ends & first, 0.0, g[t])
 
 
-def step_kernel(k, q0, h, g, z, z_out, pay_out, edge_out, nv_out=None):
+def step_kernel(k, q0, h, g, z, z_out, pay_out, edge_out, news_out=None):
     new = []
     for t in range(2):
         moved = advance(z[t, :M], whole_gain(t, q0, h, g))
         z_out[t, :M] = moved
         z_out[t, M:] = z[t, M:]
         new.append(jnp.concatenate([moved, z[t, M:]], axis=0))
-    emit(k, new, z_out, pay_out, edge_out, nv_out)
+    emit(k, new, z_out, pay_out, edge_out, news_out)
 
 
 def final_kernel(q0, h, g, z, x, out, come, go, come_sems, go_sems):
@@ -297,16 +312,21 @@
         store.wait()
 
 
-def place_kernel(order, owner, nv, r0, r1, r2, r3, out):
-    high, low = split2(nv[...].T)
-    tiles = iota((TILES, OBS), 0)
-    slots = iota((CAP, OBS), 0).astype(F32)
+def place_kernel(order, owner, n0, n1, n2, n3, r0, r1, r2, r3, out):
+    me = lax.axis_index("gx") * lax.axis_size("gy") + lax.axis_index("gy")
+    chips = iota((TILES // 2, OBS), 0)
+    seats = iota((2 * CAP, OBS), 0)
     for k, rank in enumerate((r0, r1, r2, r3)):
         b = order[k]
-        at = slice(CAP * k, CAP * k + CAP)
-        hot = jnp.where(owner[pl.ds(b, 1), :] == tiles, 1.0, 0.0).astype(BF16)
-        got = dot(jnp.concatenate([high[at], low[at]], axis=1), jnp.concatenate([hot, hot], axis=0))
-        out[pl.ds(b, 1), :] = jnp.sum(jnp.where(rank[...] == slots, got, 0.0), axis=0, keepdims=True)
+        tile = owner[pl.ds(b, 1), :]
+        away = tile ^ me
+        block = ((away >> 2) & 3) * 16 + (away & 3) * 4 + ((away >> 5) & 3)
+        hot = jnp.where(block == chips, 1.0, 0.0).astype(BF16)
+        rows = jnp.concatenate([n[pl.ds(k, 16, stride=NB), :] for n in (n0, n1, n2, n3)], axis=0)
+        high, low = split2(rows.T)
+        got = dot(jnp.concatenate([high, low], axis=1), jnp.concatenate([hot, hot], axis=0))
+        seat = ((tile >> 4) & 1) * CAP + rank[...].astype(jnp.int32)
+        out[pl.ds(b, 1), :] = jnp.sum(jnp.where(seat == seats, got, 0.0), axis=0, keepdims=True)
 
 
 VMEM = pl.BlockSpec(memory_space=pltpu.VMEM)
@@ -361,38 +381,46 @@
         name="start",
     )(own, lax.ppermute(own, "gx", core))
     ranks = []
+    xor = lambda value, bits: lax.ppermute(value, both, [(q, q ^ bits) for q in range(width * height)])
     for k in range(NB):
         last = k + 1 == NB
         far = lax.ppermute(edge, "gx", side_x)
         if last:
-            spread = jnp.broadcast_to(nv, (TILES, NB * CAP))
-            everyone = lax.all_to_all(spread, both, 0, 0, tiled=True)
+            across = xor(news, 2 * 32)
         sib_far = lax.ppermute(far, "gx", core)
         send = call(send_kernel, out_shape=shape(2, M, M), in_specs=[VMEM] * 3, out_specs=VMEM, name="send")(
             pay, far, sib_far
         )
+        send, sib_far = lax.optimization_barrier((send, sib_far))
         h = lax.ppermute(send, both, side_y)
-        q0, rank = call(
-            functools.partial(same_kernel, k),
-            out_shape=(shape(2, M, M), shape(1, OBS)),
-            in_specs=[SMEM] + [VMEM] * 4,
-            out_specs=(VMEM, VMEM),
+        extra = ((news, across), (shape(4 * NB, 128),)) if last else ((), ())
+        q0, rank, *rest = call(
+            functools.partial(same_last_kernel if last else same_kernel, k),
+            out_shape=(shape(2, M, M), shape(1, OBS)) + extra[1],
+            in_specs=[SMEM] + [VMEM] * (4 + len(extra[0])),
+            out_specs=(VMEM,) * (2 + len(extra[1])),
             name="same",
-        )(batch_order, obs_owner, pay, far, sib_far)
+        )(batch_order, obs_owner, pay, far, sib_far, *extra[0])
+        if last:
+            column = rest[0]
+            plane = jnp.concatenate([column] + [xor(column, j) for j in range(1, 4)], axis=0)
         ranks.append(rank)
         h, q0 = lax.optimization_barrier((h, q0))
         g = lax.ppermute(h, "gx", core)
-        if not last:
-            wide = (shape(1, NB * CAP),) if k + 2 == NB else ()
+        if last:
+            planes = [plane] + [xor(plane, 4 * j) for j in range(1, 4)]
+        else:
+            tail = k + 2 == NB
+            edge_shape = (shape(ROWS // 2 + 8, 128), shape(8, 128)) if tail else pay_shapes[1:]
             z, pay, edge, *rest = call(
                 functools.partial(step_kernel, k + 1),
-                out_shape=(z_shape,) + pay_shapes + wide,
+                out_shape=(z_shape, pay_shapes[0]) + edge_shape,
                 in_specs=[VMEM] * 4,
-                out_specs=(VMEM,) * (3 + len(wide)),
+                out_specs=(VMEM,) * (4 if tail else 3),
                 name="step",
             )(q0, h, g, z)
-            if rest:
-                nv = rest[0]
+            if tail:
+                news = rest[0]
     slabs = pltpu.VMEM((SLABS, M, SLAB, TY), F32)
     state = call(
         final_kernel,
@@ -400,16 +428,17 @@
         in_specs=[VMEM] * 4 + [HBM],
         out_specs=HBM,
         scratch_shapes=[slabs, slabs, pltpu.SemaphoreType.DMA((SLABS,)), pltpu.SemaphoreType.DMA((SLABS,))],
+        cost_estimate=pl.CostEstimate(flops=6 * M * M * LEV * TX * TY, bytes_accessed=8 * M * LEV * TX * TY, transcendentals=0),
         name="final",
     )(q0, h, g, z, pltpu.with_memory_space_constraint(ensemble, pltpu.HBM))
-    state, everyone = lax.optimization_barrier((state, everyone))
+    state, planes = lax.optimization_barrier((state, planes))
     innovation = call(
         place_kernel,
         out_shape=shape(NB, OBS),
-        in_specs=[SMEM] + [VMEM] * 6,
+        in_specs=[SMEM] + [VMEM] * 9,
         out_specs=VMEM,
         name="place",
-    )(batch_order, obs_owner, everyone, *ranks)
+    )(batch_order, obs_owner, *planes, *ranks)
     return state, innovation
 
 

time: 78.3 us -> 81.4 us (1.040)
  starting transfers between devices: 34.5 us -> 39.4 us
  waiting for transfers between devices: 19.8 us -> 18.7 us
    ppermute x0 -> x7, starting transfers between devices: none -> 15.1 us  [local(): lax.ppermute(value, both, [(q, q ^ bits) for q in range(width * height)])]
    all_to_all x1 -> x0, starting transfers between devices: 11.3 us -> none  [local(): everyone = lax.all_to_all(spread, both, 0, 0, tiled=True)]
    all_to_all x1 -> x0, waiting for transfers between devices: 2.9 us -> none  [local(): everyone = lax.all_to_all(spread, both, 0, 0, tiled=True)]
    ppermute x4, starting transfers between devices: 4.05 us -> 6.19 us  [local(): g = lax.ppermute(h, 'gx', core)]
    ppermute x4, waiting for transfers between devices: 3.65 us -> 4.91 us  [local(): far = lax.ppermute(edge, 'gx', side_x)]
    ppermute x0 -> x7, waiting for transfers between devices: none -> 1.01 us  [local(): lax.ppermute(value, both, [(q, q ^ bits) for q in range(width * height)])]
    ppermute x4, starting transfers between devices: 1.64 us -> 0.66 us  [local(): sib_far = lax.ppermute(far, 'gx', core)]
    ppermute x4, waiting for transfers between devices: 3.94 us -> 3.1 us  [local(): sib_far = lax.ppermute(far, 'gx', core)]
  transfers between devices with their start and end apart: 18 -> 24, of which waited for: 16 -> 17; matrix products, arithmetic and copies ran while one was open for 1% -> 0% of each run, Pallas kernels for 6% -> 15%
where the time goes in v6:
time: 81.4 us; the launch traced here: 81.2 us
  starting transfers between devices  39.4 us (48%)
  Pallas kernels  22.3 us (27%)
  waiting for transfers between devices  18.7 us (23%)
    ppermute x7, starting transfers between devices, local(): lax.ppermute(value, both, [(q, q ^ bits) for q in range(width * height)])  15.1 us
    ppermute x4, starting transfers between devices, local(): far = lax.ppermute(edge, 'gx', side_x)  11.4 us
    pallas_call x1, Pallas kernels, local(): call(final_kernel, out_shape=shape(M, LEV, TX, TY), in_specs=[VMEM] * 4 +...  8.67 us
    ppermute x4, starting transfers between devices, local(): g = lax.ppermute(h, 'gx', core)  6.19 us
    ppermute x4, waiting for transfers between devices, local(): h = lax.ppermute(send, both, side_y)  5.98 us
    ppermute x4, waiting for transfers between devices, local(): far = lax.ppermute(edge, 'gx', side_x)  4.91 us
    pallas_call x4, Pallas kernels, local(): call(functools.partial(same_last_kernel if last else same_kernel, k), out...  4.7 us
    ppermute x4, starting transfers between devices, local(): h = lax.ppermute(send, both, side_y)  4.45 us
  transfers between devices with their start and end apart: 24, of which 17 were waited for; matrix products, arithmetic and copies ran while one was open for 0% of the time, Pallas kernels for 15%

profile of v6, /device:TPU:1, one launch (start us, length us, event | category | flops | bytes accessed | tf_op | source)
XLA Modules:
  0.0 81.2 jit_solution(9493135398133739571)
XLA Ops:
  0.7 3.3 %init.1.own = f32[96,256]{1,0:T(8,128)S(1)} custom-call(s32[4]{0:T(128)} %order.9, f32[4,2048]{1,0:T(4,128)} %value_hbm.1, f32[4,2048]{1,0:T(4,128)} %variance_hbm.1, s32[4,2048]{1,0:T(4,128)} %owner.9, s32[4,2048]{1,0:T(4,128)} %cell_hbm.1, s32[4,8,2048]{2,1,0:T(8,128)} %bitcast.1, f32[80,4,32,256]{3,2,1,0:T(8,128)} %x.1), custom_call_target="tpu_custom_call" | custom-call | tf_op jit(solution)/shard_map/init/pallas_call | solution.py:360
  3.9 1.5 %collective-permute-start = (f32[96,256]{1,0:T(8,128)S(1)}, f32[96,256]{1,0:T(8,128)S(1)}, u32[]{:S(2)}, u32[]{:S(2)}) collective-permute-start(f32[96,256]{1,0:T(8,128)S(1)} %init.1.own), channel_id=1, source_target_pairs={{0,16},{32,48},{64,80},{96,112},{16,0},{48,32},{80,64},{112,96},{1... | collective-permute-start | bytes 294920 | tf_op jit(solution)/shard_map/ppermute | solution.py:382
  5.4 0.9 %collective-permute-done.sib = f32[96,256]{1,0:T(8,128)S(1)} collective-permute-done((f32[96,256]{1,0:T(8,128)S(1)}, f32[96,256]{1,0:T(8,128)S(1)}, u32[]{:S(2)}, u32[]{:S(2)}) %collective-permute-start) | collective-permute-done | bytes 98336 | tf_op jit(solution)/shard_map/ppermute | solution.py:382
  6.4 0.2 start.1
  6.5 2.9 %collective-permute-start.1 = (f32[48,128]{1,0:T(8,128)S(1)}, f32[48,128]{1,0:T(8,128)S(1)}, u32[]{:S(2)}, u32[]{:S(2)}) collective-permute-start(f32[48,128]{1,0:T(8,128)S(1)} %get-tuple-element.46), channel_id=1, source_target_pairs={{0,32},{64,96},{48,80},{112,16},{32,0},{96,64},{80,48},{16,112},{1... | collective-permute-start | bytes 73736 | tf_op jit(solution)/shard_map/ppermute | solution.py:387
  9.4 1.2 %collective-permute-done.1.far = f32[48,128]{1,0:T(8,128)S(1)} collective-permute-done((f32[48,128]{1,0:T(8,128)S(1)}, f32[48,128]{1,0:T(8,128)S(1)}, u32[]{:S(2)}, u32[]{:S(2)}) %collective-permute-start.1) | collective-permute-done | bytes 24608 | tf_op jit(solution)/shard_map/ppermute | solution.py:387
  10.6 0.2 collective-permute-start.2
  10.8 1.0 %collective-permute-done.2.sib_far = f32[48,128]{1,0:T(8,128)S(1)} collective-permute-done((f32[48,128]{1,0:T(8,128)S(1)}, f32[48,128]{1,0:T(8,128)S(1)}, u32[]{:S(2)}, u32[]{:S(2)}) %collective-permute-start.2) | collective-permute-done | bytes 24608 | tf_op jit(solution)/shard_map/ppermute | solution.py:390
  11.8 0.4 send.4
  12.2 1.3 %collective-permute-start.3 = (f32[2,80,80]{2,1,0:T(8,128)S(1)}, f32[2,80,80]{2,1,0:T(8,128)S(1)}, u32[]{:S(2)}, u32[]{:S(2)}) collective-permute-start(f32[2,80,80]{2,1,0:T(8,128)S(1)} %send.4), channel_id=1, source_target_pairs={{0,1},{2,3},{4,5},{6,7},{8,9},{10,11},{12,13},{14,15},{17,18},{19,... | collective-permute-start | bytes 153608 | tf_op jit(solution)/shard_map/ppermute | solution.py:395
  13.5 0.0 copy-done.1
  13.5 1.2 %same.4 = (f32[2,80,80]{2,1,0:T(8,128)S(1)}, f32[1,2048]{1,0:T(1,128)S(1)}) custom-call(s32[4]{0:T(128)S(1)} %copy-done.1, s32[4,2048]{1,0:T(4,128)S(1)} %copy-done, f32[2,48,128]{2,1,0:T(8,128)S(1)} %get-tuple-element.45.pay, f32[48,128]{1,0:T(8,128)S(1)} %collective-permute-done.1.far, f32[48,128]{1,0:T(8,128)S(1)} %collective-permute-done.2.sib_far), custom_call_target="tpu_custom_call" | custom-call | tf_op jit(solution)/shard_map/same/pallas_call | solution.py:397
  14.7 1.2 %collective-permute-done.3.h = f32[2,80,80]{2,1,0:T(8,128)S(1)} collective-permute-done((f32[2,80,80]{2,1,0:T(8,128)S(1)}, f32[2,80,80]{2,1,0:T(8,128)S(1)}, u32[]{:S(2)}, u32[]{:S(2)}) %collective-permute-start.3) | collective-permute-done | bytes 51232 | tf_op jit(solution)/shard_map/ppermute | solution.py:395
  15.9 1.0 %collective-permute-start.4 = (f32[2,80,80]{2,1,0:T(8,128)S(1)}, f32[2,80,80]{2,1,0:T(8,128)S(1)}, u32[]{:S(2)}, u32[]{:S(2)}) collective-permute-start(f32[2,80,80]{2,1,0:T(8,128)S(1)} %collective-permute-done.3.h), channel_id=1, source_target_pairs={{0,16},{32,48},{64,80},{96,112},{16,0},{48,32},{80,64},{112,96},{1... | collective-permute-start | bytes 153608 | tf_op jit(solution)/shard_map/ppermute | solution.py:409
  16.9 0.9 %collective-permute-done.4.g = f32[2,80,80]{2,1,0:T(8,128)S(1)} collective-permute-done((f32[2,80,80]{2,1,0:T(8,128)S(1)}, f32[2,80,80]{2,1,0:T(8,128)S(1)}, u32[]{:S(2)}, u32[]{:S(2)}) %collective-permute-start.4) | collective-permute-done | bytes 51232 | tf_op jit(solution)/shard_map/ppermute | solution.py:409
  17.9 0.4 step.3
  18.3 2.9 %collective-permute-start.5 = (f32[48,128]{1,0:T(8,128)S(1)}, f32[48,128]{1,0:T(8,128)S(1)}, u32[]{:S(2)}, u32[]{:S(2)}) collective-permute-start(f32[48,128]{1,0:T(8,128)S(1)} %get-tuple-element.54), channel_id=1, source_target_pairs={{0,32},{64,96},{48,80},{112,16},{32,0},{96,64},{80,48},{16,112},{1... | collective-permute-start | bytes 73736 | tf_op jit(solution)/shard_map/ppermute | solution.py:387
  21.2 1.2 %collective-permute-done.5.far = f32[48,128]{1,0:T(8,128)S(1)} collective-permute-done((f32[48,128]{1,0:T(8,128)S(1)}, f32[48,128]{1,0:T(8,128)S(1)}, u32[]{:S(2)}, u32[]{:S(2)}) %collective-permute-start.5) | collective-permute-done | bytes 24608 | tf_op jit(solution)/shard_map/ppermute | solution.py:387
  22.4 0.2 collective-permute-start.6
  22.5 1.0 %collective-permute-done.6.sib_far = f32[48,128]{1,0:T(8,128)S(1)} collective-permute-done((f32[48,128]{1,0:T(8,128)S(1)}, f32[48,128]{1,0:T(8,128)S(1)}, u32[]{:S(2)}, u32[]{:S(2)}) %collective-permute-start.6) | collective-permute-done | bytes 24608 | tf_op jit(solution)/shard_map/ppermute | solution.py:390
  23.6 0.4 send.5
  24.0 1.3 %collective-permute-start.7 = (f32[2,80,80]{2,1,0:T(8,128)S(1)}, f32[2,80,80]{2,1,0:T(8,128)S(1)}, u32[]{:S(2)}, u32[]{:S(2)}) collective-permute-start(f32[2,80,80]{2,1,0:T(8,128)S(1)} %send.5), channel_id=1, source_target_pairs={{0,1},{2,3},{4,5},{6,7},{8,9},{10,11},{12,13},{14,15},{17,18},{19,... | collective-permute-start | bytes 153608 | tf_op jit(solution)/shard_map/ppermute | solution.py:395
  25.3 1.2 %same.5 = (f32[2,80,80]{2,1,0:T(8,128)S(1)}, f32[1,2048]{1,0:T(1,128)S(1)}) custom-call(s32[4]{0:T(128)S(1)} %copy-done.1, s32[4,2048]{1,0:T(4,128)S(1)} %copy-done, f32[2,48,128]{2,1,0:T(8,128)S(1)} %get-tuple-element.53.pay, f32[48,128]{1,0:T(8,128)S(1)} %collective-permute-done.5.far, f32[48,128]{1,0:T(8,128)S(1)} %collective-permute-done.6.sib_far), custom_call_target="tpu_custom_call" | custom-call | tf_op jit(solution)/shard_map/same/pallas_call | solution.py:397
  26.4 1.2 %collective-permute-done.7.h = f32[2,80,80]{2,1,0:T(8,128)S(1)} collective-permute-done((f32[2,80,80]{2,1,0:T(8,128)S(1)}, f32[2,80,80]{2,1,0:T(8,128)S(1)}, u32[]{:S(2)}, u32[]{:S(2)}) %collective-permute-start.7) | collective-permute-done | bytes 51232 | tf_op jit(solution)/shard_map/ppermute | solution.py:395
  27.7 1.0 %collective-permute-start.8 = (f32[2,80,80]{2,1,0:T(8,128)S(1)}, f32[2,80,80]{2,1,0:T(8,128)S(1)}, u32[]{:S(2)}, u32[]{:S(2)}) collective-permute-start(f32[2,80,80]{2,1,0:T(8,128)S(1)} %collective-permute-done.7.h), channel_id=1, source_target_pairs={{0,16},{32,48},{64,80},{96,112},{16,0},{48,32},{80,64},{112,96},{1... | collective-permute-start | bytes 153608 | tf_op jit(solution)/shard_map/ppermute | solution.py:409
  28.7 0.9 %collective-permute-done.8.g = f32[2,80,80]{2,1,0:T(8,128)S(1)} collective-permute-done((f32[2,80,80]{2,1,0:T(8,128)S(1)}, f32[2,80,80]{2,1,0:T(8,128)S(1)}, u32[]{:S(2)}, u32[]{:S(2)}) %collective-permute-start.8) | collective-permute-done | bytes 51232 | tf_op jit(solution)/shard_map/ppermute | solution.py:409
  29.6 0.5 step.4
  30.1 2.8 %collective-permute-start.9 = (f32[48,128]{1,0:T(8,128)S(1)}, f32[48,128]{1,0:T(8,128)S(1)}, u32[]{:S(2)}, u32[]{:S(2)}) collective-permute-start(f32[48,128]{1,0:T(8,128)S(1)} %get-tuple-element.62), channel_id=1, source_target_pairs={{0,32},{64,96},{48,80},{112,16},{32,0},{96,64},{80,48},{16,112},{1... | collective-permute-start | bytes 73736 | tf_op jit(solution)/shard_map/ppermute | solution.py:387
  32.9 1.2 %collective-permute-done.9.far = f32[48,128]{1,0:T(8,128)S(1)} collective-permute-done((f32[48,128]{1,0:T(8,128)S(1)}, f32[48,128]{1,0:T(8,128)S(1)}, u32[]{:S(2)}, u32[]{:S(2)}) %collective-permute-start.9) | collective-permute-done | bytes 24608 | tf_op jit(solution)/shard_map/ppermute | solution.py:387
  34.2 0.2 collective-permute-start.10
  34.3 1.0 %collective-permute-done.10.sib_far = f32[48,128]{1,0:T(8,128)S(1)} collective-permute-done((f32[48,128]{1,0:T(8,128)S(1)}, f32[48,128]{1,0:T(8,128)S(1)}, u32[]{:S(2)}, u32[]{:S(2)}) %collective-permute-start.10) | collective-permute-done | bytes 24608 | tf_op jit(solution)/shard_map/ppermute | solution.py:390
  35.4 0.4 send.6
  35.8 1.3 %collective-permute-start.11 = (f32[2,80,80]{2,1,0:T(8,128)S(1)}, f32[2,80,80]{2,1,0:T(8,128)S(1)}, u32[]{:S(2)}, u32[]{:S(2)}) collective-permute-start(f32[2,80,80]{2,1,0:T(8,128)S(1)} %send.6), channel_id=1, source_target_pairs={{0,1},{2,3},{4,5},{6,7},{8,9},{10,11},{12,13},{14,15},{17,18},{19,... | collective-permute-start | bytes 153608 | tf_op jit(solution)/shard_map/ppermute | solution.py:395
  37.0 1.2 %same.6 = (f32[2,80,80]{2,1,0:T(8,128)S(1)}, f32[1,2048]{1,0:T(1,128)S(1)}) custom-call(s32[4]{0:T(128)S(1)} %copy-done.1, s32[4,2048]{1,0:T(4,128)S(1)} %copy-done, f32[2,48,128]{2,1,0:T(8,128)S(1)} %get-tuple-element.61.pay, f32[48,128]{1,0:T(8,128)S(1)} %collective-permute-done.9.far, f32[48,128]{1,0:T(8,128)S(1)} %collective-permute-done.10.sib_far), custom_call_target="tpu_custom_call" | custom-call | tf_op jit(solution)/shard_map/same/pallas_call | solution.py:397
  38.2 1.2 %collective-permute-done.11.h = f32[2,80,80]{2,1,0:T(8,128)S(1)} collective-permute-done((f32[2,80,80]{2,1,0:T(8,128)S(1)}, f32[2,80,80]{2,1,0:T(8,128)S(1)}, u32[]{:S(2)}, u32[]{:S(2)}) %collective-permute-start.11) | collective-permute-done | bytes 51232 | tf_op jit(solution)/shard_map/ppermute | solution.py:395
  39.4 1.0 %collective-permute-start.12 = (f32[2,80,80]{2,1,0:T(8,128)S(1)}, f32[2,80,80]{2,1,0:T(8,128)S(1)}, u32[]{:S(2)}, u32[]{:S(2)}) collective-permute-start(f32[2,80,80]{2,1,0:T(8,128)S(1)} %collective-permute-done.11.h), channel_id=1, source_target_pairs={{0,16},{32,48},{64,80},{96,112},{16,0},{48,32},{80,64},{112,96},{1... | collective-permute-start | bytes 153608 | tf_op jit(solution)/shard_map/ppermute | solution.py:409
  40.5 0.9 %collective-permute-done.12.g = f32[2,80,80]{2,1,0:T(8,128)S(1)} collective-permute-done((f32[2,80,80]{2,1,0:T(8,128)S(1)}, f32[2,80,80]{2,1,0:T(8,128)S(1)}, u32[]{:S(2)}, u32[]{:S(2)}) %collective-permute-start.12) | collective-permute-done | bytes 51232 | tf_op jit(solution)/shard_map/ppermute | solution.py:409
  41.4 0.4 step.5
  41.8 2.9 %collective-permute-start.13 = (f32[56,128]{1,0:T(8,128)S(1)}, f32[56,128]{1,0:T(8,128)S(1)}, u32[]{:S(2)}, u32[]{:S(2)}) collective-permute-start(f32[56,128]{1,0:T(8,128)S(1)} %get-tuple-element.70), channel_id=1, source_target_pairs={{0,32},{64,96},{48,80},{112,16},{32,0},{96,64},{80,48},{16,112},{1... | collective-permute-start | bytes 86024 | tf_op jit(solution)/shard_map/ppermute | solution.py:387
  44.7 1.3 %collective-permute-done.13.far = f32[56,128]{1,0:T(8,128)S(1)} collective-permute-done((f32[56,128]{1,0:T(8,128)S(1)}, f32[56,128]{1,0:T(8,128)S(1)}, u32[]{:S(2)}, u32[]{:S(2)}) %collective-permute-start.13) | collective-permute-done | bytes 28704 | tf_op jit(solution)/shard_map/ppermute | solution.py:387
  46.0 0.2 collective-permute-start.14
  46.1 3.0 %collective-permute-start.16 = (f32[8,128]{1,0:T(8,128)S(1)}, f32[8,128]{1,0:T(8,128)S(1)}, u32[]{:S(2)}, u32[]{:S(2)}) collective-permute-start(f32[8,128]{1,0:T(8,128)S(1)} %get-tuple-element.73.news), channel_id=1, source_target_pairs={{0,64},{1,65},{2,66},{3,67},{4,68},{5,69},{6,70},{7,71},{8,72},{9,... | collective-permute-start | bytes 12296 | tf_op jit(solution)/shard_map/ppermute | solution.py:384
  49.1 0.0 collective-permute-done.14.sib_far
  49.1 0.4 send.7
  49.5 0.6 collective-permute-done.16.across
  50.1 1.2 %same.7 = (f32[2,80,80]{2,1,0:T(8,128)S(1)}, f32[1,2048]{1,0:T(1,128)S(1)}, f32[16,128]{1,0:T(8,128)S(1)}) custom-call(s32[4]{0:T(128)S(1)} %copy-done.1, s32[4,2048]{1,0:T(4,128)S(1)} %copy-done, f32[2,48,128]{2,1,0:T(8,128)S(1)} %get-tuple-element.69.pay, f32[56,128]{1,0:T(8,128)S(1)} %collective-permute-done.13.far, ...), custom_call_target="tpu_custom_call" | custom-call | tf_op jit(solution)/shard_map/same/pallas_call | solution.py:397
  51.3 1.4 %collective-permute-start.18 = (f32[16,128]{1,0:T(8,128)S(1)}, f32[16,128]{1,0:T(8,128)S(1)}, u32[]{:S(2)}, u32[]{:S(2)}) collective-permute-start(f32[16,128]{1,0:T(8,128)S(1)} %get-tuple-element.78), channel_id=1, source_target_pairs={{0,1},{1,0},{2,3},{3,2},{4,5},{5,4},{6,7},{7,6},{8,9},{9,8},{10,11... | collective-permute-start | bytes 24584 | tf_op jit(solution)/shard_map/ppermute | solution.py:384
  52.6 5.4 %collective-permute-start.19 = (f32[16,128]{1,0:T(8,128)S(1)}, f32[16,128]{1,0:T(8,128)S(1)}, u32[]{:S(2)}, u32[]{:S(2)}) collective-permute-start(f32[16,128]{1,0:T(8,128)S(1)} %get-tuple-element.78), channel_id=1, source_target_pairs={{0,2},{1,3},{2,0},{3,1},{4,6},{5,7},{6,4},{7,5},{8,10},{9,11},{10,... | collective-permute-start | bytes 24584 | tf_op jit(solution)/shard_map/ppermute | solution.py:384
  58.0 0.0 collective-permute-start.20
  58.0 0.7 collective-permute-start.15
  58.7 0.0 collective-permute-done.18
  58.7 0.4 collective-permute-done.19
  59.1 2.3 %collective-permute-done.15.h = f32[2,80,80]{2,1,0:T(8,128)S(1)} collective-permute-done((f32[2,80,80]{2,1,0:T(8,128)S(1)}, f32[2,80,80]{2,1,0:T(8,128)S(1)}, u32[]{:S(2)}, u32[]{:S(2)}) %collective-permute-start.15) | collective-permute-done | bytes 51232 | tf_op jit(solution)/shard_map/ppermute | solution.py:395
  61.5 3.1 %collective-permute-start.17 = (f32[2,80,80]{2,1,0:T(8,128)S(1)}, f32[2,80,80]{2,1,0:T(8,128)S(1)}, u32[]{:S(2)}, u32[]{:S(2)}) collective-permute-start(f32[2,80,80]{2,1,0:T(8,128)S(1)} %collective-permute-done.15.h), channel_id=1, source_target_pairs={{0,16},{32,48},{64,80},{96,112},{16,0},{48,32},{80,64},{112,96},{1... | collective-permute-start | bytes 153608 | tf_op jit(solution)/shard_map/ppermute | solution.py:409
  64.6 0.0 collective-permute-done.20
  64.6 2.1 %collective-permute-start.21 = (f32[64,128]{1,0:T(8,128)S(1)}, f32[64,128]{1,0:T(8,128)S(1)}, u32[]{:S(2)}, u32[]{:S(2)}) collective-permute-start(f32[64,128]{1,0:T(8,128)S(1)} %constant_dynamic-update-slice_fusion.n0), channel_id=1, source_target_pairs={{0,4},{1,5},{2,6},{3,7},{4,0},{5,1},{6,2},{7,3},{8,12},{9,13},{10,... | collective-permute-start | bytes 98312 | tf_op jit(solution)/shard_map/ppermute | solution.py:384
  66.7 3.3 %collective-permute-start.22 = (f32[64,128]{1,0:T(8,128)S(1)}, f32[64,128]{1,0:T(8,128)S(1)}, u32[]{:S(2)}, u32[]{:S(2)}) collective-permute-start(f32[64,128]{1,0:T(8,128)S(1)} %constant_dynamic-update-slice_fusion.n0), channel_id=1, source_target_pairs={{0,8},{1,9},{2,10},{3,11},{4,12},{5,13},{6,14},{7,15},{8,0},{9,1},... | collective-permute-start | bytes 98312 | tf_op jit(solution)/shard_map/ppermute | solution.py:384
  70.0 0.0 collective-permute-start.23
  70.0 0.0 collective-permute-done.17.g
  70.0 8.7 %final.1 = f32[80,4,32,256]{3,2,1,0:T(8,128)} custom-call(f32[2,80,80]{2,1,0:T(8,128)S(1)} %get-tuple-element.75.q0, f32[2,80,80]{2,1,0:T(8,128)S(1)} %collective-permute-done.15.h, f32[2,80,80]{2,1,0:T(8,128)S(1)} %collective-permute-done.17.g, f32[2,96,384]{2,1,0:T(8,128)S(1)} %get-tuple-element.77.z, f32[80,4,32,256]{3,2,1,0:T(8,128)} %x.1), custom_call_target="tpu_custom_call" | custom-call | flops 1258291200 | bytes 20971520 | tf_op jit(solution)/shard_map/final/pallas_call | solution.py:425
  78.7 0.0 collective-permute-done.21.n1
  78.7 0.0 collective-permute-done.22.n2
  78.7 0.0 collective-permute-done.23.n3
  78.7 2.5 %place.1 = f32[4,2048]{1,0:T(4,128)} custom-call(s32[4]{0:T(128)S(1)} %copy-done.1, s32[4,2048]{1,0:T(4,128)S(1)} %copy-done, f32[64,128]{1,0:T(8,128)S(1)} %constant_dynamic-update-slice_fusion.n0, f32[64,128]{1,0:T(8,128)S(1)} %collective-permute-done.21.n1, f32[64,128]{1,0:T(8,128)S(1)} %collective-permute-done.22.n2, ...), custom_call_target="tpu_custom_call" | custom-call | tf_op jit(solution)/shard_map/place/pallas_call | solution.py:435
  (7 shorter events, 0.0 us)
Async XLA Ops:
  0.6 12.9 %copy-start = (s32[4,2048]{1,0:T(4,128)S(1)}, s32[4,2048]{1,0:T(4,128)}, u32[]{:S(2)}) copy-start(s32[4,2048]{1,0:T(4,128)} %owner.9) | copy-start | bytes 98308
  0.6 12.9 %copy-start.1 = (s32[4]{0:T(128)S(1)}, s32[4]{0:T(128)}, u32[]{:S(2)}) copy-start(s32[4]{0:T(128)} %order.9) | copy-start | bytes 52
  3.9 2.5 %collective-permute-start = (f32[96,256]{1,0:T(8,128)S(1)}, f32[96,256]{1,0:T(8,128)S(1)}, u32[]{:S(2)}, u32[]{:S(2)}) collective-permute-start(f32[96,256]{1,0:T(8,128)S(1)} %init.1.own), channel_id=1, source_target_pairs={{0,16},{32,48},{64,80},{96,112},{16,0},{48,32},{80,64},{112,96},{1... | collective-permute-start | bytes 294920 | tf_op jit(solution)/shard_map/ppermute | solution.py:382
  6.5 4.1 %collective-permute-start.1 = (f32[48,128]{1,0:T(8,128)S(1)}, f32[48,128]{1,0:T(8,128)S(1)}, u32[]{:S(2)}, u32[]{:S(2)}) collective-permute-start(f32[48,128]{1,0:T(8,128)S(1)} %get-tuple-element.46), channel_id=1, source_target_pairs={{0,32},{64,96},{48,80},{112,16},{32,0},{96,64},{80,48},{16,112},{1... | collective-permute-start | bytes 73736 | tf_op jit(solution)/shard_map/ppermute | solution.py:387
  10.6 1.2 %collective-permute-start.2 = (f32[48,128]{1,0:T(8,128)S(1)}, f32[48,128]{1,0:T(8,128)S(1)}, u32[]{:S(2)}, u32[]{:S(2)}) collective-permute-start(f32[48,128]{1,0:T(8,128)S(1)} %collective-permute-done.1.far), channel_id=1, source_target_pairs={{0,16},{32,48},{64,80},{96,112},{16,0},{48,32},{80,64},{112,96},{1... | collective-permute-start | bytes 73736 | tf_op jit(solution)/shard_map/ppermute | solution.py:390
  12.2 3.7 %collective-permute-start.3 = (f32[2,80,80]{2,1,0:T(8,128)S(1)}, f32[2,80,80]{2,1,0:T(8,128)S(1)}, u32[]{:S(2)}, u32[]{:S(2)}) collective-permute-start(f32[2,80,80]{2,1,0:T(8,128)S(1)} %send.4), channel_id=1, source_target_pairs={{0,1},{2,3},{4,5},{6,7},{8,9},{10,11},{12,13},{14,15},{17,18},{19,... | collective-permute-start | bytes 153608 | tf_op jit(solution)/shard_map/ppermute | solution.py:395
  15.9 1.9 %collective-permute-start.4 = (f32[2,80,80]{2,1,0:T(8,128)S(1)}, f32[2,80,80]{2,1,0:T(8,128)S(1)}, u32[]{:S(2)}, u32[]{:S(2)}) collective-permute-start(f32[2,80,80]{2,1,0:T(8,128)S(1)} %collective-permute-done.3.h), channel_id=1, source_target_pairs={{0,16},{32,48},{64,80},{96,112},{16,0},{48,32},{80,64},{112,96},{1... | collective-permute-start | bytes 153608 | tf_op jit(solution)/shard_map/ppermute | solution.py:409
  18.3 4.1 %collective-permute-start.5 = (f32[48,128]{1,0:T(8,128)S(1)}, f32[48,128]{1,0:T(8,128)S(1)}, u32[]{:S(2)}, u32[]{:S(2)}) collective-permute-start(f32[48,128]{1,0:T(8,128)S(1)} %get-tuple-element.54), channel_id=1, source_target_pairs={{0,32},{64,96},{48,80},{112,16},{32,0},{96,64},{80,48},{16,112},{1... | collective-permute-start | bytes 73736 | tf_op jit(solution)/shard_map/ppermute | solution.py:387
  22.4 1.2 %collective-permute-start.6 = (f32[48,128]{1,0:T(8,128)S(1)}, f32[48,128]{1,0:T(8,128)S(1)}, u32[]{:S(2)}, u32[]{:S(2)}) collective-permute-start(f32[48,128]{1,0:T(8,128)S(1)} %collective-permute-done.5.far), channel_id=1, source_target_pairs={{0,16},{32,48},{64,80},{96,112},{16,0},{48,32},{80,64},{112,96},{1... | collective-permute-start | bytes 73736 | tf_op jit(solution)/shard_map/ppermute | solution.py:390
  24.0 3.7 %collective-permute-start.7 = (f32[2,80,80]{2,1,0:T(8,128)S(1)}, f32[2,80,80]{2,1,0:T(8,128)S(1)}, u32[]{:S(2)}, u32[]{:S(2)}) collective-permute-start(f32[2,80,80]{2,1,0:T(8,128)S(1)} %send.5), channel_id=1, source_target_pairs={{0,1},{2,3},{4,5},{6,7},{8,9},{10,11},{12,13},{14,15},{17,18},{19,... | collective-permute-start | bytes 153608 | tf_op jit(solution)/shard_map/ppermute | solution.py:395
  27.7 1.9 %collective-permute-start.8 = (f32[2,80,80]{2,1,0:T(8,128)S(1)}, f32[2,80,80]{2,1,0:T(8,128)S(1)}, u32[]{:S(2)}, u32[]{:S(2)}) collective-permute-start(f32[2,80,80]{2,1,0:T(8,128)S(1)} %collective-permute-done.7.h), channel_id=1, source_target_pairs={{0,16},{32,48},{64,80},{96,112},{16,0},{48,32},{80,64},{112,96},{1... | collective-permute-start | bytes 153608 | tf_op jit(solution)/shard_map/ppermute | solution.py:409
  30.1 4.1 %collective-permute-start.9 = (f32[48,128]{1,0:T(8,128)S(1)}, f32[48,128]{1,0:T(8,128)S(1)}, u32[]{:S(2)}, u32[]{:S(2)}) collective-permute-start(f32[48,128]{1,0:T(8,128)S(1)} %get-tuple-element.62), channel_id=1, source_target_pairs={{0,32},{64,96},{48,80},{112,16},{32,0},{96,64},{80,48},{16,112},{1... | collective-permute-start | bytes 73736 | tf_op jit(solution)/shard_map/ppermute | solution.py:387
  34.2 1.2 %collective-permute-start.10 = (f32[48,128]{1,0:T(8,128)S(1)}, f32[48,128]{1,0:T(8,128)S(1)}, u32[]{:S(2)}, u32[]{:S(2)}) collective-permute-start(f32[48,128]{1,0:T(8,128)S(1)} %collective-permute-done.9.far), channel_id=1, source_target_pairs={{0,16},{32,48},{64,80},{96,112},{16,0},{48,32},{80,64},{112,96},{1... | collective-permute-start | bytes 73736 | tf_op jit(solution)/shard_map/ppermute | solution.py:390
  35.8 3.7 %collective-permute-start.11 = (f32[2,80,80]{2,1,0:T(8,128)S(1)}, f32[2,80,80]{2,1,0:T(8,128)S(1)}, u32[]{:S(2)}, u32[]{:S(2)}) collective-permute-start(f32[2,80,80]{2,1,0:T(8,128)S(1)} %send.6), channel_id=1, source_target_pairs={{0,1},{2,3},{4,5},{6,7},{8,9},{10,11},{12,13},{14,15},{17,18},{19,... | collective-permute-start | bytes 153608 | tf_op jit(solution)/shard_map/ppermute | solution.py:395
  39.4 1.9 %collective-permute-start.12 = (f32[2,80,80]{2,1,0:T(8,128)S(1)}, f32[2,80,80]{2,1,0:T(8,128)S(1)}, u32[]{:S(2)}, u32[]{:S(2)}) collective-permute-start(f32[2,80,80]{2,1,0:T(8,128)S(1)} %collective-permute-done.11.h), channel_id=1, source_target_pairs={{0,16},{32,48},{64,80},{96,112},{16,0},{48,32},{80,64},{112,96},{1... | collective-permute-start | bytes 153608 | tf_op jit(solution)/shard_map/ppermute | solution.py:409
  41.8 4.1 %collective-permute-start.13 = (f32[56,128]{1,0:T(8,128)S(1)}, f32[56,128]{1,0:T(8,128)S(1)}, u32[]{:S(2)}, u32[]{:S(2)}) collective-permute-start(f32[56,128]{1,0:T(8,128)S(1)} %get-tuple-element.70), channel_id=1, source_target_pairs={{0,32},{64,96},{48,80},{112,16},{32,0},{96,64},{80,48},{16,112},{1... | collective-permute-start | bytes 86024 | tf_op jit(solution)/shard_map/ppermute | solution.py:387
  46.0 3.1 %collective-permute-start.14 = (f32[56,128]{1,0:T(8,128)S(1)}, f32[56,128]{1,0:T(8,128)S(1)}, u32[]{:S(2)}, u32[]{:S(2)}) collective-permute-start(f32[56,128]{1,0:T(8,128)S(1)} %collective-permute-done.13.far), channel_id=1, source_target_pairs={{0,16},{32,48},{64,80},{96,112},{16,0},{48,32},{80,64},{112,96},{1... | collective-permute-start | bytes 86024 | tf_op jit(solution)/shard_map/ppermute | solution.py:390
  46.1 4.0 %collective-permute-start.16 = (f32[8,128]{1,0:T(8,128)S(1)}, f32[8,128]{1,0:T(8,128)S(1)}, u32[]{:S(2)}, u32[]{:S(2)}) collective-permute-start(f32[8,128]{1,0:T(8,128)S(1)} %get-tuple-element.73.news), channel_id=1, source_target_pairs={{0,64},{1,65},{2,66},{3,67},{4,68},{5,69},{6,70},{7,71},{8,72},{9,... | collective-permute-start | bytes 12296 | tf_op jit(solution)/shard_map/ppermute | solution.py:384
  51.3 7.4 %collective-permute-start.18 = (f32[16,128]{1,0:T(8,128)S(1)}, f32[16,128]{1,0:T(8,128)S(1)}, u32[]{:S(2)}, u32[]{:S(2)}) collective-permute-start(f32[16,128]{1,0:T(8,128)S(1)} %get-tuple-element.78), channel_id=1, source_target_pairs={{0,1},{1,0},{2,3},{3,2},{4,5},{5,4},{6,7},{7,6},{8,9},{9,8},{10,11... | collective-permute-start | bytes 24584 | tf_op jit(solution)/shard_map/ppermute | solution.py:384
  52.6 6.5 %collective-permute-start.19 = (f32[16,128]{1,0:T(8,128)S(1)}, f32[16,128]{1,0:T(8,128)S(1)}, u32[]{:S(2)}, u32[]{:S(2)}) collective-permute-start(f32[16,128]{1,0:T(8,128)S(1)} %get-tuple-element.78), channel_id=1, source_target_pairs={{0,2},{1,3},{2,0},{3,1},{4,6},{5,7},{6,4},{7,5},{8,10},{9,11},{10,... | collective-permute-start | bytes 24584 | tf_op jit(solution)/shard_map/ppermute | solution.py:384
  58.0 6.6 %collective-permute-start.20 = (f32[16,128]{1,0:T(8,128)S(1)}, f32[16,128]{1,0:T(8,128)S(1)}, u32[]{:S(2)}, u32[]{:S(2)}) collective-permute-start(f32[16,128]{1,0:T(8,128)S(1)} %get-tuple-element.78), channel_id=1, source_target_pairs={{0,3},{1,2},{2,1},{3,0},{4,7},{5,6},{6,5},{7,4},{8,11},{9,10},{10,... | collective-permute-start | bytes 24584 | tf_op jit(solution)/shard_map/ppermute | solution.py:384
  58.0 3.4 %collective-permute-start.15 = (f32[2,80,80]{2,1,0:T(8,128)S(1)}, f32[2,80,80]{2,1,0:T(8,128)S(1)}, u32[]{:S(2)}, u32[]{:S(2)}) collective-permute-start(f32[2,80,80]{2,1,0:T(8,128)S(1)} %send.7), channel_id=1, source_target_pairs={{0,1},{2,3},{4,5},{6,7},{8,9},{10,11},{12,13},{14,15},{17,18},{19,... | collective-permute-start | bytes 153608 | tf_op jit(solution)/shard_map/ppermute | solution.py:395
  61.5 8.6 %collective-permute-start.17 = (f32[2,80,80]{2,1,0:T(8,128)S(1)}, f32[2,80,80]{2,1,0:T(8,128)S(1)}, u32[]{:S(2)}, u32[]{:S(2)}) collective-permute-start(f32[2,80,80]{2,1,0:T(8,128)S(1)} %collective-permute-done.15.h), channel_id=1, source_target_pairs={{0,16},{32,48},{64,80},{96,112},{16,0},{48,32},{80,64},{112,96},{1... | collective-permute-start | bytes 153608 | tf_op jit(solution)/shard_map/ppermute | solution.py:409
  64.6 14.1 %collective-permute-start.21 = (f32[64,128]{1,0:T(8,128)S(1)}, f32[64,128]{1,0:T(8,128)S(1)}, u32[]{:S(2)}, u32[]{:S(2)}) collective-permute-start(f32[64,128]{1,0:T(8,128)S(1)} %constant_dynamic-update-slice_fusion.n0), channel_id=1, source_target_pairs={{0,4},{1,5},{2,6},{3,7},{4,0},{5,1},{6,2},{7,3},{8,12},{9,13},{10,... | collective-permute-start | bytes 98312 | tf_op jit(solution)/shard_map/ppermute | solution.py:384
  66.7 12.0 %collective-permute-start.22 = (f32[64,128]{1,0:T(8,128)S(1)}, f32[64,128]{1,0:T(8,128)S(1)}, u32[]{:S(2)}, u32[]{:S(2)}) collective-permute-start(f32[64,128]{1,0:T(8,128)S(1)} %constant_dynamic-update-slice_fusion.n0), channel_id=1, source_target_pairs={{0,8},{1,9},{2,10},{3,11},{4,12},{5,13},{6,14},{7,15},{8,0},{9,1},... | collective-permute-start | bytes 98312 | tf_op jit(solution)/shard_map/ppermute | solution.py:384
  70.0 8.7 %collective-permute-start.23 = (f32[64,128]{1,0:T(8,128)S(1)}, f32[64,128]{1,0:T(8,128)S(1)}, u32[]{:S(2)}, u32[]{:S(2)}) collective-permute-start(f32[64,128]{1,0:T(8,128)S(1)} %constant_dynamic-update-slice_fusion.n0), channel_id=1, source_target_pairs={{0,12},{1,13},{2,14},{3,15},{4,8},{5,9},{6,10},{7,11},{8,4},{9,5},... | collective-permute-start | bytes 98312 | tf_op jit(solution)/shard_map/ppermute | solution.py:384

commit v7 on v5

--- a/solution.py
+++ b/solution.py
@@ -364,9 +364,6 @@
     for k in range(NB):
         last = k + 1 == NB
         far = lax.ppermute(edge, "gx", side_x)
-        if last:
-            spread = jnp.broadcast_to(nv, (TILES, NB * CAP))
-            everyone = lax.all_to_all(spread, both, 0, 0, tiled=True)
         sib_far = lax.ppermute(far, "gx", core)
         send = call(send_kernel, out_shape=shape(2, M, M), in_specs=[VMEM] * 3, out_specs=VMEM, name="send")(
             pay, far, sib_far
@@ -380,7 +377,12 @@
             name="same",
         )(batch_order, obs_owner, pay, far, sib_far)
         ranks.append(rank)
-        h, q0 = lax.optimization_barrier((h, q0))
+        if last:
+            h, q0, nv = lax.optimization_barrier((h, q0, nv))
+            spread = jnp.broadcast_to(nv, (TILES, NB * CAP))
+            everyone = lax.all_to_all(spread, both, 0, 0, tiled=True)
+        else:
+            h, q0 = lax.optimization_barrier((h, q0))
         g = lax.ppermute(h, "gx", core)
         if not last:
             wide = (shape(1, NB * CAP),) if k + 2 == NB else ()
@@ -400,6 +402,7 @@
         in_specs=[VMEM] * 4 + [HBM],
         out_specs=HBM,
         scratch_shapes=[slabs, slabs, pltpu.SemaphoreType.DMA((SLABS,)), pltpu.SemaphoreType.DMA((SLABS,))],
+        cost_estimate=pl.CostEstimate(flops=6 * M * M * LEV * TX * TY, bytes_accessed=8 * M * LEV * TX * TY, transcendentals=0),
         name="final",
     )(q0, h, g, z, pltpu.with_memory_space_constraint(ensemble, pltpu.HBM))
     state, everyone = lax.optimization_barrier((state, everyone))

time: 78.3 us -> 79.5 us (1.015)
  starting transfers between devices: 34.5 us -> 36.4 us
    all_to_all x1, starting transfers between devices: 11.3 us -> 13.7 us  [local(): everyone = lax.all_to_all(spread, both, 0, 0, tiled=True)]
    all_to_all x1, waiting for transfers between devices: 2.9 us -> 1.5 us  [local(): everyone = lax.all_to_all(spread, both, 0, 0, tiled=True)]
    ppermute x4, waiting for transfers between devices: 3.65 us -> 4.87 us  [local(): far = lax.ppermute(edge, 'gx', side_x)]
    ppermute x4, starting transfers between devices: 1.64 us -> 0.66 us  [local(): sib_far = lax.ppermute(far, 'gx', core)]
  transfers between devices with their start and end apart: 18 -> 18, of which waited for: 16 -> 17; matrix products, arithmetic and copies ran while one was open for 1% -> 1% of each run, Pallas kernels for 6% -> 17%
where the time goes in v7:
time: 79.5 us; the launch traced here: 79.3 us
  starting transfers between devices  36.4 us (46%)
  Pallas kernels  22.3 us (28%)
  waiting for transfers between devices  19.1 us (24%)
    all_to_all x1, starting transfers between devices, local(): everyone = lax.all_to_all(spread, both, 0, 0, tiled=True)  13.7 us
    ppermute x4, starting transfers between devices, local(): far = lax.ppermute(edge, 'gx', side_x)  11.4 us
    pallas_call x1, Pallas kernels, local(): call(final_kernel, out_shape=shape(M, LEV, TX, TY), in_specs=[VMEM] * 4 +...  8.68 us
    ppermute x4, starting transfers between devices, local(): h = lax.ppermute(send, both, side_y)  5.04 us
    ppermute x4, waiting for transfers between devices, local(): h = lax.ppermute(send, both, side_y)  4.89 us
    ppermute x4, waiting for transfers between devices, local(): far = lax.ppermute(edge, 'gx', side_x)  4.87 us
    pallas_call x4, Pallas kernels, local(): call(functools.partial(same_kernel, k), out_shape=(shape(2, M, M), shape(...  4.7 us
    ppermute x4, waiting for transfers between devices, local(): sib_far = lax.ppermute(far, 'gx', core)  4.12 us
  transfers between devices with their start and end apart: 18, of which 17 were waited for; matrix products, arithmetic and copies ran while one was open for 1% of the time, Pallas kernels for 17%

profile of v7, /device:TPU:1, one launch (start us, length us, event | category | flops | bytes accessed | tf_op | source)
XLA Modules:
  0.0 79.3 jit_solution(8223597706607422822)
XLA Ops:
  0.6 0.0 copy-start
  0.6 0.0 copy-start.1
  0.7 3.3 %init.1.own = f32[96,256]{1,0:T(8,128)S(1)} custom-call(s32[4]{0:T(128)} %order.9, f32[4,2048]{1,0:T(4,128)} %value_hbm.1, f32[4,2048]{1,0:T(4,128)} %variance_hbm.1, s32[4,2048]{1,0:T(4,128)} %owner.9, s32[4,2048]{1,0:T(4,128)} %cell_hbm.1, s32[4,8,2048]{2,1,0:T(8,128)} %bitcast.7, f32[80,4,32,256]{3,2,1,0:T(8,128)} %x.1), custom_call_target="tpu_custom_call" | custom-call | tf_op jit(solution)/shard_map/init/pallas_call | solution.py:340
  3.9 1.5 %collective-permute-start = (f32[96,256]{1,0:T(8,128)S(1)}, f32[96,256]{1,0:T(8,128)S(1)}, u32[]{:S(2)}, u32[]{:S(2)}) collective-permute-start(f32[96,256]{1,0:T(8,128)S(1)} %init.1.own), channel_id=1, source_target_pairs={{0,16},{32,48},{64,80},{96,112},{16,0},{48,32},{80,64},{112,96},{1... | collective-permute-start | bytes 294920 | tf_op jit(solution)/shard_map/ppermute | solution.py:362
  5.4 0.9 %collective-permute-done.sib = f32[96,256]{1,0:T(8,128)S(1)} collective-permute-done((f32[96,256]{1,0:T(8,128)S(1)}, f32[96,256]{1,0:T(8,128)S(1)}, u32[]{:S(2)}, u32[]{:S(2)}) %collective-permute-start) | collective-permute-done | bytes 98336 | tf_op jit(solution)/shard_map/ppermute | solution.py:362
  6.4 0.2 start.1
  6.5 2.9 %collective-permute-start.1 = (f32[48,128]{1,0:T(8,128)S(1)}, f32[48,128]{1,0:T(8,128)S(1)}, u32[]{:S(2)}, u32[]{:S(2)}) collective-permute-start(f32[48,128]{1,0:T(8,128)S(1)} %get-tuple-element.35), channel_id=1, source_target_pairs={{0,32},{64,96},{48,80},{112,16},{32,0},{96,64},{80,48},{16,112},{1... | collective-permute-start | bytes 73736 | tf_op jit(solution)/shard_map/ppermute | solution.py:366
  9.4 1.2 %collective-permute-done.1.far = f32[48,128]{1,0:T(8,128)S(1)} collective-permute-done((f32[48,128]{1,0:T(8,128)S(1)}, f32[48,128]{1,0:T(8,128)S(1)}, u32[]{:S(2)}, u32[]{:S(2)}) %collective-permute-start.1) | collective-permute-done | bytes 24608 | tf_op jit(solution)/shard_map/ppermute | solution.py:366
  10.6 0.2 collective-permute-start.2
  10.8 1.0 %collective-permute-done.2.sib_far = f32[48,128]{1,0:T(8,128)S(1)} collective-permute-done((f32[48,128]{1,0:T(8,128)S(1)}, f32[48,128]{1,0:T(8,128)S(1)}, u32[]{:S(2)}, u32[]{:S(2)}) %collective-permute-start.2) | collective-permute-done | bytes 24608 | tf_op jit(solution)/shard_map/ppermute | solution.py:367
  11.8 0.4 send.4
  12.2 1.3 %collective-permute-start.3 = (f32[2,80,80]{2,1,0:T(8,128)S(1)}, f32[2,80,80]{2,1,0:T(8,128)S(1)}, u32[]{:S(2)}, u32[]{:S(2)}) collective-permute-start(f32[2,80,80]{2,1,0:T(8,128)S(1)} %send.4), channel_id=1, source_target_pairs={{0,1},{2,3},{4,5},{6,7},{8,9},{10,11},{12,13},{14,15},{17,18},{19,... | collective-permute-start | bytes 153608 | tf_op jit(solution)/shard_map/ppermute | solution.py:371
  13.5 0.0 copy-done
  13.5 0.0 copy-done.1
  13.5 1.2 %same.4 = (f32[2,80,80]{2,1,0:T(8,128)S(1)}, f32[1,2048]{1,0:T(1,128)S(1)}) custom-call(s32[4]{0:T(128)S(1)} %copy-done.1, s32[4,2048]{1,0:T(4,128)S(1)} %copy-done, f32[2,48,128]{2,1,0:T(8,128)S(1)} %get-tuple-element.34.pay, f32[48,128]{1,0:T(8,128)S(1)} %collective-permute-done.1.far, f32[48,128]{1,0:T(8,128)S(1)} %collective-permute-done.2.sib_far), custom_call_target="tpu_custom_call" | custom-call | tf_op jit(solution)/shard_map/same/pallas_call | solution.py:372
  14.7 1.2 %collective-permute-done.3.h = f32[2,80,80]{2,1,0:T(8,128)S(1)} collective-permute-done((f32[2,80,80]{2,1,0:T(8,128)S(1)}, f32[2,80,80]{2,1,0:T(8,128)S(1)}, u32[]{:S(2)}, u32[]{:S(2)}) %collective-permute-start.3) | collective-permute-done | bytes 51232 | tf_op jit(solution)/shard_map/ppermute | solution.py:371
  15.9 1.0 %collective-permute-start.4 = (f32[2,80,80]{2,1,0:T(8,128)S(1)}, f32[2,80,80]{2,1,0:T(8,128)S(1)}, u32[]{:S(2)}, u32[]{:S(2)}) collective-permute-start(f32[2,80,80]{2,1,0:T(8,128)S(1)} %collective-permute-done.3.h), channel_id=1, source_target_pairs={{0,16},{32,48},{64,80},{96,112},{16,0},{48,32},{80,64},{112,96},{1... | collective-permute-start | bytes 153608 | tf_op jit(solution)/shard_map/ppermute | solution.py:386
  16.9 0.9 %collective-permute-done.4.g = f32[2,80,80]{2,1,0:T(8,128)S(1)} collective-permute-done((f32[2,80,80]{2,1,0:T(8,128)S(1)}, f32[2,80,80]{2,1,0:T(8,128)S(1)}, u32[]{:S(2)}, u32[]{:S(2)}) %collective-permute-start.4) | collective-permute-done | bytes 51232 | tf_op jit(solution)/shard_map/ppermute | solution.py:386
  17.9 0.4 step.3
  18.3 2.9 %collective-permute-start.5 = (f32[48,128]{1,0:T(8,128)S(1)}, f32[48,128]{1,0:T(8,128)S(1)}, u32[]{:S(2)}, u32[]{:S(2)}) collective-permute-start(f32[48,128]{1,0:T(8,128)S(1)} %get-tuple-element.41), channel_id=1, source_target_pairs={{0,32},{64,96},{48,80},{112,16},{32,0},{96,64},{80,48},{16,112},{1... | collective-permute-start | bytes 73736 | tf_op jit(solution)/shard_map/ppermute | solution.py:366
  21.2 1.2 %collective-permute-done.5.far = f32[48,128]{1,0:T(8,128)S(1)} collective-permute-done((f32[48,128]{1,0:T(8,128)S(1)}, f32[48,128]{1,0:T(8,128)S(1)}, u32[]{:S(2)}, u32[]{:S(2)}) %collective-permute-start.5) | collective-permute-done | bytes 24608 | tf_op jit(solution)/shard_map/ppermute | solution.py:366
  22.4 0.2 collective-permute-start.6
  22.5 1.0 %collective-permute-done.6.sib_far = f32[48,128]{1,0:T(8,128)S(1)} collective-permute-done((f32[48,128]{1,0:T(8,128)S(1)}, f32[48,128]{1,0:T(8,128)S(1)}, u32[]{:S(2)}, u32[]{:S(2)}) %collective-permute-start.6) | collective-permute-done | bytes 24608 | tf_op jit(solution)/shard_map/ppermute | solution.py:367
  23.6 0.4 send.5
  24.0 1.3 %collective-permute-start.7 = (f32[2,80,80]{2,1,0:T(8,128)S(1)}, f32[2,80,80]{2,1,0:T(8,128)S(1)}, u32[]{:S(2)}, u32[]{:S(2)}) collective-permute-start(f32[2,80,80]{2,1,0:T(8,128)S(1)} %send.5), channel_id=1, source_target_pairs={{0,1},{2,3},{4,5},{6,7},{8,9},{10,11},{12,13},{14,15},{17,18},{19,... | collective-permute-start | bytes 153608 | tf_op jit(solution)/shard_map/ppermute | solution.py:371
  25.3 1.2 %same.5 = (f32[2,80,80]{2,1,0:T(8,128)S(1)}, f32[1,2048]{1,0:T(1,128)S(1)}) custom-call(s32[4]{0:T(128)S(1)} %copy-done.1, s32[4,2048]{1,0:T(4,128)S(1)} %copy-done, f32[2,48,128]{2,1,0:T(8,128)S(1)} %get-tuple-element.40.pay, f32[48,128]{1,0:T(8,128)S(1)} %collective-permute-done.5.far, f32[48,128]{1,0:T(8,128)S(1)} %collective-permute-done.6.sib_far), custom_call_target="tpu_custom_call" | custom-call | tf_op jit(solution)/shard_map/same/pallas_call | solution.py:372
  26.4 1.2 %collective-permute-done.7.h = f32[2,80,80]{2,1,0:T(8,128)S(1)} collective-permute-done((f32[2,80,80]{2,1,0:T(8,128)S(1)}, f32[2,80,80]{2,1,0:T(8,128)S(1)}, u32[]{:S(2)}, u32[]{:S(2)}) %collective-permute-start.7) | collective-permute-done | bytes 51232 | tf_op jit(solution)/shard_map/ppermute | solution.py:371
  27.7 1.0 %collective-permute-start.8 = (f32[2,80,80]{2,1,0:T(8,128)S(1)}, f32[2,80,80]{2,1,0:T(8,128)S(1)}, u32[]{:S(2)}, u32[]{:S(2)}) collective-permute-start(f32[2,80,80]{2,1,0:T(8,128)S(1)} %collective-permute-done.7.h), channel_id=1, source_target_pairs={{0,16},{32,48},{64,80},{96,112},{16,0},{48,32},{80,64},{112,96},{1... | collective-permute-start | bytes 153608 | tf_op jit(solution)/shard_map/ppermute | solution.py:386
  28.7 0.9 %collective-permute-done.8.g = f32[2,80,80]{2,1,0:T(8,128)S(1)} collective-permute-done((f32[2,80,80]{2,1,0:T(8,128)S(1)}, f32[2,80,80]{2,1,0:T(8,128)S(1)}, u32[]{:S(2)}, u32[]{:S(2)}) %collective-permute-start.8) | collective-permute-done | bytes 51232 | tf_op jit(solution)/shard_map/ppermute | solution.py:386
  29.6 0.5 step.4
  30.1 2.8 %collective-permute-start.9 = (f32[48,128]{1,0:T(8,128)S(1)}, f32[48,128]{1,0:T(8,128)S(1)}, u32[]{:S(2)}, u32[]{:S(2)}) collective-permute-start(f32[48,128]{1,0:T(8,128)S(1)} %get-tuple-element.47), channel_id=1, source_target_pairs={{0,32},{64,96},{48,80},{112,16},{32,0},{96,64},{80,48},{16,112},{1... | collective-permute-start | bytes 73736 | tf_op jit(solution)/shard_map/ppermute | solution.py:366
  32.9 1.2 %collective-permute-done.9.far = f32[48,128]{1,0:T(8,128)S(1)} collective-permute-done((f32[48,128]{1,0:T(8,128)S(1)}, f32[48,128]{1,0:T(8,128)S(1)}, u32[]{:S(2)}, u32[]{:S(2)}) %collective-permute-start.9) | collective-permute-done | bytes 24608 | tf_op jit(solution)/shard_map/ppermute | solution.py:366
  34.2 0.2 collective-permute-start.10
  34.3 1.0 %collective-permute-done.10.sib_far = f32[48,128]{1,0:T(8,128)S(1)} collective-permute-done((f32[48,128]{1,0:T(8,128)S(1)}, f32[48,128]{1,0:T(8,128)S(1)}, u32[]{:S(2)}, u32[]{:S(2)}) %collective-permute-start.10) | collective-permute-done | bytes 24608 | tf_op jit(solution)/shard_map/ppermute | solution.py:367
  35.3 0.4 send.6
  35.8 1.3 %collective-permute-start.11 = (f32[2,80,80]{2,1,0:T(8,128)S(1)}, f32[2,80,80]{2,1,0:T(8,128)S(1)}, u32[]{:S(2)}, u32[]{:S(2)}) collective-permute-start(f32[2,80,80]{2,1,0:T(8,128)S(1)} %send.6), channel_id=1, source_target_pairs={{0,1},{2,3},{4,5},{6,7},{8,9},{10,11},{12,13},{14,15},{17,18},{19,... | collective-permute-start | bytes 153608 | tf_op jit(solution)/shard_map/ppermute | solution.py:371
  37.0 1.2 %same.6 = (f32[2,80,80]{2,1,0:T(8,128)S(1)}, f32[1,2048]{1,0:T(1,128)S(1)}) custom-call(s32[4]{0:T(128)S(1)} %copy-done.1, s32[4,2048]{1,0:T(4,128)S(1)} %copy-done, f32[2,48,128]{2,1,0:T(8,128)S(1)} %get-tuple-element.46.pay, f32[48,128]{1,0:T(8,128)S(1)} %collective-permute-done.9.far, f32[48,128]{1,0:T(8,128)S(1)} %collective-permute-done.10.sib_far), custom_call_target="tpu_custom_call" | custom-call | tf_op jit(solution)/shard_map/same/pallas_call | solution.py:372
  38.2 1.2 %collective-permute-done.11.h = f32[2,80,80]{2,1,0:T(8,128)S(1)} collective-permute-done((f32[2,80,80]{2,1,0:T(8,128)S(1)}, f32[2,80,80]{2,1,0:T(8,128)S(1)}, u32[]{:S(2)}, u32[]{:S(2)}) %collective-permute-start.11) | collective-permute-done | bytes 51232 | tf_op jit(solution)/shard_map/ppermute | solution.py:371
  39.4 1.0 %collective-permute-start.12 = (f32[2,80,80]{2,1,0:T(8,128)S(1)}, f32[2,80,80]{2,1,0:T(8,128)S(1)}, u32[]{:S(2)}, u32[]{:S(2)}) collective-permute-start(f32[2,80,80]{2,1,0:T(8,128)S(1)} %collective-permute-done.11.h), channel_id=1, source_target_pairs={{0,16},{32,48},{64,80},{96,112},{16,0},{48,32},{80,64},{112,96},{1... | collective-permute-start | bytes 153608 | tf_op jit(solution)/shard_map/ppermute | solution.py:386
  40.5 0.9 %collective-permute-done.12.g = f32[2,80,80]{2,1,0:T(8,128)S(1)} collective-permute-done((f32[2,80,80]{2,1,0:T(8,128)S(1)}, f32[2,80,80]{2,1,0:T(8,128)S(1)}, u32[]{:S(2)}, u32[]{:S(2)}) %collective-permute-start.12) | collective-permute-done | bytes 51232 | tf_op jit(solution)/shard_map/ppermute | solution.py:386
  41.4 0.4 step.5
  41.8 2.9 %collective-permute-start.13 = (f32[48,128]{1,0:T(8,128)S(1)}, f32[48,128]{1,0:T(8,128)S(1)}, u32[]{:S(2)}, u32[]{:S(2)}) collective-permute-start(f32[48,128]{1,0:T(8,128)S(1)} %get-tuple-element.53), channel_id=1, source_target_pairs={{0,32},{64,96},{48,80},{112,16},{32,0},{96,64},{80,48},{16,112},{1... | collective-permute-start | bytes 73736 | tf_op jit(solution)/shard_map/ppermute | solution.py:366
  44.7 1.2 %collective-permute-done.13.far = f32[48,128]{1,0:T(8,128)S(1)} collective-permute-done((f32[48,128]{1,0:T(8,128)S(1)}, f32[48,128]{1,0:T(8,128)S(1)}, u32[]{:S(2)}, u32[]{:S(2)}) %collective-permute-start.13) | collective-permute-done | bytes 24608 | tf_op jit(solution)/shard_map/ppermute | solution.py:366
  45.9 0.2 collective-permute-start.14
  46.1 1.0 %collective-permute-done.14.sib_far = f32[48,128]{1,0:T(8,128)S(1)} collective-permute-done((f32[48,128]{1,0:T(8,128)S(1)}, f32[48,128]{1,0:T(8,128)S(1)}, u32[]{:S(2)}, u32[]{:S(2)}) %collective-permute-start.14) | collective-permute-done | bytes 24608 | tf_op jit(solution)/shard_map/ppermute | solution.py:367
  47.1 0.4 send.7
  47.5 1.3 %collective-permute-start.15 = (f32[2,80,80]{2,1,0:T(8,128)S(1)}, f32[2,80,80]{2,1,0:T(8,128)S(1)}, u32[]{:S(2)}, u32[]{:S(2)}) collective-permute-start(f32[2,80,80]{2,1,0:T(8,128)S(1)} %send.7), channel_id=1, source_target_pairs={{0,1},{2,3},{4,5},{6,7},{8,9},{10,11},{12,13},{14,15},{17,18},{19,... | collective-permute-start | bytes 153608 | tf_op jit(solution)/shard_map/ppermute | solution.py:371
  48.8 1.2 %same.7 = (f32[2,80,80]{2,1,0:T(8,128)S(1)}, f32[1,2048]{1,0:T(1,128)S(1)}) custom-call(s32[4]{0:T(128)S(1)} %copy-done.1, s32[4,2048]{1,0:T(4,128)S(1)} %copy-done, f32[2,48,128]{2,1,0:T(8,128)S(1)} %get-tuple-element.52.pay, f32[48,128]{1,0:T(8,128)S(1)} %collective-permute-done.13.far, f32[48,128]{1,0:T(8,128)S(1)} %collective-permute-done.14.sib_far), custom_call_target="tpu_custom_call" | custom-call | tf_op jit(solution)/shard_map/same/pallas_call | solution.py:372
  50.0 1.2 %collective-permute-done.15.h = f32[2,80,80]{2,1,0:T(8,128)S(1)} collective-permute-done((f32[2,80,80]{2,1,0:T(8,128)S(1)}, f32[2,80,80]{2,1,0:T(8,128)S(1)}, u32[]{:S(2)}, u32[]{:S(2)}) %collective-permute-start.15) | collective-permute-done | bytes 51232 | tf_op jit(solution)/shard_map/ppermute | solution.py:371
  51.2 1.0 %collective-permute-start.16 = (f32[2,80,80]{2,1,0:T(8,128)S(1)}, f32[2,80,80]{2,1,0:T(8,128)S(1)}, u32[]{:S(2)}, u32[]{:S(2)}) collective-permute-start(f32[2,80,80]{2,1,0:T(8,128)S(1)} %collective-permute-done.15.h), channel_id=1, source_target_pairs={{0,16},{32,48},{64,80},{96,112},{16,0},{48,32},{80,64},{112,96},{1... | collective-permute-start | bytes 153608 | tf_op jit(solution)/shard_map/ppermute | solution.py:386
  52.2 0.7 broadcast_in_dim.2
  53.0 13.7 %all-to-all-start = ((f32[128,1,256]{2,1,0:T(1,128)}), f32[128,1,256]{2,1,0:T(1,128)S(1)}, u32[]{:S(2)}, u32[]{:S(2)}) async-start(f32[128,1,256]{2,1,0:T(1,128)} %broadcast_in_dim.2), calls=%async_computation | async-start | bytes 262144 | tf_op jit(solution)/shard_map/all_to_all | solution.py:383
  66.7 0.0 collective-permute-done.16.g
  66.7 8.7 %final.1 = f32[80,4,32,256]{3,2,1,0:T(8,128)} custom-call(f32[2,80,80]{2,1,0:T(8,128)S(1)} %get-tuple-element.56.q0, f32[2,80,80]{2,1,0:T(8,128)S(1)} %collective-permute-done.15.h, f32[2,80,80]{2,1,0:T(8,128)S(1)} %collective-permute-done.16.g, f32[2,96,384]{2,1,0:T(8,128)S(1)} %get-tuple-element.58.z, f32[80,4,32,256]{3,2,1,0:T(8,128)} %x.1), custom_call_target="tpu_custom_call" | custom-call | flops 1258291200 | bytes 20971520 | tf_op jit(solution)/shard_map/final/pallas_call | solution.py:399
  75.4 1.5 %all-to-all-done = f32[128,1,256]{2,1,0:T(1,128)S(1)} async-done(((f32[128,1,256]{2,1,0:T(1,128)}), f32[128,1,256]{2,1,0:T(1,128)S(1)}, u32[]{:S(2)}, u32[]{:S(2)}) %all-to-all-start) | async-done | bytes 131104 | tf_op jit(solution)/shard_map/all_to_all | solution.py:383
  76.9 2.4 %place.1 = f32[4,2048]{1,0:T(4,128)} custom-call(s32[4]{0:T(128)S(1)} %copy-done.1, s32[4,2048]{1,0:T(4,128)S(1)} %copy-done, f32[128,256]{1,0:T(8,128)S(1)} %bitcast.5, f32[1,2048]{1,0:T(1,128)S(1)} %get-tuple-element.62.r0, f32[1,2048]{1,0:T(1,128)S(1)} %get-tuple-element.63.r1, f32[1,2048]{1,0:T(1,128)S(1)} %get-tuple-element.64.r2, ...), custom_call_target="tpu_custom_call" | custom-call | tf_op jit(solution)/shard_map/place/pallas_call | solution.py:409
  (1 shorter events, 0.0 us)
Async XLA Ops:
  0.6 12.9 %copy-start = (s32[4,2048]{1,0:T(4,128)S(1)}, s32[4,2048]{1,0:T(4,128)}, u32[]{:S(2)}) copy-start(s32[4,2048]{1,0:T(4,128)} %owner.9) | copy-start | bytes 98308
  0.6 12.9 %copy-start.1 = (s32[4]{0:T(128)S(1)}, s32[4]{0:T(128)}, u32[]{:S(2)}) copy-start(s32[4]{0:T(128)} %order.9) | copy-start | bytes 52
  3.9 2.5 %collective-permute-start = (f32[96,256]{1,0:T(8,128)S(1)}, f32[96,256]{1,0:T(8,128)S(1)}, u32[]{:S(2)}, u32[]{:S(2)}) collective-permute-start(f32[96,256]{1,0:T(8,128)S(1)} %init.1.own), channel_id=1, source_target_pairs={{0,16},{32,48},{64,80},{96,112},{16,0},{48,32},{80,64},{112,96},{1... | collective-permute-start | bytes 294920 | tf_op jit(solution)/shard_map/ppermute | solution.py:362
  6.5 4.1 %collective-permute-start.1 = (f32[48,128]{1,0:T(8,128)S(1)}, f32[48,128]{1,0:T(8,128)S(1)}, u32[]{:S(2)}, u32[]{:S(2)}) collective-permute-start(f32[48,128]{1,0:T(8,128)S(1)} %get-tuple-element.35), channel_id=1, source_target_pairs={{0,32},{64,96},{48,80},{112,16},{32,0},{96,64},{80,48},{16,112},{1... | collective-permute-start | bytes 73736 | tf_op jit(solution)/shard_map/ppermute | solution.py:366
  10.6 1.2 %collective-permute-start.2 = (f32[48,128]{1,0:T(8,128)S(1)}, f32[48,128]{1,0:T(8,128)S(1)}, u32[]{:S(2)}, u32[]{:S(2)}) collective-permute-start(f32[48,128]{1,0:T(8,128)S(1)} %collective-permute-done.1.far), channel_id=1, source_target_pairs={{0,16},{32,48},{64,80},{96,112},{16,0},{48,32},{80,64},{112,96},{1... | collective-permute-start | bytes 73736 | tf_op jit(solution)/shard_map/ppermute | solution.py:367
  12.2 3.7 %collective-permute-start.3 = (f32[2,80,80]{2,1,0:T(8,128)S(1)}, f32[2,80,80]{2,1,0:T(8,128)S(1)}, u32[]{:S(2)}, u32[]{:S(2)}) collective-permute-start(f32[2,80,80]{2,1,0:T(8,128)S(1)} %send.4), channel_id=1, source_target_pairs={{0,1},{2,3},{4,5},{6,7},{8,9},{10,11},{12,13},{14,15},{17,18},{19,... | collective-permute-start | bytes 153608 | tf_op jit(solution)/shard_map/ppermute | solution.py:371
  15.9 1.9 %collective-permute-start.4 = (f32[2,80,80]{2,1,0:T(8,128)S(1)}, f32[2,80,80]{2,1,0:T(8,128)S(1)}, u32[]{:S(2)}, u32[]{:S(2)}) collective-permute-start(f32[2,80,80]{2,1,0:T(8,128)S(1)} %collective-permute-done.3.h), channel_id=1, source_target_pairs={{0,16},{32,48},{64,80},{96,112},{16,0},{48,32},{80,64},{112,96},{1... | collective-permute-start | bytes 153608 | tf_op jit(solution)/shard_map/ppermute | solution.py:386
  18.3 4.1 %collective-permute-start.5 = (f32[48,128]{1,0:T(8,128)S(1)}, f32[48,128]{1,0:T(8,128)S(1)}, u32[]{:S(2)}, u32[]{:S(2)}) collective-permute-start(f32[48,128]{1,0:T(8,128)S(1)} %get-tuple-element.41), channel_id=1, source_target_pairs={{0,32},{64,96},{48,80},{112,16},{32,0},{96,64},{80,48},{16,112},{1... | collective-permute-start | bytes 73736 | tf_op jit(solution)/shard_map/ppermute | solution.py:366
  22.4 1.2 %collective-permute-start.6 = (f32[48,128]{1,0:T(8,128)S(1)}, f32[48,128]{1,0:T(8,128)S(1)}, u32[]{:S(2)}, u32[]{:S(2)}) collective-permute-start(f32[48,128]{1,0:T(8,128)S(1)} %collective-permute-done.5.far), channel_id=1, source_target_pairs={{0,16},{32,48},{64,80},{96,112},{16,0},{48,32},{80,64},{112,96},{1... | collective-permute-start | bytes 73736 | tf_op jit(solution)/shard_map/ppermute | solution.py:367
  24.0 3.7 %collective-permute-start.7 = (f32[2,80,80]{2,1,0:T(8,128)S(1)}, f32[2,80,80]{2,1,0:T(8,128)S(1)}, u32[]{:S(2)}, u32[]{:S(2)}) collective-permute-start(f32[2,80,80]{2,1,0:T(8,128)S(1)} %send.5), channel_id=1, source_target_pairs={{0,1},{2,3},{4,5},{6,7},{8,9},{10,11},{12,13},{14,15},{17,18},{19,... | collective-permute-start | bytes 153608 | tf_op jit(solution)/shard_map/ppermute | solution.py:371
  27.7 1.9 %collective-permute-start.8 = (f32[2,80,80]{2,1,0:T(8,128)S(1)}, f32[2,80,80]{2,1,0:T(8,128)S(1)}, u32[]{:S(2)}, u32[]{:S(2)}) collective-permute-start(f32[2,80,80]{2,1,0:T(8,128)S(1)} %collective-permute-done.7.h), channel_id=1, source_target_pairs={{0,16},{32,48},{64,80},{96,112},{16,0},{48,32},{80,64},{112,96},{1... | collective-permute-start | bytes 153608 | tf_op jit(solution)/shard_map/ppermute | solution.py:386
  30.1 4.1 %collective-permute-start.9 = (f32[48,128]{1,0:T(8,128)S(1)}, f32[48,128]{1,0:T(8,128)S(1)}, u32[]{:S(2)}, u32[]{:S(2)}) collective-permute-start(f32[48,128]{1,0:T(8,128)S(1)} %get-tuple-element.47), channel_id=1, source_target_pairs={{0,32},{64,96},{48,80},{112,16},{32,0},{96,64},{80,48},{16,112},{1... | collective-permute-start | bytes 73736 | tf_op jit(solution)/shard_map/ppermute | solution.py:366
  34.2 1.2 %collective-permute-start.10 = (f32[48,128]{1,0:T(8,128)S(1)}, f32[48,128]{1,0:T(8,128)S(1)}, u32[]{:S(2)}, u32[]{:S(2)}) collective-permute-start(f32[48,128]{1,0:T(8,128)S(1)} %collective-permute-done.9.far), channel_id=1, source_target_pairs={{0,16},{32,48},{64,80},{96,112},{16,0},{48,32},{80,64},{112,96},{1... | collective-permute-start | bytes 73736 | tf_op jit(solution)/shard_map/ppermute | solution.py:367
  35.8 3.7 %collective-permute-start.11 = (f32[2,80,80]{2,1,0:T(8,128)S(1)}, f32[2,80,80]{2,1,0:T(8,128)S(1)}, u32[]{:S(2)}, u32[]{:S(2)}) collective-permute-start(f32[2,80,80]{2,1,0:T(8,128)S(1)} %send.6), channel_id=1, source_target_pairs={{0,1},{2,3},{4,5},{6,7},{8,9},{10,11},{12,13},{14,15},{17,18},{19,... | collective-permute-start | bytes 153608 | tf_op jit(solution)/shard_map/ppermute | solution.py:371
  39.4 1.9 %collective-permute-start.12 = (f32[2,80,80]{2,1,0:T(8,128)S(1)}, f32[2,80,80]{2,1,0:T(8,128)S(1)}, u32[]{:S(2)}, u32[]{:S(2)}) collective-permute-start(f32[2,80,80]{2,1,0:T(8,128)S(1)} %collective-permute-done.11.h), channel_id=1, source_target_pairs={{0,16},{32,48},{64,80},{96,112},{16,0},{48,32},{80,64},{112,96},{1... | collective-permute-start | bytes 153608 | tf_op jit(solution)/shard_map/ppermute | solution.py:386
  41.8 4.1 %collective-permute-start.13 = (f32[48,128]{1,0:T(8,128)S(1)}, f32[48,128]{1,0:T(8,128)S(1)}, u32[]{:S(2)}, u32[]{:S(2)}) collective-permute-start(f32[48,128]{1,0:T(8,128)S(1)} %get-tuple-element.53), channel_id=1, source_target_pairs={{0,32},{64,96},{48,80},{112,16},{32,0},{96,64},{80,48},{16,112},{1... | collective-permute-start | bytes 73736 | tf_op jit(solution)/shard_map/ppermute | solution.py:366
  45.9 1.2 %collective-permute-start.14 = (f32[48,128]{1,0:T(8,128)S(1)}, f32[48,128]{1,0:T(8,128)S(1)}, u32[]{:S(2)}, u32[]{:S(2)}) collective-permute-start(f32[48,128]{1,0:T(8,128)S(1)} %collective-permute-done.13.far), channel_id=1, source_target_pairs={{0,16},{32,48},{64,80},{96,112},{16,0},{48,32},{80,64},{112,96},{1... | collective-permute-start | bytes 73736 | tf_op jit(solution)/shard_map/ppermute | solution.py:367
  47.5 3.7 %collective-permute-start.15 = (f32[2,80,80]{2,1,0:T(8,128)S(1)}, f32[2,80,80]{2,1,0:T(8,128)S(1)}, u32[]{:S(2)}, u32[]{:S(2)}) collective-permute-start(f32[2,80,80]{2,1,0:T(8,128)S(1)} %send.7), channel_id=1, source_target_pairs={{0,1},{2,3},{4,5},{6,7},{8,9},{10,11},{12,13},{14,15},{17,18},{19,... | collective-permute-start | bytes 153608 | tf_op jit(solution)/shard_map/ppermute | solution.py:371
  51.2 15.5 %collective-permute-start.16 = (f32[2,80,80]{2,1,0:T(8,128)S(1)}, f32[2,80,80]{2,1,0:T(8,128)S(1)}, u32[]{:S(2)}, u32[]{:S(2)}) collective-permute-start(f32[2,80,80]{2,1,0:T(8,128)S(1)} %collective-permute-done.15.h), channel_id=1, source_target_pairs={{0,16},{32,48},{64,80},{96,112},{16,0},{48,32},{80,64},{112,96},{1... | collective-permute-start | bytes 153608 | tf_op jit(solution)/shard_map/ppermute | solution.py:386
  53.0 23.9 %all-to-all-start = ((f32[128,1,256]{2,1,0:T(1,128)}), f32[128,1,256]{2,1,0:T(1,128)S(1)}, u32[]{:S(2)}, u32[]{:S(2)}) async-start(f32[128,1,256]{2,1,0:T(1,128)} %broadcast_in_dim.2), calls=%async_computation | async-start | bytes 262144 | tf_op jit(solution)/shard_map/all_to_all | solution.py:383

commit v8 on v5

--- a/solution.py
+++ b/solution.py
@@ -305,8 +305,9 @@
         b = order[k]
         at = slice(CAP * k, CAP * k + CAP)
         hot = jnp.where(owner[pl.ds(b, 1), :] == tiles, 1.0, 0.0).astype(BF16)
-        got = dot(jnp.concatenate([high[at], low[at]], axis=1), jnp.concatenate([hot, hot], axis=0))
-        out[pl.ds(b, 1), :] = jnp.sum(jnp.where(rank[...] == slots, got, 0.0), axis=0, keepdims=True)
+        got = dot(jnp.concatenate([high[at], low[at]], axis=0), hot)
+        got = jnp.where(rank[...] == slots, got[:CAP] + got[CAP:], 0.0)
+        out[pl.ds(b, 1), :] = jnp.sum(got, axis=0, keepdims=True)
 
 
 VMEM = pl.BlockSpec(memory_space=pltpu.VMEM)
@@ -400,6 +401,7 @@
         in_specs=[VMEM] * 4 + [HBM],
         out_specs=HBM,
         scratch_shapes=[slabs, slabs, pltpu.SemaphoreType.DMA((SLABS,)), pltpu.SemaphoreType.DMA((SLABS,))],
+        cost_estimate=pl.CostEstimate(flops=6 * M * M * LEV * TX * TY, bytes_accessed=8 * M * LEV * TX * TY, transcendentals=0),
         name="final",
     )(q0, h, g, z, pltpu.with_memory_space_constraint(ensemble, pltpu.HBM))
     state, everyone = lax.optimization_barrier((state, everyone))

time: 78.3 us -> 78.1 us (level)
  no operation moved by 1% of the time
where the time goes in v8:
time: 78.1 us; the launch traced here: 77.9 us
  starting transfers between devices  34.5 us (44%)
  Pallas kernels  22.1 us (28%)
  waiting for transfers between devices  19.8 us (25%)
    ppermute x4, starting transfers between devices, local(): far = lax.ppermute(edge, 'gx', side_x)  11.4 us
    all_to_all x1, starting transfers between devices, local(): everyone = lax.all_to_all(spread, both, 0, 0, tiled=True)  11.3 us
    pallas_call x1, Pallas kernels, local(): call(final_kernel, out_shape=shape(M, LEV, TX, TY), in_specs=[VMEM] * 4 +...  8.68 us
    ppermute x4, waiting for transfers between devices, local(): h = lax.ppermute(send, both, side_y)  5.59 us
    pallas_call x4, Pallas kernels, local(): call(functools.partial(same_kernel, k), out_shape=(shape(2, M, M), shape(...  4.7 us
    ppermute x4, starting transfers between devices, local(): h = lax.ppermute(send, both, side_y)  4.54 us
    ppermute x4, starting transfers between devices, local(): g = lax.ppermute(h, 'gx', core)  4.05 us
    ppermute x4, waiting for transfers between devices, local(): sib_far = lax.ppermute(far, 'gx', core)  3.94 us
  transfers between devices with their start and end apart: 18, of which 16 were waited for; matrix products, arithmetic and copies ran while one was open for 1% of the time, Pallas kernels for 6%

profile of v8, /device:TPU:1, one launch (start us, length us, event | category | flops | bytes accessed | tf_op | source)
XLA Modules:
  0.0 77.9 jit_solution(4771708843253271601)
XLA Ops:
  0.6 0.0 copy-start
  0.6 0.0 copy-start.1
  0.7 3.3 %init.1.own = f32[96,256]{1,0:T(8,128)S(1)} custom-call(s32[4]{0:T(128)} %order.9, f32[4,2048]{1,0:T(4,128)} %value_hbm.1, f32[4,2048]{1,0:T(4,128)} %variance_hbm.1, s32[4,2048]{1,0:T(4,128)} %owner.9, s32[4,2048]{1,0:T(4,128)} %cell_hbm.1, s32[4,8,2048]{2,1,0:T(8,128)} %bitcast.7, f32[80,4,32,256]{3,2,1,0:T(8,128)} %x.1), custom_call_target="tpu_custom_call" | custom-call | tf_op jit(solution)/shard_map/init/pallas_call | solution.py:341
  3.9 1.5 %collective-permute-start = (f32[96,256]{1,0:T(8,128)S(1)}, f32[96,256]{1,0:T(8,128)S(1)}, u32[]{:S(2)}, u32[]{:S(2)}) collective-permute-start(f32[96,256]{1,0:T(8,128)S(1)} %init.1.own), channel_id=1, source_target_pairs={{0,16},{32,48},{64,80},{96,112},{16,0},{48,32},{80,64},{112,96},{1... | collective-permute-start | bytes 294920 | tf_op jit(solution)/shard_map/ppermute | solution.py:363
  5.4 0.9 %collective-permute-done.sib = f32[96,256]{1,0:T(8,128)S(1)} collective-permute-done((f32[96,256]{1,0:T(8,128)S(1)}, f32[96,256]{1,0:T(8,128)S(1)}, u32[]{:S(2)}, u32[]{:S(2)}) %collective-permute-start) | collective-permute-done | bytes 98336 | tf_op jit(solution)/shard_map/ppermute | solution.py:363
  6.4 0.2 start.1
  6.5 2.9 %collective-permute-start.1 = (f32[48,128]{1,0:T(8,128)S(1)}, f32[48,128]{1,0:T(8,128)S(1)}, u32[]{:S(2)}, u32[]{:S(2)}) collective-permute-start(f32[48,128]{1,0:T(8,128)S(1)} %get-tuple-element.34), channel_id=1, source_target_pairs={{0,32},{64,96},{48,80},{112,16},{32,0},{96,64},{80,48},{16,112},{1... | collective-permute-start | bytes 73736 | tf_op jit(solution)/shard_map/ppermute | solution.py:367
  9.4 1.2 %collective-permute-done.1.far = f32[48,128]{1,0:T(8,128)S(1)} collective-permute-done((f32[48,128]{1,0:T(8,128)S(1)}, f32[48,128]{1,0:T(8,128)S(1)}, u32[]{:S(2)}, u32[]{:S(2)}) %collective-permute-start.1) | collective-permute-done | bytes 24608 | tf_op jit(solution)/shard_map/ppermute | solution.py:367
  10.6 0.2 collective-permute-start.2
  10.8 1.0 %collective-permute-done.2.sib_far = f32[48,128]{1,0:T(8,128)S(1)} collective-permute-done((f32[48,128]{1,0:T(8,128)S(1)}, f32[48,128]{1,0:T(8,128)S(1)}, u32[]{:S(2)}, u32[]{:S(2)}) %collective-permute-start.2) | collective-permute-done | bytes 24608 | tf_op jit(solution)/shard_map/ppermute | solution.py:371
  11.8 0.4 send.4
  12.2 1.3 %collective-permute-start.3 = (f32[2,80,80]{2,1,0:T(8,128)S(1)}, f32[2,80,80]{2,1,0:T(8,128)S(1)}, u32[]{:S(2)}, u32[]{:S(2)}) collective-permute-start(f32[2,80,80]{2,1,0:T(8,128)S(1)} %send.4), channel_id=1, source_target_pairs={{0,1},{2,3},{4,5},{6,7},{8,9},{10,11},{12,13},{14,15},{17,18},{19,... | collective-permute-start | bytes 153608 | tf_op jit(solution)/shard_map/ppermute | solution.py:375
  13.5 0.0 copy-done
  13.5 0.0 copy-done.1
  13.5 1.2 %same.4 = (f32[2,80,80]{2,1,0:T(8,128)S(1)}, f32[1,2048]{1,0:T(1,128)S(1)}) custom-call(s32[4]{0:T(128)S(1)} %copy-done.1, s32[4,2048]{1,0:T(4,128)S(1)} %copy-done, f32[2,48,128]{2,1,0:T(8,128)S(1)} %get-tuple-element.33.pay, f32[48,128]{1,0:T(8,128)S(1)} %collective-permute-done.1.far, f32[48,128]{1,0:T(8,128)S(1)} %collective-permute-done.2.sib_far), custom_call_target="tpu_custom_call" | custom-call | tf_op jit(solution)/shard_map/same/pallas_call | solution.py:376
  14.7 1.2 %collective-permute-done.3.h = f32[2,80,80]{2,1,0:T(8,128)S(1)} collective-permute-done((f32[2,80,80]{2,1,0:T(8,128)S(1)}, f32[2,80,80]{2,1,0:T(8,128)S(1)}, u32[]{:S(2)}, u32[]{:S(2)}) %collective-permute-start.3) | collective-permute-done | bytes 51232 | tf_op jit(solution)/shard_map/ppermute | solution.py:375
  15.9 1.0 %collective-permute-start.4 = (f32[2,80,80]{2,1,0:T(8,128)S(1)}, f32[2,80,80]{2,1,0:T(8,128)S(1)}, u32[]{:S(2)}, u32[]{:S(2)}) collective-permute-start(f32[2,80,80]{2,1,0:T(8,128)S(1)} %collective-permute-done.3.h), channel_id=1, source_target_pairs={{0,16},{32,48},{64,80},{96,112},{16,0},{48,32},{80,64},{112,96},{1... | collective-permute-start | bytes 153608 | tf_op jit(solution)/shard_map/ppermute | solution.py:385
  16.9 0.9 %collective-permute-done.4.g = f32[2,80,80]{2,1,0:T(8,128)S(1)} collective-permute-done((f32[2,80,80]{2,1,0:T(8,128)S(1)}, f32[2,80,80]{2,1,0:T(8,128)S(1)}, u32[]{:S(2)}, u32[]{:S(2)}) %collective-permute-start.4) | collective-permute-done | bytes 51232 | tf_op jit(solution)/shard_map/ppermute | solution.py:385
  17.9 0.4 step.3
  18.3 2.9 %collective-permute-start.5 = (f32[48,128]{1,0:T(8,128)S(1)}, f32[48,128]{1,0:T(8,128)S(1)}, u32[]{:S(2)}, u32[]{:S(2)}) collective-permute-start(f32[48,128]{1,0:T(8,128)S(1)} %get-tuple-element.40), channel_id=1, source_target_pairs={{0,32},{64,96},{48,80},{112,16},{32,0},{96,64},{80,48},{16,112},{1... | collective-permute-start | bytes 73736 | tf_op jit(solution)/shard_map/ppermute | solution.py:367
  21.2 1.2 %collective-permute-done.5.far = f32[48,128]{1,0:T(8,128)S(1)} collective-permute-done((f32[48,128]{1,0:T(8,128)S(1)}, f32[48,128]{1,0:T(8,128)S(1)}, u32[]{:S(2)}, u32[]{:S(2)}) %collective-permute-start.5) | collective-permute-done | bytes 24608 | tf_op jit(solution)/shard_map/ppermute | solution.py:367
  22.4 0.2 collective-permute-start.6
  22.5 1.0 %collective-permute-done.6.sib_far = f32[48,128]{1,0:T(8,128)S(1)} collective-permute-done((f32[48,128]{1,0:T(8,128)S(1)}, f32[48,128]{1,0:T(8,128)S(1)}, u32[]{:S(2)}, u32[]{:S(2)}) %collective-permute-start.6) | collective-permute-done | bytes 24608 | tf_op jit(solution)/shard_map/ppermute | solution.py:371
  23.6 0.4 send.5
  24.0 1.3 %collective-permute-start.7 = (f32[2,80,80]{2,1,0:T(8,128)S(1)}, f32[2,80,80]{2,1,0:T(8,128)S(1)}, u32[]{:S(2)}, u32[]{:S(2)}) collective-permute-start(f32[2,80,80]{2,1,0:T(8,128)S(1)} %send.5), channel_id=1, source_target_pairs={{0,1},{2,3},{4,5},{6,7},{8,9},{10,11},{12,13},{14,15},{17,18},{19,... | collective-permute-start | bytes 153608 | tf_op jit(solution)/shard_map/ppermute | solution.py:375
  25.3 1.2 %same.5 = (f32[2,80,80]{2,1,0:T(8,128)S(1)}, f32[1,2048]{1,0:T(1,128)S(1)}) custom-call(s32[4]{0:T(128)S(1)} %copy-done.1, s32[4,2048]{1,0:T(4,128)S(1)} %copy-done, f32[2,48,128]{2,1,0:T(8,128)S(1)} %get-tuple-element.39.pay, f32[48,128]{1,0:T(8,128)S(1)} %collective-permute-done.5.far, f32[48,128]{1,0:T(8,128)S(1)} %collective-permute-done.6.sib_far), custom_call_target="tpu_custom_call" | custom-call | tf_op jit(solution)/shard_map/same/pallas_call | solution.py:376
  26.4 1.2 %collective-permute-done.7.h = f32[2,80,80]{2,1,0:T(8,128)S(1)} collective-permute-done((f32[2,80,80]{2,1,0:T(8,128)S(1)}, f32[2,80,80]{2,1,0:T(8,128)S(1)}, u32[]{:S(2)}, u32[]{:S(2)}) %collective-permute-start.7) | collective-permute-done | bytes 51232 | tf_op jit(solution)/shard_map/ppermute | solution.py:375
  27.7 1.0 %collective-permute-start.8 = (f32[2,80,80]{2,1,0:T(8,128)S(1)}, f32[2,80,80]{2,1,0:T(8,128)S(1)}, u32[]{:S(2)}, u32[]{:S(2)}) collective-permute-start(f32[2,80,80]{2,1,0:T(8,128)S(1)} %collective-permute-done.7.h), channel_id=1, source_target_pairs={{0,16},{32,48},{64,80},{96,112},{16,0},{48,32},{80,64},{112,96},{1... | collective-permute-start | bytes 153608 | tf_op jit(solution)/shard_map/ppermute | solution.py:385
  28.7 0.9 %collective-permute-done.8.g = f32[2,80,80]{2,1,0:T(8,128)S(1)} collective-permute-done((f32[2,80,80]{2,1,0:T(8,128)S(1)}, f32[2,80,80]{2,1,0:T(8,128)S(1)}, u32[]{:S(2)}, u32[]{:S(2)}) %collective-permute-start.8) | collective-permute-done | bytes 51232 | tf_op jit(solution)/shard_map/ppermute | solution.py:385
  29.6 0.5 step.4
  30.1 2.8 %collective-permute-start.9 = (f32[48,128]{1,0:T(8,128)S(1)}, f32[48,128]{1,0:T(8,128)S(1)}, u32[]{:S(2)}, u32[]{:S(2)}) collective-permute-start(f32[48,128]{1,0:T(8,128)S(1)} %get-tuple-element.46), channel_id=1, source_target_pairs={{0,32},{64,96},{48,80},{112,16},{32,0},{96,64},{80,48},{16,112},{1... | collective-permute-start | bytes 73736 | tf_op jit(solution)/shard_map/ppermute | solution.py:367
  32.9 1.2 %collective-permute-done.9.far = f32[48,128]{1,0:T(8,128)S(1)} collective-permute-done((f32[48,128]{1,0:T(8,128)S(1)}, f32[48,128]{1,0:T(8,128)S(1)}, u32[]{:S(2)}, u32[]{:S(2)}) %collective-permute-start.9) | collective-permute-done | bytes 24608 | tf_op jit(solution)/shard_map/ppermute | solution.py:367
  34.2 0.2 collective-permute-start.10
  34.3 1.0 %collective-permute-done.10.sib_far = f32[48,128]{1,0:T(8,128)S(1)} collective-permute-done((f32[48,128]{1,0:T(8,128)S(1)}, f32[48,128]{1,0:T(8,128)S(1)}, u32[]{:S(2)}, u32[]{:S(2)}) %collective-permute-start.10) | collective-permute-done | bytes 24608 | tf_op jit(solution)/shard_map/ppermute | solution.py:371
  35.3 0.4 send.6
  35.8 1.3 %collective-permute-start.11 = (f32[2,80,80]{2,1,0:T(8,128)S(1)}, f32[2,80,80]{2,1,0:T(8,128)S(1)}, u32[]{:S(2)}, u32[]{:S(2)}) collective-permute-start(f32[2,80,80]{2,1,0:T(8,128)S(1)} %send.6), channel_id=1, source_target_pairs={{0,1},{2,3},{4,5},{6,7},{8,9},{10,11},{12,13},{14,15},{17,18},{19,... | collective-permute-start | bytes 153608 | tf_op jit(solution)/shard_map/ppermute | solution.py:375
  37.0 1.2 %same.6 = (f32[2,80,80]{2,1,0:T(8,128)S(1)}, f32[1,2048]{1,0:T(1,128)S(1)}) custom-call(s32[4]{0:T(128)S(1)} %copy-done.1, s32[4,2048]{1,0:T(4,128)S(1)} %copy-done, f32[2,48,128]{2,1,0:T(8,128)S(1)} %get-tuple-element.45.pay, f32[48,128]{1,0:T(8,128)S(1)} %collective-permute-done.9.far, f32[48,128]{1,0:T(8,128)S(1)} %collective-permute-done.10.sib_far), custom_call_target="tpu_custom_call" | custom-call | tf_op jit(solution)/shard_map/same/pallas_call | solution.py:376
  38.2 1.2 %collective-permute-done.11.h = f32[2,80,80]{2,1,0:T(8,128)S(1)} collective-permute-done((f32[2,80,80]{2,1,0:T(8,128)S(1)}, f32[2,80,80]{2,1,0:T(8,128)S(1)}, u32[]{:S(2)}, u32[]{:S(2)}) %collective-permute-start.11) | collective-permute-done | bytes 51232 | tf_op jit(solution)/shard_map/ppermute | solution.py:375
  39.4 1.0 %collective-permute-start.12 = (f32[2,80,80]{2,1,0:T(8,128)S(1)}, f32[2,80,80]{2,1,0:T(8,128)S(1)}, u32[]{:S(2)}, u32[]{:S(2)}) collective-permute-start(f32[2,80,80]{2,1,0:T(8,128)S(1)} %collective-permute-done.11.h), channel_id=1, source_target_pairs={{0,16},{32,48},{64,80},{96,112},{16,0},{48,32},{80,64},{112,96},{1... | collective-permute-start | bytes 153608 | tf_op jit(solution)/shard_map/ppermute | solution.py:385
  40.5 0.9 %collective-permute-done.12.g = f32[2,80,80]{2,1,0:T(8,128)S(1)} collective-permute-done((f32[2,80,80]{2,1,0:T(8,128)S(1)}, f32[2,80,80]{2,1,0:T(8,128)S(1)}, u32[]{:S(2)}, u32[]{:S(2)}) %collective-permute-start.12) | collective-permute-done | bytes 51232 | tf_op jit(solution)/shard_map/ppermute | solution.py:385
  41.4 0.4 step.5
  41.8 2.9 %collective-permute-start.13 = (f32[48,128]{1,0:T(8,128)S(1)}, f32[48,128]{1,0:T(8,128)S(1)}, u32[]{:S(2)}, u32[]{:S(2)}) collective-permute-start(f32[48,128]{1,0:T(8,128)S(1)} %get-tuple-element.52), channel_id=1, source_target_pairs={{0,32},{64,96},{48,80},{112,16},{32,0},{96,64},{80,48},{16,112},{1... | collective-permute-start | bytes 73736 | tf_op jit(solution)/shard_map/ppermute | solution.py:367
  44.7 0.7 broadcast_in_dim.2
  45.4 11.3 %all-to-all-start = ((f32[128,1,256]{2,1,0:T(1,128)}), f32[128,1,256]{2,1,0:T(1,128)S(1)}, u32[]{:S(2)}, u32[]{:S(2)}) async-start(f32[128,1,256]{2,1,0:T(1,128)} %broadcast_in_dim.2), calls=%async_computation | async-start | bytes 262144 | tf_op jit(solution)/shard_map/all_to_all | solution.py:370
  56.8 0.0 collective-permute-done.13.far
  56.8 1.1 %collective-permute-start.14 = (f32[48,128]{1,0:T(8,128)S(1)}, f32[48,128]{1,0:T(8,128)S(1)}, u32[]{:S(2)}, u32[]{:S(2)}) collective-permute-start(f32[48,128]{1,0:T(8,128)S(1)} %collective-permute-done.13.far), channel_id=1, source_target_pairs={{0,16},{32,48},{64,80},{96,112},{16,0},{48,32},{80,64},{112,96},{1... | collective-permute-start | bytes 73736 | tf_op jit(solution)/shard_map/ppermute | solution.py:371
  57.9 0.8 %collective-permute-done.14.sib_far = f32[48,128]{1,0:T(8,128)S(1)} collective-permute-done((f32[48,128]{1,0:T(8,128)S(1)}, f32[48,128]{1,0:T(8,128)S(1)}, u32[]{:S(2)}, u32[]{:S(2)}) %collective-permute-start.14) | collective-permute-done | bytes 24608 | tf_op jit(solution)/shard_map/ppermute | solution.py:371
  58.8 0.4 send.7
  59.2 0.8 collective-permute-start.15
  60.0 1.2 %same.7 = (f32[2,80,80]{2,1,0:T(8,128)S(1)}, f32[1,2048]{1,0:T(1,128)S(1)}) custom-call(s32[4]{0:T(128)S(1)} %copy-done.1, s32[4,2048]{1,0:T(4,128)S(1)} %copy-done, f32[2,48,128]{2,1,0:T(8,128)S(1)} %get-tuple-element.51.pay, f32[48,128]{1,0:T(8,128)S(1)} %collective-permute-done.13.far, f32[48,128]{1,0:T(8,128)S(1)} %collective-permute-done.14.sib_far), custom_call_target="tpu_custom_call" | custom-call | tf_op jit(solution)/shard_map/same/pallas_call | solution.py:376
  61.1 1.9 %collective-permute-done.15.h = f32[2,80,80]{2,1,0:T(8,128)S(1)} collective-permute-done((f32[2,80,80]{2,1,0:T(8,128)S(1)}, f32[2,80,80]{2,1,0:T(8,128)S(1)}, u32[]{:S(2)}, u32[]{:S(2)}) %collective-permute-start.15) | collective-permute-done | bytes 51232 | tf_op jit(solution)/shard_map/ppermute | solution.py:375
  63.1 1.0 %collective-permute-start.16 = (f32[2,80,80]{2,1,0:T(8,128)S(1)}, f32[2,80,80]{2,1,0:T(8,128)S(1)}, u32[]{:S(2)}, u32[]{:S(2)}) collective-permute-start(f32[2,80,80]{2,1,0:T(8,128)S(1)} %collective-permute-done.15.h), channel_id=1, source_target_pairs={{0,16},{32,48},{64,80},{96,112},{16,0},{48,32},{80,64},{112,96},{1... | collective-permute-start | bytes 153608 | tf_op jit(solution)/shard_map/ppermute | solution.py:385
  64.1 2.9 %all-to-all-done = f32[128,1,256]{2,1,0:T(1,128)S(1)} async-done(((f32[128,1,256]{2,1,0:T(1,128)}), f32[128,1,256]{2,1,0:T(1,128)S(1)}, u32[]{:S(2)}, u32[]{:S(2)}) %all-to-all-start) | async-done | bytes 131104 | tf_op jit(solution)/shard_map/all_to_all | solution.py:370
  67.0 0.0 collective-permute-done.16.g
  67.0 8.7 %final.1 = f32[80,4,32,256]{3,2,1,0:T(8,128)} custom-call(f32[2,80,80]{2,1,0:T(8,128)S(1)} %get-tuple-element.54.q0, f32[2,80,80]{2,1,0:T(8,128)S(1)} %collective-permute-done.15.h, f32[2,80,80]{2,1,0:T(8,128)S(1)} %collective-permute-done.16.g, f32[2,96,384]{2,1,0:T(8,128)S(1)} %get-tuple-element.56.z, f32[80,4,32,256]{3,2,1,0:T(8,128)} %x.1), custom_call_target="tpu_custom_call" | custom-call | flops 1258291200 | bytes 20971520 | tf_op jit(solution)/shard_map/final/pallas_call | solution.py:398
  75.7 2.2 %place.1 = f32[4,2048]{1,0:T(4,128)} custom-call(s32[4]{0:T(128)S(1)} %copy-done.1, s32[4,2048]{1,0:T(4,128)S(1)} %copy-done, f32[128,256]{1,0:T(8,128)S(1)} %bitcast.5, f32[1,2048]{1,0:T(1,128)S(1)} %get-tuple-element.60.r0, f32[1,2048]{1,0:T(1,128)S(1)} %get-tuple-element.61.r1, f32[1,2048]{1,0:T(1,128)S(1)} %get-tuple-element.62.r2, ...), custom_call_target="tpu_custom_call" | custom-call | tf_op jit(solution)/shard_map/place/pallas_call | solution.py:408
  (1 shorter events, 0.0 us)
Async XLA Ops:
  0.6 12.9 %copy-start = (s32[4,2048]{1,0:T(4,128)S(1)}, s32[4,2048]{1,0:T(4,128)}, u32[]{:S(2)}) copy-start(s32[4,2048]{1,0:T(4,128)} %owner.9) | copy-start | bytes 98308
  0.6 12.9 %copy-start.1 = (s32[4]{0:T(128)S(1)}, s32[4]{0:T(128)}, u32[]{:S(2)}) copy-start(s32[4]{0:T(128)} %order.9) | copy-start | bytes 52
  3.9 2.5 %collective-permute-start = (f32[96,256]{1,0:T(8,128)S(1)}, f32[96,256]{1,0:T(8,128)S(1)}, u32[]{:S(2)}, u32[]{:S(2)}) collective-permute-start(f32[96,256]{1,0:T(8,128)S(1)} %init.1.own), channel_id=1, source_target_pairs={{0,16},{32,48},{64,80},{96,112},{16,0},{48,32},{80,64},{112,96},{1... | collective-permute-start | bytes 294920 | tf_op jit(solution)/shard_map/ppermute | solution.py:363
  6.5 4.1 %collective-permute-start.1 = (f32[48,128]{1,0:T(8,128)S(1)}, f32[48,128]{1,0:T(8,128)S(1)}, u32[]{:S(2)}, u32[]{:S(2)}) collective-permute-start(f32[48,128]{1,0:T(8,128)S(1)} %get-tuple-element.34), channel_id=1, source_target_pairs={{0,32},{64,96},{48,80},{112,16},{32,0},{96,64},{80,48},{16,112},{1... | collective-permute-start | bytes 73736 | tf_op jit(solution)/shard_map/ppermute | solution.py:367
  10.6 1.2 %collective-permute-start.2 = (f32[48,128]{1,0:T(8,128)S(1)}, f32[48,128]{1,0:T(8,128)S(1)}, u32[]{:S(2)}, u32[]{:S(2)}) collective-permute-start(f32[48,128]{1,0:T(8,128)S(1)} %collective-permute-done.1.far), channel_id=1, source_target_pairs={{0,16},{32,48},{64,80},{96,112},{16,0},{48,32},{80,64},{112,96},{1... | collective-permute-start | bytes 73736 | tf_op jit(solution)/shard_map/ppermute | solution.py:371
  12.2 3.7 %collective-permute-start.3 = (f32[2,80,80]{2,1,0:T(8,128)S(1)}, f32[2,80,80]{2,1,0:T(8,128)S(1)}, u32[]{:S(2)}, u32[]{:S(2)}) collective-permute-start(f32[2,80,80]{2,1,0:T(8,128)S(1)} %send.4), channel_id=1, source_target_pairs={{0,1},{2,3},{4,5},{6,7},{8,9},{10,11},{12,13},{14,15},{17,18},{19,... | collective-permute-start | bytes 153608 | tf_op jit(solution)/shard_map/ppermute | solution.py:375
  15.9 1.9 %collective-permute-start.4 = (f32[2,80,80]{2,1,0:T(8,128)S(1)}, f32[2,80,80]{2,1,0:T(8,128)S(1)}, u32[]{:S(2)}, u32[]{:S(2)}) collective-permute-start(f32[2,80,80]{2,1,0:T(8,128)S(1)} %collective-permute-done.3.h), channel_id=1, source_target_pairs={{0,16},{32,48},{64,80},{96,112},{16,0},{48,32},{80,64},{112,96},{1... | collective-permute-start | bytes 153608 | tf_op jit(solution)/shard_map/ppermute | solution.py:385
  18.3 4.1 %collective-permute-start.5 = (f32[48,128]{1,0:T(8,128)S(1)}, f32[48,128]{1,0:T(8,128)S(1)}, u32[]{:S(2)}, u32[]{:S(2)}) collective-permute-start(f32[48,128]{1,0:T(8,128)S(1)} %get-tuple-element.40), channel_id=1, source_target_pairs={{0,32},{64,96},{48,80},{112,16},{32,0},{96,64},{80,48},{16,112},{1... | collective-permute-start | bytes 73736 | tf_op jit(solution)/shard_map/ppermute | solution.py:367
  22.4 1.2 %collective-permute-start.6 = (f32[48,128]{1,0:T(8,128)S(1)}, f32[48,128]{1,0:T(8,128)S(1)}, u32[]{:S(2)}, u32[]{:S(2)}) collective-permute-start(f32[48,128]{1,0:T(8,128)S(1)} %collective-permute-done.5.far), channel_id=1, source_target_pairs={{0,16},{32,48},{64,80},{96,112},{16,0},{48,32},{80,64},{112,96},{1... | collective-permute-start | bytes 73736 | tf_op jit(solution)/shard_map/ppermute | solution.py:371
  24.0 3.7 %collective-permute-start.7 = (f32[2,80,80]{2,1,0:T(8,128)S(1)}, f32[2,80,80]{2,1,0:T(8,128)S(1)}, u32[]{:S(2)}, u32[]{:S(2)}) collective-permute-start(f32[2,80,80]{2,1,0:T(8,128)S(1)} %send.5), channel_id=1, source_target_pairs={{0,1},{2,3},{4,5},{6,7},{8,9},{10,11},{12,13},{14,15},{17,18},{19,... | collective-permute-start | bytes 153608 | tf_op jit(solution)/shard_map/ppermute | solution.py:375
  27.7 1.9 %collective-permute-start.8 = (f32[2,80,80]{2,1,0:T(8,128)S(1)}, f32[2,80,80]{2,1,0:T(8,128)S(1)}, u32[]{:S(2)}, u32[]{:S(2)}) collective-permute-start(f32[2,80,80]{2,1,0:T(8,128)S(1)} %collective-permute-done.7.h), channel_id=1, source_target_pairs={{0,16},{32,48},{64,80},{96,112},{16,0},{48,32},{80,64},{112,96},{1... | collective-permute-start | bytes 153608 | tf_op jit(solution)/shard_map/ppermute | solution.py:385
  30.1 4.1 %collective-permute-start.9 = (f32[48,128]{1,0:T(8,128)S(1)}, f32[48,128]{1,0:T(8,128)S(1)}, u32[]{:S(2)}, u32[]{:S(2)}) collective-permute-start(f32[48,128]{1,0:T(8,128)S(1)} %get-tuple-element.46), channel_id=1, source_target_pairs={{0,32},{64,96},{48,80},{112,16},{32,0},{96,64},{80,48},{16,112},{1... | collective-permute-start | bytes 73736 | tf_op jit(solution)/shard_map/ppermute | solution.py:367
  34.2 1.2 %collective-permute-start.10 = (f32[48,128]{1,0:T(8,128)S(1)}, f32[48,128]{1,0:T(8,128)S(1)}, u32[]{:S(2)}, u32[]{:S(2)}) collective-permute-start(f32[48,128]{1,0:T(8,128)S(1)} %collective-permute-done.9.far), channel_id=1, source_target_pairs={{0,16},{32,48},{64,80},{96,112},{16,0},{48,32},{80,64},{112,96},{1... | collective-permute-start | bytes 73736 | tf_op jit(solution)/shard_map/ppermute | solution.py:371
  35.8 3.7 %collective-permute-start.11 = (f32[2,80,80]{2,1,0:T(8,128)S(1)}, f32[2,80,80]{2,1,0:T(8,128)S(1)}, u32[]{:S(2)}, u32[]{:S(2)}) collective-permute-start(f32[2,80,80]{2,1,0:T(8,128)S(1)} %send.6), channel_id=1, source_target_pairs={{0,1},{2,3},{4,5},{6,7},{8,9},{10,11},{12,13},{14,15},{17,18},{19,... | collective-permute-start | bytes 153608 | tf_op jit(solution)/shard_map/ppermute | solution.py:375
  39.4 1.9 %collective-permute-start.12 = (f32[2,80,80]{2,1,0:T(8,128)S(1)}, f32[2,80,80]{2,1,0:T(8,128)S(1)}, u32[]{:S(2)}, u32[]{:S(2)}) collective-permute-start(f32[2,80,80]{2,1,0:T(8,128)S(1)} %collective-permute-done.11.h), channel_id=1, source_target_pairs={{0,16},{32,48},{64,80},{96,112},{16,0},{48,32},{80,64},{112,96},{1... | collective-permute-start | bytes 153608 | tf_op jit(solution)/shard_map/ppermute | solution.py:385
  41.8 14.9 %collective-permute-start.13 = (f32[48,128]{1,0:T(8,128)S(1)}, f32[48,128]{1,0:T(8,128)S(1)}, u32[]{:S(2)}, u32[]{:S(2)}) collective-permute-start(f32[48,128]{1,0:T(8,128)S(1)} %get-tuple-element.52), channel_id=1, source_target_pairs={{0,32},{64,96},{48,80},{112,16},{32,0},{96,64},{80,48},{16,112},{1... | collective-permute-start | bytes 73736 | tf_op jit(solution)/shard_map/ppermute | solution.py:367
  45.4 21.5 %all-to-all-start = ((f32[128,1,256]{2,1,0:T(1,128)}), f32[128,1,256]{2,1,0:T(1,128)S(1)}, u32[]{:S(2)}, u32[]{:S(2)}) async-start(f32[128,1,256]{2,1,0:T(1,128)} %broadcast_in_dim.2), calls=%async_computation | async-start | bytes 262144 | tf_op jit(solution)/shard_map/all_to_all | solution.py:370
  56.8 2.0 %collective-permute-start.14 = (f32[48,128]{1,0:T(8,128)S(1)}, f32[48,128]{1,0:T(8,128)S(1)}, u32[]{:S(2)}, u32[]{:S(2)}) collective-permute-start(f32[48,128]{1,0:T(8,128)S(1)} %collective-permute-done.13.far), channel_id=1, source_target_pairs={{0,16},{32,48},{64,80},{96,112},{16,0},{48,32},{80,64},{112,96},{1... | collective-permute-start | bytes 73736 | tf_op jit(solution)/shard_map/ppermute | solution.py:371
  59.2 3.9 %collective-permute-start.15 = (f32[2,80,80]{2,1,0:T(8,128)S(1)}, f32[2,80,80]{2,1,0:T(8,128)S(1)}, u32[]{:S(2)}, u32[]{:S(2)}) collective-permute-start(f32[2,80,80]{2,1,0:T(8,128)S(1)} %send.7), channel_id=1, source_target_pairs={{0,1},{2,3},{4,5},{6,7},{8,9},{10,11},{12,13},{14,15},{17,18},{19,... | collective-permute-start | bytes 153608 | tf_op jit(solution)/shard_map/ppermute | solution.py:375
  63.1 3.9 %collective-permute-start.16 = (f32[2,80,80]{2,1,0:T(8,128)S(1)}, f32[2,80,80]{2,1,0:T(8,128)S(1)}, u32[]{:S(2)}, u32[]{:S(2)}) collective-permute-start(f32[2,80,80]{2,1,0:T(8,128)S(1)} %collective-permute-done.15.h), channel_id=1, source_target_pairs={{0,16},{32,48},{64,80},{96,112},{16,0},{48,32},{80,64},{112,96},{1... | collective-permute-start | bytes 153608 | tf_op jit(solution)/shard_map/ppermute | solution.py:385

commit v9 on v6

--- a/solution.py
+++ b/solution.py
@@ -254,15 +254,14 @@
         base = base + jnp.sum(hot, axis=1, keepdims=True)
 
 
-def same_last_kernel(k, order, owner, pay, far, sib_far, news, across, out, rank_out, column):
+def column_kernel(news, far, sib_far, across, out):
     first = core_of() == 0
     at = slice(ROWS // 2, ROWS // 2 + NB)
     mine, other = far[at], sib_far[at]
-    column[0:NB] = news[:NB]
-    column[NB : 2 * NB] = jnp.where(first, mine, other)
-    column[2 * NB : 3 * NB] = across[:NB]
-    column[3 * NB :] = jnp.where(first, other, mine)
-    same_kernel(k, order, owner, pay, far, sib_far, out, rank_out)
+    column = jnp.concatenate(
+        [news[:NB], jnp.where(first, mine, other), across[:NB], jnp.where(first, other, mine)], axis=0
+    )
+    out[...] = jnp.broadcast_to(column[None], out.shape)
 
 
 def advance(z, gain):
@@ -312,18 +311,17 @@
         store.wait()
 
 
-def place_kernel(order, owner, n0, n1, n2, n3, r0, r1, r2, r3, out):
-    me = lax.axis_index("gx") * lax.axis_size("gy") + lax.axis_index("gy")
+def place_kernel(order, owner, gathered, r0, r1, r2, r3, out):
+    y = lax.axis_index("gx") // 2
     chips = iota((TILES // 2, OBS), 0)
     seats = iota((2 * CAP, OBS), 0)
+    rows = gathered.reshape(TILES // 2 * NB, 2 * CAP)
     for k, rank in enumerate((r0, r1, r2, r3)):
         b = order[k]
         tile = owner[pl.ds(b, 1), :]
-        away = tile ^ me
-        block = ((away >> 2) & 3) * 16 + (away & 3) * 4 + ((away >> 5) & 3)
-        hot = jnp.where(block == chips, 1.0, 0.0).astype(BF16)
-        rows = jnp.concatenate([n[pl.ds(k, 16, stride=NB), :] for n in (n0, n1, n2, n3)], axis=0)
-        high, low = split2(rows.T)
+        chip = (tile & 15) * 4 + ((tile >> 5) ^ y)
+        hot = jnp.where(chip == chips, 1.0, 0.0).astype(BF16)
+        high, low = split2(rows[pl.ds(k, TILES // 2, stride=NB), :].T)
         got = dot(jnp.concatenate([high, low], axis=1), jnp.concatenate([hot, hot], axis=0))
         seat = ((tile >> 4) & 1) * CAP + rank[...].astype(jnp.int32)
         out[pl.ds(b, 1), :] = jnp.sum(jnp.where(seat == seats, got, 0.0), axis=0, keepdims=True)
@@ -381,35 +379,32 @@
         name="start",
     )(own, lax.ppermute(own, "gx", core))
     ranks = []
-    xor = lambda value, bits: lax.ppermute(value, both, [(q, q ^ bits) for q in range(width * height)])
     for k in range(NB):
         last = k + 1 == NB
         far = lax.ppermute(edge, "gx", side_x)
-        if last:
-            across = xor(news, 2 * 32)
         sib_far = lax.ppermute(far, "gx", core)
         send = call(send_kernel, out_shape=shape(2, M, M), in_specs=[VMEM] * 3, out_specs=VMEM, name="send")(
             pay, far, sib_far
         )
         send, sib_far = lax.optimization_barrier((send, sib_far))
         h = lax.ppermute(send, both, side_y)
-        extra = ((news, across), (shape(4 * NB, 128),)) if last else ((), ())
-        q0, rank, *rest = call(
-            functools.partial(same_last_kernel if last else same_kernel, k),
-            out_shape=(shape(2, M, M), shape(1, OBS)) + extra[1],
-            in_specs=[SMEM] + [VMEM] * (4 + len(extra[0])),
-            out_specs=(VMEM,) * (2 + len(extra[1])),
+        q0, rank = call(
+            functools.partial(same_kernel, k),
+            out_shape=(shape(2, M, M), shape(1, OBS)),
+            in_specs=[SMEM] + [VMEM] * 4,
+            out_specs=(VMEM, VMEM),
             name="same",
-        )(batch_order, obs_owner, pay, far, sib_far, *extra[0])
+        )(batch_order, obs_owner, pay, far, sib_far)
+        ranks.append(rank)
         if last:
-            column = rest[0]
-            plane = jnp.concatenate([column] + [xor(column, j) for j in range(1, 4)], axis=0)
-        ranks.append(rank)
+            across = lax.ppermute(sib_far[ROWS // 2 :], "gx", side_x)
+            column = call(
+                column_kernel, out_shape=shape(height, 4 * NB, 128), in_specs=[VMEM] * 4, out_specs=VMEM, name="column"
+            )(news, far, sib_far, across)
+            gathered = lax.all_to_all(column, "gy", 0, 0, tiled=True)
         h, q0 = lax.optimization_barrier((h, q0))
         g = lax.ppermute(h, "gx", core)
-        if last:
-            planes = [plane] + [xor(plane, 4 * j) for j in range(1, 4)]
-        else:
+        if not last:
             tail = k + 2 == NB
             edge_shape = (shape(ROWS // 2 + 8, 128), shape(8, 128)) if tail else pay_shapes[1:]
             z, pay, edge, *rest = call(
@@ -431,14 +426,14 @@
         cost_estimate=pl.CostEstimate(flops=6 * M * M * LEV * TX * TY, bytes_accessed=8 * M * LEV * TX * TY, transcendentals=0),
         name="final",
     )(q0, h, g, z, pltpu.with_memory_space_constraint(ensemble, pltpu.HBM))
-    state, planes = lax.optimization_barrier((state, planes))
+    state, gathered = lax.optimization_barrier((state, gathered))
     innovation = call(
         place_kernel,
         out_shape=shape(NB, OBS),
-        in_specs=[SMEM] + [VMEM] * 9,
+        in_specs=[SMEM] + [VMEM] * 6,
         out_specs=VMEM,
         name="place",
-    )(batch_order, obs_owner, *planes, *ranks)
+    )(batch_order, obs_owner, gathered, *ranks)
     return state, innovation
 
 

time: 81.4 us -> 79.1 us (0.972)
  starting transfers between devices: 39.4 us -> 36.4 us
    ppermute x7 -> x1, starting transfers between devices: 15.1 us -> 2.8 us  [local(): across = lax.ppermute(sib_far[ROWS // 2:], 'gx', side_x)]
    all_to_all x0 -> x1, starting transfers between devices: none -> 10.9 us  [local(): gathered = lax.all_to_all(column, 'gy', 0, 0, tiled=True)]
    ppermute x4, starting transfers between devices: 6.19 us -> 4.07 us  [local(): g = lax.ppermute(h, 'gx', core)]
    ppermute x4, waiting for transfers between devices: 5.98 us -> 4.89 us  [local(): h = lax.ppermute(send, both, side_y)]
    ppermute x4, waiting for transfers between devices: 3.1 us -> 4.13 us  [local(): sib_far = lax.ppermute(far, 'gx', core)]
    pallas_call x5 -> x6, Pallas kernels: 7.2 us -> 7.88 us  [the longest x4 4.7 us: local(): call(functools.partial(same_kernel, k), out_shape=(shape(2, M, M), shape(...]
  transfers between devices with their start and end apart: 24 -> 19, of which waited for: 17 -> 17; matrix products, arithmetic and copies ran while one was open for 0% -> 0% of each run, Pallas kernels for 15% -> 18%
where the time goes in v9:
time: 79.1 us; the launch traced here: 78.9 us
  starting transfers between devices  36.4 us (46%)
  Pallas kernels  23 us (29%)
  waiting for transfers between devices  18.6 us (24%)
    ppermute x4, starting transfers between devices, local(): far = lax.ppermute(edge, 'gx', side_x)  11.4 us
    all_to_all x1, starting transfers between devices, local(): gathered = lax.all_to_all(column, 'gy', 0, 0, tiled=True)  10.9 us
    pallas_call x1, Pallas kernels, local(): call(final_kernel, out_shape=shape(M, LEV, TX, TY), in_specs=[VMEM] * 4 +...  8.68 us
    ppermute x4, starting transfers between devices, local(): h = lax.ppermute(send, both, side_y)  5.04 us
    ppermute x4, waiting for transfers between devices, local(): far = lax.ppermute(edge, 'gx', side_x)  4.91 us
    ppermute x4, waiting for transfers between devices, local(): h = lax.ppermute(send, both, side_y)  4.89 us
    pallas_call x4, Pallas kernels, local(): call(functools.partial(same_kernel, k), out_shape=(shape(2, M, M), shape(...  4.7 us
    ppermute x4, waiting for transfers between devices, local(): sib_far = lax.ppermute(far, 'gx', core)  4.13 us
  transfers between devices with their start and end apart: 19, of which 17 were waited for; matrix products, arithmetic and copies ran while one was open for 0% of the time, Pallas kernels for 18%

profile of v9, /device:TPU:1, one launch (start us, length us, event | category | flops | bytes accessed | tf_op | source)
XLA Modules:
  0.0 78.9 jit_solution(2816791308197708756)
XLA Ops:
  0.6 0.0 copy-start
  0.6 0.0 copy-start.1
  0.7 3.3 %init.1.own = f32[96,256]{1,0:T(8,128)S(1)} custom-call(s32[4]{0:T(128)} %order.9, f32[4,2048]{1,0:T(4,128)} %value_hbm.1, f32[4,2048]{1,0:T(4,128)} %variance_hbm.1, s32[4,2048]{1,0:T(4,128)} %owner.9, s32[4,2048]{1,0:T(4,128)} %cell_hbm.1, s32[4,8,2048]{2,1,0:T(8,128)} %bitcast.1, f32[80,4,32,256]{3,2,1,0:T(8,128)} %x.1), custom_call_target="tpu_custom_call" | custom-call | tf_op jit(solution)/shard_map/init/pallas_call | solution.py:358
  3.9 1.5 %collective-permute-start = (f32[96,256]{1,0:T(8,128)S(1)}, f32[96,256]{1,0:T(8,128)S(1)}, u32[]{:S(2)}, u32[]{:S(2)}) collective-permute-start(f32[96,256]{1,0:T(8,128)S(1)} %init.1.own), channel_id=1, source_target_pairs={{0,16},{32,48},{64,80},{96,112},{16,0},{48,32},{80,64},{112,96},{1... | collective-permute-start | bytes 294920 | tf_op jit(solution)/shard_map/ppermute | solution.py:380
  5.4 0.9 %collective-permute-done.sib = f32[96,256]{1,0:T(8,128)S(1)} collective-permute-done((f32[96,256]{1,0:T(8,128)S(1)}, f32[96,256]{1,0:T(8,128)S(1)}, u32[]{:S(2)}, u32[]{:S(2)}) %collective-permute-start) | collective-permute-done | bytes 98336 | tf_op jit(solution)/shard_map/ppermute | solution.py:380
  6.4 0.2 start.1
  6.5 2.9 %collective-permute-start.1 = (f32[48,128]{1,0:T(8,128)S(1)}, f32[48,128]{1,0:T(8,128)S(1)}, u32[]{:S(2)}, u32[]{:S(2)}) collective-permute-start(f32[48,128]{1,0:T(8,128)S(1)} %get-tuple-element.42), channel_id=1, source_target_pairs={{0,32},{64,96},{48,80},{112,16},{32,0},{96,64},{80,48},{16,112},{1... | collective-permute-start | bytes 73736 | tf_op jit(solution)/shard_map/ppermute | solution.py:384
  9.4 1.2 %collective-permute-done.1.far = f32[48,128]{1,0:T(8,128)S(1)} collective-permute-done((f32[48,128]{1,0:T(8,128)S(1)}, f32[48,128]{1,0:T(8,128)S(1)}, u32[]{:S(2)}, u32[]{:S(2)}) %collective-permute-start.1) | collective-permute-done | bytes 24608 | tf_op jit(solution)/shard_map/ppermute | solution.py:384
  10.6 0.2 collective-permute-start.2
  10.8 1.0 %collective-permute-done.2.sib_far = f32[48,128]{1,0:T(8,128)S(1)} collective-permute-done((f32[48,128]{1,0:T(8,128)S(1)}, f32[48,128]{1,0:T(8,128)S(1)}, u32[]{:S(2)}, u32[]{:S(2)}) %collective-permute-start.2) | collective-permute-done | bytes 24608 | tf_op jit(solution)/shard_map/ppermute | solution.py:385
  11.8 0.4 send.4
  12.2 1.3 %collective-permute-start.3 = (f32[2,80,80]{2,1,0:T(8,128)S(1)}, f32[2,80,80]{2,1,0:T(8,128)S(1)}, u32[]{:S(2)}, u32[]{:S(2)}) collective-permute-start(f32[2,80,80]{2,1,0:T(8,128)S(1)} %send.4), channel_id=1, source_target_pairs={{0,1},{2,3},{4,5},{6,7},{8,9},{10,11},{12,13},{14,15},{17,18},{19,... | collective-permute-start | bytes 153608 | tf_op jit(solution)/shard_map/ppermute | solution.py:390
  13.5 0.0 copy-done
  13.5 0.0 copy-done.1
  13.5 1.2 %same.4 = (f32[2,80,80]{2,1,0:T(8,128)S(1)}, f32[1,2048]{1,0:T(1,128)S(1)}) custom-call(s32[4]{0:T(128)S(1)} %copy-done.1, s32[4,2048]{1,0:T(4,128)S(1)} %copy-done, f32[2,48,128]{2,1,0:T(8,128)S(1)} %get-tuple-element.41.pay, f32[48,128]{1,0:T(8,128)S(1)} %collective-permute-done.1.far, f32[48,128]{1,0:T(8,128)S(1)} %collective-permute-done.2.sib_far), custom_call_target="tpu_custom_call" | custom-call | tf_op jit(solution)/shard_map/same/pallas_call | solution.py:391
  14.7 1.2 %collective-permute-done.3.h = f32[2,80,80]{2,1,0:T(8,128)S(1)} collective-permute-done((f32[2,80,80]{2,1,0:T(8,128)S(1)}, f32[2,80,80]{2,1,0:T(8,128)S(1)}, u32[]{:S(2)}, u32[]{:S(2)}) %collective-permute-start.3) | collective-permute-done | bytes 51232 | tf_op jit(solution)/shard_map/ppermute | solution.py:390
  15.9 1.0 %collective-permute-start.4 = (f32[2,80,80]{2,1,0:T(8,128)S(1)}, f32[2,80,80]{2,1,0:T(8,128)S(1)}, u32[]{:S(2)}, u32[]{:S(2)}) collective-permute-start(f32[2,80,80]{2,1,0:T(8,128)S(1)} %collective-permute-done.3.h), channel_id=1, source_target_pairs={{0,16},{32,48},{64,80},{96,112},{16,0},{48,32},{80,64},{112,96},{1... | collective-permute-start | bytes 153608 | tf_op jit(solution)/shard_map/ppermute | solution.py:406
  16.9 0.9 %collective-permute-done.4.g = f32[2,80,80]{2,1,0:T(8,128)S(1)} collective-permute-done((f32[2,80,80]{2,1,0:T(8,128)S(1)}, f32[2,80,80]{2,1,0:T(8,128)S(1)}, u32[]{:S(2)}, u32[]{:S(2)}) %collective-permute-start.4) | collective-permute-done | bytes 51232 | tf_op jit(solution)/shard_map/ppermute | solution.py:406
  17.9 0.4 step.3
  18.3 2.9 %collective-permute-start.5 = (f32[48,128]{1,0:T(8,128)S(1)}, f32[48,128]{1,0:T(8,128)S(1)}, u32[]{:S(2)}, u32[]{:S(2)}) collective-permute-start(f32[48,128]{1,0:T(8,128)S(1)} %get-tuple-element.50), channel_id=1, source_target_pairs={{0,32},{64,96},{48,80},{112,16},{32,0},{96,64},{80,48},{16,112},{1... | collective-permute-start | bytes 73736 | tf_op jit(solution)/shard_map/ppermute | solution.py:384
  21.2 1.2 %collective-permute-done.5.far = f32[48,128]{1,0:T(8,128)S(1)} collective-permute-done((f32[48,128]{1,0:T(8,128)S(1)}, f32[48,128]{1,0:T(8,128)S(1)}, u32[]{:S(2)}, u32[]{:S(2)}) %collective-permute-start.5) | collective-permute-done | bytes 24608 | tf_op jit(solution)/shard_map/ppermute | solution.py:384
  22.4 0.2 collective-permute-start.6
  22.5 1.0 %collective-permute-done.6.sib_far = f32[48,128]{1,0:T(8,128)S(1)} collective-permute-done((f32[48,128]{1,0:T(8,128)S(1)}, f32[48,128]{1,0:T(8,128)S(1)}, u32[]{:S(2)}, u32[]{:S(2)}) %collective-permute-start.6) | collective-permute-done | bytes 24608 | tf_op jit(solution)/shard_map/ppermute | solution.py:385
  23.6 0.4 send.5
  24.0 1.3 %collective-permute-start.7 = (f32[2,80,80]{2,1,0:T(8,128)S(1)}, f32[2,80,80]{2,1,0:T(8,128)S(1)}, u32[]{:S(2)}, u32[]{:S(2)}) collective-permute-start(f32[2,80,80]{2,1,0:T(8,128)S(1)} %send.5), channel_id=1, source_target_pairs={{0,1},{2,3},{4,5},{6,7},{8,9},{10,11},{12,13},{14,15},{17,18},{19,... | collective-permute-start | bytes 153608 | tf_op jit(solution)/shard_map/ppermute | solution.py:390
  25.3 1.2 %same.5 = (f32[2,80,80]{2,1,0:T(8,128)S(1)}, f32[1,2048]{1,0:T(1,128)S(1)}) custom-call(s32[4]{0:T(128)S(1)} %copy-done.1, s32[4,2048]{1,0:T(4,128)S(1)} %copy-done, f32[2,48,128]{2,1,0:T(8,128)S(1)} %get-tuple-element.49.pay, f32[48,128]{1,0:T(8,128)S(1)} %collective-permute-done.5.far, f32[48,128]{1,0:T(8,128)S(1)} %collective-permute-done.6.sib_far), custom_call_target="tpu_custom_call" | custom-call | tf_op jit(solution)/shard_map/same/pallas_call | solution.py:391
  26.4 1.2 %collective-permute-done.7.h = f32[2,80,80]{2,1,0:T(8,128)S(1)} collective-permute-done((f32[2,80,80]{2,1,0:T(8,128)S(1)}, f32[2,80,80]{2,1,0:T(8,128)S(1)}, u32[]{:S(2)}, u32[]{:S(2)}) %collective-permute-start.7) | collective-permute-done | bytes 51232 | tf_op jit(solution)/shard_map/ppermute | solution.py:390
  27.7 1.0 %collective-permute-start.8 = (f32[2,80,80]{2,1,0:T(8,128)S(1)}, f32[2,80,80]{2,1,0:T(8,128)S(1)}, u32[]{:S(2)}, u32[]{:S(2)}) collective-permute-start(f32[2,80,80]{2,1,0:T(8,128)S(1)} %collective-permute-done.7.h), channel_id=1, source_target_pairs={{0,16},{32,48},{64,80},{96,112},{16,0},{48,32},{80,64},{112,96},{1... | collective-permute-start | bytes 153608 | tf_op jit(solution)/shard_map/ppermute | solution.py:406
  28.7 0.9 %collective-permute-done.8.g = f32[2,80,80]{2,1,0:T(8,128)S(1)} collective-permute-done((f32[2,80,80]{2,1,0:T(8,128)S(1)}, f32[2,80,80]{2,1,0:T(8,128)S(1)}, u32[]{:S(2)}, u32[]{:S(2)}) %collective-permute-start.8) | collective-permute-done | bytes 51232 | tf_op jit(solution)/shard_map/ppermute | solution.py:406
  29.6 0.5 step.4
  30.1 2.8 %collective-permute-start.9 = (f32[48,128]{1,0:T(8,128)S(1)}, f32[48,128]{1,0:T(8,128)S(1)}, u32[]{:S(2)}, u32[]{:S(2)}) collective-permute-start(f32[48,128]{1,0:T(8,128)S(1)} %get-tuple-element.58), channel_id=1, source_target_pairs={{0,32},{64,96},{48,80},{112,16},{32,0},{96,64},{80,48},{16,112},{1... | collective-permute-start | bytes 73736 | tf_op jit(solution)/shard_map/ppermute | solution.py:384
  32.9 1.2 %collective-permute-done.9.far = f32[48,128]{1,0:T(8,128)S(1)} collective-permute-done((f32[48,128]{1,0:T(8,128)S(1)}, f32[48,128]{1,0:T(8,128)S(1)}, u32[]{:S(2)}, u32[]{:S(2)}) %collective-permute-start.9) | collective-permute-done | bytes 24608 | tf_op jit(solution)/shard_map/ppermute | solution.py:384
  34.2 0.2 collective-permute-start.10
  34.3 1.0 %collective-permute-done.10.sib_far = f32[48,128]{1,0:T(8,128)S(1)} collective-permute-done((f32[48,128]{1,0:T(8,128)S(1)}, f32[48,128]{1,0:T(8,128)S(1)}, u32[]{:S(2)}, u32[]{:S(2)}) %collective-permute-start.10) | collective-permute-done | bytes 24608 | tf_op jit(solution)/shard_map/ppermute | solution.py:385
  35.3 0.4 send.6
  35.8 1.3 %collective-permute-start.11 = (f32[2,80,80]{2,1,0:T(8,128)S(1)}, f32[2,80,80]{2,1,0:T(8,128)S(1)}, u32[]{:S(2)}, u32[]{:S(2)}) collective-permute-start(f32[2,80,80]{2,1,0:T(8,128)S(1)} %send.6), channel_id=1, source_target_pairs={{0,1},{2,3},{4,5},{6,7},{8,9},{10,11},{12,13},{14,15},{17,18},{19,... | collective-permute-start | bytes 153608 | tf_op jit(solution)/shard_map/ppermute | solution.py:390
  37.0 1.2 %same.6 = (f32[2,80,80]{2,1,0:T(8,128)S(1)}, f32[1,2048]{1,0:T(1,128)S(1)}) custom-call(s32[4]{0:T(128)S(1)} %copy-done.1, s32[4,2048]{1,0:T(4,128)S(1)} %copy-done, f32[2,48,128]{2,1,0:T(8,128)S(1)} %get-tuple-element.57.pay, f32[48,128]{1,0:T(8,128)S(1)} %collective-permute-done.9.far, f32[48,128]{1,0:T(8,128)S(1)} %collective-permute-done.10.sib_far), custom_call_target="tpu_custom_call" | custom-call | tf_op jit(solution)/shard_map/same/pallas_call | solution.py:391
  38.2 1.2 %collective-permute-done.11.h = f32[2,80,80]{2,1,0:T(8,128)S(1)} collective-permute-done((f32[2,80,80]{2,1,0:T(8,128)S(1)}, f32[2,80,80]{2,1,0:T(8,128)S(1)}, u32[]{:S(2)}, u32[]{:S(2)}) %collective-permute-start.11) | collective-permute-done | bytes 51232 | tf_op jit(solution)/shard_map/ppermute | solution.py:390
  39.4 1.0 %collective-permute-start.12 = (f32[2,80,80]{2,1,0:T(8,128)S(1)}, f32[2,80,80]{2,1,0:T(8,128)S(1)}, u32[]{:S(2)}, u32[]{:S(2)}) collective-permute-start(f32[2,80,80]{2,1,0:T(8,128)S(1)} %collective-permute-done.11.h), channel_id=1, source_target_pairs={{0,16},{32,48},{64,80},{96,112},{16,0},{48,32},{80,64},{112,96},{1... | collective-permute-start | bytes 153608 | tf_op jit(solution)/shard_map/ppermute | solution.py:406
  40.5 0.9 %collective-permute-done.12.g = f32[2,80,80]{2,1,0:T(8,128)S(1)} collective-permute-done((f32[2,80,80]{2,1,0:T(8,128)S(1)}, f32[2,80,80]{2,1,0:T(8,128)S(1)}, u32[]{:S(2)}, u32[]{:S(2)}) %collective-permute-start.12) | collective-permute-done | bytes 51232 | tf_op jit(solution)/shard_map/ppermute | solution.py:406
  41.4 0.4 step.5
  41.8 2.9 %collective-permute-start.13 = (f32[56,128]{1,0:T(8,128)S(1)}, f32[56,128]{1,0:T(8,128)S(1)}, u32[]{:S(2)}, u32[]{:S(2)}) collective-permute-start(f32[56,128]{1,0:T(8,128)S(1)} %get-tuple-element.66), channel_id=1, source_target_pairs={{0,32},{64,96},{48,80},{112,16},{32,0},{96,64},{80,48},{16,112},{1... | collective-permute-start | bytes 86024 | tf_op jit(solution)/shard_map/ppermute | solution.py:384
  44.7 1.3 %collective-permute-done.13.far = f32[56,128]{1,0:T(8,128)S(1)} collective-permute-done((f32[56,128]{1,0:T(8,128)S(1)}, f32[56,128]{1,0:T(8,128)S(1)}, u32[]{:S(2)}, u32[]{:S(2)}) %collective-permute-start.13) | collective-permute-done | bytes 28704 | tf_op jit(solution)/shard_map/ppermute | solution.py:384
  46.0 0.2 collective-permute-start.14
  46.1 1.0 %collective-permute-done.14.sib_far = f32[56,128]{1,0:T(8,128)S(1)} collective-permute-done((f32[56,128]{1,0:T(8,128)S(1)}, f32[56,128]{1,0:T(8,128)S(1)}, u32[]{:S(2)}, u32[]{:S(2)}) %collective-permute-start.14) | collective-permute-done | bytes 28704 | tf_op jit(solution)/shard_map/ppermute | solution.py:385
  47.2 0.4 send.7
  47.6 1.3 %collective-permute-start.15 = (f32[2,80,80]{2,1,0:T(8,128)S(1)}, f32[2,80,80]{2,1,0:T(8,128)S(1)}, u32[]{:S(2)}, u32[]{:S(2)}) collective-permute-start(f32[2,80,80]{2,1,0:T(8,128)S(1)} %send.7), channel_id=1, source_target_pairs={{0,1},{2,3},{4,5},{6,7},{8,9},{10,11},{12,13},{14,15},{17,18},{19,... | collective-permute-start | bytes 153608 | tf_op jit(solution)/shard_map/ppermute | solution.py:390
  48.9 1.2 %same.7 = (f32[2,80,80]{2,1,0:T(8,128)S(1)}, f32[1,2048]{1,0:T(1,128)S(1)}) custom-call(s32[4]{0:T(128)S(1)} %copy-done.1, s32[4,2048]{1,0:T(4,128)S(1)} %copy-done, f32[2,48,128]{2,1,0:T(8,128)S(1)} %get-tuple-element.65.pay, f32[56,128]{1,0:T(8,128)S(1)} %collective-permute-done.13.far, f32[56,128]{1,0:T(8,128)S(1)} %collective-permute-done.14.sib_far), custom_call_target="tpu_custom_call" | custom-call | tf_op jit(solution)/shard_map/same/pallas_call | solution.py:391
  50.0 1.2 %collective-permute-done.15.h = f32[2,80,80]{2,1,0:T(8,128)S(1)} collective-permute-done((f32[2,80,80]{2,1,0:T(8,128)S(1)}, f32[2,80,80]{2,1,0:T(8,128)S(1)}, u32[]{:S(2)}, u32[]{:S(2)}) %collective-permute-start.15) | collective-permute-done | bytes 51232 | tf_op jit(solution)/shard_map/ppermute | solution.py:390
  51.3 1.0 %collective-permute-start.16 = (f32[2,80,80]{2,1,0:T(8,128)S(1)}, f32[2,80,80]{2,1,0:T(8,128)S(1)}, u32[]{:S(2)}, u32[]{:S(2)}) collective-permute-start(f32[2,80,80]{2,1,0:T(8,128)S(1)} %collective-permute-done.15.h), channel_id=1, source_target_pairs={{0,16},{32,48},{64,80},{96,112},{16,0},{48,32},{80,64},{112,96},{1... | collective-permute-start | bytes 153608 | tf_op jit(solution)/shard_map/ppermute | solution.py:406
  52.3 2.8 %collective-permute-start.17 = (f32[8,128]{1,0:T(8,128)S(1)}, f32[8,128]{1,0:T(8,128)S(1)}, u32[]{:S(2)}, u32[]{:S(2)}) collective-permute-start(f32[8,128]{1,0:T(8,128)S(1)} %slice.3), channel_id=1, source_target_pairs={{0,32},{64,96},{48,80},{112,16},{32,0},{96,64},{80,48},{16,112},{1... | collective-permute-start | bytes 12296 | tf_op jit(solution)/shard_map/ppermute | solution.py:400
  55.1 1.0 %collective-permute-done.17.across = f32[8,128]{1,0:T(8,128)S(1)} collective-permute-done((f32[8,128]{1,0:T(8,128)S(1)}, f32[8,128]{1,0:T(8,128)S(1)}, u32[]{:S(2)}, u32[]{:S(2)}) %collective-permute-start.17) | collective-permute-done | bytes 4128 | tf_op jit(solution)/shard_map/ppermute | solution.py:400
  56.1 0.7 column.1
  56.7 10.9 %all-to-all-start = ((f32[16,16,128]{2,1,0:T(8,128)}), f32[16,16,128]{2,1,0:T(8,128)S(1)}, u32[]{:S(2)}, u32[]{:S(2)}) async-start(f32[16,16,128]{2,1,0:T(8,128)} %column.1), calls=%async_computation | async-start | bytes 262144 | tf_op jit(solution)/shard_map/all_to_all | solution.py:404
  67.7 0.0 collective-permute-done.16.g
  67.7 8.7 %final.1 = f32[80,4,32,256]{3,2,1,0:T(8,128)} custom-call(f32[2,80,80]{2,1,0:T(8,128)S(1)} %get-tuple-element.70.q0, f32[2,80,80]{2,1,0:T(8,128)S(1)} %collective-permute-done.15.h, f32[2,80,80]{2,1,0:T(8,128)S(1)} %collective-permute-done.16.g, f32[2,96,384]{2,1,0:T(8,128)S(1)} %get-tuple-element.72.z, f32[80,4,32,256]{3,2,1,0:T(8,128)} %x.1), custom_call_target="tpu_custom_call" | custom-call | flops 1258291200 | bytes 20971520 | tf_op jit(solution)/shard_map/final/pallas_call | solution.py:420
  76.4 0.0 all-to-all-done.gathered
  76.4 2.5 %place.1 = f32[4,2048]{1,0:T(4,128)} custom-call(s32[4]{0:T(128)S(1)} %copy-done.1, s32[4,2048]{1,0:T(4,128)S(1)} %copy-done, f32[16,16,128]{2,1,0:T(8,128)S(1)} %all-to-all-done.gathered, f32[1,2048]{1,0:T(1,128)S(1)} %get-tuple-element.76.r0, f32[1,2048]{1,0:T(1,128)S(1)} %get-tuple-element.77.r1, f32[1,2048]{1,0:T(1,128)S(1)} %get-tuple-element.78.r2, ...), custom_call_target="tpu_custom_call" | custom-call | tf_op jit(solution)/shard_map/place/pallas_call | solution.py:430
  (1 shorter events, 0.0 us)
Async XLA Ops:
  0.6 12.9 %copy-start = (s32[4,2048]{1,0:T(4,128)S(1)}, s32[4,2048]{1,0:T(4,128)}, u32[]{:S(2)}) copy-start(s32[4,2048]{1,0:T(4,128)} %owner.9) | copy-start | bytes 98308
  0.6 12.9 %copy-start.1 = (s32[4]{0:T(128)S(1)}, s32[4]{0:T(128)}, u32[]{:S(2)}) copy-start(s32[4]{0:T(128)} %order.9) | copy-start | bytes 52
  3.9 2.5 %collective-permute-start = (f32[96,256]{1,0:T(8,128)S(1)}, f32[96,256]{1,0:T(8,128)S(1)}, u32[]{:S(2)}, u32[]{:S(2)}) collective-permute-start(f32[96,256]{1,0:T(8,128)S(1)} %init.1.own), channel_id=1, source_target_pairs={{0,16},{32,48},{64,80},{96,112},{16,0},{48,32},{80,64},{112,96},{1... | collective-permute-start | bytes 294920 | tf_op jit(solution)/shard_map/ppermute | solution.py:380
  6.5 4.1 %collective-permute-start.1 = (f32[48,128]{1,0:T(8,128)S(1)}, f32[48,128]{1,0:T(8,128)S(1)}, u32[]{:S(2)}, u32[]{:S(2)}) collective-permute-start(f32[48,128]{1,0:T(8,128)S(1)} %get-tuple-element.42), channel_id=1, source_target_pairs={{0,32},{64,96},{48,80},{112,16},{32,0},{96,64},{80,48},{16,112},{1... | collective-permute-start | bytes 73736 | tf_op jit(solution)/shard_map/ppermute | solution.py:384
  10.6 1.2 %collective-permute-start.2 = (f32[48,128]{1,0:T(8,128)S(1)}, f32[48,128]{1,0:T(8,128)S(1)}, u32[]{:S(2)}, u32[]{:S(2)}) collective-permute-start(f32[48,128]{1,0:T(8,128)S(1)} %collective-permute-done.1.far), channel_id=1, source_target_pairs={{0,16},{32,48},{64,80},{96,112},{16,0},{48,32},{80,64},{112,96},{1... | collective-permute-start | bytes 73736 | tf_op jit(solution)/shard_map/ppermute | solution.py:385
  12.2 3.7 %collective-permute-start.3 = (f32[2,80,80]{2,1,0:T(8,128)S(1)}, f32[2,80,80]{2,1,0:T(8,128)S(1)}, u32[]{:S(2)}, u32[]{:S(2)}) collective-permute-start(f32[2,80,80]{2,1,0:T(8,128)S(1)} %send.4), channel_id=1, source_target_pairs={{0,1},{2,3},{4,5},{6,7},{8,9},{10,11},{12,13},{14,15},{17,18},{19,... | collective-permute-start | bytes 153608 | tf_op jit(solution)/shard_map/ppermute | solution.py:390
  15.9 1.9 %collective-permute-start.4 = (f32[2,80,80]{2,1,0:T(8,128)S(1)}, f32[2,80,80]{2,1,0:T(8,128)S(1)}, u32[]{:S(2)}, u32[]{:S(2)}) collective-permute-start(f32[2,80,80]{2,1,0:T(8,128)S(1)} %collective-permute-done.3.h), channel_id=1, source_target_pairs={{0,16},{32,48},{64,80},{96,112},{16,0},{48,32},{80,64},{112,96},{1... | collective-permute-start | bytes 153608 | tf_op jit(solution)/shard_map/ppermute | solution.py:406
  18.3 4.1 %collective-permute-start.5 = (f32[48,128]{1,0:T(8,128)S(1)}, f32[48,128]{1,0:T(8,128)S(1)}, u32[]{:S(2)}, u32[]{:S(2)}) collective-permute-start(f32[48,128]{1,0:T(8,128)S(1)} %get-tuple-element.50), channel_id=1, source_target_pairs={{0,32},{64,96},{48,80},{112,16},{32,0},{96,64},{80,48},{16,112},{1... | collective-permute-start | bytes 73736 | tf_op jit(solution)/shard_map/ppermute | solution.py:384
  22.4 1.2 %collective-permute-start.6 = (f32[48,128]{1,0:T(8,128)S(1)}, f32[48,128]{1,0:T(8,128)S(1)}, u32[]{:S(2)}, u32[]{:S(2)}) collective-permute-start(f32[48,128]{1,0:T(8,128)S(1)} %collective-permute-done.5.far), channel_id=1, source_target_pairs={{0,16},{32,48},{64,80},{96,112},{16,0},{48,32},{80,64},{112,96},{1... | collective-permute-start | bytes 73736 | tf_op jit(solution)/shard_map/ppermute | solution.py:385
  24.0 3.7 %collective-permute-start.7 = (f32[2,80,80]{2,1,0:T(8,128)S(1)}, f32[2,80,80]{2,1,0:T(8,128)S(1)}, u32[]{:S(2)}, u32[]{:S(2)}) collective-permute-start(f32[2,80,80]{2,1,0:T(8,128)S(1)} %send.5), channel_id=1, source_target_pairs={{0,1},{2,3},{4,5},{6,7},{8,9},{10,11},{12,13},{14,15},{17,18},{19,... | collective-permute-start | bytes 153608 | tf_op jit(solution)/shard_map/ppermute | solution.py:390
  27.7 1.9 %collective-permute-start.8 = (f32[2,80,80]{2,1,0:T(8,128)S(1)}, f32[2,80,80]{2,1,0:T(8,128)S(1)}, u32[]{:S(2)}, u32[]{:S(2)}) collective-permute-start(f32[2,80,80]{2,1,0:T(8,128)S(1)} %collective-permute-done.7.h), channel_id=1, source_target_pairs={{0,16},{32,48},{64,80},{96,112},{16,0},{48,32},{80,64},{112,96},{1... | collective-permute-start | bytes 153608 | tf_op jit(solution)/shard_map/ppermute | solution.py:406
  30.1 4.1 %collective-permute-start.9 = (f32[48,128]{1,0:T(8,128)S(1)}, f32[48,128]{1,0:T(8,128)S(1)}, u32[]{:S(2)}, u32[]{:S(2)}) collective-permute-start(f32[48,128]{1,0:T(8,128)S(1)} %get-tuple-element.58), channel_id=1, source_target_pairs={{0,32},{64,96},{48,80},{112,16},{32,0},{96,64},{80,48},{16,112},{1... | collective-permute-start | bytes 73736 | tf_op jit(solution)/shard_map/ppermute | solution.py:384
  34.2 1.2 %collective-permute-start.10 = (f32[48,128]{1,0:T(8,128)S(1)}, f32[48,128]{1,0:T(8,128)S(1)}, u32[]{:S(2)}, u32[]{:S(2)}) collective-permute-start(f32[48,128]{1,0:T(8,128)S(1)} %collective-permute-done.9.far), channel_id=1, source_target_pairs={{0,16},{32,48},{64,80},{96,112},{16,0},{48,32},{80,64},{112,96},{1... | collective-permute-start | bytes 73736 | tf_op jit(solution)/shard_map/ppermute | solution.py:385
  35.8 3.7 %collective-permute-start.11 = (f32[2,80,80]{2,1,0:T(8,128)S(1)}, f32[2,80,80]{2,1,0:T(8,128)S(1)}, u32[]{:S(2)}, u32[]{:S(2)}) collective-permute-start(f32[2,80,80]{2,1,0:T(8,128)S(1)} %send.6), channel_id=1, source_target_pairs={{0,1},{2,3},{4,5},{6,7},{8,9},{10,11},{12,13},{14,15},{17,18},{19,... | collective-permute-start | bytes 153608 | tf_op jit(solution)/shard_map/ppermute | solution.py:390
  39.4 1.9 %collective-permute-start.12 = (f32[2,80,80]{2,1,0:T(8,128)S(1)}, f32[2,80,80]{2,1,0:T(8,128)S(1)}, u32[]{:S(2)}, u32[]{:S(2)}) collective-permute-start(f32[2,80,80]{2,1,0:T(8,128)S(1)} %collective-permute-done.11.h), channel_id=1, source_target_pairs={{0,16},{32,48},{64,80},{96,112},{16,0},{48,32},{80,64},{112,96},{1... | collective-permute-start | bytes 153608 | tf_op jit(solution)/shard_map/ppermute | solution.py:406
  41.8 4.1 %collective-permute-start.13 = (f32[56,128]{1,0:T(8,128)S(1)}, f32[56,128]{1,0:T(8,128)S(1)}, u32[]{:S(2)}, u32[]{:S(2)}) collective-permute-start(f32[56,128]{1,0:T(8,128)S(1)} %get-tuple-element.66), channel_id=1, source_target_pairs={{0,32},{64,96},{48,80},{112,16},{32,0},{96,64},{80,48},{16,112},{1... | collective-permute-start | bytes 86024 | tf_op jit(solution)/shard_map/ppermute | solution.py:384
  46.0 1.2 %collective-permute-start.14 = (f32[56,128]{1,0:T(8,128)S(1)}, f32[56,128]{1,0:T(8,128)S(1)}, u32[]{:S(2)}, u32[]{:S(2)}) collective-permute-start(f32[56,128]{1,0:T(8,128)S(1)} %collective-permute-done.13.far), channel_id=1, source_target_pairs={{0,16},{32,48},{64,80},{96,112},{16,0},{48,32},{80,64},{112,96},{1... | collective-permute-start | bytes 86024 | tf_op jit(solution)/shard_map/ppermute | solution.py:385
  47.6 3.7 %collective-permute-start.15 = (f32[2,80,80]{2,1,0:T(8,128)S(1)}, f32[2,80,80]{2,1,0:T(8,128)S(1)}, u32[]{:S(2)}, u32[]{:S(2)}) collective-permute-start(f32[2,80,80]{2,1,0:T(8,128)S(1)} %send.7), channel_id=1, source_target_pairs={{0,1},{2,3},{4,5},{6,7},{8,9},{10,11},{12,13},{14,15},{17,18},{19,... | collective-permute-start | bytes 153608 | tf_op jit(solution)/shard_map/ppermute | solution.py:390
  51.3 16.4 %collective-permute-start.16 = (f32[2,80,80]{2,1,0:T(8,128)S(1)}, f32[2,80,80]{2,1,0:T(8,128)S(1)}, u32[]{:S(2)}, u32[]{:S(2)}) collective-permute-start(f32[2,80,80]{2,1,0:T(8,128)S(1)} %collective-permute-done.15.h), channel_id=1, source_target_pairs={{0,16},{32,48},{64,80},{96,112},{16,0},{48,32},{80,64},{112,96},{1... | collective-permute-start | bytes 153608 | tf_op jit(solution)/shard_map/ppermute | solution.py:406
  52.3 3.8 %collective-permute-start.17 = (f32[8,128]{1,0:T(8,128)S(1)}, f32[8,128]{1,0:T(8,128)S(1)}, u32[]{:S(2)}, u32[]{:S(2)}) collective-permute-start(f32[8,128]{1,0:T(8,128)S(1)} %slice.3), channel_id=1, source_target_pairs={{0,32},{64,96},{48,80},{112,16},{32,0},{96,64},{80,48},{16,112},{1... | collective-permute-start | bytes 12296 | tf_op jit(solution)/shard_map/ppermute | solution.py:400
  56.7 19.6 %all-to-all-start = ((f32[16,16,128]{2,1,0:T(8,128)}), f32[16,16,128]{2,1,0:T(8,128)S(1)}, u32[]{:S(2)}, u32[]{:S(2)}) async-start(f32[16,16,128]{2,1,0:T(8,128)} %column.1), calls=%async_computation | async-start | bytes 262144 | tf_op jit(solution)/shard_map/all_to_all | solution.py:404

commit v10 on v9

--- a/solution.py
+++ b/solution.py
@@ -313,18 +313,25 @@
 
 def place_kernel(order, owner, gathered, r0, r1, r2, r3, out):
     y = lax.axis_index("gx") // 2
-    chips = iota((TILES // 2, OBS), 0)
-    seats = iota((2 * CAP, OBS), 0)
+    tiles = iota((TILES, OBS), 0)
+    slots = iota((CAP, OBS), 0).astype(F32)
     rows = gathered.reshape(TILES // 2 * NB, 2 * CAP)
     for k, rank in enumerate((r0, r1, r2, r3)):
         b = order[k]
         tile = owner[pl.ds(b, 1), :]
-        chip = (tile & 15) * 4 + ((tile >> 5) ^ y)
-        hot = jnp.where(chip == chips, 1.0, 0.0).astype(BF16)
-        high, low = split2(rows[pl.ds(k, TILES // 2, stride=NB), :].T)
-        got = dot(jnp.concatenate([high, low], axis=1), jnp.concatenate([hot, hot], axis=0))
-        seat = ((tile >> 4) & 1) * CAP + rank[...].astype(jnp.int32)
-        out[pl.ds(b, 1), :] = jnp.sum(jnp.where(seat == seats, got, 0.0), axis=0, keepdims=True)
+        place = ((tile >> 4) & 1) * (TILES // 2) + (tile & 15) * 4 + ((tile >> 5) ^ y)
+        turned = rows[pl.ds(k, TILES // 2, stride=NB), :].T
+        table = jnp.concatenate([turned[:CAP], turned[CAP:]], axis=1)
+        if k < NB // 2:
+            chunks = [slice(at, at + 128) for at in range(0, OBS, 128)]
+            got = jnp.concatenate([
+                jnp.take_along_axis(table, jnp.broadcast_to(place[:, at], (CAP, 128)), axis=1) for at in chunks
+            ], axis=1)
+        else:
+            hot = jnp.where(place == tiles, 1.0, 0.0).astype(BF16)
+            both = dot(jnp.concatenate(split2(table), axis=0), hot)
+            got = both[:CAP] + both[CAP:]
+        out[pl.ds(b, 1), :] = jnp.sum(jnp.where(rank[...] == slots, got, 0.0), axis=0, keepdims=True)
 
 
 VMEM = pl.BlockSpec(memory_space=pltpu.VMEM)
@@ -401,8 +408,11 @@
             column = call(
                 column_kernel, out_shape=shape(height, 4 * NB, 128), in_specs=[VMEM] * 4, out_specs=VMEM, name="column"
             )(news, far, sib_far, across)
+        if last:
+            h, q0, column = lax.optimization_barrier((h, q0, column))
             gathered = lax.all_to_all(column, "gy", 0, 0, tiled=True)
-        h, q0 = lax.optimization_barrier((h, q0))
+        else:
+            h, q0 = lax.optimization_barrier((h, q0))
         g = lax.ppermute(h, "gx", core)
         if not last:
             tail = k + 2 == NB

time: 79.1 us -> 74.8 us (0.946)
  starting transfers between devices: 36.4 us -> 34.2 us
  waiting for transfers between devices: 18.6 us -> 17 us
    ppermute x4, waiting for transfers between devices: 4.89 us -> 3.67 us  [local(): h = lax.ppermute(send, both, side_y)]
    ppermute x1, starting transfers between devices: 2.8 us -> 1.9 us  [local(): across = lax.ppermute(sib_far[ROWS // 2:], 'gx', side_x)]
  transfers between devices with their start and end apart: 19 -> 19, of which waited for: 17 -> 16; matrix products, arithmetic and copies ran while one was open for 0% -> 0% of each run, Pallas kernels for 18% -> 19%
where the time goes in v10:
time: 74.8 us; the launch traced here: 74.6 us
  starting transfers between devices  34.2 us (46%)
  Pallas kernels  22.6 us (30%)
  waiting for transfers between devices  17 us (23%)
  between operations  0.77 us (1%)
    ppermute x4, starting transfers between devices, local(): far = lax.ppermute(edge, 'gx', side_x)  11.4 us
    all_to_all x1, starting transfers between devices, local(): gathered = lax.all_to_all(column, 'gy', 0, 0, tiled=True)  10.1 us
    pallas_call x1, Pallas kernels, local(): call(final_kernel, out_shape=shape(M, LEV, TX, TY), in_specs=[VMEM] * 4 +...  8.68 us
    ppermute x4, starting transfers between devices, local(): h = lax.ppermute(send, both, side_y)  5.04 us
    ppermute x4, waiting for transfers between devices, local(): far = lax.ppermute(edge, 'gx', side_x)  4.91 us
    pallas_call x4, Pallas kernels, local(): call(functools.partial(same_kernel, k), out_shape=(shape(2, M, M), shape(...  4.7 us
    ppermute x4, waiting for transfers between devices, local(): sib_far = lax.ppermute(far, 'gx', core)  4.13 us
    ppermute x4, waiting for transfers between devices, local(): h = lax.ppermute(send, both, side_y)  3.67 us
  transfers between devices with their start and end apart: 19, of which 16 were waited for; matrix products, arithmetic and copies ran while one was open for 0% of the time, Pallas kernels for 19%

profile of v10, /device:TPU:1, one launch (start us, length us, event | category | flops | bytes accessed | tf_op | source)
XLA Modules:
  0.0 74.6 jit_solution(14579050589906670624)
XLA Ops:
  0.6 0.0 copy-start.1
  0.6 0.0 copy-start
  0.7 3.3 %init.1.own = f32[96,256]{1,0:T(8,128)S(1)} custom-call(s32[4]{0:T(128)} %order.9, f32[4,2048]{1,0:T(4,128)} %value_hbm.1, f32[4,2048]{1,0:T(4,128)} %variance_hbm.1, s32[4,2048]{1,0:T(4,128)} %owner.9, s32[4,2048]{1,0:T(4,128)} %cell_hbm.1, s32[4,8,2048]{2,1,0:T(8,128)} %bitcast.1, f32[80,4,32,256]{3,2,1,0:T(8,128)} %x.1), custom_call_target="tpu_custom_call" | custom-call | tf_op jit(solution)/shard_map/init/pallas_call | solution.py:365
  3.9 1.5 %collective-permute-start = (f32[96,256]{1,0:T(8,128)S(1)}, f32[96,256]{1,0:T(8,128)S(1)}, u32[]{:S(2)}, u32[]{:S(2)}) collective-permute-start(f32[96,256]{1,0:T(8,128)S(1)} %init.1.own), channel_id=1, source_target_pairs={{0,16},{32,48},{64,80},{96,112},{16,0},{48,32},{80,64},{112,96},{1... | collective-permute-start | bytes 294920 | tf_op jit(solution)/shard_map/ppermute | solution.py:387
  5.4 0.9 %collective-permute-done.sib = f32[96,256]{1,0:T(8,128)S(1)} collective-permute-done((f32[96,256]{1,0:T(8,128)S(1)}, f32[96,256]{1,0:T(8,128)S(1)}, u32[]{:S(2)}, u32[]{:S(2)}) %collective-permute-start) | collective-permute-done | bytes 98336 | tf_op jit(solution)/shard_map/ppermute | solution.py:387
  6.4 0.2 start.1
  6.5 2.9 %collective-permute-start.1 = (f32[48,128]{1,0:T(8,128)S(1)}, f32[48,128]{1,0:T(8,128)S(1)}, u32[]{:S(2)}, u32[]{:S(2)}) collective-permute-start(f32[48,128]{1,0:T(8,128)S(1)} %get-tuple-element.43), channel_id=1, source_target_pairs={{0,32},{64,96},{48,80},{112,16},{32,0},{96,64},{80,48},{16,112},{1... | collective-permute-start | bytes 73736 | tf_op jit(solution)/shard_map/ppermute | solution.py:391
  9.4 1.2 %collective-permute-done.1.far = f32[48,128]{1,0:T(8,128)S(1)} collective-permute-done((f32[48,128]{1,0:T(8,128)S(1)}, f32[48,128]{1,0:T(8,128)S(1)}, u32[]{:S(2)}, u32[]{:S(2)}) %collective-permute-start.1) | collective-permute-done | bytes 24608 | tf_op jit(solution)/shard_map/ppermute | solution.py:391
  10.6 0.2 collective-permute-start.2
  10.8 1.0 %collective-permute-done.2.sib_far = f32[48,128]{1,0:T(8,128)S(1)} collective-permute-done((f32[48,128]{1,0:T(8,128)S(1)}, f32[48,128]{1,0:T(8,128)S(1)}, u32[]{:S(2)}, u32[]{:S(2)}) %collective-permute-start.2) | collective-permute-done | bytes 24608 | tf_op jit(solution)/shard_map/ppermute | solution.py:392
  11.8 0.4 send.4
  12.2 1.3 %collective-permute-start.3 = (f32[2,80,80]{2,1,0:T(8,128)S(1)}, f32[2,80,80]{2,1,0:T(8,128)S(1)}, u32[]{:S(2)}, u32[]{:S(2)}) collective-permute-start(f32[2,80,80]{2,1,0:T(8,128)S(1)} %send.4), channel_id=1, source_target_pairs={{0,1},{2,3},{4,5},{6,7},{8,9},{10,11},{12,13},{14,15},{17,18},{19,... | collective-permute-start | bytes 153608 | tf_op jit(solution)/shard_map/ppermute | solution.py:397
  13.5 0.0 copy-done.1
  13.5 0.0 copy-done
  13.5 1.2 %same.4 = (f32[2,80,80]{2,1,0:T(8,128)S(1)}, f32[1,2048]{1,0:T(1,128)S(1)}) custom-call(s32[4]{0:T(128)S(1)} %copy-done.1, s32[4,2048]{1,0:T(4,128)S(1)} %copy-done, f32[2,48,128]{2,1,0:T(8,128)S(1)} %get-tuple-element.42.pay, f32[48,128]{1,0:T(8,128)S(1)} %collective-permute-done.1.far, f32[48,128]{1,0:T(8,128)S(1)} %collective-permute-done.2.sib_far), custom_call_target="tpu_custom_call" | custom-call | tf_op jit(solution)/shard_map/same/pallas_call | solution.py:398
  14.7 1.2 %collective-permute-done.3.h = f32[2,80,80]{2,1,0:T(8,128)S(1)} collective-permute-done((f32[2,80,80]{2,1,0:T(8,128)S(1)}, f32[2,80,80]{2,1,0:T(8,128)S(1)}, u32[]{:S(2)}, u32[]{:S(2)}) %collective-permute-start.3) | collective-permute-done | bytes 51232 | tf_op jit(solution)/shard_map/ppermute | solution.py:397
  15.9 1.0 %collective-permute-start.4 = (f32[2,80,80]{2,1,0:T(8,128)S(1)}, f32[2,80,80]{2,1,0:T(8,128)S(1)}, u32[]{:S(2)}, u32[]{:S(2)}) collective-permute-start(f32[2,80,80]{2,1,0:T(8,128)S(1)} %collective-permute-done.3.h), channel_id=1, source_target_pairs={{0,16},{32,48},{64,80},{96,112},{16,0},{48,32},{80,64},{112,96},{1... | collective-permute-start | bytes 153608 | tf_op jit(solution)/shard_map/ppermute | solution.py:416
  16.9 0.9 %collective-permute-done.4.g = f32[2,80,80]{2,1,0:T(8,128)S(1)} collective-permute-done((f32[2,80,80]{2,1,0:T(8,128)S(1)}, f32[2,80,80]{2,1,0:T(8,128)S(1)}, u32[]{:S(2)}, u32[]{:S(2)}) %collective-permute-start.4) | collective-permute-done | bytes 51232 | tf_op jit(solution)/shard_map/ppermute | solution.py:416
  17.9 0.4 step.3
  18.3 2.9 %collective-permute-start.5 = (f32[48,128]{1,0:T(8,128)S(1)}, f32[48,128]{1,0:T(8,128)S(1)}, u32[]{:S(2)}, u32[]{:S(2)}) collective-permute-start(f32[48,128]{1,0:T(8,128)S(1)} %get-tuple-element.51), channel_id=1, source_target_pairs={{0,32},{64,96},{48,80},{112,16},{32,0},{96,64},{80,48},{16,112},{1... | collective-permute-start | bytes 73736 | tf_op jit(solution)/shard_map/ppermute | solution.py:391
  21.2 1.2 %collective-permute-done.5.far = f32[48,128]{1,0:T(8,128)S(1)} collective-permute-done((f32[48,128]{1,0:T(8,128)S(1)}, f32[48,128]{1,0:T(8,128)S(1)}, u32[]{:S(2)}, u32[]{:S(2)}) %collective-permute-start.5) | collective-permute-done | bytes 24608 | tf_op jit(solution)/shard_map/ppermute | solution.py:391
  22.4 0.2 collective-permute-start.6
  22.5 1.0 %collective-permute-done.6.sib_far = f32[48,128]{1,0:T(8,128)S(1)} collective-permute-done((f32[48,128]{1,0:T(8,128)S(1)}, f32[48,128]{1,0:T(8,128)S(1)}, u32[]{:S(2)}, u32[]{:S(2)}) %collective-permute-start.6) | collective-permute-done | bytes 24608 | tf_op jit(solution)/shard_map/ppermute | solution.py:392
  23.6 0.4 send.5
  24.0 1.3 %collective-permute-start.7 = (f32[2,80,80]{2,1,0:T(8,128)S(1)}, f32[2,80,80]{2,1,0:T(8,128)S(1)}, u32[]{:S(2)}, u32[]{:S(2)}) collective-permute-start(f32[2,80,80]{2,1,0:T(8,128)S(1)} %send.5), channel_id=1, source_target_pairs={{0,1},{2,3},{4,5},{6,7},{8,9},{10,11},{12,13},{14,15},{17,18},{19,... | collective-permute-start | bytes 153608 | tf_op jit(solution)/shard_map/ppermute | solution.py:397
  25.3 1.2 %same.5 = (f32[2,80,80]{2,1,0:T(8,128)S(1)}, f32[1,2048]{1,0:T(1,128)S(1)}) custom-call(s32[4]{0:T(128)S(1)} %copy-done.1, s32[4,2048]{1,0:T(4,128)S(1)} %copy-done, f32[2,48,128]{2,1,0:T(8,128)S(1)} %get-tuple-element.50.pay, f32[48,128]{1,0:T(8,128)S(1)} %collective-permute-done.5.far, f32[48,128]{1,0:T(8,128)S(1)} %collective-permute-done.6.sib_far), custom_call_target="tpu_custom_call" | custom-call | tf_op jit(solution)/shard_map/same/pallas_call | solution.py:398
  26.4 1.2 %collective-permute-done.7.h = f32[2,80,80]{2,1,0:T(8,128)S(1)} collective-permute-done((f32[2,80,80]{2,1,0:T(8,128)S(1)}, f32[2,80,80]{2,1,0:T(8,128)S(1)}, u32[]{:S(2)}, u32[]{:S(2)}) %collective-permute-start.7) | collective-permute-done | bytes 51232 | tf_op jit(solution)/shard_map/ppermute | solution.py:397
  27.7 1.0 %collective-permute-start.8 = (f32[2,80,80]{2,1,0:T(8,128)S(1)}, f32[2,80,80]{2,1,0:T(8,128)S(1)}, u32[]{:S(2)}, u32[]{:S(2)}) collective-permute-start(f32[2,80,80]{2,1,0:T(8,128)S(1)} %collective-permute-done.7.h), channel_id=1, source_target_pairs={{0,16},{32,48},{64,80},{96,112},{16,0},{48,32},{80,64},{112,96},{1... | collective-permute-start | bytes 153608 | tf_op jit(solution)/shard_map/ppermute | solution.py:416
  28.7 0.9 %collective-permute-done.8.g = f32[2,80,80]{2,1,0:T(8,128)S(1)} collective-permute-done((f32[2,80,80]{2,1,0:T(8,128)S(1)}, f32[2,80,80]{2,1,0:T(8,128)S(1)}, u32[]{:S(2)}, u32[]{:S(2)}) %collective-permute-start.8) | collective-permute-done | bytes 51232 | tf_op jit(solution)/shard_map/ppermute | solution.py:416
  29.6 0.5 step.4
  30.1 2.8 %collective-permute-start.9 = (f32[48,128]{1,0:T(8,128)S(1)}, f32[48,128]{1,0:T(8,128)S(1)}, u32[]{:S(2)}, u32[]{:S(2)}) collective-permute-start(f32[48,128]{1,0:T(8,128)S(1)} %get-tuple-element.59), channel_id=1, source_target_pairs={{0,32},{64,96},{48,80},{112,16},{32,0},{96,64},{80,48},{16,112},{1... | collective-permute-start | bytes 73736 | tf_op jit(solution)/shard_map/ppermute | solution.py:391
  32.9 1.2 %collective-permute-done.9.far = f32[48,128]{1,0:T(8,128)S(1)} collective-permute-done((f32[48,128]{1,0:T(8,128)S(1)}, f32[48,128]{1,0:T(8,128)S(1)}, u32[]{:S(2)}, u32[]{:S(2)}) %collective-permute-start.9) | collective-permute-done | bytes 24608 | tf_op jit(solution)/shard_map/ppermute | solution.py:391
  34.2 0.2 collective-permute-start.10
  34.3 1.0 %collective-permute-done.10.sib_far = f32[48,128]{1,0:T(8,128)S(1)} collective-permute-done((f32[48,128]{1,0:T(8,128)S(1)}, f32[48,128]{1,0:T(8,128)S(1)}, u32[]{:S(2)}, u32[]{:S(2)}) %collective-permute-start.10) | collective-permute-done | bytes 24608 | tf_op jit(solution)/shard_map/ppermute | solution.py:392
  35.3 0.4 send.6
  35.8 1.3 %collective-permute-start.11 = (f32[2,80,80]{2,1,0:T(8,128)S(1)}, f32[2,80,80]{2,1,0:T(8,128)S(1)}, u32[]{:S(2)}, u32[]{:S(2)}) collective-permute-start(f32[2,80,80]{2,1,0:T(8,128)S(1)} %send.6), channel_id=1, source_target_pairs={{0,1},{2,3},{4,5},{6,7},{8,9},{10,11},{12,13},{14,15},{17,18},{19,... | collective-permute-start | bytes 153608 | tf_op jit(solution)/shard_map/ppermute | solution.py:397
  37.0 1.2 %same.6 = (f32[2,80,80]{2,1,0:T(8,128)S(1)}, f32[1,2048]{1,0:T(1,128)S(1)}) custom-call(s32[4]{0:T(128)S(1)} %copy-done.1, s32[4,2048]{1,0:T(4,128)S(1)} %copy-done, f32[2,48,128]{2,1,0:T(8,128)S(1)} %get-tuple-element.58.pay, f32[48,128]{1,0:T(8,128)S(1)} %collective-permute-done.9.far, f32[48,128]{1,0:T(8,128)S(1)} %collective-permute-done.10.sib_far), custom_call_target="tpu_custom_call" | custom-call | tf_op jit(solution)/shard_map/same/pallas_call | solution.py:398
  38.2 1.2 %collective-permute-done.11.h = f32[2,80,80]{2,1,0:T(8,128)S(1)} collective-permute-done((f32[2,80,80]{2,1,0:T(8,128)S(1)}, f32[2,80,80]{2,1,0:T(8,128)S(1)}, u32[]{:S(2)}, u32[]{:S(2)}) %collective-permute-start.11) | collective-permute-done | bytes 51232 | tf_op jit(solution)/shard_map/ppermute | solution.py:397
  39.4 1.0 %collective-permute-start.12 = (f32[2,80,80]{2,1,0:T(8,128)S(1)}, f32[2,80,80]{2,1,0:T(8,128)S(1)}, u32[]{:S(2)}, u32[]{:S(2)}) collective-permute-start(f32[2,80,80]{2,1,0:T(8,128)S(1)} %collective-permute-done.11.h), channel_id=1, source_target_pairs={{0,16},{32,48},{64,80},{96,112},{16,0},{48,32},{80,64},{112,96},{1... | collective-permute-start | bytes 153608 | tf_op jit(solution)/shard_map/ppermute | solution.py:416
  40.5 0.9 %collective-permute-done.12.g = f32[2,80,80]{2,1,0:T(8,128)S(1)} collective-permute-done((f32[2,80,80]{2,1,0:T(8,128)S(1)}, f32[2,80,80]{2,1,0:T(8,128)S(1)}, u32[]{:S(2)}, u32[]{:S(2)}) %collective-permute-start.12) | collective-permute-done | bytes 51232 | tf_op jit(solution)/shard_map/ppermute | solution.py:416
  41.4 0.4 step.5
  41.8 2.9 %collective-permute-start.13 = (f32[56,128]{1,0:T(8,128)S(1)}, f32[56,128]{1,0:T(8,128)S(1)}, u32[]{:S(2)}, u32[]{:S(2)}) collective-permute-start(f32[56,128]{1,0:T(8,128)S(1)} %get-tuple-element.67), channel_id=1, source_target_pairs={{0,32},{64,96},{48,80},{112,16},{32,0},{96,64},{80,48},{16,112},{1... | collective-permute-start | bytes 86024 | tf_op jit(solution)/shard_map/ppermute | solution.py:391
  44.7 1.3 %collective-permute-done.13.far = f32[56,128]{1,0:T(8,128)S(1)} collective-permute-done((f32[56,128]{1,0:T(8,128)S(1)}, f32[56,128]{1,0:T(8,128)S(1)}, u32[]{:S(2)}, u32[]{:S(2)}) %collective-permute-start.13) | collective-permute-done | bytes 28704 | tf_op jit(solution)/shard_map/ppermute | solution.py:391
  46.0 0.2 collective-permute-start.14
  46.1 1.0 %collective-permute-done.14.sib_far = f32[56,128]{1,0:T(8,128)S(1)} collective-permute-done((f32[56,128]{1,0:T(8,128)S(1)}, f32[56,128]{1,0:T(8,128)S(1)}, u32[]{:S(2)}, u32[]{:S(2)}) %collective-permute-start.14) | collective-permute-done | bytes 28704 | tf_op jit(solution)/shard_map/ppermute | solution.py:392
  47.2 0.4 send.7
  47.6 1.3 %collective-permute-start.15 = (f32[2,80,80]{2,1,0:T(8,128)S(1)}, f32[2,80,80]{2,1,0:T(8,128)S(1)}, u32[]{:S(2)}, u32[]{:S(2)}) collective-permute-start(f32[2,80,80]{2,1,0:T(8,128)S(1)} %send.7), channel_id=1, source_target_pairs={{0,1},{2,3},{4,5},{6,7},{8,9},{10,11},{12,13},{14,15},{17,18},{19,... | collective-permute-start | bytes 153608 | tf_op jit(solution)/shard_map/ppermute | solution.py:397
  48.9 1.9 %collective-permute-start.16 = (f32[8,128]{1,0:T(8,128)S(1)}, f32[8,128]{1,0:T(8,128)S(1)}, u32[]{:S(2)}, u32[]{:S(2)}) collective-permute-start(f32[8,128]{1,0:T(8,128)S(1)} %slice.3), channel_id=1, source_target_pairs={{0,32},{64,96},{48,80},{112,16},{32,0},{96,64},{80,48},{16,112},{1... | collective-permute-start | bytes 12296 | tf_op jit(solution)/shard_map/ppermute | solution.py:407
  50.8 1.2 %same.7 = (f32[2,80,80]{2,1,0:T(8,128)S(1)}, f32[1,2048]{1,0:T(1,128)S(1)}) custom-call(s32[4]{0:T(128)S(1)} %copy-done.1, s32[4,2048]{1,0:T(4,128)S(1)} %copy-done, f32[2,48,128]{2,1,0:T(8,128)S(1)} %get-tuple-element.66.pay, f32[56,128]{1,0:T(8,128)S(1)} %collective-permute-done.13.far, f32[56,128]{1,0:T(8,128)S(1)} %collective-permute-done.14.sib_far), custom_call_target="tpu_custom_call" | custom-call | tf_op jit(solution)/shard_map/same/pallas_call | solution.py:398
  51.9 0.6 collective-permute-done.16.across
  52.5 0.7 column.1
  53.2 0.0 collective-permute-done.15.h
  53.2 0.5 collective-permute-start.17
  53.7 10.1 %all-to-all-start = ((f32[16,16,128]{2,1,0:T(8,128)}), f32[16,16,128]{2,1,0:T(8,128)S(1)}, u32[]{:S(2)}, u32[]{:S(2)}) async-start(f32[16,16,128]{2,1,0:T(8,128)} %column.1), calls=%async_computation | async-start | bytes 262144 | tf_op jit(solution)/shard_map/all_to_all | solution.py:413
  63.8 0.0 collective-permute-done.17.g
  63.8 8.7 %final.1 = f32[80,4,32,256]{3,2,1,0:T(8,128)} custom-call(f32[2,80,80]{2,1,0:T(8,128)S(1)} %get-tuple-element.72.q0, f32[2,80,80]{2,1,0:T(8,128)S(1)} %collective-permute-done.15.h, f32[2,80,80]{2,1,0:T(8,128)S(1)} %collective-permute-done.17.g, f32[2,96,384]{2,1,0:T(8,128)S(1)} %get-tuple-element.74.z, f32[80,4,32,256]{3,2,1,0:T(8,128)} %x.1), custom_call_target="tpu_custom_call" | custom-call | flops 1258291200 | bytes 20971520 | tf_op jit(solution)/shard_map/final/pallas_call | solution.py:430
  72.5 0.0 all-to-all-done.gathered
  72.5 2.1 %place.1 = f32[4,2048]{1,0:T(4,128)} custom-call(s32[4]{0:T(128)S(1)} %copy-done.1, s32[4,2048]{1,0:T(4,128)S(1)} %copy-done, f32[16,16,128]{2,1,0:T(8,128)S(1)} %all-to-all-done.gathered, f32[1,2048]{1,0:T(1,128)S(1)} %get-tuple-element.78.r0, f32[1,2048]{1,0:T(1,128)S(1)} %get-tuple-element.79.r1, f32[1,2048]{1,0:T(1,128)S(1)} %get-tuple-element.80.r2, ...), custom_call_target="tpu_custom_call" | custom-call | tf_op jit(solution)/shard_map/place/pallas_call | solution.py:440
  (1 shorter events, 0.0 us)
Async XLA Ops:
  0.6 12.9 %copy-start.1 = (s32[4]{0:T(128)S(1)}, s32[4]{0:T(128)}, u32[]{:S(2)}) copy-start(s32[4]{0:T(128)} %order.9) | copy-start | bytes 52
  0.6 12.9 %copy-start = (s32[4,2048]{1,0:T(4,128)S(1)}, s32[4,2048]{1,0:T(4,128)}, u32[]{:S(2)}) copy-start(s32[4,2048]{1,0:T(4,128)} %owner.9) | copy-start | bytes 98308
  3.9 2.5 %collective-permute-start = (f32[96,256]{1,0:T(8,128)S(1)}, f32[96,256]{1,0:T(8,128)S(1)}, u32[]{:S(2)}, u32[]{:S(2)}) collective-permute-start(f32[96,256]{1,0:T(8,128)S(1)} %init.1.own), channel_id=1, source_target_pairs={{0,16},{32,48},{64,80},{96,112},{16,0},{48,32},{80,64},{112,96},{1... | collective-permute-start | bytes 294920 | tf_op jit(solution)/shard_map/ppermute | solution.py:387
  6.5 4.1 %collective-permute-start.1 = (f32[48,128]{1,0:T(8,128)S(1)}, f32[48,128]{1,0:T(8,128)S(1)}, u32[]{:S(2)}, u32[]{:S(2)}) collective-permute-start(f32[48,128]{1,0:T(8,128)S(1)} %get-tuple-element.43), channel_id=1, source_target_pairs={{0,32},{64,96},{48,80},{112,16},{32,0},{96,64},{80,48},{16,112},{1... | collective-permute-start | bytes 73736 | tf_op jit(solution)/shard_map/ppermute | solution.py:391
  10.6 1.2 %collective-permute-start.2 = (f32[48,128]{1,0:T(8,128)S(1)}, f32[48,128]{1,0:T(8,128)S(1)}, u32[]{:S(2)}, u32[]{:S(2)}) collective-permute-start(f32[48,128]{1,0:T(8,128)S(1)} %collective-permute-done.1.far), channel_id=1, source_target_pairs={{0,16},{32,48},{64,80},{96,112},{16,0},{48,32},{80,64},{112,96},{1... | collective-permute-start | bytes 73736 | tf_op jit(solution)/shard_map/ppermute | solution.py:392
  12.2 3.7 %collective-permute-start.3 = (f32[2,80,80]{2,1,0:T(8,128)S(1)}, f32[2,80,80]{2,1,0:T(8,128)S(1)}, u32[]{:S(2)}, u32[]{:S(2)}) collective-permute-start(f32[2,80,80]{2,1,0:T(8,128)S(1)} %send.4), channel_id=1, source_target_pairs={{0,1},{2,3},{4,5},{6,7},{8,9},{10,11},{12,13},{14,15},{17,18},{19,... | collective-permute-start | bytes 153608 | tf_op jit(solution)/shard_map/ppermute | solution.py:397
  15.9 1.9 %collective-permute-start.4 = (f32[2,80,80]{2,1,0:T(8,128)S(1)}, f32[2,80,80]{2,1,0:T(8,128)S(1)}, u32[]{:S(2)}, u32[]{:S(2)}) collective-permute-start(f32[2,80,80]{2,1,0:T(8,128)S(1)} %collective-permute-done.3.h), channel_id=1, source_target_pairs={{0,16},{32,48},{64,80},{96,112},{16,0},{48,32},{80,64},{112,96},{1... | collective-permute-start | bytes 153608 | tf_op jit(solution)/shard_map/ppermute | solution.py:416
  18.3 4.1 %collective-permute-start.5 = (f32[48,128]{1,0:T(8,128)S(1)}, f32[48,128]{1,0:T(8,128)S(1)}, u32[]{:S(2)}, u32[]{:S(2)}) collective-permute-start(f32[48,128]{1,0:T(8,128)S(1)} %get-tuple-element.51), channel_id=1, source_target_pairs={{0,32},{64,96},{48,80},{112,16},{32,0},{96,64},{80,48},{16,112},{1... | collective-permute-start | bytes 73736 | tf_op jit(solution)/shard_map/ppermute | solution.py:391
  22.4 1.2 %collective-permute-start.6 = (f32[48,128]{1,0:T(8,128)S(1)}, f32[48,128]{1,0:T(8,128)S(1)}, u32[]{:S(2)}, u32[]{:S(2)}) collective-permute-start(f32[48,128]{1,0:T(8,128)S(1)} %collective-permute-done.5.far), channel_id=1, source_target_pairs={{0,16},{32,48},{64,80},{96,112},{16,0},{48,32},{80,64},{112,96},{1... | collective-permute-start | bytes 73736 | tf_op jit(solution)/shard_map/ppermute | solution.py:392
  24.0 3.7 %collective-permute-start.7 = (f32[2,80,80]{2,1,0:T(8,128)S(1)}, f32[2,80,80]{2,1,0:T(8,128)S(1)}, u32[]{:S(2)}, u32[]{:S(2)}) collective-permute-start(f32[2,80,80]{2,1,0:T(8,128)S(1)} %send.5), channel_id=1, source_target_pairs={{0,1},{2,3},{4,5},{6,7},{8,9},{10,11},{12,13},{14,15},{17,18},{19,... | collective-permute-start | bytes 153608 | tf_op jit(solution)/shard_map/ppermute | solution.py:397
  27.7 1.9 %collective-permute-start.8 = (f32[2,80,80]{2,1,0:T(8,128)S(1)}, f32[2,80,80]{2,1,0:T(8,128)S(1)}, u32[]{:S(2)}, u32[]{:S(2)}) collective-permute-start(f32[2,80,80]{2,1,0:T(8,128)S(1)} %collective-permute-done.7.h), channel_id=1, source_target_pairs={{0,16},{32,48},{64,80},{96,112},{16,0},{48,32},{80,64},{112,96},{1... | collective-permute-start | bytes 153608 | tf_op jit(solution)/shard_map/ppermute | solution.py:416
  30.1 4.1 %collective-permute-start.9 = (f32[48,128]{1,0:T(8,128)S(1)}, f32[48,128]{1,0:T(8,128)S(1)}, u32[]{:S(2)}, u32[]{:S(2)}) collective-permute-start(f32[48,128]{1,0:T(8,128)S(1)} %get-tuple-element.59), channel_id=1, source_target_pairs={{0,32},{64,96},{48,80},{112,16},{32,0},{96,64},{80,48},{16,112},{1... | collective-permute-start | bytes 73736 | tf_op jit(solution)/shard_map/ppermute | solution.py:391
  34.2 1.2 %collective-permute-start.10 = (f32[48,128]{1,0:T(8,128)S(1)}, f32[48,128]{1,0:T(8,128)S(1)}, u32[]{:S(2)}, u32[]{:S(2)}) collective-permute-start(f32[48,128]{1,0:T(8,128)S(1)} %collective-permute-done.9.far), channel_id=1, source_target_pairs={{0,16},{32,48},{64,80},{96,112},{16,0},{48,32},{80,64},{112,96},{1... | collective-permute-start | bytes 73736 | tf_op jit(solution)/shard_map/ppermute | solution.py:392
  35.8 3.7 %collective-permute-start.11 = (f32[2,80,80]{2,1,0:T(8,128)S(1)}, f32[2,80,80]{2,1,0:T(8,128)S(1)}, u32[]{:S(2)}, u32[]{:S(2)}) collective-permute-start(f32[2,80,80]{2,1,0:T(8,128)S(1)} %send.6), channel_id=1, source_target_pairs={{0,1},{2,3},{4,5},{6,7},{8,9},{10,11},{12,13},{14,15},{17,18},{19,... | collective-permute-start | bytes 153608 | tf_op jit(solution)/shard_map/ppermute | solution.py:397
  39.4 1.9 %collective-permute-start.12 = (f32[2,80,80]{2,1,0:T(8,128)S(1)}, f32[2,80,80]{2,1,0:T(8,128)S(1)}, u32[]{:S(2)}, u32[]{:S(2)}) collective-permute-start(f32[2,80,80]{2,1,0:T(8,128)S(1)} %collective-permute-done.11.h), channel_id=1, source_target_pairs={{0,16},{32,48},{64,80},{96,112},{16,0},{48,32},{80,64},{112,96},{1... | collective-permute-start | bytes 153608 | tf_op jit(solution)/shard_map/ppermute | solution.py:416
  41.8 4.1 %collective-permute-start.13 = (f32[56,128]{1,0:T(8,128)S(1)}, f32[56,128]{1,0:T(8,128)S(1)}, u32[]{:S(2)}, u32[]{:S(2)}) collective-permute-start(f32[56,128]{1,0:T(8,128)S(1)} %get-tuple-element.67), channel_id=1, source_target_pairs={{0,32},{64,96},{48,80},{112,16},{32,0},{96,64},{80,48},{16,112},{1... | collective-permute-start | bytes 86024 | tf_op jit(solution)/shard_map/ppermute | solution.py:391
  46.0 1.2 %collective-permute-start.14 = (f32[56,128]{1,0:T(8,128)S(1)}, f32[56,128]{1,0:T(8,128)S(1)}, u32[]{:S(2)}, u32[]{:S(2)}) collective-permute-start(f32[56,128]{1,0:T(8,128)S(1)} %collective-permute-done.13.far), channel_id=1, source_target_pairs={{0,16},{32,48},{64,80},{96,112},{16,0},{48,32},{80,64},{112,96},{1... | collective-permute-start | bytes 86024 | tf_op jit(solution)/shard_map/ppermute | solution.py:392
  47.6 5.6 %collective-permute-start.15 = (f32[2,80,80]{2,1,0:T(8,128)S(1)}, f32[2,80,80]{2,1,0:T(8,128)S(1)}, u32[]{:S(2)}, u32[]{:S(2)}) collective-permute-start(f32[2,80,80]{2,1,0:T(8,128)S(1)} %send.7), channel_id=1, source_target_pairs={{0,1},{2,3},{4,5},{6,7},{8,9},{10,11},{12,13},{14,15},{17,18},{19,... | collective-permute-start | bytes 153608 | tf_op jit(solution)/shard_map/ppermute | solution.py:397
  48.9 3.7 %collective-permute-start.16 = (f32[8,128]{1,0:T(8,128)S(1)}, f32[8,128]{1,0:T(8,128)S(1)}, u32[]{:S(2)}, u32[]{:S(2)}) collective-permute-start(f32[8,128]{1,0:T(8,128)S(1)} %slice.3), channel_id=1, source_target_pairs={{0,32},{64,96},{48,80},{112,16},{32,0},{96,64},{80,48},{16,112},{1... | collective-permute-start | bytes 12296 | tf_op jit(solution)/shard_map/ppermute | solution.py:407
  53.2 10.6 %collective-permute-start.17 = (f32[2,80,80]{2,1,0:T(8,128)S(1)}, f32[2,80,80]{2,1,0:T(8,128)S(1)}, u32[]{:S(2)}, u32[]{:S(2)}) collective-permute-start(f32[2,80,80]{2,1,0:T(8,128)S(1)} %collective-permute-done.15.h), channel_id=1, source_target_pairs={{0,16},{32,48},{64,80},{96,112},{16,0},{48,32},{80,64},{112,96},{1... | collective-permute-start | bytes 153608 | tf_op jit(solution)/shard_map/ppermute | solution.py:416
  53.7 18.8 %all-to-all-start = ((f32[16,16,128]{2,1,0:T(8,128)}), f32[16,16,128]{2,1,0:T(8,128)S(1)}, u32[]{:S(2)}, u32[]{:S(2)}) async-start(f32[16,16,128]{2,1,0:T(8,128)} %column.1), calls=%async_computation | async-start | bytes 262144 | tf_op jit(solution)/shard_map/all_to_all | solution.py:413

commit v11 on v10

--- a/solution.py
+++ b/solution.py
@@ -18,7 +18,6 @@
 EPS = 1e-05
 F32 = jnp.float32
 BF16 = jnp.bfloat16
-HIGH = lax.Precision.HIGHEST
 SLAB = 16
 PARTS = TX // SLAB
 SLABS = LEV * PARTS
@@ -53,6 +52,12 @@
 
 def dot_t(a, b, **kw):
     return lax.dot_general(a, b, (((1,), (1,)), ((), ())), preferred_element_type=F32, **kw)
+
+
+def dot3(a, b, product=dot):
+    ah, al = split2(a)
+    bh, bl = split2(b)
+    return product(ah, bh) + (product(ah, bl) + product(al, bh))
 
 
 def pack(rows):
@@ -208,40 +213,44 @@
     return rows[ROW_A : ROW_A + 1] + rows[ROW_C : ROW_C + 1] * rows[:M]
 
 
-def gains(pay, far, sib_far, weight):
+def factor(rows, dx, dy):
+    at = ROW_W + 3 * (dx + 1) + dy + 1
+    return rows[at : at + 1]
+
+
+def toward(rows, dx):
+    return jnp.where(upward(lax.axis_index("gy")), factor(rows, dx, 1), factor(rows, dx, -1))
+
+
+def level(rows, dx):
+    return factor(rows, dx, 0)
+
+
+def inner(pay, weight):
+    blocks = [unpack(pay[t]) for t in range(2)]
+    right = jnp.concatenate([right_side(b) for b in blocks], axis=1)
+    return [
+        dot3(right, jnp.concatenate([b[:M] * weight(b, t - i) for i, b in enumerate(blocks)], axis=1), dot_t)
+        for t in range(2)
+    ]
+
+
+def outer(far, sib_far, weight):
     y, chips = lax.axis_index("gx") // 2, lax.axis_size("gx") // 2
     up = upward(y)
     first = core_of() == 0
     ends = edge(y, chips)
     far = jnp.where(ends & jnp.logical_not(first), 0.0, far[: ROWS // 2])
     sib_far = jnp.where(ends & first, 0.0, sib_far[: ROWS // 2])
-    blocks = [jnp.where(up, sib_far, far), pay[0], pay[1], jnp.where(up, far, sib_far)]
-    blocks = [unpack(b) for b in blocks]
-    rights = [right_side(b) for b in blocks]
-    results = []
-    for t in range(2):
-        left = jnp.concatenate([blocks[t + i][:M] * weight(blocks[t + i], 1 - i) for i in range(3)], axis=1)
-        right = jnp.concatenate(rights[t : t + 3], axis=1)
-        results.append(dot_t(right, left, precision=HIGH))
-    return results
-
-
-def factor(rows, dx, dy):
-    at = ROW_W + 3 * (dx + 1) + dy + 1
-    return rows[at : at + 1]
-
-
-def send_kernel(pay, far, sib_far, out):
-    up = upward(lax.axis_index("gy"))
-    both = gains(pay, far, sib_far, lambda rows, dx: jnp.where(up, factor(rows, dx, 1), factor(rows, dx, -1)))
-    for t in range(2):
-        out[t] = both[t]
-
-
-def same_kernel(k, order, owner, pay, far, sib_far, out, rank_out):
-    both = gains(pay, far, sib_far, lambda rows, dx: factor(rows, dx, 0))
-    for t in range(2):
-        out[t] = both[t]
+    blocks = [unpack(jnp.where(up, sib_far, far)), unpack(jnp.where(up, far, sib_far))]
+    return [dot3(right_side(b), b[:M] * weight(b, dx), dot_t) for b, dx in zip(blocks, (1, -1))]
+
+
+def own_kernel(k, order, owner, pay, toward_out, level_out, rank_out):
+    for t, value in enumerate(inner(pay, toward)):
+        toward_out[t] = value
+    for t, value in enumerate(inner(pay, level)):
+        level_out[t] = value
     row = owner[pl.ds(order[k], 1), :]
     upper = jnp.where(iota((128, 128), 0) < iota((128, 128), 1), 1.0, 0.0).astype(BF16)
     tiles = iota((TILES, 128), 0)
@@ -254,6 +263,16 @@
         base = base + jnp.sum(hot, axis=1, keepdims=True)
 
 
+def send_kernel(own, far, sib_far, out):
+    for t, value in enumerate(outer(far, sib_far, toward)):
+        out[t] = own[t] + value
+
+
+def same_kernel(own, far, sib_far, out):
+    for t, value in enumerate(outer(far, sib_far, level)):
+        out[t] = own[t] + value
+
+
 def column_kernel(news, far, sib_far, across, out):
     first = core_of() == 0
     at = slice(ROWS // 2, ROWS // 2 + NB)
@@ -266,7 +285,7 @@
 
 def advance(z, gain):
     anomaly = z - jnp.sum(z, axis=0, keepdims=True) / M
-    return z + dot(gain, anomaly, precision=HIGH)
+    return z + dot3(gain, anomaly)
 
 
 def whole_gain(t, q0, h, g):
@@ -389,19 +408,23 @@
     for k in range(NB):
         last = k + 1 == NB
         far = lax.ppermute(edge, "gx", side_x)
+        own_toward, own_level, rank = call(
+            functools.partial(own_kernel, k),
+            out_shape=(shape(2, M, M), shape(2, M, M), shape(1, OBS)),
+            in_specs=[SMEM, VMEM, VMEM],
+            out_specs=(VMEM,) * 3,
+            name="own",
+        )(batch_order, obs_owner, pay)
+        far, own_toward = lax.optimization_barrier((far, own_toward))
         sib_far = lax.ppermute(far, "gx", core)
         send = call(send_kernel, out_shape=shape(2, M, M), in_specs=[VMEM] * 3, out_specs=VMEM, name="send")(
-            pay, far, sib_far
+            own_toward, far, sib_far
         )
         send, sib_far = lax.optimization_barrier((send, sib_far))
         h = lax.ppermute(send, both, side_y)
-        q0, rank = call(
-            functools.partial(same_kernel, k),
-            out_shape=(shape(2, M, M), shape(1, OBS)),
-            in_specs=[SMEM] + [VMEM] * 4,
-            out_specs=(VMEM, VMEM),
-            name="same",
-        )(batch_order, obs_owner, pay, far, sib_far)
+        q0 = call(same_kernel, out_shape=shape(2, M, M), in_specs=[VMEM] * 3, out_specs=VMEM, name="same")(
+            own_level, far, sib_far
+        )
         ranks.append(rank)
         if last:
             across = lax.ppermute(sib_far[ROWS // 2 :], "gx", side_x)

time: 74.8 us -> 74.1 us (level)
  waiting for transfers between devices: 17 us -> 16 us
    ppermute x4, waiting for transfers between devices: 4.91 us -> 0.07 us  [local(): far = lax.ppermute(edge, 'gx', side_x)]
    ppermute x4, waiting for transfers between devices: 3.67 us -> 6.58 us  [local(): h = lax.ppermute(send, both, side_y)]
    pallas_call x4 -> x8, Pallas kernels: 4.7 us -> 5.96 us  [the longest x4 4.8 us: local(): call(functools.partial(own_kernel, k), out_shape=(shape(2, M, M), shape(2...]
    ppermute x1, waiting for transfers between devices: 0.58 us -> 1.47 us  [local(): across = lax.ppermute(sib_far[ROWS // 2:], 'gx', side_x)]
  transfers between devices with their start and end apart: 19 -> 19, of which waited for: 16 -> 13; matrix products, arithmetic and copies ran while one was open for 0% -> 0% of each run, Pallas kernels for 19% -> 21%
where the time goes in v11:
time: 74.1 us; the launch traced here: 73.8 us
  starting transfers between devices  34 us (46%)
  Pallas kernels  23 us (31%)
  waiting for transfers between devices  16 us (22%)
  between operations  0.8 us (1%)
    ppermute x4, starting transfers between devices, local(): far = lax.ppermute(edge, 'gx', side_x)  11.2 us
    all_to_all x1, starting transfers between devices, local(): gathered = lax.all_to_all(column, 'gy', 0, 0, tiled=True)  10.2 us
    pallas_call x1, Pallas kernels, local(): call(final_kernel, out_shape=shape(M, LEV, TX, TY), in_specs=[VMEM] * 4 +...  8.62 us
    ppermute x4, waiting for transfers between devices, local(): h = lax.ppermute(send, both, side_y)  6.58 us
    pallas_call x4, Pallas kernels, local(): call(functools.partial(own_kernel, k), out_shape=(shape(2, M, M), shape(2...  4.8 us
    ppermute x4, starting transfers between devices, local(): h = lax.ppermute(send, both, side_y)  4.76 us
    ppermute x4, waiting for transfers between devices, local(): sib_far = lax.ppermute(far, 'gx', core)  4.17 us
    ppermute x4, starting transfers between devices, local(): g = lax.ppermute(h, 'gx', core)  3.57 us
  transfers between devices with their start and end apart: 19, of which 13 were waited for; matrix products, arithmetic and copies ran while one was open for 0% of the time, Pallas kernels for 21%

profile of v11, /device:TPU:1, one launch (start us, length us, event | category | flops | bytes accessed | tf_op | source)
XLA Modules:
  0.0 73.8 jit_solution(13783729983872085484)
XLA Ops:
  0.6 0.0 copy-start.1
  0.6 0.0 copy-start
  0.7 3.3 %init.1.own = f32[96,256]{1,0:T(8,128)S(1)} custom-call(s32[4]{0:T(128)} %order.9, f32[4,2048]{1,0:T(4,128)} %value_hbm.1, f32[4,2048]{1,0:T(4,128)} %variance_hbm.1, s32[4,2048]{1,0:T(4,128)} %owner.9, s32[4,2048]{1,0:T(4,128)} %cell_hbm.1, s32[4,8,2048]{2,1,0:T(8,128)} %bitcast.1, f32[80,4,32,256]{3,2,1,0:T(8,128)} %x.1), custom_call_target="tpu_custom_call" | custom-call | tf_op jit(solution)/shard_map/init/pallas_call | solution.py:384
  3.9 1.5 %collective-permute-start = (f32[96,256]{1,0:T(8,128)S(1)}, f32[96,256]{1,0:T(8,128)S(1)}, u32[]{:S(2)}, u32[]{:S(2)}) collective-permute-start(f32[96,256]{1,0:T(8,128)S(1)} %init.1.own), channel_id=1, source_target_pairs={{0,16},{32,48},{64,80},{96,112},{16,0},{48,32},{80,64},{112,96},{1... | collective-permute-start | bytes 294920 | tf_op jit(solution)/shard_map/ppermute | solution.py:406
  5.4 0.9 %collective-permute-done.sib = f32[96,256]{1,0:T(8,128)S(1)} collective-permute-done((f32[96,256]{1,0:T(8,128)S(1)}, f32[96,256]{1,0:T(8,128)S(1)}, u32[]{:S(2)}, u32[]{:S(2)}) %collective-permute-start) | collective-permute-done | bytes 98336 | tf_op jit(solution)/shard_map/ppermute | solution.py:406
  6.4 0.2 start.1
  6.5 2.9 %collective-permute-start.1 = (f32[48,128]{1,0:T(8,128)S(1)}, f32[48,128]{1,0:T(8,128)S(1)}, u32[]{:S(2)}, u32[]{:S(2)}) collective-permute-start(f32[48,128]{1,0:T(8,128)S(1)} %get-tuple-element.54), channel_id=1, source_target_pairs={{0,32},{64,96},{48,80},{112,16},{32,0},{96,64},{80,48},{16,112},{1... | collective-permute-start | bytes 73736 | tf_op jit(solution)/shard_map/ppermute | solution.py:410
  9.4 0.0 copy-done.1
  9.4 0.0 copy-done
  9.4 1.2 %own.4 = (f32[2,80,80]{2,1,0:T(8,128)S(1)}, f32[2,80,80]{2,1,0:T(8,128)S(1)}, f32[1,2048]{1,0:T(1,128)S(1)}) custom-call(s32[4]{0:T(128)S(1)} %copy-done.1, s32[4,2048]{1,0:T(4,128)S(1)} %copy-done, f32[2,48,128]{2,1,0:T(8,128)S(1)} %get-tuple-element.55.pay), custom_call_target="tpu_custom_call" | custom-call | tf_op jit(solution)/shard_map/own/pallas_call | solution.py:411
  10.6 0.0 collective-permute-done.1.far
  10.6 0.2 collective-permute-start.2
  10.8 1.1 %collective-permute-done.2.sib_far = f32[48,128]{1,0:T(8,128)S(1)} collective-permute-done((f32[48,128]{1,0:T(8,128)S(1)}, f32[48,128]{1,0:T(8,128)S(1)}, u32[]{:S(2)}, u32[]{:S(2)}) %collective-permute-start.2) | collective-permute-done | bytes 24608 | tf_op jit(solution)/shard_map/ppermute | solution.py:419
  11.9 0.3 send.4
  12.2 1.2 %collective-permute-start.3 = (f32[2,80,80]{2,1,0:T(8,128)S(1)}, f32[2,80,80]{2,1,0:T(8,128)S(1)}, u32[]{:S(2)}, u32[]{:S(2)}) collective-permute-start(f32[2,80,80]{2,1,0:T(8,128)S(1)} %send.4), channel_id=1, source_target_pairs={{0,1},{2,3},{4,5},{6,7},{8,9},{10,11},{12,13},{14,15},{17,18},{19,... | collective-permute-start | bytes 153608 | tf_op jit(solution)/shard_map/ppermute | solution.py:424
  13.4 0.3 same.4.q0
  13.7 2.2 %collective-permute-done.3.h = f32[2,80,80]{2,1,0:T(8,128)S(1)} collective-permute-done((f32[2,80,80]{2,1,0:T(8,128)S(1)}, f32[2,80,80]{2,1,0:T(8,128)S(1)}, u32[]{:S(2)}, u32[]{:S(2)}) %collective-permute-start.3) | collective-permute-done | bytes 51232 | tf_op jit(solution)/shard_map/ppermute | solution.py:424
  15.9 1.0 %collective-permute-start.4 = (f32[2,80,80]{2,1,0:T(8,128)S(1)}, f32[2,80,80]{2,1,0:T(8,128)S(1)}, u32[]{:S(2)}, u32[]{:S(2)}) collective-permute-start(f32[2,80,80]{2,1,0:T(8,128)S(1)} %collective-permute-done.3.h), channel_id=1, source_target_pairs={{0,16},{32,48},{64,80},{96,112},{16,0},{48,32},{80,64},{112,96},{1... | collective-permute-start | bytes 153608 | tf_op jit(solution)/shard_map/ppermute | solution.py:439
  16.9 0.9 %collective-permute-done.4.g = f32[2,80,80]{2,1,0:T(8,128)S(1)} collective-permute-done((f32[2,80,80]{2,1,0:T(8,128)S(1)}, f32[2,80,80]{2,1,0:T(8,128)S(1)}, u32[]{:S(2)}, u32[]{:S(2)}) %collective-permute-start.4) | collective-permute-done | bytes 51232 | tf_op jit(solution)/shard_map/ppermute | solution.py:439
  17.8 0.4 step.3
  18.2 2.8 %collective-permute-start.5 = (f32[48,128]{1,0:T(8,128)S(1)}, f32[48,128]{1,0:T(8,128)S(1)}, u32[]{:S(2)}, u32[]{:S(2)}) collective-permute-start(f32[48,128]{1,0:T(8,128)S(1)} %get-tuple-element.65), channel_id=1, source_target_pairs={{0,32},{64,96},{48,80},{112,16},{32,0},{96,64},{80,48},{16,112},{1... | collective-permute-start | bytes 73736 | tf_op jit(solution)/shard_map/ppermute | solution.py:410
  20.9 1.2 %own.5 = (f32[2,80,80]{2,1,0:T(8,128)S(1)}, f32[2,80,80]{2,1,0:T(8,128)S(1)}, f32[1,2048]{1,0:T(1,128)S(1)}) custom-call(s32[4]{0:T(128)S(1)} %copy-done.1, s32[4,2048]{1,0:T(4,128)S(1)} %copy-done, f32[2,48,128]{2,1,0:T(8,128)S(1)} %get-tuple-element.66.pay), custom_call_target="tpu_custom_call" | custom-call | tf_op jit(solution)/shard_map/own/pallas_call | solution.py:411
  22.2 0.0 collective-permute-done.5.far
  22.2 0.2 collective-permute-start.6
  22.4 1.0 %collective-permute-done.6.sib_far = f32[48,128]{1,0:T(8,128)S(1)} collective-permute-done((f32[48,128]{1,0:T(8,128)S(1)}, f32[48,128]{1,0:T(8,128)S(1)}, u32[]{:S(2)}, u32[]{:S(2)}) %collective-permute-start.6) | collective-permute-done | bytes 24608 | tf_op jit(solution)/shard_map/ppermute | solution.py:419
  23.4 0.3 send.5
  23.7 1.2 %collective-permute-start.7 = (f32[2,80,80]{2,1,0:T(8,128)S(1)}, f32[2,80,80]{2,1,0:T(8,128)S(1)}, u32[]{:S(2)}, u32[]{:S(2)}) collective-permute-start(f32[2,80,80]{2,1,0:T(8,128)S(1)} %send.5), channel_id=1, source_target_pairs={{0,1},{2,3},{4,5},{6,7},{8,9},{10,11},{12,13},{14,15},{17,18},{19,... | collective-permute-start | bytes 153608 | tf_op jit(solution)/shard_map/ppermute | solution.py:424
  24.9 0.3 same.5.q0
  25.2 2.2 %collective-permute-done.7.h = f32[2,80,80]{2,1,0:T(8,128)S(1)} collective-permute-done((f32[2,80,80]{2,1,0:T(8,128)S(1)}, f32[2,80,80]{2,1,0:T(8,128)S(1)}, u32[]{:S(2)}, u32[]{:S(2)}) %collective-permute-start.7) | collective-permute-done | bytes 51232 | tf_op jit(solution)/shard_map/ppermute | solution.py:424
  27.4 1.0 %collective-permute-start.8 = (f32[2,80,80]{2,1,0:T(8,128)S(1)}, f32[2,80,80]{2,1,0:T(8,128)S(1)}, u32[]{:S(2)}, u32[]{:S(2)}) collective-permute-start(f32[2,80,80]{2,1,0:T(8,128)S(1)} %collective-permute-done.7.h), channel_id=1, source_target_pairs={{0,16},{32,48},{64,80},{96,112},{16,0},{48,32},{80,64},{112,96},{1... | collective-permute-start | bytes 153608 | tf_op jit(solution)/shard_map/ppermute | solution.py:439
  28.4 0.9 %collective-permute-done.8.g = f32[2,80,80]{2,1,0:T(8,128)S(1)} collective-permute-done((f32[2,80,80]{2,1,0:T(8,128)S(1)}, f32[2,80,80]{2,1,0:T(8,128)S(1)}, u32[]{:S(2)}, u32[]{:S(2)}) %collective-permute-start.8) | collective-permute-done | bytes 51232 | tf_op jit(solution)/shard_map/ppermute | solution.py:439
  29.3 0.4 step.4
  29.7 2.8 %collective-permute-start.9 = (f32[48,128]{1,0:T(8,128)S(1)}, f32[48,128]{1,0:T(8,128)S(1)}, u32[]{:S(2)}, u32[]{:S(2)}) collective-permute-start(f32[48,128]{1,0:T(8,128)S(1)} %get-tuple-element.76), channel_id=1, source_target_pairs={{0,32},{64,96},{48,80},{112,16},{32,0},{96,64},{80,48},{16,112},{1... | collective-permute-start | bytes 73736 | tf_op jit(solution)/shard_map/ppermute | solution.py:410
  32.5 1.2 %own.6 = (f32[2,80,80]{2,1,0:T(8,128)S(1)}, f32[2,80,80]{2,1,0:T(8,128)S(1)}, f32[1,2048]{1,0:T(1,128)S(1)}) custom-call(s32[4]{0:T(128)S(1)} %copy-done.1, s32[4,2048]{1,0:T(4,128)S(1)} %copy-done, f32[2,48,128]{2,1,0:T(8,128)S(1)} %get-tuple-element.77.pay), custom_call_target="tpu_custom_call" | custom-call | tf_op jit(solution)/shard_map/own/pallas_call | solution.py:411
  33.7 0.0 collective-permute-done.9.far
  33.7 0.2 collective-permute-start.10
  34.0 1.0 %collective-permute-done.10.sib_far = f32[48,128]{1,0:T(8,128)S(1)} collective-permute-done((f32[48,128]{1,0:T(8,128)S(1)}, f32[48,128]{1,0:T(8,128)S(1)}, u32[]{:S(2)}, u32[]{:S(2)}) %collective-permute-start.10) | collective-permute-done | bytes 24608 | tf_op jit(solution)/shard_map/ppermute | solution.py:419
  35.0 0.3 send.6
  35.3 1.2 %collective-permute-start.11 = (f32[2,80,80]{2,1,0:T(8,128)S(1)}, f32[2,80,80]{2,1,0:T(8,128)S(1)}, u32[]{:S(2)}, u32[]{:S(2)}) collective-permute-start(f32[2,80,80]{2,1,0:T(8,128)S(1)} %send.6), channel_id=1, source_target_pairs={{0,1},{2,3},{4,5},{6,7},{8,9},{10,11},{12,13},{14,15},{17,18},{19,... | collective-permute-start | bytes 153608 | tf_op jit(solution)/shard_map/ppermute | solution.py:424
  36.5 0.3 same.6.q0
  36.8 2.2 %collective-permute-done.11.h = f32[2,80,80]{2,1,0:T(8,128)S(1)} collective-permute-done((f32[2,80,80]{2,1,0:T(8,128)S(1)}, f32[2,80,80]{2,1,0:T(8,128)S(1)}, u32[]{:S(2)}, u32[]{:S(2)}) %collective-permute-start.11) | collective-permute-done | bytes 51232 | tf_op jit(solution)/shard_map/ppermute | solution.py:424
  39.0 1.0 %collective-permute-start.12 = (f32[2,80,80]{2,1,0:T(8,128)S(1)}, f32[2,80,80]{2,1,0:T(8,128)S(1)}, u32[]{:S(2)}, u32[]{:S(2)}) collective-permute-start(f32[2,80,80]{2,1,0:T(8,128)S(1)} %collective-permute-done.11.h), channel_id=1, source_target_pairs={{0,16},{32,48},{64,80},{96,112},{16,0},{48,32},{80,64},{112,96},{1... | collective-permute-start | bytes 153608 | tf_op jit(solution)/shard_map/ppermute | solution.py:439
  40.0 0.9 %collective-permute-done.12.g = f32[2,80,80]{2,1,0:T(8,128)S(1)} collective-permute-done((f32[2,80,80]{2,1,0:T(8,128)S(1)}, f32[2,80,80]{2,1,0:T(8,128)S(1)}, u32[]{:S(2)}, u32[]{:S(2)}) %collective-permute-start.12) | collective-permute-done | bytes 51232 | tf_op jit(solution)/shard_map/ppermute | solution.py:439
  40.9 0.4 step.5
  41.3 2.8 %collective-permute-start.13 = (f32[56,128]{1,0:T(8,128)S(1)}, f32[56,128]{1,0:T(8,128)S(1)}, u32[]{:S(2)}, u32[]{:S(2)}) collective-permute-start(f32[56,128]{1,0:T(8,128)S(1)} %get-tuple-element.87), channel_id=1, source_target_pairs={{0,32},{64,96},{48,80},{112,16},{32,0},{96,64},{80,48},{16,112},{1... | collective-permute-start | bytes 86024 | tf_op jit(solution)/shard_map/ppermute | solution.py:410
  44.0 1.2 %own.7 = (f32[2,80,80]{2,1,0:T(8,128)S(1)}, f32[2,80,80]{2,1,0:T(8,128)S(1)}, f32[1,2048]{1,0:T(1,128)S(1)}) custom-call(s32[4]{0:T(128)S(1)} %copy-done.1, s32[4,2048]{1,0:T(4,128)S(1)} %copy-done, f32[2,48,128]{2,1,0:T(8,128)S(1)} %get-tuple-element.88.pay), custom_call_target="tpu_custom_call" | custom-call | tf_op jit(solution)/shard_map/own/pallas_call | solution.py:411
  45.3 0.1 collective-permute-done.13.far
  45.3 0.2 collective-permute-start.14
  45.6 1.0 %collective-permute-done.14.sib_far = f32[56,128]{1,0:T(8,128)S(1)} collective-permute-done((f32[56,128]{1,0:T(8,128)S(1)}, f32[56,128]{1,0:T(8,128)S(1)}, u32[]{:S(2)}, u32[]{:S(2)}) %collective-permute-start.14) | collective-permute-done | bytes 28704 | tf_op jit(solution)/shard_map/ppermute | solution.py:419
  46.5 0.3 send.7
  46.8 1.2 %collective-permute-start.15 = (f32[2,80,80]{2,1,0:T(8,128)S(1)}, f32[2,80,80]{2,1,0:T(8,128)S(1)}, u32[]{:S(2)}, u32[]{:S(2)}) collective-permute-start(f32[2,80,80]{2,1,0:T(8,128)S(1)} %send.7), channel_id=1, source_target_pairs={{0,1},{2,3},{4,5},{6,7},{8,9},{10,11},{12,13},{14,15},{17,18},{19,... | collective-permute-start | bytes 153608 | tf_op jit(solution)/shard_map/ppermute | solution.py:424
  48.1 1.9 %collective-permute-start.16 = (f32[8,128]{1,0:T(8,128)S(1)}, f32[8,128]{1,0:T(8,128)S(1)}, u32[]{:S(2)}, u32[]{:S(2)}) collective-permute-start(f32[8,128]{1,0:T(8,128)S(1)} %slice.3), channel_id=1, source_target_pairs={{0,32},{64,96},{48,80},{112,16},{32,0},{96,64},{80,48},{16,112},{1... | collective-permute-start | bytes 12296 | tf_op jit(solution)/shard_map/ppermute | solution.py:430
  50.0 0.3 same.7.q0
  50.3 1.5 %collective-permute-done.16.across = f32[8,128]{1,0:T(8,128)S(1)} collective-permute-done((f32[8,128]{1,0:T(8,128)S(1)}, f32[8,128]{1,0:T(8,128)S(1)}, u32[]{:S(2)}, u32[]{:S(2)}) %collective-permute-start.16) | collective-permute-done | bytes 4128 | tf_op jit(solution)/shard_map/ppermute | solution.py:430
  51.7 0.7 column.1
  52.4 0.0 collective-permute-done.15.h
  52.4 0.5 collective-permute-start.17
  52.9 10.2 %all-to-all-start = ((f32[16,16,128]{2,1,0:T(8,128)}), f32[16,16,128]{2,1,0:T(8,128)S(1)}, u32[]{:S(2)}, u32[]{:S(2)}) async-start(f32[16,16,128]{2,1,0:T(8,128)} %column.1), calls=%async_computation | async-start | bytes 262144 | tf_op jit(solution)/shard_map/all_to_all | solution.py:436
  63.1 0.0 collective-permute-done.17.g
  63.1 8.6 %final.1 = f32[80,4,32,256]{3,2,1,0:T(8,128)} custom-call(f32[2,80,80]{2,1,0:T(8,128)S(1)} %same.7.q0, f32[2,80,80]{2,1,0:T(8,128)S(1)} %collective-permute-done.15.h, f32[2,80,80]{2,1,0:T(8,128)S(1)} %collective-permute-done.17.g, f32[2,96,384]{2,1,0:T(8,128)S(1)} %get-tuple-element.98.z, f32[80,4,32,256]{3,2,1,0:T(8,128)} %x.1), custom_call_target="tpu_custom_call" | custom-call | flops 1258291200 | bytes 20971520 | tf_op jit(solution)/shard_map/final/pallas_call | solution.py:453
  71.8 0.0 all-to-all-done.gathered
  71.8 2.1 %place.1 = f32[4,2048]{1,0:T(4,128)} custom-call(s32[4]{0:T(128)S(1)} %copy-done.1, s32[4,2048]{1,0:T(4,128)S(1)} %copy-done, f32[16,16,128]{2,1,0:T(8,128)S(1)} %all-to-all-done.gathered, f32[1,2048]{1,0:T(1,128)S(1)} %get-tuple-element.102.r0, f32[1,2048]{1,0:T(1,128)S(1)} %get-tuple-element.103.r1, f32[1,2048]{1,0:T(1,128)S(1)} %get-tuple-element.104.r2, ...), custom_call_target="tpu_custom_call" | custom-call | tf_op jit(solution)/shard_map/place/pallas_call | solution.py:463
  (1 shorter events, 0.0 us)
Async XLA Ops:
  0.6 8.8 %copy-start.1 = (s32[4]{0:T(128)S(1)}, s32[4]{0:T(128)}, u32[]{:S(2)}) copy-start(s32[4]{0:T(128)} %order.9) | copy-start | bytes 52
  0.6 8.8 %copy-start = (s32[4,2048]{1,0:T(4,128)S(1)}, s32[4,2048]{1,0:T(4,128)}, u32[]{:S(2)}) copy-start(s32[4,2048]{1,0:T(4,128)} %owner.9) | copy-start | bytes 98308
  3.9 2.5 %collective-permute-start = (f32[96,256]{1,0:T(8,128)S(1)}, f32[96,256]{1,0:T(8,128)S(1)}, u32[]{:S(2)}, u32[]{:S(2)}) collective-permute-start(f32[96,256]{1,0:T(8,128)S(1)} %init.1.own), channel_id=1, source_target_pairs={{0,16},{32,48},{64,80},{96,112},{16,0},{48,32},{80,64},{112,96},{1... | collective-permute-start | bytes 294920 | tf_op jit(solution)/shard_map/ppermute | solution.py:406
  6.5 4.1 %collective-permute-start.1 = (f32[48,128]{1,0:T(8,128)S(1)}, f32[48,128]{1,0:T(8,128)S(1)}, u32[]{:S(2)}, u32[]{:S(2)}) collective-permute-start(f32[48,128]{1,0:T(8,128)S(1)} %get-tuple-element.54), channel_id=1, source_target_pairs={{0,32},{64,96},{48,80},{112,16},{32,0},{96,64},{80,48},{16,112},{1... | collective-permute-start | bytes 73736 | tf_op jit(solution)/shard_map/ppermute | solution.py:410
  10.6 1.3 %collective-permute-start.2 = (f32[48,128]{1,0:T(8,128)S(1)}, f32[48,128]{1,0:T(8,128)S(1)}, u32[]{:S(2)}, u32[]{:S(2)}) collective-permute-start(f32[48,128]{1,0:T(8,128)S(1)} %collective-permute-done.1.far), channel_id=1, source_target_pairs={{0,16},{32,48},{64,80},{96,112},{16,0},{48,32},{80,64},{112,96},{1... | collective-permute-start | bytes 73736 | tf_op jit(solution)/shard_map/ppermute | solution.py:419
  12.2 3.7 %collective-permute-start.3 = (f32[2,80,80]{2,1,0:T(8,128)S(1)}, f32[2,80,80]{2,1,0:T(8,128)S(1)}, u32[]{:S(2)}, u32[]{:S(2)}) collective-permute-start(f32[2,80,80]{2,1,0:T(8,128)S(1)} %send.4), channel_id=1, source_target_pairs={{0,1},{2,3},{4,5},{6,7},{8,9},{10,11},{12,13},{14,15},{17,18},{19,... | collective-permute-start | bytes 153608 | tf_op jit(solution)/shard_map/ppermute | solution.py:424
  15.9 1.9 %collective-permute-start.4 = (f32[2,80,80]{2,1,0:T(8,128)S(1)}, f32[2,80,80]{2,1,0:T(8,128)S(1)}, u32[]{:S(2)}, u32[]{:S(2)}) collective-permute-start(f32[2,80,80]{2,1,0:T(8,128)S(1)} %collective-permute-done.3.h), channel_id=1, source_target_pairs={{0,16},{32,48},{64,80},{96,112},{16,0},{48,32},{80,64},{112,96},{1... | collective-permute-start | bytes 153608 | tf_op jit(solution)/shard_map/ppermute | solution.py:439
  18.2 4.0 %collective-permute-start.5 = (f32[48,128]{1,0:T(8,128)S(1)}, f32[48,128]{1,0:T(8,128)S(1)}, u32[]{:S(2)}, u32[]{:S(2)}) collective-permute-start(f32[48,128]{1,0:T(8,128)S(1)} %get-tuple-element.65), channel_id=1, source_target_pairs={{0,32},{64,96},{48,80},{112,16},{32,0},{96,64},{80,48},{16,112},{1... | collective-permute-start | bytes 73736 | tf_op jit(solution)/shard_map/ppermute | solution.py:410
  22.2 1.3 %collective-permute-start.6 = (f32[48,128]{1,0:T(8,128)S(1)}, f32[48,128]{1,0:T(8,128)S(1)}, u32[]{:S(2)}, u32[]{:S(2)}) collective-permute-start(f32[48,128]{1,0:T(8,128)S(1)} %collective-permute-done.5.far), channel_id=1, source_target_pairs={{0,16},{32,48},{64,80},{96,112},{16,0},{48,32},{80,64},{112,96},{1... | collective-permute-start | bytes 73736 | tf_op jit(solution)/shard_map/ppermute | solution.py:419
  23.7 3.7 %collective-permute-start.7 = (f32[2,80,80]{2,1,0:T(8,128)S(1)}, f32[2,80,80]{2,1,0:T(8,128)S(1)}, u32[]{:S(2)}, u32[]{:S(2)}) collective-permute-start(f32[2,80,80]{2,1,0:T(8,128)S(1)} %send.5), channel_id=1, source_target_pairs={{0,1},{2,3},{4,5},{6,7},{8,9},{10,11},{12,13},{14,15},{17,18},{19,... | collective-permute-start | bytes 153608 | tf_op jit(solution)/shard_map/ppermute | solution.py:424
  27.4 1.9 %collective-permute-start.8 = (f32[2,80,80]{2,1,0:T(8,128)S(1)}, f32[2,80,80]{2,1,0:T(8,128)S(1)}, u32[]{:S(2)}, u32[]{:S(2)}) collective-permute-start(f32[2,80,80]{2,1,0:T(8,128)S(1)} %collective-permute-done.7.h), channel_id=1, source_target_pairs={{0,16},{32,48},{64,80},{96,112},{16,0},{48,32},{80,64},{112,96},{1... | collective-permute-start | bytes 153608 | tf_op jit(solution)/shard_map/ppermute | solution.py:439
  29.7 4.0 %collective-permute-start.9 = (f32[48,128]{1,0:T(8,128)S(1)}, f32[48,128]{1,0:T(8,128)S(1)}, u32[]{:S(2)}, u32[]{:S(2)}) collective-permute-start(f32[48,128]{1,0:T(8,128)S(1)} %get-tuple-element.76), channel_id=1, source_target_pairs={{0,32},{64,96},{48,80},{112,16},{32,0},{96,64},{80,48},{16,112},{1... | collective-permute-start | bytes 73736 | tf_op jit(solution)/shard_map/ppermute | solution.py:410
  33.7 1.3 %collective-permute-start.10 = (f32[48,128]{1,0:T(8,128)S(1)}, f32[48,128]{1,0:T(8,128)S(1)}, u32[]{:S(2)}, u32[]{:S(2)}) collective-permute-start(f32[48,128]{1,0:T(8,128)S(1)} %collective-permute-done.9.far), channel_id=1, source_target_pairs={{0,16},{32,48},{64,80},{96,112},{16,0},{48,32},{80,64},{112,96},{1... | collective-permute-start | bytes 73736 | tf_op jit(solution)/shard_map/ppermute | solution.py:419
  35.3 3.7 %collective-permute-start.11 = (f32[2,80,80]{2,1,0:T(8,128)S(1)}, f32[2,80,80]{2,1,0:T(8,128)S(1)}, u32[]{:S(2)}, u32[]{:S(2)}) collective-permute-start(f32[2,80,80]{2,1,0:T(8,128)S(1)} %send.6), channel_id=1, source_target_pairs={{0,1},{2,3},{4,5},{6,7},{8,9},{10,11},{12,13},{14,15},{17,18},{19,... | collective-permute-start | bytes 153608 | tf_op jit(solution)/shard_map/ppermute | solution.py:424
  39.0 1.9 %collective-permute-start.12 = (f32[2,80,80]{2,1,0:T(8,128)S(1)}, f32[2,80,80]{2,1,0:T(8,128)S(1)}, u32[]{:S(2)}, u32[]{:S(2)}) collective-permute-start(f32[2,80,80]{2,1,0:T(8,128)S(1)} %collective-permute-done.11.h), channel_id=1, source_target_pairs={{0,16},{32,48},{64,80},{96,112},{16,0},{48,32},{80,64},{112,96},{1... | collective-permute-start | bytes 153608 | tf_op jit(solution)/shard_map/ppermute | solution.py:439
  41.3 4.0 %collective-permute-start.13 = (f32[56,128]{1,0:T(8,128)S(1)}, f32[56,128]{1,0:T(8,128)S(1)}, u32[]{:S(2)}, u32[]{:S(2)}) collective-permute-start(f32[56,128]{1,0:T(8,128)S(1)} %get-tuple-element.87), channel_id=1, source_target_pairs={{0,32},{64,96},{48,80},{112,16},{32,0},{96,64},{80,48},{16,112},{1... | collective-permute-start | bytes 86024 | tf_op jit(solution)/shard_map/ppermute | solution.py:410
  45.3 1.2 %collective-permute-start.14 = (f32[56,128]{1,0:T(8,128)S(1)}, f32[56,128]{1,0:T(8,128)S(1)}, u32[]{:S(2)}, u32[]{:S(2)}) collective-permute-start(f32[56,128]{1,0:T(8,128)S(1)} %collective-permute-done.13.far), channel_id=1, source_target_pairs={{0,16},{32,48},{64,80},{96,112},{16,0},{48,32},{80,64},{112,96},{1... | collective-permute-start | bytes 86024 | tf_op jit(solution)/shard_map/ppermute | solution.py:419
  46.8 5.6 %collective-permute-start.15 = (f32[2,80,80]{2,1,0:T(8,128)S(1)}, f32[2,80,80]{2,1,0:T(8,128)S(1)}, u32[]{:S(2)}, u32[]{:S(2)}) collective-permute-start(f32[2,80,80]{2,1,0:T(8,128)S(1)} %send.7), channel_id=1, source_target_pairs={{0,1},{2,3},{4,5},{6,7},{8,9},{10,11},{12,13},{14,15},{17,18},{19,... | collective-permute-start | bytes 153608 | tf_op jit(solution)/shard_map/ppermute | solution.py:424
  48.1 3.7 %collective-permute-start.16 = (f32[8,128]{1,0:T(8,128)S(1)}, f32[8,128]{1,0:T(8,128)S(1)}, u32[]{:S(2)}, u32[]{:S(2)}) collective-permute-start(f32[8,128]{1,0:T(8,128)S(1)} %slice.3), channel_id=1, source_target_pairs={{0,32},{64,96},{48,80},{112,16},{32,0},{96,64},{80,48},{16,112},{1... | collective-permute-start | bytes 12296 | tf_op jit(solution)/shard_map/ppermute | solution.py:430
  52.4 10.7 %collective-permute-start.17 = (f32[2,80,80]{2,1,0:T(8,128)S(1)}, f32[2,80,80]{2,1,0:T(8,128)S(1)}, u32[]{:S(2)}, u32[]{:S(2)}) collective-permute-start(f32[2,80,80]{2,1,0:T(8,128)S(1)} %collective-permute-done.15.h), channel_id=1, source_target_pairs={{0,16},{32,48},{64,80},{96,112},{16,0},{48,32},{80,64},{112,96},{1... | collective-permute-start | bytes 153608 | tf_op jit(solution)/shard_map/ppermute | solution.py:439
  52.9 18.8 %all-to-all-start = ((f32[16,16,128]{2,1,0:T(8,128)}), f32[16,16,128]{2,1,0:T(8,128)S(1)}, u32[]{:S(2)}, u32[]{:S(2)}) async-start(f32[16,16,128]{2,1,0:T(8,128)} %column.1), calls=%async_computation | async-start | bytes 262144 | tf_op jit(solution)/shard_map/all_to_all | solution.py:436

commit v12 on v11

--- a/solution.py
+++ b/solution.py
@@ -21,6 +21,7 @@
 SLAB = 16
 PARTS = TX // SLAB
 SLABS = LEV * PARTS
+EARLY = 2
 
 ROW_A = M
 ROW_C = M + 1
@@ -304,28 +305,41 @@
     emit(k, new, z_out, pay_out, edge_out, news_out)
 
 
-def final_kernel(q0, h, g, z, x, out, come, go, come_sems, go_sems):
-    def part(ref, i):
-        return ref.at[:, i // PARTS, pl.ds((i % PARTS) * SLAB, SLAB), :]
-
-    loads = [pltpu.make_async_copy(part(x, i), come.at[i], come_sems.at[i]) for i in range(SLABS)]
-    stores = [pltpu.make_async_copy(go.at[i], part(out, i), go_sems.at[i]) for i in range(SLABS)]
+def early_kernel(x, out, sems):
+    loads = [pltpu.make_async_copy(part(x, i), out.at[i], sems.at[i]) for i in range(EARLY)]
+    for load in loads:
+        load.start()
+    for load in loads:
+        load.wait()
+
+
+def part(ref, i, at=0, rows=SLAB):
+    return ref.at[:, i // PARTS, pl.ds((i % PARTS) * SLAB + at, rows), :]
+
+
+def final_kernel(q0, h, g, z, early, x, out, come, go, come_sems, go_sems):
+    loads = [pltpu.make_async_copy(part(x, i), come.at[i - EARLY], come_sems.at[i - EARLY]) for i in range(EARLY, SLABS)]
     for load in loads:
         load.start()
     c = core_of()
     t = advance(z[c, :M, NB * CAP :], whole_gain(c, q0, h, g))[:, :M]
     th, tl = split2(t)
     w = jnp.concatenate([th, th, tl], axis=1)
+    stores = []
     for i in range(SLABS):
-        loads[i].wait()
+        if i >= EARLY:
+            loads[i - EARLY].wait()
         for j in range(0, SLAB, 8):
-            turned = jnp.swapaxes(come[i, :, j : j + 8, :], 0, 1)
+            block = early[i, :, j : j + 8, :] if i < EARLY else come[i - EARLY, :, j : j + 8, :]
+            turned = jnp.swapaxes(block, 0, 1)
             rows = []
             for r in range(8):
                 xh, xl = split2(turned[r])
                 rows.append(dot(w, jnp.concatenate([xh, xl, xh], axis=0))[None])
             go[i, :, j : j + 8, :] = jnp.swapaxes(jnp.concatenate(rows, axis=0), 0, 1)
-        stores[i].start()
+            sem = go_sems.at[i * (SLAB // 8) + j // 8]
+            stores.append(pltpu.make_async_copy(go.at[i, :, pl.ds(j, 8), :], part(out, i, j, 8), sem))
+            stores[-1].start()
     for store in stores:
         store.wait()
 
@@ -405,6 +419,7 @@
         name="start",
     )(own, lax.ppermute(own, "gx", core))
     ranks = []
+    state_hbm = pltpu.with_memory_space_constraint(ensemble, pltpu.HBM)
     for k in range(NB):
         last = k + 1 == NB
         far = lax.ppermute(edge, "gx", side_x)
@@ -415,7 +430,18 @@
             out_specs=(VMEM,) * 3,
             name="own",
         )(batch_order, obs_owner, pay)
-        far, own_toward = lax.optimization_barrier((far, own_toward))
+        if last:
+            early = call(
+                early_kernel,
+                out_shape=shape(EARLY, M, SLAB, TY),
+                in_specs=[HBM],
+                out_specs=VMEM,
+                scratch_shapes=[pltpu.SemaphoreType.DMA((EARLY,))],
+                name="early",
+            )(state_hbm)
+            far, own_toward, early = lax.optimization_barrier((far, own_toward, early))
+        else:
+            far, own_toward = lax.optimization_barrier((far, own_toward))
         sib_far = lax.ppermute(far, "gx", core)
         send = call(send_kernel, out_shape=shape(2, M, M), in_specs=[VMEM] * 3, out_specs=VMEM, name="send")(
             own_toward, far, sib_far
@@ -449,16 +475,18 @@
             )(q0, h, g, z)
             if tail:
                 news = rest[0]
-    slabs = pltpu.VMEM((SLABS, M, SLAB, TY), F32)
     state = call(
         final_kernel,
         out_shape=shape(M, LEV, TX, TY),
-        in_specs=[VMEM] * 4 + [HBM],
+        in_specs=[VMEM] * 5 + [HBM],
         out_specs=HBM,
-        scratch_shapes=[slabs, slabs, pltpu.SemaphoreType.DMA((SLABS,)), pltpu.SemaphoreType.DMA((SLABS,))],
+        scratch_shapes=[
+            pltpu.VMEM((SLABS - EARLY, M, SLAB, TY), F32), pltpu.VMEM((SLABS, M, SLAB, TY), F32),
+            pltpu.SemaphoreType.DMA((SLABS - EARLY,)), pltpu.SemaphoreType.DMA((SLABS * SLAB // 8,)),
+        ],
         cost_estimate=pl.CostEstimate(flops=6 * M * M * LEV * TX * TY, bytes_accessed=8 * M * LEV * TX * TY, transcendentals=0),
         name="final",
-    )(q0, h, g, z, pltpu.with_memory_space_constraint(ensemble, pltpu.HBM))
+    )(q0, h, g, z, early, state_hbm)
     state, gathered = lax.optimization_barrier((state, gathered))
     innovation = call(
         place_kernel,

time: 74.1 us -> 75.5 us (1.019)
  Pallas kernels: 23 us -> 24.4 us
    pallas_call x1 -> x2, Pallas kernels: 8.62 us -> 10 us  [the longest x1 8.3 us: local(): call(final_kernel, out_shape=shape(M, LEV, TX, TY), in_specs=[VMEM] * 5 +...]
    ppermute x4, starting transfers between devices: 4.76 us -> 3.62 us  [local(): h = lax.ppermute(send, both, side_y)]
    ppermute x4, starting transfers between devices: 3.57 us -> 4.56 us  [local(): g = lax.ppermute(h, 'gx', core)]
  transfers between devices with their start and end apart: 19 -> 19, of which waited for: 13 -> 12; matrix products, arithmetic and copies ran while one was open for 0% -> 0% of each run, Pallas kernels for 21% -> 22%
where the time goes in v12:
time: 75.5 us; the launch traced here: 75.2 us
  starting transfers between devices  33.5 us (44%)
  Pallas kernels  24.4 us (32%)
  waiting for transfers between devices  16.4 us (22%)
  between operations  0.84 us (1%)
    ppermute x4, starting transfers between devices, local(): far = lax.ppermute(edge, 'gx', side_x)  11.2 us
    all_to_all x1, starting transfers between devices, local(): gathered = lax.all_to_all(column, 'gy', 0, 0, tiled=True)  10.2 us
    pallas_call x1, Pallas kernels, local(): call(final_kernel, out_shape=shape(M, LEV, TX, TY), in_specs=[VMEM] * 5 +...  8.3 us
    ppermute x4, waiting for transfers between devices, local(): h = lax.ppermute(send, both, side_y)  6.58 us
    pallas_call x4, Pallas kernels, local(): call(functools.partial(own_kernel, k), out_shape=(shape(2, M, M), shape(2...  4.8 us
    ppermute x4, starting transfers between devices, local(): g = lax.ppermute(h, 'gx', core)  4.56 us
    ppermute x4, waiting for transfers between devices, local(): sib_far = lax.ppermute(far, 'gx', core)  4.36 us
    ppermute x4, starting transfers between devices, local(): h = lax.ppermute(send, both, side_y)  3.62 us
  transfers between devices with their start and end apart: 19, of which 12 were waited for; matrix products, arithmetic and copies ran while one was open for 0% of the time, Pallas kernels for 22%

profile of v12, /device:TPU:1, one launch (start us, length us, event | category | flops | bytes accessed | tf_op | source)
XLA Modules:
  0.0 75.2 jit_solution(11303863514079102431)
XLA Ops:
  0.6 0.0 copy-start.1
  0.6 0.0 copy-start
  0.7 3.3 %init.1.own = f32[96,256]{1,0:T(8,128)S(1)} custom-call(s32[4]{0:T(128)} %order.9, f32[4,2048]{1,0:T(4,128)} %value_hbm.1, f32[4,2048]{1,0:T(4,128)} %variance_hbm.1, s32[4,2048]{1,0:T(4,128)} %owner.9, s32[4,2048]{1,0:T(4,128)} %cell_hbm.1, s32[4,8,2048]{2,1,0:T(8,128)} %bitcast.1, f32[80,4,32,256]{3,2,1,0:T(8,128)} %x.3), custom_call_target="tpu_custom_call" | custom-call | tf_op jit(solution)/shard_map/init/pallas_call | solution.py:398
  3.9 1.5 %collective-permute-start = (f32[96,256]{1,0:T(8,128)S(1)}, f32[96,256]{1,0:T(8,128)S(1)}, u32[]{:S(2)}, u32[]{:S(2)}) collective-permute-start(f32[96,256]{1,0:T(8,128)S(1)} %init.1.own), channel_id=1, source_target_pairs={{0,16},{32,48},{64,80},{96,112},{16,0},{48,32},{80,64},{112,96},{1... | collective-permute-start | bytes 294920 | tf_op jit(solution)/shard_map/ppermute | solution.py:420
  5.4 0.9 %collective-permute-done.sib = f32[96,256]{1,0:T(8,128)S(1)} collective-permute-done((f32[96,256]{1,0:T(8,128)S(1)}, f32[96,256]{1,0:T(8,128)S(1)}, u32[]{:S(2)}, u32[]{:S(2)}) %collective-permute-start) | collective-permute-done | bytes 98336 | tf_op jit(solution)/shard_map/ppermute | solution.py:420
  6.4 0.2 start.1
  6.5 2.9 %collective-permute-start.1 = (f32[48,128]{1,0:T(8,128)S(1)}, f32[48,128]{1,0:T(8,128)S(1)}, u32[]{:S(2)}, u32[]{:S(2)}) collective-permute-start(f32[48,128]{1,0:T(8,128)S(1)} %get-tuple-element.55), channel_id=1, source_target_pairs={{0,32},{64,96},{48,80},{112,16},{32,0},{96,64},{80,48},{16,112},{1... | collective-permute-start | bytes 73736 | tf_op jit(solution)/shard_map/ppermute | solution.py:425
  9.4 0.0 copy-done.1
  9.4 0.0 copy-done
  9.4 1.2 %own.4 = (f32[2,80,80]{2,1,0:T(8,128)S(1)}, f32[2,80,80]{2,1,0:T(8,128)S(1)}, f32[1,2048]{1,0:T(1,128)S(1)}) custom-call(s32[4]{0:T(128)S(1)} %copy-done.1, s32[4,2048]{1,0:T(4,128)S(1)} %copy-done, f32[2,48,128]{2,1,0:T(8,128)S(1)} %get-tuple-element.56.pay), custom_call_target="tpu_custom_call" | custom-call | tf_op jit(solution)/shard_map/own/pallas_call | solution.py:426
  10.6 0.0 collective-permute-done.1.far
  10.6 0.2 collective-permute-start.2
  10.8 1.1 %collective-permute-done.2.sib_far = f32[48,128]{1,0:T(8,128)S(1)} collective-permute-done((f32[48,128]{1,0:T(8,128)S(1)}, f32[48,128]{1,0:T(8,128)S(1)}, u32[]{:S(2)}, u32[]{:S(2)}) %collective-permute-start.2) | collective-permute-done | bytes 24608 | tf_op jit(solution)/shard_map/ppermute | solution.py:445
  11.9 0.3 send.4
  12.2 1.2 %collective-permute-start.3 = (f32[2,80,80]{2,1,0:T(8,128)S(1)}, f32[2,80,80]{2,1,0:T(8,128)S(1)}, u32[]{:S(2)}, u32[]{:S(2)}) collective-permute-start(f32[2,80,80]{2,1,0:T(8,128)S(1)} %send.4), channel_id=1, source_target_pairs={{0,1},{2,3},{4,5},{6,7},{8,9},{10,11},{12,13},{14,15},{17,18},{19,... | collective-permute-start | bytes 153608 | tf_op jit(solution)/shard_map/ppermute | solution.py:450
  13.4 0.3 same.4.q0
  13.7 2.2 %collective-permute-done.3.h = f32[2,80,80]{2,1,0:T(8,128)S(1)} collective-permute-done((f32[2,80,80]{2,1,0:T(8,128)S(1)}, f32[2,80,80]{2,1,0:T(8,128)S(1)}, u32[]{:S(2)}, u32[]{:S(2)}) %collective-permute-start.3) | collective-permute-done | bytes 51232 | tf_op jit(solution)/shard_map/ppermute | solution.py:450
  15.9 1.0 %collective-permute-start.4 = (f32[2,80,80]{2,1,0:T(8,128)S(1)}, f32[2,80,80]{2,1,0:T(8,128)S(1)}, u32[]{:S(2)}, u32[]{:S(2)}) collective-permute-start(f32[2,80,80]{2,1,0:T(8,128)S(1)} %collective-permute-done.3.h), channel_id=1, source_target_pairs={{0,16},{32,48},{64,80},{96,112},{16,0},{48,32},{80,64},{112,96},{1... | collective-permute-start | bytes 153608 | tf_op jit(solution)/shard_map/ppermute | solution.py:465
  16.9 0.9 %collective-permute-done.4.g = f32[2,80,80]{2,1,0:T(8,128)S(1)} collective-permute-done((f32[2,80,80]{2,1,0:T(8,128)S(1)}, f32[2,80,80]{2,1,0:T(8,128)S(1)}, u32[]{:S(2)}, u32[]{:S(2)}) %collective-permute-start.4) | collective-permute-done | bytes 51232 | tf_op jit(solution)/shard_map/ppermute | solution.py:465
  17.8 0.4 step.3
  18.2 2.8 %collective-permute-start.5 = (f32[48,128]{1,0:T(8,128)S(1)}, f32[48,128]{1,0:T(8,128)S(1)}, u32[]{:S(2)}, u32[]{:S(2)}) collective-permute-start(f32[48,128]{1,0:T(8,128)S(1)} %get-tuple-element.66), channel_id=1, source_target_pairs={{0,32},{64,96},{48,80},{112,16},{32,0},{96,64},{80,48},{16,112},{1... | collective-permute-start | bytes 73736 | tf_op jit(solution)/shard_map/ppermute | solution.py:425
  20.9 1.2 %own.5 = (f32[2,80,80]{2,1,0:T(8,128)S(1)}, f32[2,80,80]{2,1,0:T(8,128)S(1)}, f32[1,2048]{1,0:T(1,128)S(1)}) custom-call(s32[4]{0:T(128)S(1)} %copy-done.1, s32[4,2048]{1,0:T(4,128)S(1)} %copy-done, f32[2,48,128]{2,1,0:T(8,128)S(1)} %get-tuple-element.67.pay), custom_call_target="tpu_custom_call" | custom-call | tf_op jit(solution)/shard_map/own/pallas_call | solution.py:426
  22.2 0.0 collective-permute-done.5.far
  22.2 0.2 collective-permute-start.6
  22.4 1.0 %collective-permute-done.6.sib_far = f32[48,128]{1,0:T(8,128)S(1)} collective-permute-done((f32[48,128]{1,0:T(8,128)S(1)}, f32[48,128]{1,0:T(8,128)S(1)}, u32[]{:S(2)}, u32[]{:S(2)}) %collective-permute-start.6) | collective-permute-done | bytes 24608 | tf_op jit(solution)/shard_map/ppermute | solution.py:445
  23.4 0.3 send.5
  23.7 1.2 %collective-permute-start.7 = (f32[2,80,80]{2,1,0:T(8,128)S(1)}, f32[2,80,80]{2,1,0:T(8,128)S(1)}, u32[]{:S(2)}, u32[]{:S(2)}) collective-permute-start(f32[2,80,80]{2,1,0:T(8,128)S(1)} %send.5), channel_id=1, source_target_pairs={{0,1},{2,3},{4,5},{6,7},{8,9},{10,11},{12,13},{14,15},{17,18},{19,... | collective-permute-start | bytes 153608 | tf_op jit(solution)/shard_map/ppermute | solution.py:450
  24.9 0.3 same.5.q0
  25.2 2.2 %collective-permute-done.7.h = f32[2,80,80]{2,1,0:T(8,128)S(1)} collective-permute-done((f32[2,80,80]{2,1,0:T(8,128)S(1)}, f32[2,80,80]{2,1,0:T(8,128)S(1)}, u32[]{:S(2)}, u32[]{:S(2)}) %collective-permute-start.7) | collective-permute-done | bytes 51232 | tf_op jit(solution)/shard_map/ppermute | solution.py:450
  27.4 1.0 %collective-permute-start.8 = (f32[2,80,80]{2,1,0:T(8,128)S(1)}, f32[2,80,80]{2,1,0:T(8,128)S(1)}, u32[]{:S(2)}, u32[]{:S(2)}) collective-permute-start(f32[2,80,80]{2,1,0:T(8,128)S(1)} %collective-permute-done.7.h), channel_id=1, source_target_pairs={{0,16},{32,48},{64,80},{96,112},{16,0},{48,32},{80,64},{112,96},{1... | collective-permute-start | bytes 153608 | tf_op jit(solution)/shard_map/ppermute | solution.py:465
  28.4 0.9 %collective-permute-done.8.g = f32[2,80,80]{2,1,0:T(8,128)S(1)} collective-permute-done((f32[2,80,80]{2,1,0:T(8,128)S(1)}, f32[2,80,80]{2,1,0:T(8,128)S(1)}, u32[]{:S(2)}, u32[]{:S(2)}) %collective-permute-start.8) | collective-permute-done | bytes 51232 | tf_op jit(solution)/shard_map/ppermute | solution.py:465
  29.3 0.4 step.4
  29.7 2.8 %collective-permute-start.9 = (f32[48,128]{1,0:T(8,128)S(1)}, f32[48,128]{1,0:T(8,128)S(1)}, u32[]{:S(2)}, u32[]{:S(2)}) collective-permute-start(f32[48,128]{1,0:T(8,128)S(1)} %get-tuple-element.77), channel_id=1, source_target_pairs={{0,32},{64,96},{48,80},{112,16},{32,0},{96,64},{80,48},{16,112},{1... | collective-permute-start | bytes 73736 | tf_op jit(solution)/shard_map/ppermute | solution.py:425
  32.5 1.2 %own.6 = (f32[2,80,80]{2,1,0:T(8,128)S(1)}, f32[2,80,80]{2,1,0:T(8,128)S(1)}, f32[1,2048]{1,0:T(1,128)S(1)}) custom-call(s32[4]{0:T(128)S(1)} %copy-done.1, s32[4,2048]{1,0:T(4,128)S(1)} %copy-done, f32[2,48,128]{2,1,0:T(8,128)S(1)} %get-tuple-element.78.pay), custom_call_target="tpu_custom_call" | custom-call | tf_op jit(solution)/shard_map/own/pallas_call | solution.py:426
  33.7 0.0 collective-permute-done.9.far
  33.7 0.2 collective-permute-start.10
  34.0 1.0 %collective-permute-done.10.sib_far = f32[48,128]{1,0:T(8,128)S(1)} collective-permute-done((f32[48,128]{1,0:T(8,128)S(1)}, f32[48,128]{1,0:T(8,128)S(1)}, u32[]{:S(2)}, u32[]{:S(2)}) %collective-permute-start.10) | collective-permute-done | bytes 24608 | tf_op jit(solution)/shard_map/ppermute | solution.py:445
  35.0 0.3 send.6
  35.3 1.2 %collective-permute-start.11 = (f32[2,80,80]{2,1,0:T(8,128)S(1)}, f32[2,80,80]{2,1,0:T(8,128)S(1)}, u32[]{:S(2)}, u32[]{:S(2)}) collective-permute-start(f32[2,80,80]{2,1,0:T(8,128)S(1)} %send.6), channel_id=1, source_target_pairs={{0,1},{2,3},{4,5},{6,7},{8,9},{10,11},{12,13},{14,15},{17,18},{19,... | collective-permute-start | bytes 153608 | tf_op jit(solution)/shard_map/ppermute | solution.py:450
  36.5 0.3 same.6.q0
  36.8 2.2 %collective-permute-done.11.h = f32[2,80,80]{2,1,0:T(8,128)S(1)} collective-permute-done((f32[2,80,80]{2,1,0:T(8,128)S(1)}, f32[2,80,80]{2,1,0:T(8,128)S(1)}, u32[]{:S(2)}, u32[]{:S(2)}) %collective-permute-start.11) | collective-permute-done | bytes 51232 | tf_op jit(solution)/shard_map/ppermute | solution.py:450
  39.0 1.0 %collective-permute-start.12 = (f32[2,80,80]{2,1,0:T(8,128)S(1)}, f32[2,80,80]{2,1,0:T(8,128)S(1)}, u32[]{:S(2)}, u32[]{:S(2)}) collective-permute-start(f32[2,80,80]{2,1,0:T(8,128)S(1)} %collective-permute-done.11.h), channel_id=1, source_target_pairs={{0,16},{32,48},{64,80},{96,112},{16,0},{48,32},{80,64},{112,96},{1... | collective-permute-start | bytes 153608 | tf_op jit(solution)/shard_map/ppermute | solution.py:465
  40.0 0.9 %collective-permute-done.12.g = f32[2,80,80]{2,1,0:T(8,128)S(1)} collective-permute-done((f32[2,80,80]{2,1,0:T(8,128)S(1)}, f32[2,80,80]{2,1,0:T(8,128)S(1)}, u32[]{:S(2)}, u32[]{:S(2)}) %collective-permute-start.12) | collective-permute-done | bytes 51232 | tf_op jit(solution)/shard_map/ppermute | solution.py:465
  40.9 0.4 step.5
  41.3 2.8 %collective-permute-start.13 = (f32[56,128]{1,0:T(8,128)S(1)}, f32[56,128]{1,0:T(8,128)S(1)}, u32[]{:S(2)}, u32[]{:S(2)}) collective-permute-start(f32[56,128]{1,0:T(8,128)S(1)} %get-tuple-element.88), channel_id=1, source_target_pairs={{0,32},{64,96},{48,80},{112,16},{32,0},{96,64},{80,48},{16,112},{1... | collective-permute-start | bytes 86024 | tf_op jit(solution)/shard_map/ppermute | solution.py:425
  44.0 1.7 %early.1 = f32[2,80,16,256]{3,2,1,0:T(8,128)S(1)} custom-call(f32[80,4,32,256]{3,2,1,0:T(8,128)} %x.3), custom_call_target="tpu_custom_call" | custom-call | tf_op jit(solution)/shard_map/early/pallas_call | solution.py:434
  45.8 1.2 %own.7 = (f32[2,80,80]{2,1,0:T(8,128)S(1)}, f32[2,80,80]{2,1,0:T(8,128)S(1)}, f32[1,2048]{1,0:T(1,128)S(1)}) custom-call(s32[4]{0:T(128)S(1)} %copy-done.1, s32[4,2048]{1,0:T(4,128)S(1)} %copy-done, f32[2,48,128]{2,1,0:T(8,128)S(1)} %get-tuple-element.89.pay), custom_call_target="tpu_custom_call" | custom-call | tf_op jit(solution)/shard_map/own/pallas_call | solution.py:426
  47.0 0.0 collective-permute-done.13.far
  47.0 0.1 collective-permute-start.14
  47.1 1.2 %collective-permute-done.14.sib_far = f32[56,128]{1,0:T(8,128)S(1)} collective-permute-done((f32[56,128]{1,0:T(8,128)S(1)}, f32[56,128]{1,0:T(8,128)S(1)}, u32[]{:S(2)}, u32[]{:S(2)}) %collective-permute-start.14) | collective-permute-done | bytes 28704 | tf_op jit(solution)/shard_map/ppermute | solution.py:445
  48.3 0.3 send.7
  48.6 0.1 collective-permute-start.15
  48.7 1.7 %collective-permute-start.16 = (f32[8,128]{1,0:T(8,128)S(1)}, f32[8,128]{1,0:T(8,128)S(1)}, u32[]{:S(2)}, u32[]{:S(2)}) collective-permute-start(f32[8,128]{1,0:T(8,128)S(1)} %slice.3), channel_id=1, source_target_pairs={{0,32},{64,96},{48,80},{112,16},{32,0},{96,64},{80,48},{16,112},{1... | collective-permute-start | bytes 12296 | tf_op jit(solution)/shard_map/ppermute | solution.py:456
  50.4 0.3 same.7.q0
  50.7 1.7 %collective-permute-done.16.across = f32[8,128]{1,0:T(8,128)S(1)} collective-permute-done((f32[8,128]{1,0:T(8,128)S(1)}, f32[8,128]{1,0:T(8,128)S(1)}, u32[]{:S(2)}, u32[]{:S(2)}) %collective-permute-start.16) | collective-permute-done | bytes 4128 | tf_op jit(solution)/shard_map/ppermute | solution.py:456
  52.4 0.7 column.1
  53.1 0.0 collective-permute-done.15.h
  53.1 1.5 %collective-permute-start.17 = (f32[2,80,80]{2,1,0:T(8,128)S(1)}, f32[2,80,80]{2,1,0:T(8,128)S(1)}, u32[]{:S(2)}, u32[]{:S(2)}) collective-permute-start(f32[2,80,80]{2,1,0:T(8,128)S(1)} %collective-permute-done.15.h), channel_id=1, source_target_pairs={{0,16},{32,48},{64,80},{96,112},{16,0},{48,32},{80,64},{112,96},{1... | collective-permute-start | bytes 153608 | tf_op jit(solution)/shard_map/ppermute | solution.py:465
  54.6 10.2 %all-to-all-start = ((f32[16,16,128]{2,1,0:T(8,128)}), f32[16,16,128]{2,1,0:T(8,128)S(1)}, u32[]{:S(2)}, u32[]{:S(2)}) async-start(f32[16,16,128]{2,1,0:T(8,128)} %column.1), calls=%async_computation | async-start | bytes 262144 | tf_op jit(solution)/shard_map/all_to_all | solution.py:462
  64.8 0.0 collective-permute-done.17.g
  64.8 8.3 %final.1 = f32[80,4,32,256]{3,2,1,0:T(8,128)} custom-call(f32[2,80,80]{2,1,0:T(8,128)S(1)} %same.7.q0, f32[2,80,80]{2,1,0:T(8,128)S(1)} %collective-permute-done.15.h, f32[2,80,80]{2,1,0:T(8,128)S(1)} %collective-permute-done.17.g, f32[2,96,384]{2,1,0:T(8,128)S(1)} %get-tuple-element.99.z, f32[2,80,16,256]{3,2,1,0:T(8,128)S(1)} %early.1, f32[80,4,32,256]{3,2,1,0:T(8,128)} %x.3), custom_call_target="tpu_custom_call" | custom-call | flops 1258291200 | bytes 20971520 | tf_op jit(solution)/shard_map/final/pallas_call | solution.py:478
  73.1 0.0 all-to-all-done.gathered
  73.1 2.1 %place.1 = f32[4,2048]{1,0:T(4,128)} custom-call(s32[4]{0:T(128)S(1)} %copy-done.1, s32[4,2048]{1,0:T(4,128)S(1)} %copy-done, f32[16,16,128]{2,1,0:T(8,128)S(1)} %all-to-all-done.gathered, f32[1,2048]{1,0:T(1,128)S(1)} %get-tuple-element.104.r0, f32[1,2048]{1,0:T(1,128)S(1)} %get-tuple-element.105.r1, f32[1,2048]{1,0:T(1,128)S(1)} %get-tuple-element.106.r2, ...), custom_call_target="tpu_custom_call" | custom-call | tf_op jit(solution)/shard_map/place/pallas_call | solution.py:491
  (1 shorter events, 0.0 us)
Async XLA Ops:
  0.6 8.8 %copy-start.1 = (s32[4]{0:T(128)S(1)}, s32[4]{0:T(128)}, u32[]{:S(2)}) copy-start(s32[4]{0:T(128)} %order.9) | copy-start | bytes 52
  0.6 8.8 %copy-start = (s32[4,2048]{1,0:T(4,128)S(1)}, s32[4,2048]{1,0:T(4,128)}, u32[]{:S(2)}) copy-start(s32[4,2048]{1,0:T(4,128)} %owner.9) | copy-start | bytes 98308
  3.9 2.5 %collective-permute-start = (f32[96,256]{1,0:T(8,128)S(1)}, f32[96,256]{1,0:T(8,128)S(1)}, u32[]{:S(2)}, u32[]{:S(2)}) collective-permute-start(f32[96,256]{1,0:T(8,128)S(1)} %init.1.own), channel_id=1, source_target_pairs={{0,16},{32,48},{64,80},{96,112},{16,0},{48,32},{80,64},{112,96},{1... | collective-permute-start | bytes 294920 | tf_op jit(solution)/shard_map/ppermute | solution.py:420
  6.5 4.1 %collective-permute-start.1 = (f32[48,128]{1,0:T(8,128)S(1)}, f32[48,128]{1,0:T(8,128)S(1)}, u32[]{:S(2)}, u32[]{:S(2)}) collective-permute-start(f32[48,128]{1,0:T(8,128)S(1)} %get-tuple-element.55), channel_id=1, source_target_pairs={{0,32},{64,96},{48,80},{112,16},{32,0},{96,64},{80,48},{16,112},{1... | collective-permute-start | bytes 73736 | tf_op jit(solution)/shard_map/ppermute | solution.py:425
  10.6 1.3 %collective-permute-start.2 = (f32[48,128]{1,0:T(8,128)S(1)}, f32[48,128]{1,0:T(8,128)S(1)}, u32[]{:S(2)}, u32[]{:S(2)}) collective-permute-start(f32[48,128]{1,0:T(8,128)S(1)} %collective-permute-done.1.far), channel_id=1, source_target_pairs={{0,16},{32,48},{64,80},{96,112},{16,0},{48,32},{80,64},{112,96},{1... | collective-permute-start | bytes 73736 | tf_op jit(solution)/shard_map/ppermute | solution.py:445
  12.2 3.7 %collective-permute-start.3 = (f32[2,80,80]{2,1,0:T(8,128)S(1)}, f32[2,80,80]{2,1,0:T(8,128)S(1)}, u32[]{:S(2)}, u32[]{:S(2)}) collective-permute-start(f32[2,80,80]{2,1,0:T(8,128)S(1)} %send.4), channel_id=1, source_target_pairs={{0,1},{2,3},{4,5},{6,7},{8,9},{10,11},{12,13},{14,15},{17,18},{19,... | collective-permute-start | bytes 153608 | tf_op jit(solution)/shard_map/ppermute | solution.py:450
  15.9 1.9 %collective-permute-start.4 = (f32[2,80,80]{2,1,0:T(8,128)S(1)}, f32[2,80,80]{2,1,0:T(8,128)S(1)}, u32[]{:S(2)}, u32[]{:S(2)}) collective-permute-start(f32[2,80,80]{2,1,0:T(8,128)S(1)} %collective-permute-done.3.h), channel_id=1, source_target_pairs={{0,16},{32,48},{64,80},{96,112},{16,0},{48,32},{80,64},{112,96},{1... | collective-permute-start | bytes 153608 | tf_op jit(solution)/shard_map/ppermute | solution.py:465
  18.2 4.0 %collective-permute-start.5 = (f32[48,128]{1,0:T(8,128)S(1)}, f32[48,128]{1,0:T(8,128)S(1)}, u32[]{:S(2)}, u32[]{:S(2)}) collective-permute-start(f32[48,128]{1,0:T(8,128)S(1)} %get-tuple-element.66), channel_id=1, source_target_pairs={{0,32},{64,96},{48,80},{112,16},{32,0},{96,64},{80,48},{16,112},{1... | collective-permute-start | bytes 73736 | tf_op jit(solution)/shard_map/ppermute | solution.py:425
  22.2 1.3 %collective-permute-start.6 = (f32[48,128]{1,0:T(8,128)S(1)}, f32[48,128]{1,0:T(8,128)S(1)}, u32[]{:S(2)}, u32[]{:S(2)}) collective-permute-start(f32[48,128]{1,0:T(8,128)S(1)} %collective-permute-done.5.far), channel_id=1, source_target_pairs={{0,16},{32,48},{64,80},{96,112},{16,0},{48,32},{80,64},{112,96},{1... | collective-permute-start | bytes 73736 | tf_op jit(solution)/shard_map/ppermute | solution.py:445
  23.7 3.7 %collective-permute-start.7 = (f32[2,80,80]{2,1,0:T(8,128)S(1)}, f32[2,80,80]{2,1,0:T(8,128)S(1)}, u32[]{:S(2)}, u32[]{:S(2)}) collective-permute-start(f32[2,80,80]{2,1,0:T(8,128)S(1)} %send.5), channel_id=1, source_target_pairs={{0,1},{2,3},{4,5},{6,7},{8,9},{10,11},{12,13},{14,15},{17,18},{19,... | collective-permute-start | bytes 153608 | tf_op jit(solution)/shard_map/ppermute | solution.py:450
  27.4 1.9 %collective-permute-start.8 = (f32[2,80,80]{2,1,0:T(8,128)S(1)}, f32[2,80,80]{2,1,0:T(8,128)S(1)}, u32[]{:S(2)}, u32[]{:S(2)}) collective-permute-start(f32[2,80,80]{2,1,0:T(8,128)S(1)} %collective-permute-done.7.h), channel_id=1, source_target_pairs={{0,16},{32,48},{64,80},{96,112},{16,0},{48,32},{80,64},{112,96},{1... | collective-permute-start | bytes 153608 | tf_op jit(solution)/shard_map/ppermute | solution.py:465
  29.7 4.0 %collective-permute-start.9 = (f32[48,128]{1,0:T(8,128)S(1)}, f32[48,128]{1,0:T(8,128)S(1)}, u32[]{:S(2)}, u32[]{:S(2)}) collective-permute-start(f32[48,128]{1,0:T(8,128)S(1)} %get-tuple-element.77), channel_id=1, source_target_pairs={{0,32},{64,96},{48,80},{112,16},{32,0},{96,64},{80,48},{16,112},{1... | collective-permute-start | bytes 73736 | tf_op jit(solution)/shard_map/ppermute | solution.py:425
  33.7 1.3 %collective-permute-start.10 = (f32[48,128]{1,0:T(8,128)S(1)}, f32[48,128]{1,0:T(8,128)S(1)}, u32[]{:S(2)}, u32[]{:S(2)}) collective-permute-start(f32[48,128]{1,0:T(8,128)S(1)} %collective-permute-done.9.far), channel_id=1, source_target_pairs={{0,16},{32,48},{64,80},{96,112},{16,0},{48,32},{80,64},{112,96},{1... | collective-permute-start | bytes 73736 | tf_op jit(solution)/shard_map/ppermute | solution.py:445
  35.3 3.7 %collective-permute-start.11 = (f32[2,80,80]{2,1,0:T(8,128)S(1)}, f32[2,80,80]{2,1,0:T(8,128)S(1)}, u32[]{:S(2)}, u32[]{:S(2)}) collective-permute-start(f32[2,80,80]{2,1,0:T(8,128)S(1)} %send.6), channel_id=1, source_target_pairs={{0,1},{2,3},{4,5},{6,7},{8,9},{10,11},{12,13},{14,15},{17,18},{19,... | collective-permute-start | bytes 153608 | tf_op jit(solution)/shard_map/ppermute | solution.py:450
  39.0 1.9 %collective-permute-start.12 = (f32[2,80,80]{2,1,0:T(8,128)S(1)}, f32[2,80,80]{2,1,0:T(8,128)S(1)}, u32[]{:S(2)}, u32[]{:S(2)}) collective-permute-start(f32[2,80,80]{2,1,0:T(8,128)S(1)} %collective-permute-done.11.h), channel_id=1, source_target_pairs={{0,16},{32,48},{64,80},{96,112},{16,0},{48,32},{80,64},{112,96},{1... | collective-permute-start | bytes 153608 | tf_op jit(solution)/shard_map/ppermute | solution.py:465
  41.3 5.7 %collective-permute-start.13 = (f32[56,128]{1,0:T(8,128)S(1)}, f32[56,128]{1,0:T(8,128)S(1)}, u32[]{:S(2)}, u32[]{:S(2)}) collective-permute-start(f32[56,128]{1,0:T(8,128)S(1)} %get-tuple-element.88), channel_id=1, source_target_pairs={{0,32},{64,96},{48,80},{112,16},{32,0},{96,64},{80,48},{16,112},{1... | collective-permute-start | bytes 86024 | tf_op jit(solution)/shard_map/ppermute | solution.py:425
  47.0 1.3 %collective-permute-start.14 = (f32[56,128]{1,0:T(8,128)S(1)}, f32[56,128]{1,0:T(8,128)S(1)}, u32[]{:S(2)}, u32[]{:S(2)}) collective-permute-start(f32[56,128]{1,0:T(8,128)S(1)} %collective-permute-done.13.far), channel_id=1, source_target_pairs={{0,16},{32,48},{64,80},{96,112},{16,0},{48,32},{80,64},{112,96},{1... | collective-permute-start | bytes 86024 | tf_op jit(solution)/shard_map/ppermute | solution.py:445
  48.6 4.5 %collective-permute-start.15 = (f32[2,80,80]{2,1,0:T(8,128)S(1)}, f32[2,80,80]{2,1,0:T(8,128)S(1)}, u32[]{:S(2)}, u32[]{:S(2)}) collective-permute-start(f32[2,80,80]{2,1,0:T(8,128)S(1)} %send.7), channel_id=1, source_target_pairs={{0,1},{2,3},{4,5},{6,7},{8,9},{10,11},{12,13},{14,15},{17,18},{19,... | collective-permute-start | bytes 153608 | tf_op jit(solution)/shard_map/ppermute | solution.py:450
  48.7 3.7 %collective-permute-start.16 = (f32[8,128]{1,0:T(8,128)S(1)}, f32[8,128]{1,0:T(8,128)S(1)}, u32[]{:S(2)}, u32[]{:S(2)}) collective-permute-start(f32[8,128]{1,0:T(8,128)S(1)} %slice.3), channel_id=1, source_target_pairs={{0,32},{64,96},{48,80},{112,16},{32,0},{96,64},{80,48},{16,112},{1... | collective-permute-start | bytes 12296 | tf_op jit(solution)/shard_map/ppermute | solution.py:456
  53.1 11.7 %collective-permute-start.17 = (f32[2,80,80]{2,1,0:T(8,128)S(1)}, f32[2,80,80]{2,1,0:T(8,128)S(1)}, u32[]{:S(2)}, u32[]{:S(2)}) collective-permute-start(f32[2,80,80]{2,1,0:T(8,128)S(1)} %collective-permute-done.15.h), channel_id=1, source_target_pairs={{0,16},{32,48},{64,80},{96,112},{16,0},{48,32},{80,64},{112,96},{1... | collective-permute-start | bytes 153608 | tf_op jit(solution)/shard_map/ppermute | solution.py:465
  54.6 18.5 %all-to-all-start = ((f32[16,16,128]{2,1,0:T(8,128)}), f32[16,16,128]{2,1,0:T(8,128)S(1)}, u32[]{:S(2)}, u32[]{:S(2)}) async-start(f32[16,16,128]{2,1,0:T(8,128)} %column.1), calls=%async_computation | async-start | bytes 262144 | tf_op jit(solution)/shard_map/all_to_all | solution.py:462

commit v13 on v11

--- a/solution.py
+++ b/solution.py
@@ -21,6 +21,7 @@
 SLAB = 16
 PARTS = TX // SLAB
 SLABS = LEV * PARTS
+TURN = 2
 
 ROW_A = M
 ROW_C = M + 1
@@ -156,8 +157,8 @@
     load.wait()
     group = 16
     for g in range(M // group):
-        h, m, l = split3(surface[group * g : group * g + group].reshape(group * TX, TY))
-        picked = dot(h, hot_y) + dot(m, hot_y) + dot(l, hot_y)
+        high, low = split2(surface[group * g : group * g + group].reshape(group * TX, TY))
+        picked = dot(high, hot_y) + dot(low, hot_y)
         out[group * g : group * g + group] = jnp.sum(
             picked.reshape(group, TX, NB * CAP) * hot_x[None], axis=1
         )
@@ -304,11 +305,52 @@
     emit(k, new, z_out, pay_out, edge_out, news_out)
 
 
-def final_kernel(q0, h, g, z, x, out, come, go, come_sems, go_sems):
-    def part(ref, i):
-        return ref.at[:, i // PARTS, pl.ds((i % PARTS) * SLAB, SLAB), :]
-
-    loads = [pltpu.make_async_copy(part(x, i), come.at[i], come_sems.at[i]) for i in range(SLABS)]
+def part(ref, i):
+    return ref.at[:, i // PARTS, pl.ds((i % PARTS) * SLAB, SLAB), :]
+
+
+def turn(block, out, at):
+    high, low = split2(jnp.swapaxes(block, 0, 1))
+    out[at : at + 8, :M] = high
+    out[at : at + 8, M:] = low
+
+
+def turn_kernel(first, x, out, come, sems):
+    loads = [pltpu.make_async_copy(part(x, first + i), come.at[i], sems.at[i]) for i in range(TURN)]
+    for load in loads:
+        load.start()
+    for i in range(TURN):
+        loads[i].wait()
+        for j in range(0, SLAB, 8):
+            turn(come[i, :, j : j + 8, :], out, SLAB * i + j)
+
+
+def turn_away_kernel(first, x, out, come, turned, sems, out_sems):
+    loads = [pltpu.make_async_copy(part(x, first + i), come.at[i], sems.at[i]) for i in range(TURN)]
+    stores = [
+        pltpu.make_async_copy(turned.at[pl.ds(SLAB * i, SLAB)], out.at[pl.ds(SLAB * i, SLAB)], out_sems.at[i])
+        for i in range(TURN)
+    ]
+    for load in loads:
+        load.start()
+    for i in range(TURN):
+        loads[i].wait()
+        for j in range(0, SLAB, 8):
+            turn(come[i, :, j : j + 8, :], turned, SLAB * i + j)
+        stores[i].start()
+    for store in stores:
+        store.wait()
+
+
+def final_kernel(q0, h, g, z, near, far0, far1, x, out, back, come, go, back_sems, come_sems, go_sems):
+    loads = [
+        pltpu.make_async_copy(
+            (far0, far1)[i // TURN].at[pl.ds(SLAB * (i % TURN), SLAB)], back.at[pl.ds(SLAB * i, SLAB)], back_sems.at[i]
+        )
+        for i in range(2 * TURN)
+    ]
+    raw = 3 * TURN
+    loads += [pltpu.make_async_copy(part(x, i), come.at[i - raw], come_sems.at[i - raw]) for i in range(raw, SLABS)]
     stores = [pltpu.make_async_copy(go.at[i], part(out, i), go_sems.at[i]) for i in range(SLABS)]
     for load in loads:
         load.start()
@@ -317,13 +359,20 @@
     th, tl = split2(t)
     w = jnp.concatenate([th, th, tl], axis=1)
     for i in range(SLABS):
-        loads[i].wait()
+        if i >= TURN:
+            loads[i - TURN].wait()
         for j in range(0, SLAB, 8):
-            turned = jnp.swapaxes(come[i, :, j : j + 8, :], 0, 1)
+            if i >= raw:
+                turned = jnp.swapaxes(come[i - raw, :, j : j + 8, :], 0, 1)
             rows = []
             for r in range(8):
-                xh, xl = split2(turned[r])
-                rows.append(dot(w, jnp.concatenate([xh, xl, xh], axis=0))[None])
+                if i >= raw:
+                    xh, xl = split2(turned[r])
+                    stack = [xh, xl, xh]
+                else:
+                    both = near[SLAB * i + j + r] if i < TURN else back[SLAB * (i - TURN) + j + r]
+                    stack = [both, both[:M]]
+                rows.append(dot(w, jnp.concatenate(stack, axis=0))[None])
             go[i, :, j : j + 8, :] = jnp.swapaxes(jnp.concatenate(rows, axis=0), 0, 1)
         stores[i].start()
     for store in stores:
@@ -404,7 +453,8 @@
         out_specs=(VMEM,) * 3,
         name="start",
     )(own, lax.ppermute(own, "gx", core))
-    ranks = []
+    ranks, aways = [], []
+    state_hbm = pltpu.with_memory_space_constraint(ensemble, pltpu.HBM)
     for k in range(NB):
         last = k + 1 == NB
         far = lax.ppermute(edge, "gx", side_x)
@@ -435,7 +485,32 @@
             h, q0, column = lax.optimization_barrier((h, q0, column))
             gathered = lax.all_to_all(column, "gy", 0, 0, tiled=True)
         else:
-            h, q0 = lax.optimization_barrier((h, q0))
+            turned_shape = jax.ShapeDtypeStruct((TURN * SLAB, 2 * M, TY), BF16)
+            come = pltpu.VMEM((TURN, M, SLAB, TY), F32)
+            if k + 2 < NB:
+                turned = call(
+                    functools.partial(turn_away_kernel, TURN * (k + 1)),
+                    out_shape=pltpu.HBM(turned_shape.shape, BF16),
+                    in_specs=[HBM],
+                    out_specs=HBM,
+                    scratch_shapes=[
+                        come, pltpu.VMEM((TURN * SLAB, 2 * M, TY), BF16),
+                        pltpu.SemaphoreType.DMA((TURN,)), pltpu.SemaphoreType.DMA((TURN,)),
+                    ],
+                    name="turn",
+                )(state_hbm)
+                h, q0, turned = lax.optimization_barrier((h, q0, turned))
+                aways.append(turned)
+            else:
+                near = call(
+                    functools.partial(turn_kernel, 0),
+                    out_shape=turned_shape,
+                    in_specs=[HBM],
+                    out_specs=VMEM,
+                    scratch_shapes=[come, pltpu.SemaphoreType.DMA((TURN,))],
+                    name="turn",
+                )(state_hbm)
+                h, q0, near = lax.optimization_barrier((h, q0, near))
         g = lax.ppermute(h, "gx", core)
         if not last:
             tail = k + 2 == NB
@@ -449,16 +524,21 @@
             )(q0, h, g, z)
             if tail:
                 news = rest[0]
-    slabs = pltpu.VMEM((SLABS, M, SLAB, TY), F32)
+    dma = lambda n: pltpu.SemaphoreType.DMA((n,))
     state = call(
         final_kernel,
         out_shape=shape(M, LEV, TX, TY),
-        in_specs=[VMEM] * 4 + [HBM],
+        in_specs=[VMEM] * 5 + [HBM] * 3,
         out_specs=HBM,
-        scratch_shapes=[slabs, slabs, pltpu.SemaphoreType.DMA((SLABS,)), pltpu.SemaphoreType.DMA((SLABS,))],
+        scratch_shapes=[
+            pltpu.VMEM((2 * TURN * SLAB, 2 * M, TY), BF16),
+            pltpu.VMEM((SLABS - 3 * TURN, M, SLAB, TY), F32),
+            pltpu.VMEM((SLABS, M, SLAB, TY), F32),
+            dma(2 * TURN), dma(SLABS - 3 * TURN), dma(SLABS),
+        ],
         cost_estimate=pl.CostEstimate(flops=6 * M * M * LEV * TX * TY, bytes_accessed=8 * M * LEV * TX * TY, transcendentals=0),
         name="final",
-    )(q0, h, g, z, pltpu.with_memory_space_constraint(ensemble, pltpu.HBM))
+    )(q0, h, g, z, near, *(pltpu.with_memory_space_constraint(value, pltpu.HBM) for value in aways), state_hbm)
     state, gathered = lax.optimization_barrier((state, gathered))
     innovation = call(
         place_kernel,

time: 74.1 us -> 73.8 us (level)
  Pallas kernels: 23 us -> 31 us
  waiting for transfers between devices: 16 us -> 9.61 us
  starting transfers between devices: 34 us -> 32.1 us
    pallas_call x1 -> x4, Pallas kernels: 8.62 us -> 16.9 us  [the longest x1 8.13 us: local(): call(final_kernel, out_shape=shape(M, LEV, TX, TY), in_specs=[VMEM] * 5 +...]
    ppermute x4, waiting for transfers between devices: 6.58 us -> 0.15 us  [local(): h = lax.ppermute(send, both, side_y)]
    ppermute x4, starting transfers between devices: 3.57 us -> 2.64 us  [local(): g = lax.ppermute(h, 'gx', core)]
  transfers between devices with their start and end apart: 19 -> 19, of which waited for: 13 -> 12; matrix products, arithmetic and copies ran while one was open for 0% -> 0% of each run, Pallas kernels for 21% -> 32%
where the time goes in v13:
time: 73.8 us; the launch traced here: 73.5 us
  starting transfers between devices  32.1 us (43%)
  Pallas kernels  31 us (42%)
  waiting for transfers between devices  9.61 us (13%)
  between operations  0.84 us (1%)
    ppermute x4, starting transfers between devices, local(): far = lax.ppermute(edge, 'gx', side_x)  11.1 us
    all_to_all x1, starting transfers between devices, local(): gathered = lax.all_to_all(column, 'gy', 0, 0, tiled=True)  9.55 us
    pallas_call x1, Pallas kernels, local(): call(final_kernel, out_shape=shape(M, LEV, TX, TY), in_specs=[VMEM] * 5 +...  8.13 us
    pallas_call x2, Pallas kernels, local(): call(functools.partial(turn_away_kernel, TURN * (k + 1)), out_shape=pltpu...  6.58 us
    pallas_call x4, Pallas kernels, local(): call(functools.partial(own_kernel, k), out_shape=(shape(2, M, M), shape(2...  4.81 us
    ppermute x4, starting transfers between devices, local(): h = lax.ppermute(send, both, side_y)  4.44 us
    ppermute x4, waiting for transfers between devices, local(): sib_far = lax.ppermute(far, 'gx', core)  4 us
    pallas_call x1, Pallas kernels, local(): call(init_kernel, out_shape=shape(ROWS, NB * CAP), in_specs=[HBM] * 7, ou...  2.91 us
  transfers between devices with their start and end apart: 19, of which 12 were waited for; matrix products, arithmetic and copies ran while one was open for 0% of the time, Pallas kernels for 32%

profile of v13, /device:TPU:1, one launch (start us, length us, event | category | flops | bytes accessed | tf_op | source)
XLA Modules:
  0.0 73.5 jit_solution(8597068652603578492)
XLA Ops:
  0.6 0.0 copy-start
  0.6 0.0 copy-start.1
  0.7 2.9 %init.1.own = f32[96,256]{1,0:T(8,128)S(1)} custom-call(s32[4]{0:T(128)} %order.9, f32[4,2048]{1,0:T(4,128)} %value_hbm.1, f32[4,2048]{1,0:T(4,128)} %variance_hbm.1, s32[4,2048]{1,0:T(4,128)} %owner.9, s32[4,2048]{1,0:T(4,128)} %cell_hbm.1, s32[4,8,2048]{2,1,0:T(8,128)} %bitcast.1, f32[80,4,32,256]{3,2,1,0:T(8,128)} %x.7), custom_call_target="tpu_custom_call" | custom-call | tf_op jit(solution)/shard_map/init/pallas_call | solution.py:433
  3.6 1.5 %collective-permute-start = (f32[96,256]{1,0:T(8,128)S(1)}, f32[96,256]{1,0:T(8,128)S(1)}, u32[]{:S(2)}, u32[]{:S(2)}) collective-permute-start(f32[96,256]{1,0:T(8,128)S(1)} %init.1.own), channel_id=1, source_target_pairs={{0,16},{32,48},{64,80},{96,112},{16,0},{48,32},{80,64},{112,96},{1... | collective-permute-start | bytes 294920 | tf_op jit(solution)/shard_map/ppermute | solution.py:455
  5.1 0.9 %collective-permute-done.sib = f32[96,256]{1,0:T(8,128)S(1)} collective-permute-done((f32[96,256]{1,0:T(8,128)S(1)}, f32[96,256]{1,0:T(8,128)S(1)}, u32[]{:S(2)}, u32[]{:S(2)}) %collective-permute-start) | collective-permute-done | bytes 98336 | tf_op jit(solution)/shard_map/ppermute | solution.py:455
  6.0 0.2 start.1
  6.2 2.9 %collective-permute-start.1 = (f32[48,128]{1,0:T(8,128)S(1)}, f32[48,128]{1,0:T(8,128)S(1)}, u32[]{:S(2)}, u32[]{:S(2)}) collective-permute-start(f32[48,128]{1,0:T(8,128)S(1)} %get-tuple-element.57), channel_id=1, source_target_pairs={{0,32},{64,96},{48,80},{112,16},{32,0},{96,64},{80,48},{16,112},{1... | collective-permute-start | bytes 73736 | tf_op jit(solution)/shard_map/ppermute | solution.py:460
  9.0 0.0 copy-done
  9.0 1.2 %own.4 = (f32[2,80,80]{2,1,0:T(8,128)S(1)}, f32[2,80,80]{2,1,0:T(8,128)S(1)}, f32[1,2048]{1,0:T(1,128)S(1)}) custom-call(s32[4]{0:T(128)S(1)} %copy-done.1, s32[4,2048]{1,0:T(4,128)S(1)} %copy-done, f32[2,48,128]{2,1,0:T(8,128)S(1)} %get-tuple-element.58.pay), custom_call_target="tpu_custom_call" | custom-call | tf_op jit(solution)/shard_map/own/pallas_call | solution.py:461
  10.3 0.0 collective-permute-done.1.far
  10.3 0.1 collective-permute-start.2
  10.4 1.1 %collective-permute-done.2.sib_far = f32[48,128]{1,0:T(8,128)S(1)} collective-permute-done((f32[48,128]{1,0:T(8,128)S(1)}, f32[48,128]{1,0:T(8,128)S(1)}, u32[]{:S(2)}, u32[]{:S(2)}) %collective-permute-start.2) | collective-permute-done | bytes 24608 | tf_op jit(solution)/shard_map/ppermute | solution.py:469
  11.5 0.3 send.4
  11.8 1.2 %collective-permute-start.3 = (f32[2,80,80]{2,1,0:T(8,128)S(1)}, f32[2,80,80]{2,1,0:T(8,128)S(1)}, u32[]{:S(2)}, u32[]{:S(2)}) collective-permute-start(f32[2,80,80]{2,1,0:T(8,128)S(1)} %send.4), channel_id=1, source_target_pairs={{0,1},{2,3},{4,5},{6,7},{8,9},{10,11},{12,13},{14,15},{17,18},{19,... | collective-permute-start | bytes 153608 | tf_op jit(solution)/shard_map/ppermute | solution.py:474
  13.0 3.3 %turn.3.far0 = bf16[32,160,256]{2,1,0:T(8,128)(2,1)} custom-call(f32[80,4,32,256]{3,2,1,0:T(8,128)} %x.7), custom_call_target="tpu_custom_call" | custom-call | tf_op jit(solution)/shard_map/turn/pallas_call | solution.py:491
  16.3 0.3 same.4.q0
  16.6 0.0 collective-permute-done.3.h
  16.6 0.6 collective-permute-start.4
  17.3 0.9 %collective-permute-done.4.g = f32[2,80,80]{2,1,0:T(8,128)S(1)} collective-permute-done((f32[2,80,80]{2,1,0:T(8,128)S(1)}, f32[2,80,80]{2,1,0:T(8,128)S(1)}, u32[]{:S(2)}, u32[]{:S(2)}) %collective-permute-start.4) | collective-permute-done | bytes 51232 | tf_op jit(solution)/shard_map/ppermute | solution.py:514
  18.2 0.4 step.3
  18.6 2.8 %collective-permute-start.5 = (f32[48,128]{1,0:T(8,128)S(1)}, f32[48,128]{1,0:T(8,128)S(1)}, u32[]{:S(2)}, u32[]{:S(2)}) collective-permute-start(f32[48,128]{1,0:T(8,128)S(1)} %get-tuple-element.68), channel_id=1, source_target_pairs={{0,32},{64,96},{48,80},{112,16},{32,0},{96,64},{80,48},{16,112},{1... | collective-permute-start | bytes 73736 | tf_op jit(solution)/shard_map/ppermute | solution.py:460
  21.3 1.2 %own.5 = (f32[2,80,80]{2,1,0:T(8,128)S(1)}, f32[2,80,80]{2,1,0:T(8,128)S(1)}, f32[1,2048]{1,0:T(1,128)S(1)}) custom-call(s32[4]{0:T(128)S(1)} %copy-done.1, s32[4,2048]{1,0:T(4,128)S(1)} %copy-done, f32[2,48,128]{2,1,0:T(8,128)S(1)} %get-tuple-element.69.pay), custom_call_target="tpu_custom_call" | custom-call | tf_op jit(solution)/shard_map/own/pallas_call | solution.py:461
  22.5 0.0 collective-permute-done.5.far
  22.6 0.2 collective-permute-start.6
  22.8 1.0 %collective-permute-done.6.sib_far = f32[48,128]{1,0:T(8,128)S(1)} collective-permute-done((f32[48,128]{1,0:T(8,128)S(1)}, f32[48,128]{1,0:T(8,128)S(1)}, u32[]{:S(2)}, u32[]{:S(2)}) %collective-permute-start.6) | collective-permute-done | bytes 24608 | tf_op jit(solution)/shard_map/ppermute | solution.py:469
  23.8 0.3 send.5
  24.1 1.2 %collective-permute-start.7 = (f32[2,80,80]{2,1,0:T(8,128)S(1)}, f32[2,80,80]{2,1,0:T(8,128)S(1)}, u32[]{:S(2)}, u32[]{:S(2)}) collective-permute-start(f32[2,80,80]{2,1,0:T(8,128)S(1)} %send.5), channel_id=1, source_target_pairs={{0,1},{2,3},{4,5},{6,7},{8,9},{10,11},{12,13},{14,15},{17,18},{19,... | collective-permute-start | bytes 153608 | tf_op jit(solution)/shard_map/ppermute | solution.py:474
  25.3 3.3 %turn.4.far1 = bf16[32,160,256]{2,1,0:T(8,128)(2,1)} custom-call(f32[80,4,32,256]{3,2,1,0:T(8,128)} %x.7), custom_call_target="tpu_custom_call" | custom-call | tf_op jit(solution)/shard_map/turn/pallas_call | solution.py:491
  28.6 0.3 same.5.q0
  28.9 0.0 collective-permute-done.7.h
  28.9 0.4 collective-permute-start.8
  29.4 0.9 %collective-permute-done.8.g = f32[2,80,80]{2,1,0:T(8,128)S(1)} collective-permute-done((f32[2,80,80]{2,1,0:T(8,128)S(1)}, f32[2,80,80]{2,1,0:T(8,128)S(1)}, u32[]{:S(2)}, u32[]{:S(2)}) %collective-permute-start.8) | collective-permute-done | bytes 51232 | tf_op jit(solution)/shard_map/ppermute | solution.py:514
  30.3 0.4 step.4
  30.7 2.6 %collective-permute-start.9 = (f32[48,128]{1,0:T(8,128)S(1)}, f32[48,128]{1,0:T(8,128)S(1)}, u32[]{:S(2)}, u32[]{:S(2)}) collective-permute-start(f32[48,128]{1,0:T(8,128)S(1)} %get-tuple-element.79), channel_id=1, source_target_pairs={{0,32},{64,96},{48,80},{112,16},{32,0},{96,64},{80,48},{16,112},{1... | collective-permute-start | bytes 73736 | tf_op jit(solution)/shard_map/ppermute | solution.py:460
  33.3 1.2 %own.6 = (f32[2,80,80]{2,1,0:T(8,128)S(1)}, f32[2,80,80]{2,1,0:T(8,128)S(1)}, f32[1,2048]{1,0:T(1,128)S(1)}) custom-call(s32[4]{0:T(128)S(1)} %copy-done.1, s32[4,2048]{1,0:T(4,128)S(1)} %copy-done, f32[2,48,128]{2,1,0:T(8,128)S(1)} %get-tuple-element.80.pay), custom_call_target="tpu_custom_call" | custom-call | tf_op jit(solution)/shard_map/own/pallas_call | solution.py:461
  34.5 0.1 collective-permute-done.9.far
  34.6 0.3 collective-permute-start.10
  34.9 0.9 %collective-permute-done.10.sib_far = f32[48,128]{1,0:T(8,128)S(1)} collective-permute-done((f32[48,128]{1,0:T(8,128)S(1)}, f32[48,128]{1,0:T(8,128)S(1)}, u32[]{:S(2)}, u32[]{:S(2)}) %collective-permute-start.10) | collective-permute-done | bytes 24608 | tf_op jit(solution)/shard_map/ppermute | solution.py:469
  35.8 0.3 send.6
  36.1 1.0 %collective-permute-start.11 = (f32[2,80,80]{2,1,0:T(8,128)S(1)}, f32[2,80,80]{2,1,0:T(8,128)S(1)}, u32[]{:S(2)}, u32[]{:S(2)}) collective-permute-start(f32[2,80,80]{2,1,0:T(8,128)S(1)} %send.6), channel_id=1, source_target_pairs={{0,1},{2,3},{4,5},{6,7},{8,9},{10,11},{12,13},{14,15},{17,18},{19,... | collective-permute-start | bytes 153608 | tf_op jit(solution)/shard_map/ppermute | solution.py:474
  37.2 2.2 %turn.5.near = bf16[32,160,256]{2,1,0:T(8,128)(2,1)S(1)} custom-call(f32[80,4,32,256]{3,2,1,0:T(8,128)} %x.7), custom_call_target="tpu_custom_call" | custom-call | tf_op jit(solution)/shard_map/turn/pallas_call | solution.py:505
  39.3 0.3 same.6.q0
  39.6 0.1 collective-permute-done.11.h
  39.8 1.1 %collective-permute-start.12 = (f32[2,80,80]{2,1,0:T(8,128)S(1)}, f32[2,80,80]{2,1,0:T(8,128)S(1)}, u32[]{:S(2)}, u32[]{:S(2)}) collective-permute-start(f32[2,80,80]{2,1,0:T(8,128)S(1)} %collective-permute-done.11.h), channel_id=1, source_target_pairs={{0,16},{32,48},{64,80},{96,112},{16,0},{48,32},{80,64},{112,96},{1... | collective-permute-start | bytes 153608 | tf_op jit(solution)/shard_map/ppermute | solution.py:514
  40.9 0.9 %collective-permute-done.12.g = f32[2,80,80]{2,1,0:T(8,128)S(1)} collective-permute-done((f32[2,80,80]{2,1,0:T(8,128)S(1)}, f32[2,80,80]{2,1,0:T(8,128)S(1)}, u32[]{:S(2)}, u32[]{:S(2)}) %collective-permute-start.12) | collective-permute-done | bytes 51232 | tf_op jit(solution)/shard_map/ppermute | solution.py:514
  41.8 0.4 step.5
  42.2 2.8 %collective-permute-start.13 = (f32[56,128]{1,0:T(8,128)S(1)}, f32[56,128]{1,0:T(8,128)S(1)}, u32[]{:S(2)}, u32[]{:S(2)}) collective-permute-start(f32[56,128]{1,0:T(8,128)S(1)} %get-tuple-element.90), channel_id=1, source_target_pairs={{0,32},{64,96},{48,80},{112,16},{32,0},{96,64},{80,48},{16,112},{1... | collective-permute-start | bytes 86024 | tf_op jit(solution)/shard_map/ppermute | solution.py:460
  45.0 1.2 %own.7 = (f32[2,80,80]{2,1,0:T(8,128)S(1)}, f32[2,80,80]{2,1,0:T(8,128)S(1)}, f32[1,2048]{1,0:T(1,128)S(1)}) custom-call(s32[4]{0:T(128)S(1)} %copy-done.1, s32[4,2048]{1,0:T(4,128)S(1)} %copy-done, f32[2,48,128]{2,1,0:T(8,128)S(1)} %get-tuple-element.91.pay), custom_call_target="tpu_custom_call" | custom-call | tf_op jit(solution)/shard_map/own/pallas_call | solution.py:461
  46.2 0.1 collective-permute-done.13.far
  46.4 0.3 collective-permute-start.14
  46.7 0.9 %collective-permute-done.14.sib_far = f32[56,128]{1,0:T(8,128)S(1)} collective-permute-done((f32[56,128]{1,0:T(8,128)S(1)}, f32[56,128]{1,0:T(8,128)S(1)}, u32[]{:S(2)}, u32[]{:S(2)}) %collective-permute-start.14) | collective-permute-done | bytes 28704 | tf_op jit(solution)/shard_map/ppermute | solution.py:469
  47.6 0.3 send.7
  47.9 1.0 %collective-permute-start.15 = (f32[2,80,80]{2,1,0:T(8,128)S(1)}, f32[2,80,80]{2,1,0:T(8,128)S(1)}, u32[]{:S(2)}, u32[]{:S(2)}) collective-permute-start(f32[2,80,80]{2,1,0:T(8,128)S(1)} %send.7), channel_id=1, source_target_pairs={{0,1},{2,3},{4,5},{6,7},{8,9},{10,11},{12,13},{14,15},{17,18},{19,... | collective-permute-start | bytes 153608 | tf_op jit(solution)/shard_map/ppermute | solution.py:474
  48.9 1.9 %collective-permute-start.16 = (f32[8,128]{1,0:T(8,128)S(1)}, f32[8,128]{1,0:T(8,128)S(1)}, u32[]{:S(2)}, u32[]{:S(2)}) collective-permute-start(f32[8,128]{1,0:T(8,128)S(1)} %slice.3), channel_id=1, source_target_pairs={{0,32},{64,96},{48,80},{112,16},{32,0},{96,64},{80,48},{16,112},{1... | collective-permute-start | bytes 12296 | tf_op jit(solution)/shard_map/ppermute | solution.py:480
  50.8 0.3 same.7.q0
  51.1 1.5 %collective-permute-done.16.across = f32[8,128]{1,0:T(8,128)S(1)} collective-permute-done((f32[8,128]{1,0:T(8,128)S(1)}, f32[8,128]{1,0:T(8,128)S(1)}, u32[]{:S(2)}, u32[]{:S(2)}) %collective-permute-start.16) | collective-permute-done | bytes 4128 | tf_op jit(solution)/shard_map/ppermute | solution.py:480
  52.6 0.7 column.1
  53.3 0.0 collective-permute-done.15.h
  53.3 0.5 collective-permute-start.17
  53.7 9.5 %all-to-all-start = ((f32[16,16,128]{2,1,0:T(8,128)}), f32[16,16,128]{2,1,0:T(8,128)S(1)}, u32[]{:S(2)}, u32[]{:S(2)}) async-start(f32[16,16,128]{2,1,0:T(8,128)} %column.1), calls=%async_computation | async-start | bytes 262144 | tf_op jit(solution)/shard_map/all_to_all | solution.py:486
  63.3 0.0 collective-permute-done.17.g
  63.3 8.1 %final.1 = f32[80,4,32,256]{3,2,1,0:T(8,128)} custom-call(f32[2,80,80]{2,1,0:T(8,128)S(1)} %same.7.q0, f32[2,80,80]{2,1,0:T(8,128)S(1)} %collective-permute-done.15.h, f32[2,80,80]{2,1,0:T(8,128)S(1)} %collective-permute-done.17.g, f32[2,96,384]{2,1,0:T(8,128)S(1)} %get-tuple-element.101.z, bf16[32,160,256]{2,1,0:T(8,128)(2,1)S(1)} %turn.5.near, ...), custom_call_target="tpu_custom_call" | custom-call | flops 1258291200 | bytes 20971520 | tf_op jit(solution)/shard_map/final/pallas_call | solution.py:528
  71.4 0.0 all-to-all-done.gathered
  71.4 2.1 %place.1 = f32[4,2048]{1,0:T(4,128)} custom-call(s32[4]{0:T(128)S(1)} %copy-done.1, s32[4,2048]{1,0:T(4,128)S(1)} %copy-done, f32[16,16,128]{2,1,0:T(8,128)S(1)} %all-to-all-done.gathered, f32[1,2048]{1,0:T(1,128)S(1)} %get-tuple-element.108.r0, f32[1,2048]{1,0:T(1,128)S(1)} %get-tuple-element.109.r1, f32[1,2048]{1,0:T(1,128)S(1)} %get-tuple-element.110.r2, ...), custom_call_target="tpu_custom_call" | custom-call | tf_op jit(solution)/shard_map/place/pallas_call | solution.py:543
  (2 shorter events, 0.0 us)
Async XLA Ops:
  0.6 8.4 %copy-start = (s32[4,2048]{1,0:T(4,128)S(1)}, s32[4,2048]{1,0:T(4,128)}, u32[]{:S(2)}) copy-start(s32[4,2048]{1,0:T(4,128)} %owner.9) | copy-start | bytes 98308
  0.6 8.4 %copy-start.1 = (s32[4]{0:T(128)S(1)}, s32[4]{0:T(128)}, u32[]{:S(2)}) copy-start(s32[4]{0:T(128)} %order.9) | copy-start | bytes 52
  3.6 2.4 %collective-permute-start = (f32[96,256]{1,0:T(8,128)S(1)}, f32[96,256]{1,0:T(8,128)S(1)}, u32[]{:S(2)}, u32[]{:S(2)}) collective-permute-start(f32[96,256]{1,0:T(8,128)S(1)} %init.1.own), channel_id=1, source_target_pairs={{0,16},{32,48},{64,80},{96,112},{16,0},{48,32},{80,64},{112,96},{1... | collective-permute-start | bytes 294920 | tf_op jit(solution)/shard_map/ppermute | solution.py:455
  6.2 4.1 %collective-permute-start.1 = (f32[48,128]{1,0:T(8,128)S(1)}, f32[48,128]{1,0:T(8,128)S(1)}, u32[]{:S(2)}, u32[]{:S(2)}) collective-permute-start(f32[48,128]{1,0:T(8,128)S(1)} %get-tuple-element.57), channel_id=1, source_target_pairs={{0,32},{64,96},{48,80},{112,16},{32,0},{96,64},{80,48},{16,112},{1... | collective-permute-start | bytes 73736 | tf_op jit(solution)/shard_map/ppermute | solution.py:460
  10.3 1.3 %collective-permute-start.2 = (f32[48,128]{1,0:T(8,128)S(1)}, f32[48,128]{1,0:T(8,128)S(1)}, u32[]{:S(2)}, u32[]{:S(2)}) collective-permute-start(f32[48,128]{1,0:T(8,128)S(1)} %collective-permute-done.1.far), channel_id=1, source_target_pairs={{0,16},{32,48},{64,80},{96,112},{16,0},{48,32},{80,64},{112,96},{1... | collective-permute-start | bytes 73736 | tf_op jit(solution)/shard_map/ppermute | solution.py:469
  11.8 4.8 %collective-permute-start.3 = (f32[2,80,80]{2,1,0:T(8,128)S(1)}, f32[2,80,80]{2,1,0:T(8,128)S(1)}, u32[]{:S(2)}, u32[]{:S(2)}) collective-permute-start(f32[2,80,80]{2,1,0:T(8,128)S(1)} %send.4), channel_id=1, source_target_pairs={{0,1},{2,3},{4,5},{6,7},{8,9},{10,11},{12,13},{14,15},{17,18},{19,... | collective-permute-start | bytes 153608 | tf_op jit(solution)/shard_map/ppermute | solution.py:474
  16.6 1.6 %collective-permute-start.4 = (f32[2,80,80]{2,1,0:T(8,128)S(1)}, f32[2,80,80]{2,1,0:T(8,128)S(1)}, u32[]{:S(2)}, u32[]{:S(2)}) collective-permute-start(f32[2,80,80]{2,1,0:T(8,128)S(1)} %collective-permute-done.3.h), channel_id=1, source_target_pairs={{0,16},{32,48},{64,80},{96,112},{16,0},{48,32},{80,64},{112,96},{1... | collective-permute-start | bytes 153608 | tf_op jit(solution)/shard_map/ppermute | solution.py:514
  18.6 4.0 %collective-permute-start.5 = (f32[48,128]{1,0:T(8,128)S(1)}, f32[48,128]{1,0:T(8,128)S(1)}, u32[]{:S(2)}, u32[]{:S(2)}) collective-permute-start(f32[48,128]{1,0:T(8,128)S(1)} %get-tuple-element.68), channel_id=1, source_target_pairs={{0,32},{64,96},{48,80},{112,16},{32,0},{96,64},{80,48},{16,112},{1... | collective-permute-start | bytes 73736 | tf_op jit(solution)/shard_map/ppermute | solution.py:460
  22.6 1.3 %collective-permute-start.6 = (f32[48,128]{1,0:T(8,128)S(1)}, f32[48,128]{1,0:T(8,128)S(1)}, u32[]{:S(2)}, u32[]{:S(2)}) collective-permute-start(f32[48,128]{1,0:T(8,128)S(1)} %collective-permute-done.5.far), channel_id=1, source_target_pairs={{0,16},{32,48},{64,80},{96,112},{16,0},{48,32},{80,64},{112,96},{1... | collective-permute-start | bytes 73736 | tf_op jit(solution)/shard_map/ppermute | solution.py:469
  24.1 4.8 %collective-permute-start.7 = (f32[2,80,80]{2,1,0:T(8,128)S(1)}, f32[2,80,80]{2,1,0:T(8,128)S(1)}, u32[]{:S(2)}, u32[]{:S(2)}) collective-permute-start(f32[2,80,80]{2,1,0:T(8,128)S(1)} %send.5), channel_id=1, source_target_pairs={{0,1},{2,3},{4,5},{6,7},{8,9},{10,11},{12,13},{14,15},{17,18},{19,... | collective-permute-start | bytes 153608 | tf_op jit(solution)/shard_map/ppermute | solution.py:474
  28.9 1.4 %collective-permute-start.8 = (f32[2,80,80]{2,1,0:T(8,128)S(1)}, f32[2,80,80]{2,1,0:T(8,128)S(1)}, u32[]{:S(2)}, u32[]{:S(2)}) collective-permute-start(f32[2,80,80]{2,1,0:T(8,128)S(1)} %collective-permute-done.7.h), channel_id=1, source_target_pairs={{0,16},{32,48},{64,80},{96,112},{16,0},{48,32},{80,64},{112,96},{1... | collective-permute-start | bytes 153608 | tf_op jit(solution)/shard_map/ppermute | solution.py:514
  30.7 3.9 %collective-permute-start.9 = (f32[48,128]{1,0:T(8,128)S(1)}, f32[48,128]{1,0:T(8,128)S(1)}, u32[]{:S(2)}, u32[]{:S(2)}) collective-permute-start(f32[48,128]{1,0:T(8,128)S(1)} %get-tuple-element.79), channel_id=1, source_target_pairs={{0,32},{64,96},{48,80},{112,16},{32,0},{96,64},{80,48},{16,112},{1... | collective-permute-start | bytes 73736 | tf_op jit(solution)/shard_map/ppermute | solution.py:460
  34.6 1.2 %collective-permute-start.10 = (f32[48,128]{1,0:T(8,128)S(1)}, f32[48,128]{1,0:T(8,128)S(1)}, u32[]{:S(2)}, u32[]{:S(2)}) collective-permute-start(f32[48,128]{1,0:T(8,128)S(1)} %collective-permute-done.9.far), channel_id=1, source_target_pairs={{0,16},{32,48},{64,80},{96,112},{16,0},{48,32},{80,64},{112,96},{1... | collective-permute-start | bytes 73736 | tf_op jit(solution)/shard_map/ppermute | solution.py:469
  36.1 3.7 %collective-permute-start.11 = (f32[2,80,80]{2,1,0:T(8,128)S(1)}, f32[2,80,80]{2,1,0:T(8,128)S(1)}, u32[]{:S(2)}, u32[]{:S(2)}) collective-permute-start(f32[2,80,80]{2,1,0:T(8,128)S(1)} %send.6), channel_id=1, source_target_pairs={{0,1},{2,3},{4,5},{6,7},{8,9},{10,11},{12,13},{14,15},{17,18},{19,... | collective-permute-start | bytes 153608 | tf_op jit(solution)/shard_map/ppermute | solution.py:474
  39.8 2.1 %collective-permute-start.12 = (f32[2,80,80]{2,1,0:T(8,128)S(1)}, f32[2,80,80]{2,1,0:T(8,128)S(1)}, u32[]{:S(2)}, u32[]{:S(2)}) collective-permute-start(f32[2,80,80]{2,1,0:T(8,128)S(1)} %collective-permute-done.11.h), channel_id=1, source_target_pairs={{0,16},{32,48},{64,80},{96,112},{16,0},{48,32},{80,64},{112,96},{1... | collective-permute-start | bytes 153608 | tf_op jit(solution)/shard_map/ppermute | solution.py:514
  42.2 4.2 %collective-permute-start.13 = (f32[56,128]{1,0:T(8,128)S(1)}, f32[56,128]{1,0:T(8,128)S(1)}, u32[]{:S(2)}, u32[]{:S(2)}) collective-permute-start(f32[56,128]{1,0:T(8,128)S(1)} %get-tuple-element.90), channel_id=1, source_target_pairs={{0,32},{64,96},{48,80},{112,16},{32,0},{96,64},{80,48},{16,112},{1... | collective-permute-start | bytes 86024 | tf_op jit(solution)/shard_map/ppermute | solution.py:460
  46.4 1.2 %collective-permute-start.14 = (f32[56,128]{1,0:T(8,128)S(1)}, f32[56,128]{1,0:T(8,128)S(1)}, u32[]{:S(2)}, u32[]{:S(2)}) collective-permute-start(f32[56,128]{1,0:T(8,128)S(1)} %collective-permute-done.13.far), channel_id=1, source_target_pairs={{0,16},{32,48},{64,80},{96,112},{16,0},{48,32},{80,64},{112,96},{1... | collective-permute-start | bytes 86024 | tf_op jit(solution)/shard_map/ppermute | solution.py:469
  47.9 5.4 %collective-permute-start.15 = (f32[2,80,80]{2,1,0:T(8,128)S(1)}, f32[2,80,80]{2,1,0:T(8,128)S(1)}, u32[]{:S(2)}, u32[]{:S(2)}) collective-permute-start(f32[2,80,80]{2,1,0:T(8,128)S(1)} %send.7), channel_id=1, source_target_pairs={{0,1},{2,3},{4,5},{6,7},{8,9},{10,11},{12,13},{14,15},{17,18},{19,... | collective-permute-start | bytes 153608 | tf_op jit(solution)/shard_map/ppermute | solution.py:474
  48.9 3.7 %collective-permute-start.16 = (f32[8,128]{1,0:T(8,128)S(1)}, f32[8,128]{1,0:T(8,128)S(1)}, u32[]{:S(2)}, u32[]{:S(2)}) collective-permute-start(f32[8,128]{1,0:T(8,128)S(1)} %slice.3), channel_id=1, source_target_pairs={{0,32},{64,96},{48,80},{112,16},{32,0},{96,64},{80,48},{16,112},{1... | collective-permute-start | bytes 12296 | tf_op jit(solution)/shard_map/ppermute | solution.py:480
  53.3 10.0 %collective-permute-start.17 = (f32[2,80,80]{2,1,0:T(8,128)S(1)}, f32[2,80,80]{2,1,0:T(8,128)S(1)}, u32[]{:S(2)}, u32[]{:S(2)}) collective-permute-start(f32[2,80,80]{2,1,0:T(8,128)S(1)} %collective-permute-done.15.h), channel_id=1, source_target_pairs={{0,16},{32,48},{64,80},{96,112},{16,0},{48,32},{80,64},{112,96},{1... | collective-permute-start | bytes 153608 | tf_op jit(solution)/shard_map/ppermute | solution.py:514
  53.7 17.7 %all-to-all-start = ((f32[16,16,128]{2,1,0:T(8,128)}), f32[16,16,128]{2,1,0:T(8,128)S(1)}, u32[]{:S(2)}, u32[]{:S(2)}) async-start(f32[16,16,128]{2,1,0:T(8,128)} %column.1), calls=%async_computation | async-start | bytes 262144 | tf_op jit(solution)/shard_map/all_to_all | solution.py:486

commit v14 on v11

--- a/solution.py
+++ b/solution.py
@@ -21,6 +21,7 @@
 SLAB = 16
 PARTS = TX // SLAB
 SLABS = LEV * PARTS
+TURN = 2
 
 ROW_A = M
 ROW_C = M + 1
@@ -156,8 +157,8 @@
     load.wait()
     group = 16
     for g in range(M // group):
-        h, m, l = split3(surface[group * g : group * g + group].reshape(group * TX, TY))
-        picked = dot(h, hot_y) + dot(m, hot_y) + dot(l, hot_y)
+        high, low = split2(surface[group * g : group * g + group].reshape(group * TX, TY))
+        picked = dot(high, hot_y) + dot(low, hot_y)
         out[group * g : group * g + group] = jnp.sum(
             picked.reshape(group, TX, NB * CAP) * hot_x[None], axis=1
         )
@@ -304,19 +305,37 @@
     emit(k, new, z_out, pay_out, edge_out, news_out)
 
 
-def final_kernel(q0, h, g, z, x, out, come, go, come_sems, go_sems):
-    def part(ref, i):
-        return ref.at[:, i // PARTS, pl.ds((i % PARTS) * SLAB, SLAB), :]
-
-    loads = [pltpu.make_async_copy(part(x, i), come.at[i], come_sems.at[i]) for i in range(SLABS)]
-    stores = [pltpu.make_async_copy(go.at[i], part(out, i), go_sems.at[i]) for i in range(SLABS)]
+def part(ref, i):
+    return ref.at[:, i // PARTS, pl.ds((i % PARTS) * SLAB, SLAB), :]
+
+
+def turn(block, out, at):
+    high, low = split2(jnp.swapaxes(block, 0, 1))
+    out[at : at + 8, :M] = high
+    out[at : at + 8, M:] = low
+
+
+def turn_kernel(first, x, out, come, sems):
+    loads = [pltpu.make_async_copy(part(x, first + i), come.at[i], sems.at[i]) for i in range(TURN)]
+    for load in loads:
+        load.start()
+    for i in range(TURN):
+        loads[i].wait()
+        for j in range(0, SLAB, 8):
+            turn(come[i, :, j : j + 8, :], out, SLAB * i + j)
+
+
+def final_kernel(q0, h, g, z, x, out, mix, come, go, come_sems, go_sems):
+    loads = [pltpu.make_async_copy(part(x, i), come.at[i], come_sems.at[i]) for i in range(SLABS - TURN)]
+    stores = [pltpu.make_async_copy(go.at[i], part(out, i), go_sems.at[i]) for i in range(SLABS - TURN)]
     for load in loads:
         load.start()
     c = core_of()
     t = advance(z[c, :M, NB * CAP :], whole_gain(c, q0, h, g))[:, :M]
     th, tl = split2(t)
     w = jnp.concatenate([th, th, tl], axis=1)
-    for i in range(SLABS):
+    mix[...] = w
+    for i in range(SLABS - TURN):
         loads[i].wait()
         for j in range(0, SLAB, 8):
             turned = jnp.swapaxes(come[i, :, j : j + 8, :], 0, 1)
@@ -326,6 +345,22 @@
                 rows.append(dot(w, jnp.concatenate([xh, xl, xh], axis=0))[None])
             go[i, :, j : j + 8, :] = jnp.swapaxes(jnp.concatenate(rows, axis=0), 0, 1)
         stores[i].start()
+    for store in stores:
+        store.wait()
+
+
+def last_kernel(done, mix, near, order, owner, gathered, r0, r1, r2, r3, out, placed, go, go_sems):
+    stores = [pltpu.make_async_copy(go.at[i], part(out, SLABS - TURN + i), go_sems.at[i]) for i in range(TURN)]
+    w = mix[...]
+    for i in range(TURN):
+        for j in range(0, SLAB, 8):
+            rows = []
+            for r in range(8):
+                both = near[SLAB * i + j + r]
+                rows.append(dot(w, jnp.concatenate([both, both[:M]], axis=0))[None])
+            go[i, :, j : j + 8, :] = jnp.swapaxes(jnp.concatenate(rows, axis=0), 0, 1)
+        stores[i].start()
+    place_kernel(order, owner, gathered, r0, r1, r2, r3, placed)
     for store in stores:
         store.wait()
 
@@ -405,6 +440,7 @@
         name="start",
     )(own, lax.ppermute(own, "gx", core))
     ranks = []
+    state_hbm = pltpu.with_memory_space_constraint(ensemble, pltpu.HBM)
     for k in range(NB):
         last = k + 1 == NB
         far = lax.ppermute(edge, "gx", side_x)
@@ -435,7 +471,20 @@
             h, q0, column = lax.optimization_barrier((h, q0, column))
             gathered = lax.all_to_all(column, "gy", 0, 0, tiled=True)
         else:
-            h, q0 = lax.optimization_barrier((h, q0))
+            turned_shape = jax.ShapeDtypeStruct((TURN * SLAB, 2 * M, TY), BF16)
+            come = pltpu.VMEM((TURN, M, SLAB, TY), F32)
+            if k + 2 < NB:
+                h, q0 = lax.optimization_barrier((h, q0))
+            else:
+                near = call(
+                    functools.partial(turn_kernel, SLABS - TURN),
+                    out_shape=turned_shape,
+                    in_specs=[HBM],
+                    out_specs=VMEM,
+                    scratch_shapes=[come, pltpu.SemaphoreType.DMA((TURN,))],
+                    name="turn",
+                )(state_hbm)
+                h, q0, near = lax.optimization_barrier((h, q0, near))
         g = lax.ppermute(h, "gx", core)
         if not last:
             tail = k + 2 == NB
@@ -449,24 +498,30 @@
             )(q0, h, g, z)
             if tail:
                 news = rest[0]
-    slabs = pltpu.VMEM((SLABS, M, SLAB, TY), F32)
-    state = call(
+    dma = lambda n: pltpu.SemaphoreType.DMA((n,))
+    state, mix = call(
         final_kernel,
-        out_shape=shape(M, LEV, TX, TY),
+        out_shape=(shape(M, LEV, TX, TY), jax.ShapeDtypeStruct((M, 3 * M), BF16)),
         in_specs=[VMEM] * 4 + [HBM],
-        out_specs=HBM,
-        scratch_shapes=[slabs, slabs, pltpu.SemaphoreType.DMA((SLABS,)), pltpu.SemaphoreType.DMA((SLABS,))],
+        out_specs=(HBM, VMEM),
+        scratch_shapes=[
+            pltpu.VMEM((SLABS - TURN, M, SLAB, TY), F32),
+            pltpu.VMEM((SLABS - TURN, M, SLAB, TY), F32),
+            dma(SLABS - TURN), dma(SLABS - TURN),
+        ],
         cost_estimate=pl.CostEstimate(flops=6 * M * M * LEV * TX * TY, bytes_accessed=8 * M * LEV * TX * TY, transcendentals=0),
         name="final",
-    )(q0, h, g, z, pltpu.with_memory_space_constraint(ensemble, pltpu.HBM))
-    state, gathered = lax.optimization_barrier((state, gathered))
-    innovation = call(
-        place_kernel,
-        out_shape=shape(NB, OBS),
-        in_specs=[SMEM] + [VMEM] * 6,
-        out_specs=VMEM,
-        name="place",
-    )(batch_order, obs_owner, gathered, *ranks)
+    )(q0, h, g, z, state_hbm)
+    mix, gathered = lax.optimization_barrier((mix, gathered))
+    state, innovation = call(
+        last_kernel,
+        out_shape=(shape(M, LEV, TX, TY), shape(NB, OBS)),
+        in_specs=[HBM, VMEM, VMEM, SMEM] + [VMEM] * 6,
+        out_specs=(HBM, VMEM),
+        scratch_shapes=[pltpu.VMEM((TURN, M, SLAB, TY), F32), dma(TURN)],
+        input_output_aliases={0: 0},
+        name="last",
+    )(state, mix, near, batch_order, obs_owner, gathered, *ranks)
     return state, innovation
 
 

time: 74.1 us -> 74 us (level)
  waiting for transfers between devices: 16 us -> 13.8 us
  Pallas kernels: 23 us -> 24.8 us
    ppermute x4, waiting for transfers between devices: 6.58 us -> 4.39 us  [local(): h = lax.ppermute(send, both, side_y)]
    pallas_call x2 -> x3, Pallas kernels: 10.7 us -> 12.8 us  [the longest x1 7.06 us: local(): call(final_kernel, out_shape=(shape(M, LEV, TX, TY), jax.ShapeDtypeStruct...]
  transfers between devices with their start and end apart: 19 -> 19, of which waited for: 13 -> 11; matrix products, arithmetic and copies ran while one was open for 0% -> 0% of each run, Pallas kernels for 21% -> 22%
where the time goes in v14:
time: 74 us; the launch traced here: 73.8 us
  starting transfers between devices  34.2 us (46%)
  Pallas kernels  24.8 us (34%)
  waiting for transfers between devices  13.8 us (19%)
  between operations  0.98 us (1%)
    ppermute x4, starting transfers between devices, local(): far = lax.ppermute(edge, 'gx', side_x)  11.2 us
    all_to_all x1, starting transfers between devices, local(): gathered = lax.all_to_all(column, 'gy', 0, 0, tiled=True)  10.4 us
    pallas_call x1, Pallas kernels, local(): call(final_kernel, out_shape=(shape(M, LEV, TX, TY), jax.ShapeDtypeStruct...  7.06 us
    pallas_call x4, Pallas kernels, local(): call(functools.partial(own_kernel, k), out_shape=(shape(2, M, M), shape(2...  4.81 us
    ppermute x4, starting transfers between devices, local(): h = lax.ppermute(send, both, side_y)  4.75 us
    ppermute x4, waiting for transfers between devices, local(): h = lax.ppermute(send, both, side_y)  4.39 us
    ppermute x4, waiting for transfers between devices, local(): sib_far = lax.ppermute(far, 'gx', core)  4.19 us
    pallas_call x1, Pallas kernels, local(): call(last_kernel, out_shape=(shape(M, LEV, TX, TY), shape(NB, OBS)), in_s...  3.58 us
  transfers between devices with their start and end apart: 19, of which 11 were waited for; matrix products, arithmetic and copies ran while one was open for 0% of the time, Pallas kernels for 22%

profile of v14, /device:TPU:1, one launch (start us, length us, event | category | flops | bytes accessed | tf_op | source)
XLA Modules:
  0.0 73.8 jit_solution(13721210823809263094)
XLA Ops:
  0.6 0.0 copy-start.1
  0.6 0.0 copy-start
  0.7 2.9 %init.1.own = f32[96,256]{1,0:T(8,128)S(1)} custom-call(s32[4]{0:T(128)} %order.9, f32[4,2048]{1,0:T(4,128)} %value_hbm.1, f32[4,2048]{1,0:T(4,128)} %variance_hbm.1, s32[4,2048]{1,0:T(4,128)} %owner.9, s32[4,2048]{1,0:T(4,128)} %cell_hbm.1, s32[4,8,2048]{2,1,0:T(8,128)} %bitcast.1, f32[80,4,32,256]{3,2,1,0:T(8,128)} %x.3), custom_call_target="tpu_custom_call" | custom-call | tf_op jit(solution)/shard_map/init/pallas_call | solution.py:419
  3.6 1.5 %collective-permute-start = (f32[96,256]{1,0:T(8,128)S(1)}, f32[96,256]{1,0:T(8,128)S(1)}, u32[]{:S(2)}, u32[]{:S(2)}) collective-permute-start(f32[96,256]{1,0:T(8,128)S(1)} %init.1.own), channel_id=1, source_target_pairs={{0,16},{32,48},{64,80},{96,112},{16,0},{48,32},{80,64},{112,96},{1... | collective-permute-start | bytes 294920 | tf_op jit(solution)/shard_map/ppermute | solution.py:441
  5.1 0.9 %collective-permute-done.sib = f32[96,256]{1,0:T(8,128)S(1)} collective-permute-done((f32[96,256]{1,0:T(8,128)S(1)}, f32[96,256]{1,0:T(8,128)S(1)}, u32[]{:S(2)}, u32[]{:S(2)}) %collective-permute-start) | collective-permute-done | bytes 98336 | tf_op jit(solution)/shard_map/ppermute | solution.py:441
  6.0 0.2 start.1
  6.2 2.9 %collective-permute-start.1 = (f32[48,128]{1,0:T(8,128)S(1)}, f32[48,128]{1,0:T(8,128)S(1)}, u32[]{:S(2)}, u32[]{:S(2)}) collective-permute-start(f32[48,128]{1,0:T(8,128)S(1)} %get-tuple-element.57), channel_id=1, source_target_pairs={{0,32},{64,96},{48,80},{112,16},{32,0},{96,64},{80,48},{16,112},{1... | collective-permute-start | bytes 73736 | tf_op jit(solution)/shard_map/ppermute | solution.py:446
  9.0 0.0 copy-done.1
  9.0 0.0 copy-done
  9.0 1.2 %own.4 = (f32[2,80,80]{2,1,0:T(8,128)S(1)}, f32[2,80,80]{2,1,0:T(8,128)S(1)}, f32[1,2048]{1,0:T(1,128)S(1)}) custom-call(s32[4]{0:T(128)S(1)} %copy-done.1, s32[4,2048]{1,0:T(4,128)S(1)} %copy-done, f32[2,48,128]{2,1,0:T(8,128)S(1)} %get-tuple-element.58.pay), custom_call_target="tpu_custom_call" | custom-call | tf_op jit(solution)/shard_map/own/pallas_call | solution.py:447
  10.3 0.0 collective-permute-done.1.far
  10.3 0.1 collective-permute-start.2
  10.4 1.1 %collective-permute-done.2.sib_far = f32[48,128]{1,0:T(8,128)S(1)} collective-permute-done((f32[48,128]{1,0:T(8,128)S(1)}, f32[48,128]{1,0:T(8,128)S(1)}, u32[]{:S(2)}, u32[]{:S(2)}) %collective-permute-start.2) | collective-permute-done | bytes 24608 | tf_op jit(solution)/shard_map/ppermute | solution.py:455
  11.5 0.3 send.4
  11.8 1.2 %collective-permute-start.3 = (f32[2,80,80]{2,1,0:T(8,128)S(1)}, f32[2,80,80]{2,1,0:T(8,128)S(1)}, u32[]{:S(2)}, u32[]{:S(2)}) collective-permute-start(f32[2,80,80]{2,1,0:T(8,128)S(1)} %send.4), channel_id=1, source_target_pairs={{0,1},{2,3},{4,5},{6,7},{8,9},{10,11},{12,13},{14,15},{17,18},{19,... | collective-permute-start | bytes 153608 | tf_op jit(solution)/shard_map/ppermute | solution.py:460
  13.0 0.3 same.4.q0
  13.3 2.2 %collective-permute-done.3.h = f32[2,80,80]{2,1,0:T(8,128)S(1)} collective-permute-done((f32[2,80,80]{2,1,0:T(8,128)S(1)}, f32[2,80,80]{2,1,0:T(8,128)S(1)}, u32[]{:S(2)}, u32[]{:S(2)}) %collective-permute-start.3) | collective-permute-done | bytes 51232 | tf_op jit(solution)/shard_map/ppermute | solution.py:460
  15.5 1.0 %collective-permute-start.4 = (f32[2,80,80]{2,1,0:T(8,128)S(1)}, f32[2,80,80]{2,1,0:T(8,128)S(1)}, u32[]{:S(2)}, u32[]{:S(2)}) collective-permute-start(f32[2,80,80]{2,1,0:T(8,128)S(1)} %collective-permute-done.3.h), channel_id=1, source_target_pairs={{0,16},{32,48},{64,80},{96,112},{16,0},{48,32},{80,64},{112,96},{1... | collective-permute-start | bytes 153608 | tf_op jit(solution)/shard_map/ppermute | solution.py:488
  16.5 0.9 %collective-permute-done.4.g = f32[2,80,80]{2,1,0:T(8,128)S(1)} collective-permute-done((f32[2,80,80]{2,1,0:T(8,128)S(1)}, f32[2,80,80]{2,1,0:T(8,128)S(1)}, u32[]{:S(2)}, u32[]{:S(2)}) %collective-permute-start.4) | collective-permute-done | bytes 51232 | tf_op jit(solution)/shard_map/ppermute | solution.py:488
  17.4 0.4 step.3
  17.8 2.8 %collective-permute-start.5 = (f32[48,128]{1,0:T(8,128)S(1)}, f32[48,128]{1,0:T(8,128)S(1)}, u32[]{:S(2)}, u32[]{:S(2)}) collective-permute-start(f32[48,128]{1,0:T(8,128)S(1)} %get-tuple-element.68), channel_id=1, source_target_pairs={{0,32},{64,96},{48,80},{112,16},{32,0},{96,64},{80,48},{16,112},{1... | collective-permute-start | bytes 73736 | tf_op jit(solution)/shard_map/ppermute | solution.py:446
  20.6 1.2 %own.5 = (f32[2,80,80]{2,1,0:T(8,128)S(1)}, f32[2,80,80]{2,1,0:T(8,128)S(1)}, f32[1,2048]{1,0:T(1,128)S(1)}) custom-call(s32[4]{0:T(128)S(1)} %copy-done.1, s32[4,2048]{1,0:T(4,128)S(1)} %copy-done, f32[2,48,128]{2,1,0:T(8,128)S(1)} %get-tuple-element.69.pay), custom_call_target="tpu_custom_call" | custom-call | tf_op jit(solution)/shard_map/own/pallas_call | solution.py:447
  21.8 0.0 collective-permute-done.5.far
  21.8 0.2 collective-permute-start.6
  22.1 1.0 %collective-permute-done.6.sib_far = f32[48,128]{1,0:T(8,128)S(1)} collective-permute-done((f32[48,128]{1,0:T(8,128)S(1)}, f32[48,128]{1,0:T(8,128)S(1)}, u32[]{:S(2)}, u32[]{:S(2)}) %collective-permute-start.6) | collective-permute-done | bytes 24608 | tf_op jit(solution)/shard_map/ppermute | solution.py:455
  23.1 0.3 send.5
  23.4 1.2 %collective-permute-start.7 = (f32[2,80,80]{2,1,0:T(8,128)S(1)}, f32[2,80,80]{2,1,0:T(8,128)S(1)}, u32[]{:S(2)}, u32[]{:S(2)}) collective-permute-start(f32[2,80,80]{2,1,0:T(8,128)S(1)} %send.5), channel_id=1, source_target_pairs={{0,1},{2,3},{4,5},{6,7},{8,9},{10,11},{12,13},{14,15},{17,18},{19,... | collective-permute-start | bytes 153608 | tf_op jit(solution)/shard_map/ppermute | solution.py:460
  24.6 0.3 same.5.q0
  24.9 2.2 %collective-permute-done.7.h = f32[2,80,80]{2,1,0:T(8,128)S(1)} collective-permute-done((f32[2,80,80]{2,1,0:T(8,128)S(1)}, f32[2,80,80]{2,1,0:T(8,128)S(1)}, u32[]{:S(2)}, u32[]{:S(2)}) %collective-permute-start.7) | collective-permute-done | bytes 51232 | tf_op jit(solution)/shard_map/ppermute | solution.py:460
  27.0 1.0 %collective-permute-start.8 = (f32[2,80,80]{2,1,0:T(8,128)S(1)}, f32[2,80,80]{2,1,0:T(8,128)S(1)}, u32[]{:S(2)}, u32[]{:S(2)}) collective-permute-start(f32[2,80,80]{2,1,0:T(8,128)S(1)} %collective-permute-done.7.h), channel_id=1, source_target_pairs={{0,16},{32,48},{64,80},{96,112},{16,0},{48,32},{80,64},{112,96},{1... | collective-permute-start | bytes 153608 | tf_op jit(solution)/shard_map/ppermute | solution.py:488
  28.1 0.9 %collective-permute-done.8.g = f32[2,80,80]{2,1,0:T(8,128)S(1)} collective-permute-done((f32[2,80,80]{2,1,0:T(8,128)S(1)}, f32[2,80,80]{2,1,0:T(8,128)S(1)}, u32[]{:S(2)}, u32[]{:S(2)}) %collective-permute-start.8) | collective-permute-done | bytes 51232 | tf_op jit(solution)/shard_map/ppermute | solution.py:488
  29.0 0.4 step.4
  29.4 2.8 %collective-permute-start.9 = (f32[48,128]{1,0:T(8,128)S(1)}, f32[48,128]{1,0:T(8,128)S(1)}, u32[]{:S(2)}, u32[]{:S(2)}) collective-permute-start(f32[48,128]{1,0:T(8,128)S(1)} %get-tuple-element.79), channel_id=1, source_target_pairs={{0,32},{64,96},{48,80},{112,16},{32,0},{96,64},{80,48},{16,112},{1... | collective-permute-start | bytes 73736 | tf_op jit(solution)/shard_map/ppermute | solution.py:446
  32.1 1.2 %own.6 = (f32[2,80,80]{2,1,0:T(8,128)S(1)}, f32[2,80,80]{2,1,0:T(8,128)S(1)}, f32[1,2048]{1,0:T(1,128)S(1)}) custom-call(s32[4]{0:T(128)S(1)} %copy-done.1, s32[4,2048]{1,0:T(4,128)S(1)} %copy-done, f32[2,48,128]{2,1,0:T(8,128)S(1)} %get-tuple-element.80.pay), custom_call_target="tpu_custom_call" | custom-call | tf_op jit(solution)/shard_map/own/pallas_call | solution.py:447
  33.4 0.0 collective-permute-done.9.far
  33.4 0.2 collective-permute-start.10
  33.6 1.0 %collective-permute-done.10.sib_far = f32[48,128]{1,0:T(8,128)S(1)} collective-permute-done((f32[48,128]{1,0:T(8,128)S(1)}, f32[48,128]{1,0:T(8,128)S(1)}, u32[]{:S(2)}, u32[]{:S(2)}) %collective-permute-start.10) | collective-permute-done | bytes 24608 | tf_op jit(solution)/shard_map/ppermute | solution.py:455
  34.6 0.3 send.6
  34.9 1.2 %collective-permute-start.11 = (f32[2,80,80]{2,1,0:T(8,128)S(1)}, f32[2,80,80]{2,1,0:T(8,128)S(1)}, u32[]{:S(2)}, u32[]{:S(2)}) collective-permute-start(f32[2,80,80]{2,1,0:T(8,128)S(1)} %send.6), channel_id=1, source_target_pairs={{0,1},{2,3},{4,5},{6,7},{8,9},{10,11},{12,13},{14,15},{17,18},{19,... | collective-permute-start | bytes 153608 | tf_op jit(solution)/shard_map/ppermute | solution.py:460
  36.1 2.2 %turn.1.near = bf16[32,160,256]{2,1,0:T(8,128)(2,1)S(1)} custom-call(f32[80,4,32,256]{3,2,1,0:T(8,128)} %x.3), custom_call_target="tpu_custom_call" | custom-call | tf_op jit(solution)/shard_map/turn/pallas_call | solution.py:479
  38.3 0.3 same.6.q0
  38.6 0.0 collective-permute-done.11.h
  38.6 1.0 %collective-permute-start.12 = (f32[2,80,80]{2,1,0:T(8,128)S(1)}, f32[2,80,80]{2,1,0:T(8,128)S(1)}, u32[]{:S(2)}, u32[]{:S(2)}) collective-permute-start(f32[2,80,80]{2,1,0:T(8,128)S(1)} %collective-permute-done.11.h), channel_id=1, source_target_pairs={{0,16},{32,48},{64,80},{96,112},{16,0},{48,32},{80,64},{112,96},{1... | collective-permute-start | bytes 153608 | tf_op jit(solution)/shard_map/ppermute | solution.py:488
  39.6 0.9 %collective-permute-done.12.g = f32[2,80,80]{2,1,0:T(8,128)S(1)} collective-permute-done((f32[2,80,80]{2,1,0:T(8,128)S(1)}, f32[2,80,80]{2,1,0:T(8,128)S(1)}, u32[]{:S(2)}, u32[]{:S(2)}) %collective-permute-start.12) | collective-permute-done | bytes 51232 | tf_op jit(solution)/shard_map/ppermute | solution.py:488
  40.5 0.4 step.5
  40.9 2.8 %collective-permute-start.13 = (f32[56,128]{1,0:T(8,128)S(1)}, f32[56,128]{1,0:T(8,128)S(1)}, u32[]{:S(2)}, u32[]{:S(2)}) collective-permute-start(f32[56,128]{1,0:T(8,128)S(1)} %get-tuple-element.90), channel_id=1, source_target_pairs={{0,32},{64,96},{48,80},{112,16},{32,0},{96,64},{80,48},{16,112},{1... | collective-permute-start | bytes 86024 | tf_op jit(solution)/shard_map/ppermute | solution.py:446
  43.7 1.2 %own.7 = (f32[2,80,80]{2,1,0:T(8,128)S(1)}, f32[2,80,80]{2,1,0:T(8,128)S(1)}, f32[1,2048]{1,0:T(1,128)S(1)}) custom-call(s32[4]{0:T(128)S(1)} %copy-done.1, s32[4,2048]{1,0:T(4,128)S(1)} %copy-done, f32[2,48,128]{2,1,0:T(8,128)S(1)} %get-tuple-element.91.pay), custom_call_target="tpu_custom_call" | custom-call | tf_op jit(solution)/shard_map/own/pallas_call | solution.py:447
  44.9 0.1 collective-permute-done.13.far
  45.0 0.2 collective-permute-start.14
  45.2 1.0 %collective-permute-done.14.sib_far = f32[56,128]{1,0:T(8,128)S(1)} collective-permute-done((f32[56,128]{1,0:T(8,128)S(1)}, f32[56,128]{1,0:T(8,128)S(1)}, u32[]{:S(2)}, u32[]{:S(2)}) %collective-permute-start.14) | collective-permute-done | bytes 28704 | tf_op jit(solution)/shard_map/ppermute | solution.py:455
  46.2 0.3 send.7
  46.5 1.2 %collective-permute-start.15 = (f32[2,80,80]{2,1,0:T(8,128)S(1)}, f32[2,80,80]{2,1,0:T(8,128)S(1)}, u32[]{:S(2)}, u32[]{:S(2)}) collective-permute-start(f32[2,80,80]{2,1,0:T(8,128)S(1)} %send.7), channel_id=1, source_target_pairs={{0,1},{2,3},{4,5},{6,7},{8,9},{10,11},{12,13},{14,15},{17,18},{19,... | collective-permute-start | bytes 153608 | tf_op jit(solution)/shard_map/ppermute | solution.py:460
  47.7 1.9 %collective-permute-start.16 = (f32[8,128]{1,0:T(8,128)S(1)}, f32[8,128]{1,0:T(8,128)S(1)}, u32[]{:S(2)}, u32[]{:S(2)}) collective-permute-start(f32[8,128]{1,0:T(8,128)S(1)} %slice.3), channel_id=1, source_target_pairs={{0,32},{64,96},{48,80},{112,16},{32,0},{96,64},{80,48},{16,112},{1... | collective-permute-start | bytes 12296 | tf_op jit(solution)/shard_map/ppermute | solution.py:466
  49.6 0.3 same.7.q0
  49.9 1.5 %collective-permute-done.16.across = f32[8,128]{1,0:T(8,128)S(1)} collective-permute-done((f32[8,128]{1,0:T(8,128)S(1)}, f32[8,128]{1,0:T(8,128)S(1)}, u32[]{:S(2)}, u32[]{:S(2)}) %collective-permute-start.16) | collective-permute-done | bytes 4128 | tf_op jit(solution)/shard_map/ppermute | solution.py:466
  51.4 0.7 column.1
  52.0 0.0 collective-permute-done.15.h
  52.0 0.5 collective-permute-start.17
  52.5 10.4 %all-to-all-start = ((f32[16,16,128]{2,1,0:T(8,128)}), f32[16,16,128]{2,1,0:T(8,128)S(1)}, u32[]{:S(2)}, u32[]{:S(2)}) async-start(f32[16,16,128]{2,1,0:T(8,128)} %column.1), calls=%async_computation | async-start | bytes 262144 | tf_op jit(solution)/shard_map/all_to_all | solution.py:472
  62.9 0.0 collective-permute-done.17.g
  63.0 7.1 %final.1 = (f32[80,4,32,256]{3,2,1,0:T(8,128)}, bf16[80,240]{1,0:T(8,128)(2,1)S(1)}) custom-call(f32[2,80,80]{2,1,0:T(8,128)S(1)} %same.7.q0, f32[2,80,80]{2,1,0:T(8,128)S(1)} %collective-permute-done.15.h, f32[2,80,80]{2,1,0:T(8,128)S(1)} %collective-permute-done.17.g, f32[2,96,384]{2,1,0:T(8,128)S(1)} %get-tuple-element.101.z, f32[80,4,32,256]{3,2,1,0:T(8,128)} %x.3), custom_call_target="tpu_custom_call" | custom-call | flops 1258291200 | bytes 20971520 | tf_op jit(solution)/shard_map/final/pallas_call | solution.py:502
  70.0 0.0 all-to-all-done.gathered
  70.0 3.6 %last.1 = (f32[80,4,32,256]{3,2,1,0:T(8,128)}, f32[4,2048]{1,0:T(4,128)}) custom-call(f32[80,4,32,256]{3,2,1,0:T(8,128)} %get-tuple-element.102.done, bf16[80,240]{1,0:T(8,128)(2,1)S(1)} %get-tuple-element.105.mix, bf16[32,160,256]{2,1,0:T(8,128)(2,1)S(1)} %turn.1.near, s32[4]{0:T(128)S(1)} %copy-done.1, ...), custom_call_target="tpu_custom_call", output_to_operand_aliasing={{0}: (0, {})} | custom-call | tf_op jit(solution)/shard_map/last/pallas_call | solution.py:516
  (1 shorter events, 0.0 us)
Async XLA Ops:
  0.6 8.4 %copy-start.1 = (s32[4]{0:T(128)S(1)}, s32[4]{0:T(128)}, u32[]{:S(2)}) copy-start(s32[4]{0:T(128)} %order.9) | copy-start | bytes 52
  0.6 8.4 %copy-start = (s32[4,2048]{1,0:T(4,128)S(1)}, s32[4,2048]{1,0:T(4,128)}, u32[]{:S(2)}) copy-start(s32[4,2048]{1,0:T(4,128)} %owner.9) | copy-start | bytes 98308
  3.6 2.4 %collective-permute-start = (f32[96,256]{1,0:T(8,128)S(1)}, f32[96,256]{1,0:T(8,128)S(1)}, u32[]{:S(2)}, u32[]{:S(2)}) collective-permute-start(f32[96,256]{1,0:T(8,128)S(1)} %init.1.own), channel_id=1, source_target_pairs={{0,16},{32,48},{64,80},{96,112},{16,0},{48,32},{80,64},{112,96},{1... | collective-permute-start | bytes 294920 | tf_op jit(solution)/shard_map/ppermute | solution.py:441
  6.2 4.1 %collective-permute-start.1 = (f32[48,128]{1,0:T(8,128)S(1)}, f32[48,128]{1,0:T(8,128)S(1)}, u32[]{:S(2)}, u32[]{:S(2)}) collective-permute-start(f32[48,128]{1,0:T(8,128)S(1)} %get-tuple-element.57), channel_id=1, source_target_pairs={{0,32},{64,96},{48,80},{112,16},{32,0},{96,64},{80,48},{16,112},{1... | collective-permute-start | bytes 73736 | tf_op jit(solution)/shard_map/ppermute | solution.py:446
  10.3 1.3 %collective-permute-start.2 = (f32[48,128]{1,0:T(8,128)S(1)}, f32[48,128]{1,0:T(8,128)S(1)}, u32[]{:S(2)}, u32[]{:S(2)}) collective-permute-start(f32[48,128]{1,0:T(8,128)S(1)} %collective-permute-done.1.far), channel_id=1, source_target_pairs={{0,16},{32,48},{64,80},{96,112},{16,0},{48,32},{80,64},{112,96},{1... | collective-permute-start | bytes 73736 | tf_op jit(solution)/shard_map/ppermute | solution.py:455
  11.8 3.7 %collective-permute-start.3 = (f32[2,80,80]{2,1,0:T(8,128)S(1)}, f32[2,80,80]{2,1,0:T(8,128)S(1)}, u32[]{:S(2)}, u32[]{:S(2)}) collective-permute-start(f32[2,80,80]{2,1,0:T(8,128)S(1)} %send.4), channel_id=1, source_target_pairs={{0,1},{2,3},{4,5},{6,7},{8,9},{10,11},{12,13},{14,15},{17,18},{19,... | collective-permute-start | bytes 153608 | tf_op jit(solution)/shard_map/ppermute | solution.py:460
  15.5 1.9 %collective-permute-start.4 = (f32[2,80,80]{2,1,0:T(8,128)S(1)}, f32[2,80,80]{2,1,0:T(8,128)S(1)}, u32[]{:S(2)}, u32[]{:S(2)}) collective-permute-start(f32[2,80,80]{2,1,0:T(8,128)S(1)} %collective-permute-done.3.h), channel_id=1, source_target_pairs={{0,16},{32,48},{64,80},{96,112},{16,0},{48,32},{80,64},{112,96},{1... | collective-permute-start | bytes 153608 | tf_op jit(solution)/shard_map/ppermute | solution.py:488
  17.8 4.0 %collective-permute-start.5 = (f32[48,128]{1,0:T(8,128)S(1)}, f32[48,128]{1,0:T(8,128)S(1)}, u32[]{:S(2)}, u32[]{:S(2)}) collective-permute-start(f32[48,128]{1,0:T(8,128)S(1)} %get-tuple-element.68), channel_id=1, source_target_pairs={{0,32},{64,96},{48,80},{112,16},{32,0},{96,64},{80,48},{16,112},{1... | collective-permute-start | bytes 73736 | tf_op jit(solution)/shard_map/ppermute | solution.py:446
  21.8 1.3 %collective-permute-start.6 = (f32[48,128]{1,0:T(8,128)S(1)}, f32[48,128]{1,0:T(8,128)S(1)}, u32[]{:S(2)}, u32[]{:S(2)}) collective-permute-start(f32[48,128]{1,0:T(8,128)S(1)} %collective-permute-done.5.far), channel_id=1, source_target_pairs={{0,16},{32,48},{64,80},{96,112},{16,0},{48,32},{80,64},{112,96},{1... | collective-permute-start | bytes 73736 | tf_op jit(solution)/shard_map/ppermute | solution.py:455
  23.4 3.7 %collective-permute-start.7 = (f32[2,80,80]{2,1,0:T(8,128)S(1)}, f32[2,80,80]{2,1,0:T(8,128)S(1)}, u32[]{:S(2)}, u32[]{:S(2)}) collective-permute-start(f32[2,80,80]{2,1,0:T(8,128)S(1)} %send.5), channel_id=1, source_target_pairs={{0,1},{2,3},{4,5},{6,7},{8,9},{10,11},{12,13},{14,15},{17,18},{19,... | collective-permute-start | bytes 153608 | tf_op jit(solution)/shard_map/ppermute | solution.py:460
  27.0 1.9 %collective-permute-start.8 = (f32[2,80,80]{2,1,0:T(8,128)S(1)}, f32[2,80,80]{2,1,0:T(8,128)S(1)}, u32[]{:S(2)}, u32[]{:S(2)}) collective-permute-start(f32[2,80,80]{2,1,0:T(8,128)S(1)} %collective-permute-done.7.h), channel_id=1, source_target_pairs={{0,16},{32,48},{64,80},{96,112},{16,0},{48,32},{80,64},{112,96},{1... | collective-permute-start | bytes 153608 | tf_op jit(solution)/shard_map/ppermute | solution.py:488
  29.4 4.0 %collective-permute-start.9 = (f32[48,128]{1,0:T(8,128)S(1)}, f32[48,128]{1,0:T(8,128)S(1)}, u32[]{:S(2)}, u32[]{:S(2)}) collective-permute-start(f32[48,128]{1,0:T(8,128)S(1)} %get-tuple-element.79), channel_id=1, source_target_pairs={{0,32},{64,96},{48,80},{112,16},{32,0},{96,64},{80,48},{16,112},{1... | collective-permute-start | bytes 73736 | tf_op jit(solution)/shard_map/ppermute | solution.py:446
  33.4 1.3 %collective-permute-start.10 = (f32[48,128]{1,0:T(8,128)S(1)}, f32[48,128]{1,0:T(8,128)S(1)}, u32[]{:S(2)}, u32[]{:S(2)}) collective-permute-start(f32[48,128]{1,0:T(8,128)S(1)} %collective-permute-done.9.far), channel_id=1, source_target_pairs={{0,16},{32,48},{64,80},{96,112},{16,0},{48,32},{80,64},{112,96},{1... | collective-permute-start | bytes 73736 | tf_op jit(solution)/shard_map/ppermute | solution.py:455
  34.9 3.7 %collective-permute-start.11 = (f32[2,80,80]{2,1,0:T(8,128)S(1)}, f32[2,80,80]{2,1,0:T(8,128)S(1)}, u32[]{:S(2)}, u32[]{:S(2)}) collective-permute-start(f32[2,80,80]{2,1,0:T(8,128)S(1)} %send.6), channel_id=1, source_target_pairs={{0,1},{2,3},{4,5},{6,7},{8,9},{10,11},{12,13},{14,15},{17,18},{19,... | collective-permute-start | bytes 153608 | tf_op jit(solution)/shard_map/ppermute | solution.py:460
  38.6 1.9 %collective-permute-start.12 = (f32[2,80,80]{2,1,0:T(8,128)S(1)}, f32[2,80,80]{2,1,0:T(8,128)S(1)}, u32[]{:S(2)}, u32[]{:S(2)}) collective-permute-start(f32[2,80,80]{2,1,0:T(8,128)S(1)} %collective-permute-done.11.h), channel_id=1, source_target_pairs={{0,16},{32,48},{64,80},{96,112},{16,0},{48,32},{80,64},{112,96},{1... | collective-permute-start | bytes 153608 | tf_op jit(solution)/shard_map/ppermute | solution.py:488
  40.9 4.0 %collective-permute-start.13 = (f32[56,128]{1,0:T(8,128)S(1)}, f32[56,128]{1,0:T(8,128)S(1)}, u32[]{:S(2)}, u32[]{:S(2)}) collective-permute-start(f32[56,128]{1,0:T(8,128)S(1)} %get-tuple-element.90), channel_id=1, source_target_pairs={{0,32},{64,96},{48,80},{112,16},{32,0},{96,64},{80,48},{16,112},{1... | collective-permute-start | bytes 86024 | tf_op jit(solution)/shard_map/ppermute | solution.py:446
  45.0 1.2 %collective-permute-start.14 = (f32[56,128]{1,0:T(8,128)S(1)}, f32[56,128]{1,0:T(8,128)S(1)}, u32[]{:S(2)}, u32[]{:S(2)}) collective-permute-start(f32[56,128]{1,0:T(8,128)S(1)} %collective-permute-done.13.far), channel_id=1, source_target_pairs={{0,16},{32,48},{64,80},{96,112},{16,0},{48,32},{80,64},{112,96},{1... | collective-permute-start | bytes 86024 | tf_op jit(solution)/shard_map/ppermute | solution.py:455
  46.5 5.6 %collective-permute-start.15 = (f32[2,80,80]{2,1,0:T(8,128)S(1)}, f32[2,80,80]{2,1,0:T(8,128)S(1)}, u32[]{:S(2)}, u32[]{:S(2)}) collective-permute-start(f32[2,80,80]{2,1,0:T(8,128)S(1)} %send.7), channel_id=1, source_target_pairs={{0,1},{2,3},{4,5},{6,7},{8,9},{10,11},{12,13},{14,15},{17,18},{19,... | collective-permute-start | bytes 153608 | tf_op jit(solution)/shard_map/ppermute | solution.py:460
  47.7 3.7 %collective-permute-start.16 = (f32[8,128]{1,0:T(8,128)S(1)}, f32[8,128]{1,0:T(8,128)S(1)}, u32[]{:S(2)}, u32[]{:S(2)}) collective-permute-start(f32[8,128]{1,0:T(8,128)S(1)} %slice.3), channel_id=1, source_target_pairs={{0,32},{64,96},{48,80},{112,16},{32,0},{96,64},{80,48},{16,112},{1... | collective-permute-start | bytes 12296 | tf_op jit(solution)/shard_map/ppermute | solution.py:466
  52.0 10.9 %collective-permute-start.17 = (f32[2,80,80]{2,1,0:T(8,128)S(1)}, f32[2,80,80]{2,1,0:T(8,128)S(1)}, u32[]{:S(2)}, u32[]{:S(2)}) collective-permute-start(f32[2,80,80]{2,1,0:T(8,128)S(1)} %collective-permute-done.15.h), channel_id=1, source_target_pairs={{0,16},{32,48},{64,80},{96,112},{16,0},{48,32},{80,64},{112,96},{1... | collective-permute-start | bytes 153608 | tf_op jit(solution)/shard_map/ppermute | solution.py:488
  52.5 17.5 %all-to-all-start = ((f32[16,16,128]{2,1,0:T(8,128)}), f32[16,16,128]{2,1,0:T(8,128)S(1)}, u32[]{:S(2)}, u32[]{:S(2)}) async-start(f32[16,16,128]{2,1,0:T(8,128)} %column.1), calls=%async_computation | async-start | bytes 262144 | tf_op jit(solution)/shard_map/all_to_all | solution.py:472

commit v15 on v13

--- a/solution.py
+++ b/solution.py
@@ -325,32 +325,8 @@
             turn(come[i, :, j : j + 8, :], out, SLAB * i + j)
 
 
-def turn_away_kernel(first, x, out, come, turned, sems, out_sems):
-    loads = [pltpu.make_async_copy(part(x, first + i), come.at[i], sems.at[i]) for i in range(TURN)]
-    stores = [
-        pltpu.make_async_copy(turned.at[pl.ds(SLAB * i, SLAB)], out.at[pl.ds(SLAB * i, SLAB)], out_sems.at[i])
-        for i in range(TURN)
-    ]
-    for load in loads:
-        load.start()
-    for i in range(TURN):
-        loads[i].wait()
-        for j in range(0, SLAB, 8):
-            turn(come[i, :, j : j + 8, :], turned, SLAB * i + j)
-        stores[i].start()
-    for store in stores:
-        store.wait()
-
-
-def final_kernel(q0, h, g, z, near, far0, far1, x, out, back, come, go, back_sems, come_sems, go_sems):
-    loads = [
-        pltpu.make_async_copy(
-            (far0, far1)[i // TURN].at[pl.ds(SLAB * (i % TURN), SLAB)], back.at[pl.ds(SLAB * i, SLAB)], back_sems.at[i]
-        )
-        for i in range(2 * TURN)
-    ]
-    raw = 3 * TURN
-    loads += [pltpu.make_async_copy(part(x, i), come.at[i - raw], come_sems.at[i - raw]) for i in range(raw, SLABS)]
+def final_kernel(q0, h, g, z, near, x, out, come, go, come_sems, go_sems):
+    loads = [pltpu.make_async_copy(part(x, i), come.at[i - TURN], come_sems.at[i - TURN]) for i in range(TURN, SLABS)]
     stores = [pltpu.make_async_copy(go.at[i], part(out, i), go_sems.at[i]) for i in range(SLABS)]
     for load in loads:
         load.start()
@@ -362,15 +338,15 @@
         if i >= TURN:
             loads[i - TURN].wait()
         for j in range(0, SLAB, 8):
-            if i >= raw:
-                turned = jnp.swapaxes(come[i - raw, :, j : j + 8, :], 0, 1)
+            if i >= TURN:
+                turned = jnp.swapaxes(come[i - TURN, :, j : j + 8, :], 0, 1)
             rows = []
             for r in range(8):
-                if i >= raw:
+                if i >= TURN:
                     xh, xl = split2(turned[r])
                     stack = [xh, xl, xh]
                 else:
-                    both = near[SLAB * i + j + r] if i < TURN else back[SLAB * (i - TURN) + j + r]
+                    both = near[SLAB * i + j + r]
                     stack = [both, both[:M]]
                 rows.append(dot(w, jnp.concatenate(stack, axis=0))[None])
             go[i, :, j : j + 8, :] = jnp.swapaxes(jnp.concatenate(rows, axis=0), 0, 1)
@@ -453,7 +429,7 @@
         out_specs=(VMEM,) * 3,
         name="start",
     )(own, lax.ppermute(own, "gx", core))
-    ranks, aways = [], []
+    ranks = []
     state_hbm = pltpu.with_memory_space_constraint(ensemble, pltpu.HBM)
     for k in range(NB):
         last = k + 1 == NB
@@ -488,19 +464,7 @@
             turned_shape = jax.ShapeDtypeStruct((TURN * SLAB, 2 * M, TY), BF16)
             come = pltpu.VMEM((TURN, M, SLAB, TY), F32)
             if k + 2 < NB:
-                turned = call(
-                    functools.partial(turn_away_kernel, TURN * (k + 1)),
-                    out_shape=pltpu.HBM(turned_shape.shape, BF16),
-                    in_specs=[HBM],
-                    out_specs=HBM,
-                    scratch_shapes=[
-                        come, pltpu.VMEM((TURN * SLAB, 2 * M, TY), BF16),
-                        pltpu.SemaphoreType.DMA((TURN,)), pltpu.SemaphoreType.DMA((TURN,)),
-                    ],
-                    name="turn",
-                )(state_hbm)
-                h, q0, turned = lax.optimization_barrier((h, q0, turned))
-                aways.append(turned)
+                h, q0 = lax.optimization_barrier((h, q0))
             else:
                 near = call(
                     functools.partial(turn_kernel, 0),
@@ -528,17 +492,15 @@
     state = call(
         final_kernel,
         out_shape=shape(M, LEV, TX, TY),
-        in_specs=[VMEM] * 5 + [HBM] * 3,
+        in_specs=[VMEM] * 5 + [HBM],
         out_specs=HBM,
         scratch_shapes=[
-            pltpu.VMEM((2 * TURN * SLAB, 2 * M, TY), BF16),
-            pltpu.VMEM((SLABS - 3 * TURN, M, SLAB, TY), F32),
-            pltpu.VMEM((SLABS, M, SLAB, TY), F32),
-            dma(2 * TURN), dma(SLABS - 3 * TURN), dma(SLABS),
+            pltpu.VMEM((SLABS - TURN, M, SLAB, TY), F32), pltpu.VMEM((SLABS, M, SLAB, TY), F32),
+            dma(SLABS - TURN), dma(SLABS),
         ],
         cost_estimate=pl.CostEstimate(flops=6 * M * M * LEV * TX * TY, bytes_accessed=8 * M * LEV * TX * TY, transcendentals=0),
         name="final",
-    )(q0, h, g, z, near, *(pltpu.with_memory_space_constraint(value, pltpu.HBM) for value in aways), state_hbm)
+    )(q0, h, g, z, near, state_hbm)
     state, gathered = lax.optimization_barrier((state, gathered))
     innovation = call(
         place_kernel,

time: 73.8 us -> 74.1 us (level)
  Pallas kernels: 31 us -> 25.1 us
  waiting for transfers between devices: 9.61 us -> 13.8 us
  starting transfers between devices: 32.1 us -> 34.2 us
    pallas_call x2 -> x0, Pallas kernels: 6.58 us -> none  [local(): call(functools.partial(turn_away_kernel, TURN * (k + 1)), out_shape=pltpu...]
    ppermute x4, waiting for transfers between devices: 0.15 us -> 4.39 us  [local(): h = lax.ppermute(send, both, side_y)]
    ppermute x4, starting transfers between devices: 2.64 us -> 3.54 us  [local(): g = lax.ppermute(h, 'gx', core)]
    all_to_all x1, starting transfers between devices: 9.55 us -> 10.4 us  [local(): gathered = lax.all_to_all(column, 'gy', 0, 0, tiled=True)]
  transfers between devices with their start and end apart: 19 -> 19, of which waited for: 12 -> 11; matrix products, arithmetic and copies ran while one was open for 0% -> 0% of each run, Pallas kernels for 32% -> 24%
where the time goes in v15:
time: 74.1 us; the launch traced here: 73.9 us
  starting transfers between devices  34.2 us (46%)
  Pallas kernels  25.1 us (34%)
  waiting for transfers between devices  13.8 us (19%)
  between operations  0.82 us (1%)
    ppermute x4, starting transfers between devices, local(): far = lax.ppermute(edge, 'gx', side_x)  11.2 us
    all_to_all x1, starting transfers between devices, local(): gathered = lax.all_to_all(column, 'gy', 0, 0, tiled=True)  10.4 us
    pallas_call x1, Pallas kernels, local(): call(final_kernel, out_shape=shape(M, LEV, TX, TY), in_specs=[VMEM] * 5 +...  8.85 us
    pallas_call x4, Pallas kernels, local(): call(functools.partial(own_kernel, k), out_shape=(shape(2, M, M), shape(2...  4.81 us
    ppermute x4, starting transfers between devices, local(): h = lax.ppermute(send, both, side_y)  4.75 us
    ppermute x4, waiting for transfers between devices, local(): h = lax.ppermute(send, both, side_y)  4.39 us
    ppermute x4, waiting for transfers between devices, local(): sib_far = lax.ppermute(far, 'gx', core)  4.19 us
    ppermute x4, starting transfers between devices, local(): g = lax.ppermute(h, 'gx', core)  3.54 us
  transfers between devices with their start and end apart: 19, of which 11 were waited for; matrix products, arithmetic and copies ran while one was open for 0% of the time, Pallas kernels for 24%

profile of v15, /device:TPU:1, one launch (start us, length us, event | category | flops | bytes accessed | tf_op | source)
XLA Modules:
  0.0 73.9 jit_solution(16008203174987383859)
XLA Ops:
  0.6 0.0 copy-start.1
  0.6 0.0 copy-start
  0.7 2.9 %init.1.own = f32[96,256]{1,0:T(8,128)S(1)} custom-call(s32[4]{0:T(128)} %order.9, f32[4,2048]{1,0:T(4,128)} %value_hbm.1, f32[4,2048]{1,0:T(4,128)} %variance_hbm.1, s32[4,2048]{1,0:T(4,128)} %owner.9, s32[4,2048]{1,0:T(4,128)} %cell_hbm.1, s32[4,8,2048]{2,1,0:T(8,128)} %bitcast.1, f32[80,4,32,256]{3,2,1,0:T(8,128)} %x.3), custom_call_target="tpu_custom_call" | custom-call | tf_op jit(solution)/shard_map/init/pallas_call | solution.py:409
  3.6 1.5 %collective-permute-start = (f32[96,256]{1,0:T(8,128)S(1)}, f32[96,256]{1,0:T(8,128)S(1)}, u32[]{:S(2)}, u32[]{:S(2)}) collective-permute-start(f32[96,256]{1,0:T(8,128)S(1)} %init.1.own), channel_id=1, source_target_pairs={{0,16},{32,48},{64,80},{96,112},{16,0},{48,32},{80,64},{112,96},{1... | collective-permute-start | bytes 294920 | tf_op jit(solution)/shard_map/ppermute | solution.py:431
  5.1 0.9 %collective-permute-done.sib = f32[96,256]{1,0:T(8,128)S(1)} collective-permute-done((f32[96,256]{1,0:T(8,128)S(1)}, f32[96,256]{1,0:T(8,128)S(1)}, u32[]{:S(2)}, u32[]{:S(2)}) %collective-permute-start) | collective-permute-done | bytes 98336 | tf_op jit(solution)/shard_map/ppermute | solution.py:431
  6.0 0.2 start.1
  6.2 2.9 %collective-permute-start.1 = (f32[48,128]{1,0:T(8,128)S(1)}, f32[48,128]{1,0:T(8,128)S(1)}, u32[]{:S(2)}, u32[]{:S(2)}) collective-permute-start(f32[48,128]{1,0:T(8,128)S(1)} %get-tuple-element.55), channel_id=1, source_target_pairs={{0,32},{64,96},{48,80},{112,16},{32,0},{96,64},{80,48},{16,112},{1... | collective-permute-start | bytes 73736 | tf_op jit(solution)/shard_map/ppermute | solution.py:436
  9.0 0.0 copy-done.1
  9.0 0.0 copy-done
  9.0 1.2 %own.4 = (f32[2,80,80]{2,1,0:T(8,128)S(1)}, f32[2,80,80]{2,1,0:T(8,128)S(1)}, f32[1,2048]{1,0:T(1,128)S(1)}) custom-call(s32[4]{0:T(128)S(1)} %copy-done.1, s32[4,2048]{1,0:T(4,128)S(1)} %copy-done, f32[2,48,128]{2,1,0:T(8,128)S(1)} %get-tuple-element.56.pay), custom_call_target="tpu_custom_call" | custom-call | tf_op jit(solution)/shard_map/own/pallas_call | solution.py:437
  10.3 0.0 collective-permute-done.1.far
  10.3 0.1 collective-permute-start.2
  10.4 1.1 %collective-permute-done.2.sib_far = f32[48,128]{1,0:T(8,128)S(1)} collective-permute-done((f32[48,128]{1,0:T(8,128)S(1)}, f32[48,128]{1,0:T(8,128)S(1)}, u32[]{:S(2)}, u32[]{:S(2)}) %collective-permute-start.2) | collective-permute-done | bytes 24608 | tf_op jit(solution)/shard_map/ppermute | solution.py:445
  11.5 0.3 send.4
  11.8 1.2 %collective-permute-start.3 = (f32[2,80,80]{2,1,0:T(8,128)S(1)}, f32[2,80,80]{2,1,0:T(8,128)S(1)}, u32[]{:S(2)}, u32[]{:S(2)}) collective-permute-start(f32[2,80,80]{2,1,0:T(8,128)S(1)} %send.4), channel_id=1, source_target_pairs={{0,1},{2,3},{4,5},{6,7},{8,9},{10,11},{12,13},{14,15},{17,18},{19,... | collective-permute-start | bytes 153608 | tf_op jit(solution)/shard_map/ppermute | solution.py:450
  13.0 0.3 same.4.q0
  13.3 2.2 %collective-permute-done.3.h = f32[2,80,80]{2,1,0:T(8,128)S(1)} collective-permute-done((f32[2,80,80]{2,1,0:T(8,128)S(1)}, f32[2,80,80]{2,1,0:T(8,128)S(1)}, u32[]{:S(2)}, u32[]{:S(2)}) %collective-permute-start.3) | collective-permute-done | bytes 51232 | tf_op jit(solution)/shard_map/ppermute | solution.py:450
  15.5 1.0 %collective-permute-start.4 = (f32[2,80,80]{2,1,0:T(8,128)S(1)}, f32[2,80,80]{2,1,0:T(8,128)S(1)}, u32[]{:S(2)}, u32[]{:S(2)}) collective-permute-start(f32[2,80,80]{2,1,0:T(8,128)S(1)} %collective-permute-done.3.h), channel_id=1, source_target_pairs={{0,16},{32,48},{64,80},{96,112},{16,0},{48,32},{80,64},{112,96},{1... | collective-permute-start | bytes 153608 | tf_op jit(solution)/shard_map/ppermute | solution.py:478
  16.5 0.9 %collective-permute-done.4.g = f32[2,80,80]{2,1,0:T(8,128)S(1)} collective-permute-done((f32[2,80,80]{2,1,0:T(8,128)S(1)}, f32[2,80,80]{2,1,0:T(8,128)S(1)}, u32[]{:S(2)}, u32[]{:S(2)}) %collective-permute-start.4) | collective-permute-done | bytes 51232 | tf_op jit(solution)/shard_map/ppermute | solution.py:478
  17.4 0.4 step.3
  17.8 2.8 %collective-permute-start.5 = (f32[48,128]{1,0:T(8,128)S(1)}, f32[48,128]{1,0:T(8,128)S(1)}, u32[]{:S(2)}, u32[]{:S(2)}) collective-permute-start(f32[48,128]{1,0:T(8,128)S(1)} %get-tuple-element.66), channel_id=1, source_target_pairs={{0,32},{64,96},{48,80},{112,16},{32,0},{96,64},{80,48},{16,112},{1... | collective-permute-start | bytes 73736 | tf_op jit(solution)/shard_map/ppermute | solution.py:436
  20.6 1.2 %own.5 = (f32[2,80,80]{2,1,0:T(8,128)S(1)}, f32[2,80,80]{2,1,0:T(8,128)S(1)}, f32[1,2048]{1,0:T(1,128)S(1)}) custom-call(s32[4]{0:T(128)S(1)} %copy-done.1, s32[4,2048]{1,0:T(4,128)S(1)} %copy-done, f32[2,48,128]{2,1,0:T(8,128)S(1)} %get-tuple-element.67.pay), custom_call_target="tpu_custom_call" | custom-call | tf_op jit(solution)/shard_map/own/pallas_call | solution.py:437
  21.8 0.0 collective-permute-done.5.far
  21.8 0.2 collective-permute-start.6
  22.1 1.0 %collective-permute-done.6.sib_far = f32[48,128]{1,0:T(8,128)S(1)} collective-permute-done((f32[48,128]{1,0:T(8,128)S(1)}, f32[48,128]{1,0:T(8,128)S(1)}, u32[]{:S(2)}, u32[]{:S(2)}) %collective-permute-start.6) | collective-permute-done | bytes 24608 | tf_op jit(solution)/shard_map/ppermute | solution.py:445
  23.1 0.3 send.5
  23.4 1.2 %collective-permute-start.7 = (f32[2,80,80]{2,1,0:T(8,128)S(1)}, f32[2,80,80]{2,1,0:T(8,128)S(1)}, u32[]{:S(2)}, u32[]{:S(2)}) collective-permute-start(f32[2,80,80]{2,1,0:T(8,128)S(1)} %send.5), channel_id=1, source_target_pairs={{0,1},{2,3},{4,5},{6,7},{8,9},{10,11},{12,13},{14,15},{17,18},{19,... | collective-permute-start | bytes 153608 | tf_op jit(solution)/shard_map/ppermute | solution.py:450
  24.6 0.3 same.5.q0
  24.9 2.2 %collective-permute-done.7.h = f32[2,80,80]{2,1,0:T(8,128)S(1)} collective-permute-done((f32[2,80,80]{2,1,0:T(8,128)S(1)}, f32[2,80,80]{2,1,0:T(8,128)S(1)}, u32[]{:S(2)}, u32[]{:S(2)}) %collective-permute-start.7) | collective-permute-done | bytes 51232 | tf_op jit(solution)/shard_map/ppermute | solution.py:450
  27.0 1.0 %collective-permute-start.8 = (f32[2,80,80]{2,1,0:T(8,128)S(1)}, f32[2,80,80]{2,1,0:T(8,128)S(1)}, u32[]{:S(2)}, u32[]{:S(2)}) collective-permute-start(f32[2,80,80]{2,1,0:T(8,128)S(1)} %collective-permute-done.7.h), channel_id=1, source_target_pairs={{0,16},{32,48},{64,80},{96,112},{16,0},{48,32},{80,64},{112,96},{1... | collective-permute-start | bytes 153608 | tf_op jit(solution)/shard_map/ppermute | solution.py:478
  28.1 0.9 %collective-permute-done.8.g = f32[2,80,80]{2,1,0:T(8,128)S(1)} collective-permute-done((f32[2,80,80]{2,1,0:T(8,128)S(1)}, f32[2,80,80]{2,1,0:T(8,128)S(1)}, u32[]{:S(2)}, u32[]{:S(2)}) %collective-permute-start.8) | collective-permute-done | bytes 51232 | tf_op jit(solution)/shard_map/ppermute | solution.py:478
  29.0 0.4 step.4
  29.4 2.8 %collective-permute-start.9 = (f32[48,128]{1,0:T(8,128)S(1)}, f32[48,128]{1,0:T(8,128)S(1)}, u32[]{:S(2)}, u32[]{:S(2)}) collective-permute-start(f32[48,128]{1,0:T(8,128)S(1)} %get-tuple-element.77), channel_id=1, source_target_pairs={{0,32},{64,96},{48,80},{112,16},{32,0},{96,64},{80,48},{16,112},{1... | collective-permute-start | bytes 73736 | tf_op jit(solution)/shard_map/ppermute | solution.py:436
  32.1 1.2 %own.6 = (f32[2,80,80]{2,1,0:T(8,128)S(1)}, f32[2,80,80]{2,1,0:T(8,128)S(1)}, f32[1,2048]{1,0:T(1,128)S(1)}) custom-call(s32[4]{0:T(128)S(1)} %copy-done.1, s32[4,2048]{1,0:T(4,128)S(1)} %copy-done, f32[2,48,128]{2,1,0:T(8,128)S(1)} %get-tuple-element.78.pay), custom_call_target="tpu_custom_call" | custom-call | tf_op jit(solution)/shard_map/own/pallas_call | solution.py:437
  33.4 0.0 collective-permute-done.9.far
  33.4 0.2 collective-permute-start.10
  33.6 1.0 %collective-permute-done.10.sib_far = f32[48,128]{1,0:T(8,128)S(1)} collective-permute-done((f32[48,128]{1,0:T(8,128)S(1)}, f32[48,128]{1,0:T(8,128)S(1)}, u32[]{:S(2)}, u32[]{:S(2)}) %collective-permute-start.10) | collective-permute-done | bytes 24608 | tf_op jit(solution)/shard_map/ppermute | solution.py:445
  34.6 0.3 send.6
  34.9 1.2 %collective-permute-start.11 = (f32[2,80,80]{2,1,0:T(8,128)S(1)}, f32[2,80,80]{2,1,0:T(8,128)S(1)}, u32[]{:S(2)}, u32[]{:S(2)}) collective-permute-start(f32[2,80,80]{2,1,0:T(8,128)S(1)} %send.6), channel_id=1, source_target_pairs={{0,1},{2,3},{4,5},{6,7},{8,9},{10,11},{12,13},{14,15},{17,18},{19,... | collective-permute-start | bytes 153608 | tf_op jit(solution)/shard_map/ppermute | solution.py:450
  36.1 2.2 %turn.1.near = bf16[32,160,256]{2,1,0:T(8,128)(2,1)S(1)} custom-call(f32[80,4,32,256]{3,2,1,0:T(8,128)} %x.3), custom_call_target="tpu_custom_call" | custom-call | tf_op jit(solution)/shard_map/turn/pallas_call | solution.py:469
  38.3 0.3 same.6.q0
  38.6 0.0 collective-permute-done.11.h
  38.6 1.0 %collective-permute-start.12 = (f32[2,80,80]{2,1,0:T(8,128)S(1)}, f32[2,80,80]{2,1,0:T(8,128)S(1)}, u32[]{:S(2)}, u32[]{:S(2)}) collective-permute-start(f32[2,80,80]{2,1,0:T(8,128)S(1)} %collective-permute-done.11.h), channel_id=1, source_target_pairs={{0,16},{32,48},{64,80},{96,112},{16,0},{48,32},{80,64},{112,96},{1... | collective-permute-start | bytes 153608 | tf_op jit(solution)/shard_map/ppermute | solution.py:478
  39.6 0.9 %collective-permute-done.12.g = f32[2,80,80]{2,1,0:T(8,128)S(1)} collective-permute-done((f32[2,80,80]{2,1,0:T(8,128)S(1)}, f32[2,80,80]{2,1,0:T(8,128)S(1)}, u32[]{:S(2)}, u32[]{:S(2)}) %collective-permute-start.12) | collective-permute-done | bytes 51232 | tf_op jit(solution)/shard_map/ppermute | solution.py:478
  40.5 0.4 step.5
  40.9 2.8 %collective-permute-start.13 = (f32[56,128]{1,0:T(8,128)S(1)}, f32[56,128]{1,0:T(8,128)S(1)}, u32[]{:S(2)}, u32[]{:S(2)}) collective-permute-start(f32[56,128]{1,0:T(8,128)S(1)} %get-tuple-element.88), channel_id=1, source_target_pairs={{0,32},{64,96},{48,80},{112,16},{32,0},{96,64},{80,48},{16,112},{1... | collective-permute-start | bytes 86024 | tf_op jit(solution)/shard_map/ppermute | solution.py:436
  43.7 1.2 %own.7 = (f32[2,80,80]{2,1,0:T(8,128)S(1)}, f32[2,80,80]{2,1,0:T(8,128)S(1)}, f32[1,2048]{1,0:T(1,128)S(1)}) custom-call(s32[4]{0:T(128)S(1)} %copy-done.1, s32[4,2048]{1,0:T(4,128)S(1)} %copy-done, f32[2,48,128]{2,1,0:T(8,128)S(1)} %get-tuple-element.89.pay), custom_call_target="tpu_custom_call" | custom-call | tf_op jit(solution)/shard_map/own/pallas_call | solution.py:437
  44.9 0.1 collective-permute-done.13.far
  45.0 0.2 collective-permute-start.14
  45.2 1.0 %collective-permute-done.14.sib_far = f32[56,128]{1,0:T(8,128)S(1)} collective-permute-done((f32[56,128]{1,0:T(8,128)S(1)}, f32[56,128]{1,0:T(8,128)S(1)}, u32[]{:S(2)}, u32[]{:S(2)}) %collective-permute-start.14) | collective-permute-done | bytes 28704 | tf_op jit(solution)/shard_map/ppermute | solution.py:445
  46.2 0.3 send.7
  46.5 1.2 %collective-permute-start.15 = (f32[2,80,80]{2,1,0:T(8,128)S(1)}, f32[2,80,80]{2,1,0:T(8,128)S(1)}, u32[]{:S(2)}, u32[]{:S(2)}) collective-permute-start(f32[2,80,80]{2,1,0:T(8,128)S(1)} %send.7), channel_id=1, source_target_pairs={{0,1},{2,3},{4,5},{6,7},{8,9},{10,11},{12,13},{14,15},{17,18},{19,... | collective-permute-start | bytes 153608 | tf_op jit(solution)/shard_map/ppermute | solution.py:450
  47.7 1.9 %collective-permute-start.16 = (f32[8,128]{1,0:T(8,128)S(1)}, f32[8,128]{1,0:T(8,128)S(1)}, u32[]{:S(2)}, u32[]{:S(2)}) collective-permute-start(f32[8,128]{1,0:T(8,128)S(1)} %slice.3), channel_id=1, source_target_pairs={{0,32},{64,96},{48,80},{112,16},{32,0},{96,64},{80,48},{16,112},{1... | collective-permute-start | bytes 12296 | tf_op jit(solution)/shard_map/ppermute | solution.py:456
  49.6 0.3 same.7.q0
  49.9 1.5 %collective-permute-done.16.across = f32[8,128]{1,0:T(8,128)S(1)} collective-permute-done((f32[8,128]{1,0:T(8,128)S(1)}, f32[8,128]{1,0:T(8,128)S(1)}, u32[]{:S(2)}, u32[]{:S(2)}) %collective-permute-start.16) | collective-permute-done | bytes 4128 | tf_op jit(solution)/shard_map/ppermute | solution.py:456
  51.4 0.7 column.1
  52.0 0.0 collective-permute-done.15.h
  52.0 0.5 collective-permute-start.17
  52.5 10.4 %all-to-all-start = ((f32[16,16,128]{2,1,0:T(8,128)}), f32[16,16,128]{2,1,0:T(8,128)S(1)}, u32[]{:S(2)}, u32[]{:S(2)}) async-start(f32[16,16,128]{2,1,0:T(8,128)} %column.1), calls=%async_computation | async-start | bytes 262144 | tf_op jit(solution)/shard_map/all_to_all | solution.py:462
  62.9 0.0 collective-permute-done.17.g
  63.0 8.9 %final.1 = f32[80,4,32,256]{3,2,1,0:T(8,128)} custom-call(f32[2,80,80]{2,1,0:T(8,128)S(1)} %same.7.q0, f32[2,80,80]{2,1,0:T(8,128)S(1)} %collective-permute-done.15.h, f32[2,80,80]{2,1,0:T(8,128)S(1)} %collective-permute-done.17.g, f32[2,96,384]{2,1,0:T(8,128)S(1)} %get-tuple-element.99.z, bf16[32,160,256]{2,1,0:T(8,128)(2,1)S(1)} %turn.1.near, ...), custom_call_target="tpu_custom_call" | custom-call | flops 1258291200 | bytes 20971520 | tf_op jit(solution)/shard_map/final/pallas_call | solution.py:492
  71.8 0.0 all-to-all-done.gathered
  71.8 2.1 %place.1 = f32[4,2048]{1,0:T(4,128)} custom-call(s32[4]{0:T(128)S(1)} %copy-done.1, s32[4,2048]{1,0:T(4,128)S(1)} %copy-done, f32[16,16,128]{2,1,0:T(8,128)S(1)} %all-to-all-done.gathered, f32[1,2048]{1,0:T(1,128)S(1)} %get-tuple-element.104.r0, f32[1,2048]{1,0:T(1,128)S(1)} %get-tuple-element.105.r1, f32[1,2048]{1,0:T(1,128)S(1)} %get-tuple-element.106.r2, ...), custom_call_target="tpu_custom_call" | custom-call | tf_op jit(solution)/shard_map/place/pallas_call | solution.py:505
  (1 shorter events, 0.0 us)
Async XLA Ops:
  0.6 8.4 %copy-start.1 = (s32[4]{0:T(128)S(1)}, s32[4]{0:T(128)}, u32[]{:S(2)}) copy-start(s32[4]{0:T(128)} %order.9) | copy-start | bytes 52
  0.6 8.4 %copy-start = (s32[4,2048]{1,0:T(4,128)S(1)}, s32[4,2048]{1,0:T(4,128)}, u32[]{:S(2)}) copy-start(s32[4,2048]{1,0:T(4,128)} %owner.9) | copy-start | bytes 98308
  3.6 2.4 %collective-permute-start = (f32[96,256]{1,0:T(8,128)S(1)}, f32[96,256]{1,0:T(8,128)S(1)}, u32[]{:S(2)}, u32[]{:S(2)}) collective-permute-start(f32[96,256]{1,0:T(8,128)S(1)} %init.1.own), channel_id=1, source_target_pairs={{0,16},{32,48},{64,80},{96,112},{16,0},{48,32},{80,64},{112,96},{1... | collective-permute-start | bytes 294920 | tf_op jit(solution)/shard_map/ppermute | solution.py:431
  6.2 4.1 %collective-permute-start.1 = (f32[48,128]{1,0:T(8,128)S(1)}, f32[48,128]{1,0:T(8,128)S(1)}, u32[]{:S(2)}, u32[]{:S(2)}) collective-permute-start(f32[48,128]{1,0:T(8,128)S(1)} %get-tuple-element.55), channel_id=1, source_target_pairs={{0,32},{64,96},{48,80},{112,16},{32,0},{96,64},{80,48},{16,112},{1... | collective-permute-start | bytes 73736 | tf_op jit(solution)/shard_map/ppermute | solution.py:436
  10.3 1.3 %collective-permute-start.2 = (f32[48,128]{1,0:T(8,128)S(1)}, f32[48,128]{1,0:T(8,128)S(1)}, u32[]{:S(2)}, u32[]{:S(2)}) collective-permute-start(f32[48,128]{1,0:T(8,128)S(1)} %collective-permute-done.1.far), channel_id=1, source_target_pairs={{0,16},{32,48},{64,80},{96,112},{16,0},{48,32},{80,64},{112,96},{1... | collective-permute-start | bytes 73736 | tf_op jit(solution)/shard_map/ppermute | solution.py:445
  11.8 3.7 %collective-permute-start.3 = (f32[2,80,80]{2,1,0:T(8,128)S(1)}, f32[2,80,80]{2,1,0:T(8,128)S(1)}, u32[]{:S(2)}, u32[]{:S(2)}) collective-permute-start(f32[2,80,80]{2,1,0:T(8,128)S(1)} %send.4), channel_id=1, source_target_pairs={{0,1},{2,3},{4,5},{6,7},{8,9},{10,11},{12,13},{14,15},{17,18},{19,... | collective-permute-start | bytes 153608 | tf_op jit(solution)/shard_map/ppermute | solution.py:450
  15.5 1.9 %collective-permute-start.4 = (f32[2,80,80]{2,1,0:T(8,128)S(1)}, f32[2,80,80]{2,1,0:T(8,128)S(1)}, u32[]{:S(2)}, u32[]{:S(2)}) collective-permute-start(f32[2,80,80]{2,1,0:T(8,128)S(1)} %collective-permute-done.3.h), channel_id=1, source_target_pairs={{0,16},{32,48},{64,80},{96,112},{16,0},{48,32},{80,64},{112,96},{1... | collective-permute-start | bytes 153608 | tf_op jit(solution)/shard_map/ppermute | solution.py:478
  17.8 4.0 %collective-permute-start.5 = (f32[48,128]{1,0:T(8,128)S(1)}, f32[48,128]{1,0:T(8,128)S(1)}, u32[]{:S(2)}, u32[]{:S(2)}) collective-permute-start(f32[48,128]{1,0:T(8,128)S(1)} %get-tuple-element.66), channel_id=1, source_target_pairs={{0,32},{64,96},{48,80},{112,16},{32,0},{96,64},{80,48},{16,112},{1... | collective-permute-start | bytes 73736 | tf_op jit(solution)/shard_map/ppermute | solution.py:436
  21.8 1.3 %collective-permute-start.6 = (f32[48,128]{1,0:T(8,128)S(1)}, f32[48,128]{1,0:T(8,128)S(1)}, u32[]{:S(2)}, u32[]{:S(2)}) collective-permute-start(f32[48,128]{1,0:T(8,128)S(1)} %collective-permute-done.5.far), channel_id=1, source_target_pairs={{0,16},{32,48},{64,80},{96,112},{16,0},{48,32},{80,64},{112,96},{1... | collective-permute-start | bytes 73736 | tf_op jit(solution)/shard_map/ppermute | solution.py:445
  23.4 3.7 %collective-permute-start.7 = (f32[2,80,80]{2,1,0:T(8,128)S(1)}, f32[2,80,80]{2,1,0:T(8,128)S(1)}, u32[]{:S(2)}, u32[]{:S(2)}) collective-permute-start(f32[2,80,80]{2,1,0:T(8,128)S(1)} %send.5), channel_id=1, source_target_pairs={{0,1},{2,3},{4,5},{6,7},{8,9},{10,11},{12,13},{14,15},{17,18},{19,... | collective-permute-start | bytes 153608 | tf_op jit(solution)/shard_map/ppermute | solution.py:450
  27.0 1.9 %collective-permute-start.8 = (f32[2,80,80]{2,1,0:T(8,128)S(1)}, f32[2,80,80]{2,1,0:T(8,128)S(1)}, u32[]{:S(2)}, u32[]{:S(2)}) collective-permute-start(f32[2,80,80]{2,1,0:T(8,128)S(1)} %collective-permute-done.7.h), channel_id=1, source_target_pairs={{0,16},{32,48},{64,80},{96,112},{16,0},{48,32},{80,64},{112,96},{1... | collective-permute-start | bytes 153608 | tf_op jit(solution)/shard_map/ppermute | solution.py:478
  29.4 4.0 %collective-permute-start.9 = (f32[48,128]{1,0:T(8,128)S(1)}, f32[48,128]{1,0:T(8,128)S(1)}, u32[]{:S(2)}, u32[]{:S(2)}) collective-permute-start(f32[48,128]{1,0:T(8,128)S(1)} %get-tuple-element.77), channel_id=1, source_target_pairs={{0,32},{64,96},{48,80},{112,16},{32,0},{96,64},{80,48},{16,112},{1... | collective-permute-start | bytes 73736 | tf_op jit(solution)/shard_map/ppermute | solution.py:436
  33.4 1.3 %collective-permute-start.10 = (f32[48,128]{1,0:T(8,128)S(1)}, f32[48,128]{1,0:T(8,128)S(1)}, u32[]{:S(2)}, u32[]{:S(2)}) collective-permute-start(f32[48,128]{1,0:T(8,128)S(1)} %collective-permute-done.9.far), channel_id=1, source_target_pairs={{0,16},{32,48},{64,80},{96,112},{16,0},{48,32},{80,64},{112,96},{1... | collective-permute-start | bytes 73736 | tf_op jit(solution)/shard_map/ppermute | solution.py:445
  34.9 3.7 %collective-permute-start.11 = (f32[2,80,80]{2,1,0:T(8,128)S(1)}, f32[2,80,80]{2,1,0:T(8,128)S(1)}, u32[]{:S(2)}, u32[]{:S(2)}) collective-permute-start(f32[2,80,80]{2,1,0:T(8,128)S(1)} %send.6), channel_id=1, source_target_pairs={{0,1},{2,3},{4,5},{6,7},{8,9},{10,11},{12,13},{14,15},{17,18},{19,... | collective-permute-start | bytes 153608 | tf_op jit(solution)/shard_map/ppermute | solution.py:450
  38.6 1.9 %collective-permute-start.12 = (f32[2,80,80]{2,1,0:T(8,128)S(1)}, f32[2,80,80]{2,1,0:T(8,128)S(1)}, u32[]{:S(2)}, u32[]{:S(2)}) collective-permute-start(f32[2,80,80]{2,1,0:T(8,128)S(1)} %collective-permute-done.11.h), channel_id=1, source_target_pairs={{0,16},{32,48},{64,80},{96,112},{16,0},{48,32},{80,64},{112,96},{1... | collective-permute-start | bytes 153608 | tf_op jit(solution)/shard_map/ppermute | solution.py:478
  40.9 4.0 %collective-permute-start.13 = (f32[56,128]{1,0:T(8,128)S(1)}, f32[56,128]{1,0:T(8,128)S(1)}, u32[]{:S(2)}, u32[]{:S(2)}) collective-permute-start(f32[56,128]{1,0:T(8,128)S(1)} %get-tuple-element.88), channel_id=1, source_target_pairs={{0,32},{64,96},{48,80},{112,16},{32,0},{96,64},{80,48},{16,112},{1... | collective-permute-start | bytes 86024 | tf_op jit(solution)/shard_map/ppermute | solution.py:436
  45.0 1.2 %collective-permute-start.14 = (f32[56,128]{1,0:T(8,128)S(1)}, f32[56,128]{1,0:T(8,128)S(1)}, u32[]{:S(2)}, u32[]{:S(2)}) collective-permute-start(f32[56,128]{1,0:T(8,128)S(1)} %collective-permute-done.13.far), channel_id=1, source_target_pairs={{0,16},{32,48},{64,80},{96,112},{16,0},{48,32},{80,64},{112,96},{1... | collective-permute-start | bytes 86024 | tf_op jit(solution)/shard_map/ppermute | solution.py:445
  46.5 5.6 %collective-permute-start.15 = (f32[2,80,80]{2,1,0:T(8,128)S(1)}, f32[2,80,80]{2,1,0:T(8,128)S(1)}, u32[]{:S(2)}, u32[]{:S(2)}) collective-permute-start(f32[2,80,80]{2,1,0:T(8,128)S(1)} %send.7), channel_id=1, source_target_pairs={{0,1},{2,3},{4,5},{6,7},{8,9},{10,11},{12,13},{14,15},{17,18},{19,... | collective-permute-start | bytes 153608 | tf_op jit(solution)/shard_map/ppermute | solution.py:450
  47.7 3.7 %collective-permute-start.16 = (f32[8,128]{1,0:T(8,128)S(1)}, f32[8,128]{1,0:T(8,128)S(1)}, u32[]{:S(2)}, u32[]{:S(2)}) collective-permute-start(f32[8,128]{1,0:T(8,128)S(1)} %slice.3), channel_id=1, source_target_pairs={{0,32},{64,96},{48,80},{112,16},{32,0},{96,64},{80,48},{16,112},{1... | collective-permute-start | bytes 12296 | tf_op jit(solution)/shard_map/ppermute | solution.py:456
  52.0 10.9 %collective-permute-start.17 = (f32[2,80,80]{2,1,0:T(8,128)S(1)}, f32[2,80,80]{2,1,0:T(8,128)S(1)}, u32[]{:S(2)}, u32[]{:S(2)}) collective-permute-start(f32[2,80,80]{2,1,0:T(8,128)S(1)} %collective-permute-done.15.h), channel_id=1, source_target_pairs={{0,16},{32,48},{64,80},{96,112},{16,0},{48,32},{80,64},{112,96},{1... | collective-permute-start | bytes 153608 | tf_op jit(solution)/shard_map/ppermute | solution.py:478
  52.5 19.3 %all-to-all-start = ((f32[16,16,128]{2,1,0:T(8,128)}), f32[16,16,128]{2,1,0:T(8,128)S(1)}, u32[]{:S(2)}, u32[]{:S(2)}) async-start(f32[16,16,128]{2,1,0:T(8,128)} %column.1), calls=%async_computation | async-start | bytes 262144 | tf_op jit(solution)/shard_map/all_to_all | solution.py:462

commit v16 on v15

--- a/solution.py
+++ b/solution.py
@@ -305,8 +305,8 @@
     emit(k, new, z_out, pay_out, edge_out, news_out)
 
 
-def part(ref, i):
-    return ref.at[:, i // PARTS, pl.ds((i % PARTS) * SLAB, SLAB), :]
+def part(ref, i, at=0, rows=SLAB):
+    return ref.at[:, i // PARTS, pl.ds((i % PARTS) * SLAB + at, rows), :]
 
 
 def turn(block, out, at):
@@ -327,7 +327,7 @@
 
 def final_kernel(q0, h, g, z, near, x, out, come, go, come_sems, go_sems):
     loads = [pltpu.make_async_copy(part(x, i), come.at[i - TURN], come_sems.at[i - TURN]) for i in range(TURN, SLABS)]
-    stores = [pltpu.make_async_copy(go.at[i], part(out, i), go_sems.at[i]) for i in range(SLABS)]
+    stores = []
     for load in loads:
         load.start()
     c = core_of()
@@ -350,7 +350,9 @@
                     stack = [both, both[:M]]
                 rows.append(dot(w, jnp.concatenate(stack, axis=0))[None])
             go[i, :, j : j + 8, :] = jnp.swapaxes(jnp.concatenate(rows, axis=0), 0, 1)
-        stores[i].start()
+            sem = go_sems.at[(SLAB * i + j) // 8]
+            stores.append(pltpu.make_async_copy(go.at[i, :, pl.ds(j, 8), :], part(out, i, j, 8), sem))
+            stores[-1].start()
     for store in stores:
         store.wait()
 
@@ -496,7 +498,7 @@
         out_specs=HBM,
         scratch_shapes=[
             pltpu.VMEM((SLABS - TURN, M, SLAB, TY), F32), pltpu.VMEM((SLABS, M, SLAB, TY), F32),
-            dma(SLABS - TURN), dma(SLABS),
+            dma(SLABS - TURN), dma(SLABS * SLAB // 8),
         ],
         cost_estimate=pl.CostEstimate(flops=6 * M * M * LEV * TX * TY, bytes_accessed=8 * M * LEV * TX * TY, transcendentals=0),
         name="final",

time: 74.1 us -> 73.8 us (level)
  no operation moved by 1% of the time
where the time goes in v16:
time: 73.8 us; the launch traced here: 73.6 us
  starting transfers between devices  34.2 us (46%)
  Pallas kernels  24.8 us (34%)
  waiting for transfers between devices  13.8 us (19%)
  between operations  0.82 us (1%)
    ppermute x4, starting transfers between devices, local(): far = lax.ppermute(edge, 'gx', side_x)  11.2 us
    all_to_all x1, starting transfers between devices, local(): gathered = lax.all_to_all(column, 'gy', 0, 0, tiled=True)  10.4 us
    pallas_call x1, Pallas kernels, local(): call(final_kernel, out_shape=shape(M, LEV, TX, TY), in_specs=[VMEM] * 5 +...  8.56 us
    pallas_call x4, Pallas kernels, local(): call(functools.partial(own_kernel, k), out_shape=(shape(2, M, M), shape(2...  4.81 us
    ppermute x4, starting transfers between devices, local(): h = lax.ppermute(send, both, side_y)  4.75 us
    ppermute x4, waiting for transfers between devices, local(): h = lax.ppermute(send, both, side_y)  4.39 us
    ppermute x4, waiting for transfers between devices, local(): sib_far = lax.ppermute(far, 'gx', core)  4.19 us
    ppermute x4, starting transfers between devices, local(): g = lax.ppermute(h, 'gx', core)  3.54 us
  transfers between devices with their start and end apart: 19, of which 11 were waited for; matrix products, arithmetic and copies ran while one was open for 0% of the time, Pallas kernels for 24%

profile of v16, /device:TPU:1, one launch (start us, length us, event | category | flops | bytes accessed | tf_op | source)
XLA Modules:
  0.0 73.6 jit_solution(8092869939418459327)
XLA Ops:
  0.6 0.0 copy-start.1
  0.6 0.0 copy-start
  0.7 2.9 %init.1.own = f32[96,256]{1,0:T(8,128)S(1)} custom-call(s32[4]{0:T(128)} %order.9, f32[4,2048]{1,0:T(4,128)} %value_hbm.1, f32[4,2048]{1,0:T(4,128)} %variance_hbm.1, s32[4,2048]{1,0:T(4,128)} %owner.9, s32[4,2048]{1,0:T(4,128)} %cell_hbm.1, s32[4,8,2048]{2,1,0:T(8,128)} %bitcast.1, f32[80,4,32,256]{3,2,1,0:T(8,128)} %x.3), custom_call_target="tpu_custom_call" | custom-call | tf_op jit(solution)/shard_map/init/pallas_call | solution.py:411
  3.6 1.5 %collective-permute-start = (f32[96,256]{1,0:T(8,128)S(1)}, f32[96,256]{1,0:T(8,128)S(1)}, u32[]{:S(2)}, u32[]{:S(2)}) collective-permute-start(f32[96,256]{1,0:T(8,128)S(1)} %init.1.own), channel_id=1, source_target_pairs={{0,16},{32,48},{64,80},{96,112},{16,0},{48,32},{80,64},{112,96},{1... | collective-permute-start | bytes 294920 | tf_op jit(solution)/shard_map/ppermute | solution.py:433
  5.1 0.9 %collective-permute-done.sib = f32[96,256]{1,0:T(8,128)S(1)} collective-permute-done((f32[96,256]{1,0:T(8,128)S(1)}, f32[96,256]{1,0:T(8,128)S(1)}, u32[]{:S(2)}, u32[]{:S(2)}) %collective-permute-start) | collective-permute-done | bytes 98336 | tf_op jit(solution)/shard_map/ppermute | solution.py:433
  6.0 0.2 start.1
  6.2 2.9 %collective-permute-start.1 = (f32[48,128]{1,0:T(8,128)S(1)}, f32[48,128]{1,0:T(8,128)S(1)}, u32[]{:S(2)}, u32[]{:S(2)}) collective-permute-start(f32[48,128]{1,0:T(8,128)S(1)} %get-tuple-element.55), channel_id=1, source_target_pairs={{0,32},{64,96},{48,80},{112,16},{32,0},{96,64},{80,48},{16,112},{1... | collective-permute-start | bytes 73736 | tf_op jit(solution)/shard_map/ppermute | solution.py:438
  9.0 0.0 copy-done.1
  9.0 0.0 copy-done
  9.0 1.2 %own.4 = (f32[2,80,80]{2,1,0:T(8,128)S(1)}, f32[2,80,80]{2,1,0:T(8,128)S(1)}, f32[1,2048]{1,0:T(1,128)S(1)}) custom-call(s32[4]{0:T(128)S(1)} %copy-done.1, s32[4,2048]{1,0:T(4,128)S(1)} %copy-done, f32[2,48,128]{2,1,0:T(8,128)S(1)} %get-tuple-element.56.pay), custom_call_target="tpu_custom_call" | custom-call | tf_op jit(solution)/shard_map/own/pallas_call | solution.py:439
  10.3 0.0 collective-permute-done.1.far
  10.3 0.1 collective-permute-start.2
  10.4 1.1 %collective-permute-done.2.sib_far = f32[48,128]{1,0:T(8,128)S(1)} collective-permute-done((f32[48,128]{1,0:T(8,128)S(1)}, f32[48,128]{1,0:T(8,128)S(1)}, u32[]{:S(2)}, u32[]{:S(2)}) %collective-permute-start.2) | collective-permute-done | bytes 24608 | tf_op jit(solution)/shard_map/ppermute | solution.py:447
  11.5 0.3 send.4
  11.8 1.2 %collective-permute-start.3 = (f32[2,80,80]{2,1,0:T(8,128)S(1)}, f32[2,80,80]{2,1,0:T(8,128)S(1)}, u32[]{:S(2)}, u32[]{:S(2)}) collective-permute-start(f32[2,80,80]{2,1,0:T(8,128)S(1)} %send.4), channel_id=1, source_target_pairs={{0,1},{2,3},{4,5},{6,7},{8,9},{10,11},{12,13},{14,15},{17,18},{19,... | collective-permute-start | bytes 153608 | tf_op jit(solution)/shard_map/ppermute | solution.py:452
  13.0 0.3 same.4.q0
  13.3 2.2 %collective-permute-done.3.h = f32[2,80,80]{2,1,0:T(8,128)S(1)} collective-permute-done((f32[2,80,80]{2,1,0:T(8,128)S(1)}, f32[2,80,80]{2,1,0:T(8,128)S(1)}, u32[]{:S(2)}, u32[]{:S(2)}) %collective-permute-start.3) | collective-permute-done | bytes 51232 | tf_op jit(solution)/shard_map/ppermute | solution.py:452
  15.5 1.0 %collective-permute-start.4 = (f32[2,80,80]{2,1,0:T(8,128)S(1)}, f32[2,80,80]{2,1,0:T(8,128)S(1)}, u32[]{:S(2)}, u32[]{:S(2)}) collective-permute-start(f32[2,80,80]{2,1,0:T(8,128)S(1)} %collective-permute-done.3.h), channel_id=1, source_target_pairs={{0,16},{32,48},{64,80},{96,112},{16,0},{48,32},{80,64},{112,96},{1... | collective-permute-start | bytes 153608 | tf_op jit(solution)/shard_map/ppermute | solution.py:480
  16.5 0.9 %collective-permute-done.4.g = f32[2,80,80]{2,1,0:T(8,128)S(1)} collective-permute-done((f32[2,80,80]{2,1,0:T(8,128)S(1)}, f32[2,80,80]{2,1,0:T(8,128)S(1)}, u32[]{:S(2)}, u32[]{:S(2)}) %collective-permute-start.4) | collective-permute-done | bytes 51232 | tf_op jit(solution)/shard_map/ppermute | solution.py:480
  17.4 0.4 step.3
  17.8 2.8 %collective-permute-start.5 = (f32[48,128]{1,0:T(8,128)S(1)}, f32[48,128]{1,0:T(8,128)S(1)}, u32[]{:S(2)}, u32[]{:S(2)}) collective-permute-start(f32[48,128]{1,0:T(8,128)S(1)} %get-tuple-element.66), channel_id=1, source_target_pairs={{0,32},{64,96},{48,80},{112,16},{32,0},{96,64},{80,48},{16,112},{1... | collective-permute-start | bytes 73736 | tf_op jit(solution)/shard_map/ppermute | solution.py:438
  20.6 1.2 %own.5 = (f32[2,80,80]{2,1,0:T(8,128)S(1)}, f32[2,80,80]{2,1,0:T(8,128)S(1)}, f32[1,2048]{1,0:T(1,128)S(1)}) custom-call(s32[4]{0:T(128)S(1)} %copy-done.1, s32[4,2048]{1,0:T(4,128)S(1)} %copy-done, f32[2,48,128]{2,1,0:T(8,128)S(1)} %get-tuple-element.67.pay), custom_call_target="tpu_custom_call" | custom-call | tf_op jit(solution)/shard_map/own/pallas_call | solution.py:439
  21.8 0.0 collective-permute-done.5.far
  21.8 0.2 collective-permute-start.6
  22.1 1.0 %collective-permute-done.6.sib_far = f32[48,128]{1,0:T(8,128)S(1)} collective-permute-done((f32[48,128]{1,0:T(8,128)S(1)}, f32[48,128]{1,0:T(8,128)S(1)}, u32[]{:S(2)}, u32[]{:S(2)}) %collective-permute-start.6) | collective-permute-done | bytes 24608 | tf_op jit(solution)/shard_map/ppermute | solution.py:447
  23.1 0.3 send.5
  23.4 1.2 %collective-permute-start.7 = (f32[2,80,80]{2,1,0:T(8,128)S(1)}, f32[2,80,80]{2,1,0:T(8,128)S(1)}, u32[]{:S(2)}, u32[]{:S(2)}) collective-permute-start(f32[2,80,80]{2,1,0:T(8,128)S(1)} %send.5), channel_id=1, source_target_pairs={{0,1},{2,3},{4,5},{6,7},{8,9},{10,11},{12,13},{14,15},{17,18},{19,... | collective-permute-start | bytes 153608 | tf_op jit(solution)/shard_map/ppermute | solution.py:452
  24.6 0.3 same.5.q0
  24.9 2.2 %collective-permute-done.7.h = f32[2,80,80]{2,1,0:T(8,128)S(1)} collective-permute-done((f32[2,80,80]{2,1,0:T(8,128)S(1)}, f32[2,80,80]{2,1,0:T(8,128)S(1)}, u32[]{:S(2)}, u32[]{:S(2)}) %collective-permute-start.7) | collective-permute-done | bytes 51232 | tf_op jit(solution)/shard_map/ppermute | solution.py:452
  27.0 1.0 %collective-permute-start.8 = (f32[2,80,80]{2,1,0:T(8,128)S(1)}, f32[2,80,80]{2,1,0:T(8,128)S(1)}, u32[]{:S(2)}, u32[]{:S(2)}) collective-permute-start(f32[2,80,80]{2,1,0:T(8,128)S(1)} %collective-permute-done.7.h), channel_id=1, source_target_pairs={{0,16},{32,48},{64,80},{96,112},{16,0},{48,32},{80,64},{112,96},{1... | collective-permute-start | bytes 153608 | tf_op jit(solution)/shard_map/ppermute | solution.py:480
  28.1 0.9 %collective-permute-done.8.g = f32[2,80,80]{2,1,0:T(8,128)S(1)} collective-permute-done((f32[2,80,80]{2,1,0:T(8,128)S(1)}, f32[2,80,80]{2,1,0:T(8,128)S(1)}, u32[]{:S(2)}, u32[]{:S(2)}) %collective-permute-start.8) | collective-permute-done | bytes 51232 | tf_op jit(solution)/shard_map/ppermute | solution.py:480
  29.0 0.4 step.4
  29.4 2.8 %collective-permute-start.9 = (f32[48,128]{1,0:T(8,128)S(1)}, f32[48,128]{1,0:T(8,128)S(1)}, u32[]{:S(2)}, u32[]{:S(2)}) collective-permute-start(f32[48,128]{1,0:T(8,128)S(1)} %get-tuple-element.77), channel_id=1, source_target_pairs={{0,32},{64,96},{48,80},{112,16},{32,0},{96,64},{80,48},{16,112},{1... | collective-permute-start | bytes 73736 | tf_op jit(solution)/shard_map/ppermute | solution.py:438
  32.1 1.2 %own.6 = (f32[2,80,80]{2,1,0:T(8,128)S(1)}, f32[2,80,80]{2,1,0:T(8,128)S(1)}, f32[1,2048]{1,0:T(1,128)S(1)}) custom-call(s32[4]{0:T(128)S(1)} %copy-done.1, s32[4,2048]{1,0:T(4,128)S(1)} %copy-done, f32[2,48,128]{2,1,0:T(8,128)S(1)} %get-tuple-element.78.pay), custom_call_target="tpu_custom_call" | custom-call | tf_op jit(solution)/shard_map/own/pallas_call | solution.py:439
  33.4 0.0 collective-permute-done.9.far
  33.4 0.2 collective-permute-start.10
  33.6 1.0 %collective-permute-done.10.sib_far = f32[48,128]{1,0:T(8,128)S(1)} collective-permute-done((f32[48,128]{1,0:T(8,128)S(1)}, f32[48,128]{1,0:T(8,128)S(1)}, u32[]{:S(2)}, u32[]{:S(2)}) %collective-permute-start.10) | collective-permute-done | bytes 24608 | tf_op jit(solution)/shard_map/ppermute | solution.py:447
  34.6 0.3 send.6
  34.9 1.2 %collective-permute-start.11 = (f32[2,80,80]{2,1,0:T(8,128)S(1)}, f32[2,80,80]{2,1,0:T(8,128)S(1)}, u32[]{:S(2)}, u32[]{:S(2)}) collective-permute-start(f32[2,80,80]{2,1,0:T(8,128)S(1)} %send.6), channel_id=1, source_target_pairs={{0,1},{2,3},{4,5},{6,7},{8,9},{10,11},{12,13},{14,15},{17,18},{19,... | collective-permute-start | bytes 153608 | tf_op jit(solution)/shard_map/ppermute | solution.py:452
  36.1 2.2 %turn.1.near = bf16[32,160,256]{2,1,0:T(8,128)(2,1)S(1)} custom-call(f32[80,4,32,256]{3,2,1,0:T(8,128)} %x.3), custom_call_target="tpu_custom_call" | custom-call | tf_op jit(solution)/shard_map/turn/pallas_call | solution.py:471
  38.3 0.3 same.6.q0
  38.6 0.0 collective-permute-done.11.h
  38.6 1.0 %collective-permute-start.12 = (f32[2,80,80]{2,1,0:T(8,128)S(1)}, f32[2,80,80]{2,1,0:T(8,128)S(1)}, u32[]{:S(2)}, u32[]{:S(2)}) collective-permute-start(f32[2,80,80]{2,1,0:T(8,128)S(1)} %collective-permute-done.11.h), channel_id=1, source_target_pairs={{0,16},{32,48},{64,80},{96,112},{16,0},{48,32},{80,64},{112,96},{1... | collective-permute-start | bytes 153608 | tf_op jit(solution)/shard_map/ppermute | solution.py:480
  39.6 0.9 %collective-permute-done.12.g = f32[2,80,80]{2,1,0:T(8,128)S(1)} collective-permute-done((f32[2,80,80]{2,1,0:T(8,128)S(1)}, f32[2,80,80]{2,1,0:T(8,128)S(1)}, u32[]{:S(2)}, u32[]{:S(2)}) %collective-permute-start.12) | collective-permute-done | bytes 51232 | tf_op jit(solution)/shard_map/ppermute | solution.py:480
  40.5 0.4 step.5
  40.9 2.8 %collective-permute-start.13 = (f32[56,128]{1,0:T(8,128)S(1)}, f32[56,128]{1,0:T(8,128)S(1)}, u32[]{:S(2)}, u32[]{:S(2)}) collective-permute-start(f32[56,128]{1,0:T(8,128)S(1)} %get-tuple-element.88), channel_id=1, source_target_pairs={{0,32},{64,96},{48,80},{112,16},{32,0},{96,64},{80,48},{16,112},{1... | collective-permute-start | bytes 86024 | tf_op jit(solution)/shard_map/ppermute | solution.py:438
  43.7 1.2 %own.7 = (f32[2,80,80]{2,1,0:T(8,128)S(1)}, f32[2,80,80]{2,1,0:T(8,128)S(1)}, f32[1,2048]{1,0:T(1,128)S(1)}) custom-call(s32[4]{0:T(128)S(1)} %copy-done.1, s32[4,2048]{1,0:T(4,128)S(1)} %copy-done, f32[2,48,128]{2,1,0:T(8,128)S(1)} %get-tuple-element.89.pay), custom_call_target="tpu_custom_call" | custom-call | tf_op jit(solution)/shard_map/own/pallas_call | solution.py:439
  44.9 0.1 collective-permute-done.13.far
  45.0 0.2 collective-permute-start.14
  45.2 1.0 %collective-permute-done.14.sib_far = f32[56,128]{1,0:T(8,128)S(1)} collective-permute-done((f32[56,128]{1,0:T(8,128)S(1)}, f32[56,128]{1,0:T(8,128)S(1)}, u32[]{:S(2)}, u32[]{:S(2)}) %collective-permute-start.14) | collective-permute-done | bytes 28704 | tf_op jit(solution)/shard_map/ppermute | solution.py:447
  46.2 0.3 send.7
  46.5 1.2 %collective-permute-start.15 = (f32[2,80,80]{2,1,0:T(8,128)S(1)}, f32[2,80,80]{2,1,0:T(8,128)S(1)}, u32[]{:S(2)}, u32[]{:S(2)}) collective-permute-start(f32[2,80,80]{2,1,0:T(8,128)S(1)} %send.7), channel_id=1, source_target_pairs={{0,1},{2,3},{4,5},{6,7},{8,9},{10,11},{12,13},{14,15},{17,18},{19,... | collective-permute-start | bytes 153608 | tf_op jit(solution)/shard_map/ppermute | solution.py:452
  47.7 1.9 %collective-permute-start.16 = (f32[8,128]{1,0:T(8,128)S(1)}, f32[8,128]{1,0:T(8,128)S(1)}, u32[]{:S(2)}, u32[]{:S(2)}) collective-permute-start(f32[8,128]{1,0:T(8,128)S(1)} %slice.3), channel_id=1, source_target_pairs={{0,32},{64,96},{48,80},{112,16},{32,0},{96,64},{80,48},{16,112},{1... | collective-permute-start | bytes 12296 | tf_op jit(solution)/shard_map/ppermute | solution.py:458
  49.6 0.3 same.7.q0
  49.9 1.5 %collective-permute-done.16.across = f32[8,128]{1,0:T(8,128)S(1)} collective-permute-done((f32[8,128]{1,0:T(8,128)S(1)}, f32[8,128]{1,0:T(8,128)S(1)}, u32[]{:S(2)}, u32[]{:S(2)}) %collective-permute-start.16) | collective-permute-done | bytes 4128 | tf_op jit(solution)/shard_map/ppermute | solution.py:458
  51.4 0.7 column.1
  52.0 0.0 collective-permute-done.15.h
  52.0 0.5 collective-permute-start.17
  52.5 10.4 %all-to-all-start = ((f32[16,16,128]{2,1,0:T(8,128)}), f32[16,16,128]{2,1,0:T(8,128)S(1)}, u32[]{:S(2)}, u32[]{:S(2)}) async-start(f32[16,16,128]{2,1,0:T(8,128)} %column.1), calls=%async_computation | async-start | bytes 262144 | tf_op jit(solution)/shard_map/all_to_all | solution.py:464
  62.9 0.0 collective-permute-done.17.g
  63.0 8.6 %final.1 = f32[80,4,32,256]{3,2,1,0:T(8,128)} custom-call(f32[2,80,80]{2,1,0:T(8,128)S(1)} %same.7.q0, f32[2,80,80]{2,1,0:T(8,128)S(1)} %collective-permute-done.15.h, f32[2,80,80]{2,1,0:T(8,128)S(1)} %collective-permute-done.17.g, f32[2,96,384]{2,1,0:T(8,128)S(1)} %get-tuple-element.99.z, bf16[32,160,256]{2,1,0:T(8,128)(2,1)S(1)} %turn.1.near, ...), custom_call_target="tpu_custom_call" | custom-call | flops 1258291200 | bytes 20971520 | tf_op jit(solution)/shard_map/final/pallas_call | solution.py:494
  71.5 0.0 all-to-all-done.gathered
  71.5 2.1 %place.1 = f32[4,2048]{1,0:T(4,128)} custom-call(s32[4]{0:T(128)S(1)} %copy-done.1, s32[4,2048]{1,0:T(4,128)S(1)} %copy-done, f32[16,16,128]{2,1,0:T(8,128)S(1)} %all-to-all-done.gathered, f32[1,2048]{1,0:T(1,128)S(1)} %get-tuple-element.104.r0, f32[1,2048]{1,0:T(1,128)S(1)} %get-tuple-element.105.r1, f32[1,2048]{1,0:T(1,128)S(1)} %get-tuple-element.106.r2, ...), custom_call_target="tpu_custom_call" | custom-call | tf_op jit(solution)/shard_map/place/pallas_call | solution.py:507
  (1 shorter events, 0.0 us)
Async XLA Ops:
  0.6 8.4 %copy-start.1 = (s32[4]{0:T(128)S(1)}, s32[4]{0:T(128)}, u32[]{:S(2)}) copy-start(s32[4]{0:T(128)} %order.9) | copy-start | bytes 52
  0.6 8.4 %copy-start = (s32[4,2048]{1,0:T(4,128)S(1)}, s32[4,2048]{1,0:T(4,128)}, u32[]{:S(2)}) copy-start(s32[4,2048]{1,0:T(4,128)} %owner.9) | copy-start | bytes 98308
  3.6 2.4 %collective-permute-start = (f32[96,256]{1,0:T(8,128)S(1)}, f32[96,256]{1,0:T(8,128)S(1)}, u32[]{:S(2)}, u32[]{:S(2)}) collective-permute-start(f32[96,256]{1,0:T(8,128)S(1)} %init.1.own), channel_id=1, source_target_pairs={{0,16},{32,48},{64,80},{96,112},{16,0},{48,32},{80,64},{112,96},{1... | collective-permute-start | bytes 294920 | tf_op jit(solution)/shard_map/ppermute | solution.py:433
  6.2 4.1 %collective-permute-start.1 = (f32[48,128]{1,0:T(8,128)S(1)}, f32[48,128]{1,0:T(8,128)S(1)}, u32[]{:S(2)}, u32[]{:S(2)}) collective-permute-start(f32[48,128]{1,0:T(8,128)S(1)} %get-tuple-element.55), channel_id=1, source_target_pairs={{0,32},{64,96},{48,80},{112,16},{32,0},{96,64},{80,48},{16,112},{1... | collective-permute-start | bytes 73736 | tf_op jit(solution)/shard_map/ppermute | solution.py:438
  10.3 1.3 %collective-permute-start.2 = (f32[48,128]{1,0:T(8,128)S(1)}, f32[48,128]{1,0:T(8,128)S(1)}, u32[]{:S(2)}, u32[]{:S(2)}) collective-permute-start(f32[48,128]{1,0:T(8,128)S(1)} %collective-permute-done.1.far), channel_id=1, source_target_pairs={{0,16},{32,48},{64,80},{96,112},{16,0},{48,32},{80,64},{112,96},{1... | collective-permute-start | bytes 73736 | tf_op jit(solution)/shard_map/ppermute | solution.py:447
  11.8 3.7 %collective-permute-start.3 = (f32[2,80,80]{2,1,0:T(8,128)S(1)}, f32[2,80,80]{2,1,0:T(8,128)S(1)}, u32[]{:S(2)}, u32[]{:S(2)}) collective-permute-start(f32[2,80,80]{2,1,0:T(8,128)S(1)} %send.4), channel_id=1, source_target_pairs={{0,1},{2,3},{4,5},{6,7},{8,9},{10,11},{12,13},{14,15},{17,18},{19,... | collective-permute-start | bytes 153608 | tf_op jit(solution)/shard_map/ppermute | solution.py:452
  15.5 1.9 %collective-permute-start.4 = (f32[2,80,80]{2,1,0:T(8,128)S(1)}, f32[2,80,80]{2,1,0:T(8,128)S(1)}, u32[]{:S(2)}, u32[]{:S(2)}) collective-permute-start(f32[2,80,80]{2,1,0:T(8,128)S(1)} %collective-permute-done.3.h), channel_id=1, source_target_pairs={{0,16},{32,48},{64,80},{96,112},{16,0},{48,32},{80,64},{112,96},{1... | collective-permute-start | bytes 153608 | tf_op jit(solution)/shard_map/ppermute | solution.py:480
  17.8 4.0 %collective-permute-start.5 = (f32[48,128]{1,0:T(8,128)S(1)}, f32[48,128]{1,0:T(8,128)S(1)}, u32[]{:S(2)}, u32[]{:S(2)}) collective-permute-start(f32[48,128]{1,0:T(8,128)S(1)} %get-tuple-element.66), channel_id=1, source_target_pairs={{0,32},{64,96},{48,80},{112,16},{32,0},{96,64},{80,48},{16,112},{1... | collective-permute-start | bytes 73736 | tf_op jit(solution)/shard_map/ppermute | solution.py:438
  21.8 1.3 %collective-permute-start.6 = (f32[48,128]{1,0:T(8,128)S(1)}, f32[48,128]{1,0:T(8,128)S(1)}, u32[]{:S(2)}, u32[]{:S(2)}) collective-permute-start(f32[48,128]{1,0:T(8,128)S(1)} %collective-permute-done.5.far), channel_id=1, source_target_pairs={{0,16},{32,48},{64,80},{96,112},{16,0},{48,32},{80,64},{112,96},{1... | collective-permute-start | bytes 73736 | tf_op jit(solution)/shard_map/ppermute | solution.py:447
  23.4 3.7 %collective-permute-start.7 = (f32[2,80,80]{2,1,0:T(8,128)S(1)}, f32[2,80,80]{2,1,0:T(8,128)S(1)}, u32[]{:S(2)}, u32[]{:S(2)}) collective-permute-start(f32[2,80,80]{2,1,0:T(8,128)S(1)} %send.5), channel_id=1, source_target_pairs={{0,1},{2,3},{4,5},{6,7},{8,9},{10,11},{12,13},{14,15},{17,18},{19,... | collective-permute-start | bytes 153608 | tf_op jit(solution)/shard_map/ppermute | solution.py:452
  27.0 1.9 %collective-permute-start.8 = (f32[2,80,80]{2,1,0:T(8,128)S(1)}, f32[2,80,80]{2,1,0:T(8,128)S(1)}, u32[]{:S(2)}, u32[]{:S(2)}) collective-permute-start(f32[2,80,80]{2,1,0:T(8,128)S(1)} %collective-permute-done.7.h), channel_id=1, source_target_pairs={{0,16},{32,48},{64,80},{96,112},{16,0},{48,32},{80,64},{112,96},{1... | collective-permute-start | bytes 153608 | tf_op jit(solution)/shard_map/ppermute | solution.py:480
  29.4 4.0 %collective-permute-start.9 = (f32[48,128]{1,0:T(8,128)S(1)}, f32[48,128]{1,0:T(8,128)S(1)}, u32[]{:S(2)}, u32[]{:S(2)}) collective-permute-start(f32[48,128]{1,0:T(8,128)S(1)} %get-tuple-element.77), channel_id=1, source_target_pairs={{0,32},{64,96},{48,80},{112,16},{32,0},{96,64},{80,48},{16,112},{1... | collective-permute-start | bytes 73736 | tf_op jit(solution)/shard_map/ppermute | solution.py:438
  33.4 1.3 %collective-permute-start.10 = (f32[48,128]{1,0:T(8,128)S(1)}, f32[48,128]{1,0:T(8,128)S(1)}, u32[]{:S(2)}, u32[]{:S(2)}) collective-permute-start(f32[48,128]{1,0:T(8,128)S(1)} %collective-permute-done.9.far), channel_id=1, source_target_pairs={{0,16},{32,48},{64,80},{96,112},{16,0},{48,32},{80,64},{112,96},{1... | collective-permute-start | bytes 73736 | tf_op jit(solution)/shard_map/ppermute | solution.py:447
  34.9 3.7 %collective-permute-start.11 = (f32[2,80,80]{2,1,0:T(8,128)S(1)}, f32[2,80,80]{2,1,0:T(8,128)S(1)}, u32[]{:S(2)}, u32[]{:S(2)}) collective-permute-start(f32[2,80,80]{2,1,0:T(8,128)S(1)} %send.6), channel_id=1, source_target_pairs={{0,1},{2,3},{4,5},{6,7},{8,9},{10,11},{12,13},{14,15},{17,18},{19,... | collective-permute-start | bytes 153608 | tf_op jit(solution)/shard_map/ppermute | solution.py:452
  38.6 1.9 %collective-permute-start.12 = (f32[2,80,80]{2,1,0:T(8,128)S(1)}, f32[2,80,80]{2,1,0:T(8,128)S(1)}, u32[]{:S(2)}, u32[]{:S(2)}) collective-permute-start(f32[2,80,80]{2,1,0:T(8,128)S(1)} %collective-permute-done.11.h), channel_id=1, source_target_pairs={{0,16},{32,48},{64,80},{96,112},{16,0},{48,32},{80,64},{112,96},{1... | collective-permute-start | bytes 153608 | tf_op jit(solution)/shard_map/ppermute | solution.py:480
  40.9 4.0 %collective-permute-start.13 = (f32[56,128]{1,0:T(8,128)S(1)}, f32[56,128]{1,0:T(8,128)S(1)}, u32[]{:S(2)}, u32[]{:S(2)}) collective-permute-start(f32[56,128]{1,0:T(8,128)S(1)} %get-tuple-element.88), channel_id=1, source_target_pairs={{0,32},{64,96},{48,80},{112,16},{32,0},{96,64},{80,48},{16,112},{1... | collective-permute-start | bytes 86024 | tf_op jit(solution)/shard_map/ppermute | solution.py:438
  45.0 1.2 %collective-permute-start.14 = (f32[56,128]{1,0:T(8,128)S(1)}, f32[56,128]{1,0:T(8,128)S(1)}, u32[]{:S(2)}, u32[]{:S(2)}) collective-permute-start(f32[56,128]{1,0:T(8,128)S(1)} %collective-permute-done.13.far), channel_id=1, source_target_pairs={{0,16},{32,48},{64,80},{96,112},{16,0},{48,32},{80,64},{112,96},{1... | collective-permute-start | bytes 86024 | tf_op jit(solution)/shard_map/ppermute | solution.py:447
  46.5 5.6 %collective-permute-start.15 = (f32[2,80,80]{2,1,0:T(8,128)S(1)}, f32[2,80,80]{2,1,0:T(8,128)S(1)}, u32[]{:S(2)}, u32[]{:S(2)}) collective-permute-start(f32[2,80,80]{2,1,0:T(8,128)S(1)} %send.7), channel_id=1, source_target_pairs={{0,1},{2,3},{4,5},{6,7},{8,9},{10,11},{12,13},{14,15},{17,18},{19,... | collective-permute-start | bytes 153608 | tf_op jit(solution)/shard_map/ppermute | solution.py:452
  47.7 3.7 %collective-permute-start.16 = (f32[8,128]{1,0:T(8,128)S(1)}, f32[8,128]{1,0:T(8,128)S(1)}, u32[]{:S(2)}, u32[]{:S(2)}) collective-permute-start(f32[8,128]{1,0:T(8,128)S(1)} %slice.3), channel_id=1, source_target_pairs={{0,32},{64,96},{48,80},{112,16},{32,0},{96,64},{80,48},{16,112},{1... | collective-permute-start | bytes 12296 | tf_op jit(solution)/shard_map/ppermute | solution.py:458
  52.0 10.9 %collective-permute-start.17 = (f32[2,80,80]{2,1,0:T(8,128)S(1)}, f32[2,80,80]{2,1,0:T(8,128)S(1)}, u32[]{:S(2)}, u32[]{:S(2)}) collective-permute-start(f32[2,80,80]{2,1,0:T(8,128)S(1)} %collective-permute-done.15.h), channel_id=1, source_target_pairs={{0,16},{32,48},{64,80},{96,112},{16,0},{48,32},{80,64},{112,96},{1... | collective-permute-start | bytes 153608 | tf_op jit(solution)/shard_map/ppermute | solution.py:480
  52.5 19.0 %all-to-all-start = ((f32[16,16,128]{2,1,0:T(8,128)}), f32[16,16,128]{2,1,0:T(8,128)S(1)}, u32[]{:S(2)}, u32[]{:S(2)}) async-start(f32[16,16,128]{2,1,0:T(8,128)} %column.1), calls=%async_computation | async-start | bytes 262144 | tf_op jit(solution)/shard_map/all_to_all | solution.py:464

commit v17 on v16

--- a/solution.py
+++ b/solution.py
@@ -334,7 +334,7 @@
     t = advance(z[c, :M, NB * CAP :], whole_gain(c, q0, h, g))[:, :M]
     th, tl = split2(t)
     w = jnp.concatenate([th, th, tl], axis=1)
-    for i in range(SLABS):
+    for i in (0, *range(TURN, SLABS), *range(1, TURN)):
         if i >= TURN:
             loads[i - TURN].wait()
         for j in range(0, SLAB, 8):
@@ -457,7 +457,7 @@
         if last:
             across = lax.ppermute(sib_far[ROWS // 2 :], "gx", side_x)
             column = call(
-                column_kernel, out_shape=shape(height, 4 * NB, 128), in_specs=[VMEM] * 4, out_specs=VMEM, name="column"
+                column_kernel, out_shape=pltpu.VMEM((height, 4 * NB, 128), F32), in_specs=[VMEM] * 4, out_specs=VMEM, name="column"
             )(news, far, sib_far, across)
         if last:
             h, q0, column = lax.optimization_barrier((h, q0, column))

time: 73.8 us -> 73 us (0.989)
  Pallas kernels: 24.8 us -> 23.9 us
    pallas_call x1, Pallas kernels: 8.56 us -> 7.7 us  [local(): call(final_kernel, out_shape=shape(M, LEV, TX, TY), in_specs=[VMEM] * 5 +...]
  transfers between devices with their start and end apart: 19 -> 19, of which waited for: 11 -> 11; matrix products, arithmetic and copies ran while one was open for 0% -> 0% of each run, Pallas kernels for 24% -> 23%
where the time goes in v17:
time: 73 us; the launch traced here: 72.7 us
  starting transfers between devices  34.2 us (47%)
  Pallas kernels  23.9 us (33%)
  waiting for transfers between devices  13.8 us (19%)
  between operations  0.82 us (1%)
    ppermute x4, starting transfers between devices, local(): far = lax.ppermute(edge, 'gx', side_x)  11.2 us
    all_to_all x1, starting transfers between devices, local(): gathered = lax.all_to_all(column, 'gy', 0, 0, tiled=True)  10.4 us
    pallas_call x1, Pallas kernels, local(): call(final_kernel, out_shape=shape(M, LEV, TX, TY), in_specs=[VMEM] * 5 +...  7.7 us
    pallas_call x4, Pallas kernels, local(): call(functools.partial(own_kernel, k), out_shape=(shape(2, M, M), shape(2...  4.81 us
    ppermute x4, starting transfers between devices, local(): h = lax.ppermute(send, both, side_y)  4.75 us
    ppermute x4, waiting for transfers between devices, local(): h = lax.ppermute(send, both, side_y)  4.39 us
    ppermute x4, waiting for transfers between devices, local(): sib_far = lax.ppermute(far, 'gx', core)  4.19 us
    ppermute x4, starting transfers between devices, local(): g = lax.ppermute(h, 'gx', core)  3.54 us
  transfers between devices with their start and end apart: 19, of which 11 were waited for; matrix products, arithmetic and copies ran while one was open for 0% of the time, Pallas kernels for 23%

profile of v17, /device:TPU:1, one launch (start us, length us, event | category | flops | bytes accessed | tf_op | source)
XLA Modules:
  0.0 72.7 jit_solution(3583637122371315503)
XLA Ops:
  0.6 0.0 copy-start.1
  0.6 0.0 copy-start
  0.7 2.9 %init.1.own = f32[96,256]{1,0:T(8,128)S(1)} custom-call(s32[4]{0:T(128)} %order.9, f32[4,2048]{1,0:T(4,128)} %value_hbm.1, f32[4,2048]{1,0:T(4,128)} %variance_hbm.1, s32[4,2048]{1,0:T(4,128)} %owner.9, s32[4,2048]{1,0:T(4,128)} %cell_hbm.1, s32[4,8,2048]{2,1,0:T(8,128)} %bitcast.1, f32[80,4,32,256]{3,2,1,0:T(8,128)} %x.3), custom_call_target="tpu_custom_call" | custom-call | tf_op jit(solution)/shard_map/init/pallas_call | solution.py:411
  3.6 1.5 %collective-permute-start = (f32[96,256]{1,0:T(8,128)S(1)}, f32[96,256]{1,0:T(8,128)S(1)}, u32[]{:S(2)}, u32[]{:S(2)}) collective-permute-start(f32[96,256]{1,0:T(8,128)S(1)} %init.1.own), channel_id=1, source_target_pairs={{0,16},{32,48},{64,80},{96,112},{16,0},{48,32},{80,64},{112,96},{1... | collective-permute-start | bytes 294920 | tf_op jit(solution)/shard_map/ppermute | solution.py:433
  5.1 0.9 %collective-permute-done.sib = f32[96,256]{1,0:T(8,128)S(1)} collective-permute-done((f32[96,256]{1,0:T(8,128)S(1)}, f32[96,256]{1,0:T(8,128)S(1)}, u32[]{:S(2)}, u32[]{:S(2)}) %collective-permute-start) | collective-permute-done | bytes 98336 | tf_op jit(solution)/shard_map/ppermute | solution.py:433
  6.0 0.2 start.1
  6.2 2.9 %collective-permute-start.1 = (f32[48,128]{1,0:T(8,128)S(1)}, f32[48,128]{1,0:T(8,128)S(1)}, u32[]{:S(2)}, u32[]{:S(2)}) collective-permute-start(f32[48,128]{1,0:T(8,128)S(1)} %get-tuple-element.55), channel_id=1, source_target_pairs={{0,32},{64,96},{48,80},{112,16},{32,0},{96,64},{80,48},{16,112},{1... | collective-permute-start | bytes 73736 | tf_op jit(solution)/shard_map/ppermute | solution.py:438
  9.0 0.0 copy-done.1
  9.0 0.0 copy-done
  9.0 1.2 %own.4 = (f32[2,80,80]{2,1,0:T(8,128)S(1)}, f32[2,80,80]{2,1,0:T(8,128)S(1)}, f32[1,2048]{1,0:T(1,128)S(1)}) custom-call(s32[4]{0:T(128)S(1)} %copy-done.1, s32[4,2048]{1,0:T(4,128)S(1)} %copy-done, f32[2,48,128]{2,1,0:T(8,128)S(1)} %get-tuple-element.56.pay), custom_call_target="tpu_custom_call" | custom-call | tf_op jit(solution)/shard_map/own/pallas_call | solution.py:439
  10.3 0.0 collective-permute-done.1.far
  10.3 0.1 collective-permute-start.2
  10.4 1.1 %collective-permute-done.2.sib_far = f32[48,128]{1,0:T(8,128)S(1)} collective-permute-done((f32[48,128]{1,0:T(8,128)S(1)}, f32[48,128]{1,0:T(8,128)S(1)}, u32[]{:S(2)}, u32[]{:S(2)}) %collective-permute-start.2) | collective-permute-done | bytes 24608 | tf_op jit(solution)/shard_map/ppermute | solution.py:447
  11.5 0.3 send.4
  11.8 1.2 %collective-permute-start.3 = (f32[2,80,80]{2,1,0:T(8,128)S(1)}, f32[2,80,80]{2,1,0:T(8,128)S(1)}, u32[]{:S(2)}, u32[]{:S(2)}) collective-permute-start(f32[2,80,80]{2,1,0:T(8,128)S(1)} %send.4), channel_id=1, source_target_pairs={{0,1},{2,3},{4,5},{6,7},{8,9},{10,11},{12,13},{14,15},{17,18},{19,... | collective-permute-start | bytes 153608 | tf_op jit(solution)/shard_map/ppermute | solution.py:452
  13.0 0.3 same.4.q0
  13.3 2.2 %collective-permute-done.3.h = f32[2,80,80]{2,1,0:T(8,128)S(1)} collective-permute-done((f32[2,80,80]{2,1,0:T(8,128)S(1)}, f32[2,80,80]{2,1,0:T(8,128)S(1)}, u32[]{:S(2)}, u32[]{:S(2)}) %collective-permute-start.3) | collective-permute-done | bytes 51232 | tf_op jit(solution)/shard_map/ppermute | solution.py:452
  15.5 1.0 %collective-permute-start.4 = (f32[2,80,80]{2,1,0:T(8,128)S(1)}, f32[2,80,80]{2,1,0:T(8,128)S(1)}, u32[]{:S(2)}, u32[]{:S(2)}) collective-permute-start(f32[2,80,80]{2,1,0:T(8,128)S(1)} %collective-permute-done.3.h), channel_id=1, source_target_pairs={{0,16},{32,48},{64,80},{96,112},{16,0},{48,32},{80,64},{112,96},{1... | collective-permute-start | bytes 153608 | tf_op jit(solution)/shard_map/ppermute | solution.py:480
  16.5 0.9 %collective-permute-done.4.g = f32[2,80,80]{2,1,0:T(8,128)S(1)} collective-permute-done((f32[2,80,80]{2,1,0:T(8,128)S(1)}, f32[2,80,80]{2,1,0:T(8,128)S(1)}, u32[]{:S(2)}, u32[]{:S(2)}) %collective-permute-start.4) | collective-permute-done | bytes 51232 | tf_op jit(solution)/shard_map/ppermute | solution.py:480
  17.4 0.4 step.3
  17.8 2.8 %collective-permute-start.5 = (f32[48,128]{1,0:T(8,128)S(1)}, f32[48,128]{1,0:T(8,128)S(1)}, u32[]{:S(2)}, u32[]{:S(2)}) collective-permute-start(f32[48,128]{1,0:T(8,128)S(1)} %get-tuple-element.66), channel_id=1, source_target_pairs={{0,32},{64,96},{48,80},{112,16},{32,0},{96,64},{80,48},{16,112},{1... | collective-permute-start | bytes 73736 | tf_op jit(solution)/shard_map/ppermute | solution.py:438
  20.6 1.2 %own.5 = (f32[2,80,80]{2,1,0:T(8,128)S(1)}, f32[2,80,80]{2,1,0:T(8,128)S(1)}, f32[1,2048]{1,0:T(1,128)S(1)}) custom-call(s32[4]{0:T(128)S(1)} %copy-done.1, s32[4,2048]{1,0:T(4,128)S(1)} %copy-done, f32[2,48,128]{2,1,0:T(8,128)S(1)} %get-tuple-element.67.pay), custom_call_target="tpu_custom_call" | custom-call | tf_op jit(solution)/shard_map/own/pallas_call | solution.py:439
  21.8 0.0 collective-permute-done.5.far
  21.8 0.2 collective-permute-start.6
  22.1 1.0 %collective-permute-done.6.sib_far = f32[48,128]{1,0:T(8,128)S(1)} collective-permute-done((f32[48,128]{1,0:T(8,128)S(1)}, f32[48,128]{1,0:T(8,128)S(1)}, u32[]{:S(2)}, u32[]{:S(2)}) %collective-permute-start.6) | collective-permute-done | bytes 24608 | tf_op jit(solution)/shard_map/ppermute | solution.py:447
  23.1 0.3 send.5
  23.4 1.2 %collective-permute-start.7 = (f32[2,80,80]{2,1,0:T(8,128)S(1)}, f32[2,80,80]{2,1,0:T(8,128)S(1)}, u32[]{:S(2)}, u32[]{:S(2)}) collective-permute-start(f32[2,80,80]{2,1,0:T(8,128)S(1)} %send.5), channel_id=1, source_target_pairs={{0,1},{2,3},{4,5},{6,7},{8,9},{10,11},{12,13},{14,15},{17,18},{19,... | collective-permute-start | bytes 153608 | tf_op jit(solution)/shard_map/ppermute | solution.py:452
  24.6 0.3 same.5.q0
  24.9 2.2 %collective-permute-done.7.h = f32[2,80,80]{2,1,0:T(8,128)S(1)} collective-permute-done((f32[2,80,80]{2,1,0:T(8,128)S(1)}, f32[2,80,80]{2,1,0:T(8,128)S(1)}, u32[]{:S(2)}, u32[]{:S(2)}) %collective-permute-start.7) | collective-permute-done | bytes 51232 | tf_op jit(solution)/shard_map/ppermute | solution.py:452
  27.0 1.0 %collective-permute-start.8 = (f32[2,80,80]{2,1,0:T(8,128)S(1)}, f32[2,80,80]{2,1,0:T(8,128)S(1)}, u32[]{:S(2)}, u32[]{:S(2)}) collective-permute-start(f32[2,80,80]{2,1,0:T(8,128)S(1)} %collective-permute-done.7.h), channel_id=1, source_target_pairs={{0,16},{32,48},{64,80},{96,112},{16,0},{48,32},{80,64},{112,96},{1... | collective-permute-start | bytes 153608 | tf_op jit(solution)/shard_map/ppermute | solution.py:480
  28.1 0.9 %collective-permute-done.8.g = f32[2,80,80]{2,1,0:T(8,128)S(1)} collective-permute-done((f32[2,80,80]{2,1,0:T(8,128)S(1)}, f32[2,80,80]{2,1,0:T(8,128)S(1)}, u32[]{:S(2)}, u32[]{:S(2)}) %collective-permute-start.8) | collective-permute-done | bytes 51232 | tf_op jit(solution)/shard_map/ppermute | solution.py:480
  29.0 0.4 step.4
  29.4 2.8 %collective-permute-start.9 = (f32[48,128]{1,0:T(8,128)S(1)}, f32[48,128]{1,0:T(8,128)S(1)}, u32[]{:S(2)}, u32[]{:S(2)}) collective-permute-start(f32[48,128]{1,0:T(8,128)S(1)} %get-tuple-element.77), channel_id=1, source_target_pairs={{0,32},{64,96},{48,80},{112,16},{32,0},{96,64},{80,48},{16,112},{1... | collective-permute-start | bytes 73736 | tf_op jit(solution)/shard_map/ppermute | solution.py:438
  32.1 1.2 %own.6 = (f32[2,80,80]{2,1,0:T(8,128)S(1)}, f32[2,80,80]{2,1,0:T(8,128)S(1)}, f32[1,2048]{1,0:T(1,128)S(1)}) custom-call(s32[4]{0:T(128)S(1)} %copy-done.1, s32[4,2048]{1,0:T(4,128)S(1)} %copy-done, f32[2,48,128]{2,1,0:T(8,128)S(1)} %get-tuple-element.78.pay), custom_call_target="tpu_custom_call" | custom-call | tf_op jit(solution)/shard_map/own/pallas_call | solution.py:439
  33.4 0.0 collective-permute-done.9.far
  33.4 0.2 collective-permute-start.10
  33.6 1.0 %collective-permute-done.10.sib_far = f32[48,128]{1,0:T(8,128)S(1)} collective-permute-done((f32[48,128]{1,0:T(8,128)S(1)}, f32[48,128]{1,0:T(8,128)S(1)}, u32[]{:S(2)}, u32[]{:S(2)}) %collective-permute-start.10) | collective-permute-done | bytes 24608 | tf_op jit(solution)/shard_map/ppermute | solution.py:447
  34.6 0.3 send.6
  34.9 1.2 %collective-permute-start.11 = (f32[2,80,80]{2,1,0:T(8,128)S(1)}, f32[2,80,80]{2,1,0:T(8,128)S(1)}, u32[]{:S(2)}, u32[]{:S(2)}) collective-permute-start(f32[2,80,80]{2,1,0:T(8,128)S(1)} %send.6), channel_id=1, source_target_pairs={{0,1},{2,3},{4,5},{6,7},{8,9},{10,11},{12,13},{14,15},{17,18},{19,... | collective-permute-start | bytes 153608 | tf_op jit(solution)/shard_map/ppermute | solution.py:452
  36.1 2.2 %turn.1.near = bf16[32,160,256]{2,1,0:T(8,128)(2,1)S(1)} custom-call(f32[80,4,32,256]{3,2,1,0:T(8,128)} %x.3), custom_call_target="tpu_custom_call" | custom-call | tf_op jit(solution)/shard_map/turn/pallas_call | solution.py:471
  38.3 0.3 same.6.q0
  38.6 0.0 collective-permute-done.11.h
  38.6 1.0 %collective-permute-start.12 = (f32[2,80,80]{2,1,0:T(8,128)S(1)}, f32[2,80,80]{2,1,0:T(8,128)S(1)}, u32[]{:S(2)}, u32[]{:S(2)}) collective-permute-start(f32[2,80,80]{2,1,0:T(8,128)S(1)} %collective-permute-done.11.h), channel_id=1, source_target_pairs={{0,16},{32,48},{64,80},{96,112},{16,0},{48,32},{80,64},{112,96},{1... | collective-permute-start | bytes 153608 | tf_op jit(solution)/shard_map/ppermute | solution.py:480
  39.6 0.9 %collective-permute-done.12.g = f32[2,80,80]{2,1,0:T(8,128)S(1)} collective-permute-done((f32[2,80,80]{2,1,0:T(8,128)S(1)}, f32[2,80,80]{2,1,0:T(8,128)S(1)}, u32[]{:S(2)}, u32[]{:S(2)}) %collective-permute-start.12) | collective-permute-done | bytes 51232 | tf_op jit(solution)/shard_map/ppermute | solution.py:480
  40.5 0.4 step.5
  40.9 2.8 %collective-permute-start.13 = (f32[56,128]{1,0:T(8,128)S(1)}, f32[56,128]{1,0:T(8,128)S(1)}, u32[]{:S(2)}, u32[]{:S(2)}) collective-permute-start(f32[56,128]{1,0:T(8,128)S(1)} %get-tuple-element.88), channel_id=1, source_target_pairs={{0,32},{64,96},{48,80},{112,16},{32,0},{96,64},{80,48},{16,112},{1... | collective-permute-start | bytes 86024 | tf_op jit(solution)/shard_map/ppermute | solution.py:438
  43.7 1.2 %own.7 = (f32[2,80,80]{2,1,0:T(8,128)S(1)}, f32[2,80,80]{2,1,0:T(8,128)S(1)}, f32[1,2048]{1,0:T(1,128)S(1)}) custom-call(s32[4]{0:T(128)S(1)} %copy-done.1, s32[4,2048]{1,0:T(4,128)S(1)} %copy-done, f32[2,48,128]{2,1,0:T(8,128)S(1)} %get-tuple-element.89.pay), custom_call_target="tpu_custom_call" | custom-call | tf_op jit(solution)/shard_map/own/pallas_call | solution.py:439
  44.9 0.1 collective-permute-done.13.far
  45.0 0.2 collective-permute-start.14
  45.2 1.0 %collective-permute-done.14.sib_far = f32[56,128]{1,0:T(8,128)S(1)} collective-permute-done((f32[56,128]{1,0:T(8,128)S(1)}, f32[56,128]{1,0:T(8,128)S(1)}, u32[]{:S(2)}, u32[]{:S(2)}) %collective-permute-start.14) | collective-permute-done | bytes 28704 | tf_op jit(solution)/shard_map/ppermute | solution.py:447
  46.2 0.3 send.7
  46.5 1.2 %collective-permute-start.15 = (f32[2,80,80]{2,1,0:T(8,128)S(1)}, f32[2,80,80]{2,1,0:T(8,128)S(1)}, u32[]{:S(2)}, u32[]{:S(2)}) collective-permute-start(f32[2,80,80]{2,1,0:T(8,128)S(1)} %send.7), channel_id=1, source_target_pairs={{0,1},{2,3},{4,5},{6,7},{8,9},{10,11},{12,13},{14,15},{17,18},{19,... | collective-permute-start | bytes 153608 | tf_op jit(solution)/shard_map/ppermute | solution.py:452
  47.7 1.9 %collective-permute-start.16 = (f32[8,128]{1,0:T(8,128)S(1)}, f32[8,128]{1,0:T(8,128)S(1)}, u32[]{:S(2)}, u32[]{:S(2)}) collective-permute-start(f32[8,128]{1,0:T(8,128)S(1)} %slice.3), channel_id=1, source_target_pairs={{0,32},{64,96},{48,80},{112,16},{32,0},{96,64},{80,48},{16,112},{1... | collective-permute-start | bytes 12296 | tf_op jit(solution)/shard_map/ppermute | solution.py:458
  49.6 0.3 same.7.q0
  49.9 1.5 %collective-permute-done.16.across = f32[8,128]{1,0:T(8,128)S(1)} collective-permute-done((f32[8,128]{1,0:T(8,128)S(1)}, f32[8,128]{1,0:T(8,128)S(1)}, u32[]{:S(2)}, u32[]{:S(2)}) %collective-permute-start.16) | collective-permute-done | bytes 4128 | tf_op jit(solution)/shard_map/ppermute | solution.py:458
  51.4 0.7 column.1
  52.0 0.0 collective-permute-done.15.h
  52.0 0.5 collective-permute-start.17
  52.5 10.4 %all-to-all-start = ((f32[16,16,128]{2,1,0:T(8,128)}), f32[16,16,128]{2,1,0:T(8,128)S(1)}, u32[]{:S(2)}, u32[]{:S(2)}) async-start(f32[16,16,128]{2,1,0:T(8,128)} %column.1), calls=%async_computation | async-start | bytes 262144 | tf_op jit(solution)/shard_map/all_to_all | solution.py:464
  62.9 0.0 collective-permute-done.17.g
  63.0 7.7 %final.1 = f32[80,4,32,256]{3,2,1,0:T(8,128)} custom-call(f32[2,80,80]{2,1,0:T(8,128)S(1)} %same.7.q0, f32[2,80,80]{2,1,0:T(8,128)S(1)} %collective-permute-done.15.h, f32[2,80,80]{2,1,0:T(8,128)S(1)} %collective-permute-done.17.g, f32[2,96,384]{2,1,0:T(8,128)S(1)} %get-tuple-element.99.z, bf16[32,160,256]{2,1,0:T(8,128)(2,1)S(1)} %turn.1.near, ...), custom_call_target="tpu_custom_call" | custom-call | flops 1258291200 | bytes 20971520 | tf_op jit(solution)/shard_map/final/pallas_call | solution.py:494
  70.7 0.0 all-to-all-done.gathered
  70.7 2.1 %place.1 = f32[4,2048]{1,0:T(4,128)} custom-call(s32[4]{0:T(128)S(1)} %copy-done.1, s32[4,2048]{1,0:T(4,128)S(1)} %copy-done, f32[16,16,128]{2,1,0:T(8,128)S(1)} %all-to-all-done.gathered, f32[1,2048]{1,0:T(1,128)S(1)} %get-tuple-element.104.r0, f32[1,2048]{1,0:T(1,128)S(1)} %get-tuple-element.105.r1, f32[1,2048]{1,0:T(1,128)S(1)} %get-tuple-element.106.r2, ...), custom_call_target="tpu_custom_call" | custom-call | tf_op jit(solution)/shard_map/place/pallas_call | solution.py:507
  (1 shorter events, 0.0 us)
Async XLA Ops:
  0.6 8.4 %copy-start.1 = (s32[4]{0:T(128)S(1)}, s32[4]{0:T(128)}, u32[]{:S(2)}) copy-start(s32[4]{0:T(128)} %order.9) | copy-start | bytes 52
  0.6 8.4 %copy-start = (s32[4,2048]{1,0:T(4,128)S(1)}, s32[4,2048]{1,0:T(4,128)}, u32[]{:S(2)}) copy-start(s32[4,2048]{1,0:T(4,128)} %owner.9) | copy-start | bytes 98308
  3.6 2.4 %collective-permute-start = (f32[96,256]{1,0:T(8,128)S(1)}, f32[96,256]{1,0:T(8,128)S(1)}, u32[]{:S(2)}, u32[]{:S(2)}) collective-permute-start(f32[96,256]{1,0:T(8,128)S(1)} %init.1.own), channel_id=1, source_target_pairs={{0,16},{32,48},{64,80},{96,112},{16,0},{48,32},{80,64},{112,96},{1... | collective-permute-start | bytes 294920 | tf_op jit(solution)/shard_map/ppermute | solution.py:433
  6.2 4.1 %collective-permute-start.1 = (f32[48,128]{1,0:T(8,128)S(1)}, f32[48,128]{1,0:T(8,128)S(1)}, u32[]{:S(2)}, u32[]{:S(2)}) collective-permute-start(f32[48,128]{1,0:T(8,128)S(1)} %get-tuple-element.55), channel_id=1, source_target_pairs={{0,32},{64,96},{48,80},{112,16},{32,0},{96,64},{80,48},{16,112},{1... | collective-permute-start | bytes 73736 | tf_op jit(solution)/shard_map/ppermute | solution.py:438
  10.3 1.3 %collective-permute-start.2 = (f32[48,128]{1,0:T(8,128)S(1)}, f32[48,128]{1,0:T(8,128)S(1)}, u32[]{:S(2)}, u32[]{:S(2)}) collective-permute-start(f32[48,128]{1,0:T(8,128)S(1)} %collective-permute-done.1.far), channel_id=1, source_target_pairs={{0,16},{32,48},{64,80},{96,112},{16,0},{48,32},{80,64},{112,96},{1... | collective-permute-start | bytes 73736 | tf_op jit(solution)/shard_map/ppermute | solution.py:447
  11.8 3.7 %collective-permute-start.3 = (f32[2,80,80]{2,1,0:T(8,128)S(1)}, f32[2,80,80]{2,1,0:T(8,128)S(1)}, u32[]{:S(2)}, u32[]{:S(2)}) collective-permute-start(f32[2,80,80]{2,1,0:T(8,128)S(1)} %send.4), channel_id=1, source_target_pairs={{0,1},{2,3},{4,5},{6,7},{8,9},{10,11},{12,13},{14,15},{17,18},{19,... | collective-permute-start | bytes 153608 | tf_op jit(solution)/shard_map/ppermute | solution.py:452
  15.5 1.9 %collective-permute-start.4 = (f32[2,80,80]{2,1,0:T(8,128)S(1)}, f32[2,80,80]{2,1,0:T(8,128)S(1)}, u32[]{:S(2)}, u32[]{:S(2)}) collective-permute-start(f32[2,80,80]{2,1,0:T(8,128)S(1)} %collective-permute-done.3.h), channel_id=1, source_target_pairs={{0,16},{32,48},{64,80},{96,112},{16,0},{48,32},{80,64},{112,96},{1... | collective-permute-start | bytes 153608 | tf_op jit(solution)/shard_map/ppermute | solution.py:480
  17.8 4.0 %collective-permute-start.5 = (f32[48,128]{1,0:T(8,128)S(1)}, f32[48,128]{1,0:T(8,128)S(1)}, u32[]{:S(2)}, u32[]{:S(2)}) collective-permute-start(f32[48,128]{1,0:T(8,128)S(1)} %get-tuple-element.66), channel_id=1, source_target_pairs={{0,32},{64,96},{48,80},{112,16},{32,0},{96,64},{80,48},{16,112},{1... | collective-permute-start | bytes 73736 | tf_op jit(solution)/shard_map/ppermute | solution.py:438
  21.8 1.3 %collective-permute-start.6 = (f32[48,128]{1,0:T(8,128)S(1)}, f32[48,128]{1,0:T(8,128)S(1)}, u32[]{:S(2)}, u32[]{:S(2)}) collective-permute-start(f32[48,128]{1,0:T(8,128)S(1)} %collective-permute-done.5.far), channel_id=1, source_target_pairs={{0,16},{32,48},{64,80},{96,112},{16,0},{48,32},{80,64},{112,96},{1... | collective-permute-start | bytes 73736 | tf_op jit(solution)/shard_map/ppermute | solution.py:447
  23.4 3.7 %collective-permute-start.7 = (f32[2,80,80]{2,1,0:T(8,128)S(1)}, f32[2,80,80]{2,1,0:T(8,128)S(1)}, u32[]{:S(2)}, u32[]{:S(2)}) collective-permute-start(f32[2,80,80]{2,1,0:T(8,128)S(1)} %send.5), channel_id=1, source_target_pairs={{0,1},{2,3},{4,5},{6,7},{8,9},{10,11},{12,13},{14,15},{17,18},{19,... | collective-permute-start | bytes 153608 | tf_op jit(solution)/shard_map/ppermute | solution.py:452
  27.0 1.9 %collective-permute-start.8 = (f32[2,80,80]{2,1,0:T(8,128)S(1)}, f32[2,80,80]{2,1,0:T(8,128)S(1)}, u32[]{:S(2)}, u32[]{:S(2)}) collective-permute-start(f32[2,80,80]{2,1,0:T(8,128)S(1)} %collective-permute-done.7.h), channel_id=1, source_target_pairs={{0,16},{32,48},{64,80},{96,112},{16,0},{48,32},{80,64},{112,96},{1... | collective-permute-start | bytes 153608 | tf_op jit(solution)/shard_map/ppermute | solution.py:480
  29.4 4.0 %collective-permute-start.9 = (f32[48,128]{1,0:T(8,128)S(1)}, f32[48,128]{1,0:T(8,128)S(1)}, u32[]{:S(2)}, u32[]{:S(2)}) collective-permute-start(f32[48,128]{1,0:T(8,128)S(1)} %get-tuple-element.77), channel_id=1, source_target_pairs={{0,32},{64,96},{48,80},{112,16},{32,0},{96,64},{80,48},{16,112},{1... | collective-permute-start | bytes 73736 | tf_op jit(solution)/shard_map/ppermute | solution.py:438
  33.4 1.3 %collective-permute-start.10 = (f32[48,128]{1,0:T(8,128)S(1)}, f32[48,128]{1,0:T(8,128)S(1)}, u32[]{:S(2)}, u32[]{:S(2)}) collective-permute-start(f32[48,128]{1,0:T(8,128)S(1)} %collective-permute-done.9.far), channel_id=1, source_target_pairs={{0,16},{32,48},{64,80},{96,112},{16,0},{48,32},{80,64},{112,96},{1... | collective-permute-start | bytes 73736 | tf_op jit(solution)/shard_map/ppermute | solution.py:447
  34.9 3.7 %collective-permute-start.11 = (f32[2,80,80]{2,1,0:T(8,128)S(1)}, f32[2,80,80]{2,1,0:T(8,128)S(1)}, u32[]{:S(2)}, u32[]{:S(2)}) collective-permute-start(f32[2,80,80]{2,1,0:T(8,128)S(1)} %send.6), channel_id=1, source_target_pairs={{0,1},{2,3},{4,5},{6,7},{8,9},{10,11},{12,13},{14,15},{17,18},{19,... | collective-permute-start | bytes 153608 | tf_op jit(solution)/shard_map/ppermute | solution.py:452
  38.6 1.9 %collective-permute-start.12 = (f32[2,80,80]{2,1,0:T(8,128)S(1)}, f32[2,80,80]{2,1,0:T(8,128)S(1)}, u32[]{:S(2)}, u32[]{:S(2)}) collective-permute-start(f32[2,80,80]{2,1,0:T(8,128)S(1)} %collective-permute-done.11.h), channel_id=1, source_target_pairs={{0,16},{32,48},{64,80},{96,112},{16,0},{48,32},{80,64},{112,96},{1... | collective-permute-start | bytes 153608 | tf_op jit(solution)/shard_map/ppermute | solution.py:480
  40.9 4.0 %collective-permute-start.13 = (f32[56,128]{1,0:T(8,128)S(1)}, f32[56,128]{1,0:T(8,128)S(1)}, u32[]{:S(2)}, u32[]{:S(2)}) collective-permute-start(f32[56,128]{1,0:T(8,128)S(1)} %get-tuple-element.88), channel_id=1, source_target_pairs={{0,32},{64,96},{48,80},{112,16},{32,0},{96,64},{80,48},{16,112},{1... | collective-permute-start | bytes 86024 | tf_op jit(solution)/shard_map/ppermute | solution.py:438
  45.0 1.2 %collective-permute-start.14 = (f32[56,128]{1,0:T(8,128)S(1)}, f32[56,128]{1,0:T(8,128)S(1)}, u32[]{:S(2)}, u32[]{:S(2)}) collective-permute-start(f32[56,128]{1,0:T(8,128)S(1)} %collective-permute-done.13.far), channel_id=1, source_target_pairs={{0,16},{32,48},{64,80},{96,112},{16,0},{48,32},{80,64},{112,96},{1... | collective-permute-start | bytes 86024 | tf_op jit(solution)/shard_map/ppermute | solution.py:447
  46.5 5.6 %collective-permute-start.15 = (f32[2,80,80]{2,1,0:T(8,128)S(1)}, f32[2,80,80]{2,1,0:T(8,128)S(1)}, u32[]{:S(2)}, u32[]{:S(2)}) collective-permute-start(f32[2,80,80]{2,1,0:T(8,128)S(1)} %send.7), channel_id=1, source_target_pairs={{0,1},{2,3},{4,5},{6,7},{8,9},{10,11},{12,13},{14,15},{17,18},{19,... | collective-permute-start | bytes 153608 | tf_op jit(solution)/shard_map/ppermute | solution.py:452
  47.7 3.7 %collective-permute-start.16 = (f32[8,128]{1,0:T(8,128)S(1)}, f32[8,128]{1,0:T(8,128)S(1)}, u32[]{:S(2)}, u32[]{:S(2)}) collective-permute-start(f32[8,128]{1,0:T(8,128)S(1)} %slice.3), channel_id=1, source_target_pairs={{0,32},{64,96},{48,80},{112,16},{32,0},{96,64},{80,48},{16,112},{1... | collective-permute-start | bytes 12296 | tf_op jit(solution)/shard_map/ppermute | solution.py:458
  52.0 10.9 %collective-permute-start.17 = (f32[2,80,80]{2,1,0:T(8,128)S(1)}, f32[2,80,80]{2,1,0:T(8,128)S(1)}, u32[]{:S(2)}, u32[]{:S(2)}) collective-permute-start(f32[2,80,80]{2,1,0:T(8,128)S(1)} %collective-permute-done.15.h), channel_id=1, source_target_pairs={{0,16},{32,48},{64,80},{96,112},{16,0},{48,32},{80,64},{112,96},{1... | collective-permute-start | bytes 153608 | tf_op jit(solution)/shard_map/ppermute | solution.py:480
  52.5 18.1 %all-to-all-start = ((f32[16,16,128]{2,1,0:T(8,128)}), f32[16,16,128]{2,1,0:T(8,128)S(1)}, u32[]{:S(2)}, u32[]{:S(2)}) async-start(f32[16,16,128]{2,1,0:T(8,128)} %column.1), calls=%async_computation | async-start | bytes 262144 | tf_op jit(solution)/shard_map/all_to_all | solution.py:464

commit v18 on v17

--- a/solution.py
+++ b/solution.py
@@ -334,10 +334,11 @@
     t = advance(z[c, :M, NB * CAP :], whole_gain(c, q0, h, g))[:, :M]
     th, tl = split2(t)
     w = jnp.concatenate([th, th, tl], axis=1)
-    for i in (0, *range(TURN, SLABS), *range(1, TURN)):
+    whole = range(0, SLAB, 8)
+    for i, halves in ((0, whole[:1]), *((i, whole) for i in range(TURN, SLABS)), (0, whole[1:]), (1, whole)):
         if i >= TURN:
             loads[i - TURN].wait()
-        for j in range(0, SLAB, 8):
+        for j in halves:
             if i >= TURN:
                 turned = jnp.swapaxes(come[i - TURN, :, j : j + 8, :], 0, 1)
             rows = []

time: 73 us -> 72.9 us (level)
  no operation moved by 1% of the time
where the time goes in v18:
time: 72.9 us; the launch traced here: 72.7 us
  starting transfers between devices  34.2 us (47%)
  Pallas kernels  23.8 us (33%)
  waiting for transfers between devices  13.8 us (19%)
  between operations  0.82 us (1%)
    ppermute x4, starting transfers between devices, local(): far = lax.ppermute(edge, 'gx', side_x)  11.2 us
    all_to_all x1, starting transfers between devices, local(): gathered = lax.all_to_all(column, 'gy', 0, 0, tiled=True)  10.4 us
    pallas_call x1, Pallas kernels, local(): call(final_kernel, out_shape=shape(M, LEV, TX, TY), in_specs=[VMEM] * 5 +...  7.63 us
    pallas_call x4, Pallas kernels, local(): call(functools.partial(own_kernel, k), out_shape=(shape(2, M, M), shape(2...  4.81 us
    ppermute x4, starting transfers between devices, local(): h = lax.ppermute(send, both, side_y)  4.75 us
    ppermute x4, waiting for transfers between devices, local(): h = lax.ppermute(send, both, side_y)  4.39 us
    ppermute x4, waiting for transfers between devices, local(): sib_far = lax.ppermute(far, 'gx', core)  4.19 us
    ppermute x4, starting transfers between devices, local(): g = lax.ppermute(h, 'gx', core)  3.54 us
  transfers between devices with their start and end apart: 19, of which 11 were waited for; matrix products, arithmetic and copies ran while one was open for 0% of the time, Pallas kernels for 23%

profile of v18, /device:TPU:1, one launch (start us, length us, event | category | flops | bytes accessed | tf_op | source)
XLA Modules:
  0.0 72.7 jit_solution(17743526900921580930)
XLA Ops:
  0.6 0.0 copy-start.1
  0.6 0.0 copy-start
  0.7 2.9 %init.1.own = f32[96,256]{1,0:T(8,128)S(1)} custom-call(s32[4]{0:T(128)} %order.9, f32[4,2048]{1,0:T(4,128)} %value_hbm.1, f32[4,2048]{1,0:T(4,128)} %variance_hbm.1, s32[4,2048]{1,0:T(4,128)} %owner.9, s32[4,2048]{1,0:T(4,128)} %cell_hbm.1, s32[4,8,2048]{2,1,0:T(8,128)} %bitcast.1, f32[80,4,32,256]{3,2,1,0:T(8,128)} %x.3), custom_call_target="tpu_custom_call" | custom-call | tf_op jit(solution)/shard_map/init/pallas_call | solution.py:412
  3.6 1.5 %collective-permute-start = (f32[96,256]{1,0:T(8,128)S(1)}, f32[96,256]{1,0:T(8,128)S(1)}, u32[]{:S(2)}, u32[]{:S(2)}) collective-permute-start(f32[96,256]{1,0:T(8,128)S(1)} %init.1.own), channel_id=1, source_target_pairs={{0,16},{32,48},{64,80},{96,112},{16,0},{48,32},{80,64},{112,96},{1... | collective-permute-start | bytes 294920 | tf_op jit(solution)/shard_map/ppermute | solution.py:434
  5.1 0.9 %collective-permute-done.sib = f32[96,256]{1,0:T(8,128)S(1)} collective-permute-done((f32[96,256]{1,0:T(8,128)S(1)}, f32[96,256]{1,0:T(8,128)S(1)}, u32[]{:S(2)}, u32[]{:S(2)}) %collective-permute-start) | collective-permute-done | bytes 98336 | tf_op jit(solution)/shard_map/ppermute | solution.py:434
  6.0 0.2 start.1
  6.2 2.9 %collective-permute-start.1 = (f32[48,128]{1,0:T(8,128)S(1)}, f32[48,128]{1,0:T(8,128)S(1)}, u32[]{:S(2)}, u32[]{:S(2)}) collective-permute-start(f32[48,128]{1,0:T(8,128)S(1)} %get-tuple-element.55), channel_id=1, source_target_pairs={{0,32},{64,96},{48,80},{112,16},{32,0},{96,64},{80,48},{16,112},{1... | collective-permute-start | bytes 73736 | tf_op jit(solution)/shard_map/ppermute | solution.py:439
  9.0 0.0 copy-done.1
  9.0 0.0 copy-done
  9.0 1.2 %own.4 = (f32[2,80,80]{2,1,0:T(8,128)S(1)}, f32[2,80,80]{2,1,0:T(8,128)S(1)}, f32[1,2048]{1,0:T(1,128)S(1)}) custom-call(s32[4]{0:T(128)S(1)} %copy-done.1, s32[4,2048]{1,0:T(4,128)S(1)} %copy-done, f32[2,48,128]{2,1,0:T(8,128)S(1)} %get-tuple-element.56.pay), custom_call_target="tpu_custom_call" | custom-call | tf_op jit(solution)/shard_map/own/pallas_call | solution.py:440
  10.3 0.0 collective-permute-done.1.far
  10.3 0.1 collective-permute-start.2
  10.4 1.1 %collective-permute-done.2.sib_far = f32[48,128]{1,0:T(8,128)S(1)} collective-permute-done((f32[48,128]{1,0:T(8,128)S(1)}, f32[48,128]{1,0:T(8,128)S(1)}, u32[]{:S(2)}, u32[]{:S(2)}) %collective-permute-start.2) | collective-permute-done | bytes 24608 | tf_op jit(solution)/shard_map/ppermute | solution.py:448
  11.5 0.3 send.4
  11.8 1.2 %collective-permute-start.3 = (f32[2,80,80]{2,1,0:T(8,128)S(1)}, f32[2,80,80]{2,1,0:T(8,128)S(1)}, u32[]{:S(2)}, u32[]{:S(2)}) collective-permute-start(f32[2,80,80]{2,1,0:T(8,128)S(1)} %send.4), channel_id=1, source_target_pairs={{0,1},{2,3},{4,5},{6,7},{8,9},{10,11},{12,13},{14,15},{17,18},{19,... | collective-permute-start | bytes 153608 | tf_op jit(solution)/shard_map/ppermute | solution.py:453
  13.0 0.3 same.4.q0
  13.3 2.2 %collective-permute-done.3.h = f32[2,80,80]{2,1,0:T(8,128)S(1)} collective-permute-done((f32[2,80,80]{2,1,0:T(8,128)S(1)}, f32[2,80,80]{2,1,0:T(8,128)S(1)}, u32[]{:S(2)}, u32[]{:S(2)}) %collective-permute-start.3) | collective-permute-done | bytes 51232 | tf_op jit(solution)/shard_map/ppermute | solution.py:453
  15.5 1.0 %collective-permute-start.4 = (f32[2,80,80]{2,1,0:T(8,128)S(1)}, f32[2,80,80]{2,1,0:T(8,128)S(1)}, u32[]{:S(2)}, u32[]{:S(2)}) collective-permute-start(f32[2,80,80]{2,1,0:T(8,128)S(1)} %collective-permute-done.3.h), channel_id=1, source_target_pairs={{0,16},{32,48},{64,80},{96,112},{16,0},{48,32},{80,64},{112,96},{1... | collective-permute-start | bytes 153608 | tf_op jit(solution)/shard_map/ppermute | solution.py:481
  16.5 0.9 %collective-permute-done.4.g = f32[2,80,80]{2,1,0:T(8,128)S(1)} collective-permute-done((f32[2,80,80]{2,1,0:T(8,128)S(1)}, f32[2,80,80]{2,1,0:T(8,128)S(1)}, u32[]{:S(2)}, u32[]{:S(2)}) %collective-permute-start.4) | collective-permute-done | bytes 51232 | tf_op jit(solution)/shard_map/ppermute | solution.py:481
  17.4 0.4 step.3
  17.8 2.8 %collective-permute-start.5 = (f32[48,128]{1,0:T(8,128)S(1)}, f32[48,128]{1,0:T(8,128)S(1)}, u32[]{:S(2)}, u32[]{:S(2)}) collective-permute-start(f32[48,128]{1,0:T(8,128)S(1)} %get-tuple-element.66), channel_id=1, source_target_pairs={{0,32},{64,96},{48,80},{112,16},{32,0},{96,64},{80,48},{16,112},{1... | collective-permute-start | bytes 73736 | tf_op jit(solution)/shard_map/ppermute | solution.py:439
  20.6 1.2 %own.5 = (f32[2,80,80]{2,1,0:T(8,128)S(1)}, f32[2,80,80]{2,1,0:T(8,128)S(1)}, f32[1,2048]{1,0:T(1,128)S(1)}) custom-call(s32[4]{0:T(128)S(1)} %copy-done.1, s32[4,2048]{1,0:T(4,128)S(1)} %copy-done, f32[2,48,128]{2,1,0:T(8,128)S(1)} %get-tuple-element.67.pay), custom_call_target="tpu_custom_call" | custom-call | tf_op jit(solution)/shard_map/own/pallas_call | solution.py:440
  21.8 0.0 collective-permute-done.5.far
  21.8 0.2 collective-permute-start.6
  22.1 1.0 %collective-permute-done.6.sib_far = f32[48,128]{1,0:T(8,128)S(1)} collective-permute-done((f32[48,128]{1,0:T(8,128)S(1)}, f32[48,128]{1,0:T(8,128)S(1)}, u32[]{:S(2)}, u32[]{:S(2)}) %collective-permute-start.6) | collective-permute-done | bytes 24608 | tf_op jit(solution)/shard_map/ppermute | solution.py:448
  23.1 0.3 send.5
  23.4 1.2 %collective-permute-start.7 = (f32[2,80,80]{2,1,0:T(8,128)S(1)}, f32[2,80,80]{2,1,0:T(8,128)S(1)}, u32[]{:S(2)}, u32[]{:S(2)}) collective-permute-start(f32[2,80,80]{2,1,0:T(8,128)S(1)} %send.5), channel_id=1, source_target_pairs={{0,1},{2,3},{4,5},{6,7},{8,9},{10,11},{12,13},{14,15},{17,18},{19,... | collective-permute-start | bytes 153608 | tf_op jit(solution)/shard_map/ppermute | solution.py:453
  24.6 0.3 same.5.q0
  24.9 2.2 %collective-permute-done.7.h = f32[2,80,80]{2,1,0:T(8,128)S(1)} collective-permute-done((f32[2,80,80]{2,1,0:T(8,128)S(1)}, f32[2,80,80]{2,1,0:T(8,128)S(1)}, u32[]{:S(2)}, u32[]{:S(2)}) %collective-permute-start.7) | collective-permute-done | bytes 51232 | tf_op jit(solution)/shard_map/ppermute | solution.py:453
  27.0 1.0 %collective-permute-start.8 = (f32[2,80,80]{2,1,0:T(8,128)S(1)}, f32[2,80,80]{2,1,0:T(8,128)S(1)}, u32[]{:S(2)}, u32[]{:S(2)}) collective-permute-start(f32[2,80,80]{2,1,0:T(8,128)S(1)} %collective-permute-done.7.h), channel_id=1, source_target_pairs={{0,16},{32,48},{64,80},{96,112},{16,0},{48,32},{80,64},{112,96},{1... | collective-permute-start | bytes 153608 | tf_op jit(solution)/shard_map/ppermute | solution.py:481
  28.1 0.9 %collective-permute-done.8.g = f32[2,80,80]{2,1,0:T(8,128)S(1)} collective-permute-done((f32[2,80,80]{2,1,0:T(8,128)S(1)}, f32[2,80,80]{2,1,0:T(8,128)S(1)}, u32[]{:S(2)}, u32[]{:S(2)}) %collective-permute-start.8) | collective-permute-done | bytes 51232 | tf_op jit(solution)/shard_map/ppermute | solution.py:481
  29.0 0.4 step.4
  29.4 2.8 %collective-permute-start.9 = (f32[48,128]{1,0:T(8,128)S(1)}, f32[48,128]{1,0:T(8,128)S(1)}, u32[]{:S(2)}, u32[]{:S(2)}) collective-permute-start(f32[48,128]{1,0:T(8,128)S(1)} %get-tuple-element.77), channel_id=1, source_target_pairs={{0,32},{64,96},{48,80},{112,16},{32,0},{96,64},{80,48},{16,112},{1... | collective-permute-start | bytes 73736 | tf_op jit(solution)/shard_map/ppermute | solution.py:439
  32.1 1.2 %own.6 = (f32[2,80,80]{2,1,0:T(8,128)S(1)}, f32[2,80,80]{2,1,0:T(8,128)S(1)}, f32[1,2048]{1,0:T(1,128)S(1)}) custom-call(s32[4]{0:T(128)S(1)} %copy-done.1, s32[4,2048]{1,0:T(4,128)S(1)} %copy-done, f32[2,48,128]{2,1,0:T(8,128)S(1)} %get-tuple-element.78.pay), custom_call_target="tpu_custom_call" | custom-call | tf_op jit(solution)/shard_map/own/pallas_call | solution.py:440
  33.4 0.0 collective-permute-done.9.far
  33.4 0.2 collective-permute-start.10
  33.6 1.0 %collective-permute-done.10.sib_far = f32[48,128]{1,0:T(8,128)S(1)} collective-permute-done((f32[48,128]{1,0:T(8,128)S(1)}, f32[48,128]{1,0:T(8,128)S(1)}, u32[]{:S(2)}, u32[]{:S(2)}) %collective-permute-start.10) | collective-permute-done | bytes 24608 | tf_op jit(solution)/shard_map/ppermute | solution.py:448
  34.6 0.3 send.6
  34.9 1.2 %collective-permute-start.11 = (f32[2,80,80]{2,1,0:T(8,128)S(1)}, f32[2,80,80]{2,1,0:T(8,128)S(1)}, u32[]{:S(2)}, u32[]{:S(2)}) collective-permute-start(f32[2,80,80]{2,1,0:T(8,128)S(1)} %send.6), channel_id=1, source_target_pairs={{0,1},{2,3},{4,5},{6,7},{8,9},{10,11},{12,13},{14,15},{17,18},{19,... | collective-permute-start | bytes 153608 | tf_op jit(solution)/shard_map/ppermute | solution.py:453
  36.1 2.2 %turn.1.near = bf16[32,160,256]{2,1,0:T(8,128)(2,1)S(1)} custom-call(f32[80,4,32,256]{3,2,1,0:T(8,128)} %x.3), custom_call_target="tpu_custom_call" | custom-call | tf_op jit(solution)/shard_map/turn/pallas_call | solution.py:472
  38.3 0.3 same.6.q0
  38.6 0.0 collective-permute-done.11.h
  38.6 1.0 %collective-permute-start.12 = (f32[2,80,80]{2,1,0:T(8,128)S(1)}, f32[2,80,80]{2,1,0:T(8,128)S(1)}, u32[]{:S(2)}, u32[]{:S(2)}) collective-permute-start(f32[2,80,80]{2,1,0:T(8,128)S(1)} %collective-permute-done.11.h), channel_id=1, source_target_pairs={{0,16},{32,48},{64,80},{96,112},{16,0},{48,32},{80,64},{112,96},{1... | collective-permute-start | bytes 153608 | tf_op jit(solution)/shard_map/ppermute | solution.py:481
  39.6 0.9 %collective-permute-done.12.g = f32[2,80,80]{2,1,0:T(8,128)S(1)} collective-permute-done((f32[2,80,80]{2,1,0:T(8,128)S(1)}, f32[2,80,80]{2,1,0:T(8,128)S(1)}, u32[]{:S(2)}, u32[]{:S(2)}) %collective-permute-start.12) | collective-permute-done | bytes 51232 | tf_op jit(solution)/shard_map/ppermute | solution.py:481
  40.5 0.4 step.5
  40.9 2.8 %collective-permute-start.13 = (f32[56,128]{1,0:T(8,128)S(1)}, f32[56,128]{1,0:T(8,128)S(1)}, u32[]{:S(2)}, u32[]{:S(2)}) collective-permute-start(f32[56,128]{1,0:T(8,128)S(1)} %get-tuple-element.88), channel_id=1, source_target_pairs={{0,32},{64,96},{48,80},{112,16},{32,0},{96,64},{80,48},{16,112},{1... | collective-permute-start | bytes 86024 | tf_op jit(solution)/shard_map/ppermute | solution.py:439
  43.7 1.2 %own.7 = (f32[2,80,80]{2,1,0:T(8,128)S(1)}, f32[2,80,80]{2,1,0:T(8,128)S(1)}, f32[1,2048]{1,0:T(1,128)S(1)}) custom-call(s32[4]{0:T(128)S(1)} %copy-done.1, s32[4,2048]{1,0:T(4,128)S(1)} %copy-done, f32[2,48,128]{2,1,0:T(8,128)S(1)} %get-tuple-element.89.pay), custom_call_target="tpu_custom_call" | custom-call | tf_op jit(solution)/shard_map/own/pallas_call | solution.py:440
  44.9 0.1 collective-permute-done.13.far
  45.0 0.2 collective-permute-start.14
  45.2 1.0 %collective-permute-done.14.sib_far = f32[56,128]{1,0:T(8,128)S(1)} collective-permute-done((f32[56,128]{1,0:T(8,128)S(1)}, f32[56,128]{1,0:T(8,128)S(1)}, u32[]{:S(2)}, u32[]{:S(2)}) %collective-permute-start.14) | collective-permute-done | bytes 28704 | tf_op jit(solution)/shard_map/ppermute | solution.py:448
  46.2 0.3 send.7
  46.5 1.2 %collective-permute-start.15 = (f32[2,80,80]{2,1,0:T(8,128)S(1)}, f32[2,80,80]{2,1,0:T(8,128)S(1)}, u32[]{:S(2)}, u32[]{:S(2)}) collective-permute-start(f32[2,80,80]{2,1,0:T(8,128)S(1)} %send.7), channel_id=1, source_target_pairs={{0,1},{2,3},{4,5},{6,7},{8,9},{10,11},{12,13},{14,15},{17,18},{19,... | collective-permute-start | bytes 153608 | tf_op jit(solution)/shard_map/ppermute | solution.py:453
  47.7 1.9 %collective-permute-start.16 = (f32[8,128]{1,0:T(8,128)S(1)}, f32[8,128]{1,0:T(8,128)S(1)}, u32[]{:S(2)}, u32[]{:S(2)}) collective-permute-start(f32[8,128]{1,0:T(8,128)S(1)} %slice.3), channel_id=1, source_target_pairs={{0,32},{64,96},{48,80},{112,16},{32,0},{96,64},{80,48},{16,112},{1... | collective-permute-start | bytes 12296 | tf_op jit(solution)/shard_map/ppermute | solution.py:459
  49.6 0.3 same.7.q0
  49.9 1.5 %collective-permute-done.16.across = f32[8,128]{1,0:T(8,128)S(1)} collective-permute-done((f32[8,128]{1,0:T(8,128)S(1)}, f32[8,128]{1,0:T(8,128)S(1)}, u32[]{:S(2)}, u32[]{:S(2)}) %collective-permute-start.16) | collective-permute-done | bytes 4128 | tf_op jit(solution)/shard_map/ppermute | solution.py:459
  51.4 0.7 column.1
  52.0 0.0 collective-permute-done.15.h
  52.0 0.5 collective-permute-start.17
  52.5 10.4 %all-to-all-start = ((f32[16,16,128]{2,1,0:T(8,128)}), f32[16,16,128]{2,1,0:T(8,128)S(1)}, u32[]{:S(2)}, u32[]{:S(2)}) async-start(f32[16,16,128]{2,1,0:T(8,128)} %column.1), calls=%async_computation | async-start | bytes 262144 | tf_op jit(solution)/shard_map/all_to_all | solution.py:465
  62.9 0.0 collective-permute-done.17.g
  63.0 7.6 %final.1 = f32[80,4,32,256]{3,2,1,0:T(8,128)} custom-call(f32[2,80,80]{2,1,0:T(8,128)S(1)} %same.7.q0, f32[2,80,80]{2,1,0:T(8,128)S(1)} %collective-permute-done.15.h, f32[2,80,80]{2,1,0:T(8,128)S(1)} %collective-permute-done.17.g, f32[2,96,384]{2,1,0:T(8,128)S(1)} %get-tuple-element.99.z, bf16[32,160,256]{2,1,0:T(8,128)(2,1)S(1)} %turn.1.near, ...), custom_call_target="tpu_custom_call" | custom-call | flops 1258291200 | bytes 20971520 | tf_op jit(solution)/shard_map/final/pallas_call | solution.py:495
  70.6 0.0 all-to-all-done.gathered
  70.6 2.1 %place.1 = f32[4,2048]{1,0:T(4,128)} custom-call(s32[4]{0:T(128)S(1)} %copy-done.1, s32[4,2048]{1,0:T(4,128)S(1)} %copy-done, f32[16,16,128]{2,1,0:T(8,128)S(1)} %all-to-all-done.gathered, f32[1,2048]{1,0:T(1,128)S(1)} %get-tuple-element.104.r0, f32[1,2048]{1,0:T(1,128)S(1)} %get-tuple-element.105.r1, f32[1,2048]{1,0:T(1,128)S(1)} %get-tuple-element.106.r2, ...), custom_call_target="tpu_custom_call" | custom-call | tf_op jit(solution)/shard_map/place/pallas_call | solution.py:508
  (1 shorter events, 0.0 us)
Async XLA Ops:
  0.6 8.4 %copy-start.1 = (s32[4]{0:T(128)S(1)}, s32[4]{0:T(128)}, u32[]{:S(2)}) copy-start(s32[4]{0:T(128)} %order.9) | copy-start | bytes 52
  0.6 8.4 %copy-start = (s32[4,2048]{1,0:T(4,128)S(1)}, s32[4,2048]{1,0:T(4,128)}, u32[]{:S(2)}) copy-start(s32[4,2048]{1,0:T(4,128)} %owner.9) | copy-start | bytes 98308
  3.6 2.4 %collective-permute-start = (f32[96,256]{1,0:T(8,128)S(1)}, f32[96,256]{1,0:T(8,128)S(1)}, u32[]{:S(2)}, u32[]{:S(2)}) collective-permute-start(f32[96,256]{1,0:T(8,128)S(1)} %init.1.own), channel_id=1, source_target_pairs={{0,16},{32,48},{64,80},{96,112},{16,0},{48,32},{80,64},{112,96},{1... | collective-permute-start | bytes 294920 | tf_op jit(solution)/shard_map/ppermute | solution.py:434
  6.2 4.1 %collective-permute-start.1 = (f32[48,128]{1,0:T(8,128)S(1)}, f32[48,128]{1,0:T(8,128)S(1)}, u32[]{:S(2)}, u32[]{:S(2)}) collective-permute-start(f32[48,128]{1,0:T(8,128)S(1)} %get-tuple-element.55), channel_id=1, source_target_pairs={{0,32},{64,96},{48,80},{112,16},{32,0},{96,64},{80,48},{16,112},{1... | collective-permute-start | bytes 73736 | tf_op jit(solution)/shard_map/ppermute | solution.py:439
  10.3 1.3 %collective-permute-start.2 = (f32[48,128]{1,0:T(8,128)S(1)}, f32[48,128]{1,0:T(8,128)S(1)}, u32[]{:S(2)}, u32[]{:S(2)}) collective-permute-start(f32[48,128]{1,0:T(8,128)S(1)} %collective-permute-done.1.far), channel_id=1, source_target_pairs={{0,16},{32,48},{64,80},{96,112},{16,0},{48,32},{80,64},{112,96},{1... | collective-permute-start | bytes 73736 | tf_op jit(solution)/shard_map/ppermute | solution.py:448
  11.8 3.7 %collective-permute-start.3 = (f32[2,80,80]{2,1,0:T(8,128)S(1)}, f32[2,80,80]{2,1,0:T(8,128)S(1)}, u32[]{:S(2)}, u32[]{:S(2)}) collective-permute-start(f32[2,80,80]{2,1,0:T(8,128)S(1)} %send.4), channel_id=1, source_target_pairs={{0,1},{2,3},{4,5},{6,7},{8,9},{10,11},{12,13},{14,15},{17,18},{19,... | collective-permute-start | bytes 153608 | tf_op jit(solution)/shard_map/ppermute | solution.py:453
  15.5 1.9 %collective-permute-start.4 = (f32[2,80,80]{2,1,0:T(8,128)S(1)}, f32[2,80,80]{2,1,0:T(8,128)S(1)}, u32[]{:S(2)}, u32[]{:S(2)}) collective-permute-start(f32[2,80,80]{2,1,0:T(8,128)S(1)} %collective-permute-done.3.h), channel_id=1, source_target_pairs={{0,16},{32,48},{64,80},{96,112},{16,0},{48,32},{80,64},{112,96},{1... | collective-permute-start | bytes 153608 | tf_op jit(solution)/shard_map/ppermute | solution.py:481
  17.8 4.0 %collective-permute-start.5 = (f32[48,128]{1,0:T(8,128)S(1)}, f32[48,128]{1,0:T(8,128)S(1)}, u32[]{:S(2)}, u32[]{:S(2)}) collective-permute-start(f32[48,128]{1,0:T(8,128)S(1)} %get-tuple-element.66), channel_id=1, source_target_pairs={{0,32},{64,96},{48,80},{112,16},{32,0},{96,64},{80,48},{16,112},{1... | collective-permute-start | bytes 73736 | tf_op jit(solution)/shard_map/ppermute | solution.py:439
  21.8 1.3 %collective-permute-start.6 = (f32[48,128]{1,0:T(8,128)S(1)}, f32[48,128]{1,0:T(8,128)S(1)}, u32[]{:S(2)}, u32[]{:S(2)}) collective-permute-start(f32[48,128]{1,0:T(8,128)S(1)} %collective-permute-done.5.far), channel_id=1, source_target_pairs={{0,16},{32,48},{64,80},{96,112},{16,0},{48,32},{80,64},{112,96},{1... | collective-permute-start | bytes 73736 | tf_op jit(solution)/shard_map/ppermute | solution.py:448
  23.4 3.7 %collective-permute-start.7 = (f32[2,80,80]{2,1,0:T(8,128)S(1)}, f32[2,80,80]{2,1,0:T(8,128)S(1)}, u32[]{:S(2)}, u32[]{:S(2)}) collective-permute-start(f32[2,80,80]{2,1,0:T(8,128)S(1)} %send.5), channel_id=1, source_target_pairs={{0,1},{2,3},{4,5},{6,7},{8,9},{10,11},{12,13},{14,15},{17,18},{19,... | collective-permute-start | bytes 153608 | tf_op jit(solution)/shard_map/ppermute | solution.py:453
  27.0 1.9 %collective-permute-start.8 = (f32[2,80,80]{2,1,0:T(8,128)S(1)}, f32[2,80,80]{2,1,0:T(8,128)S(1)}, u32[]{:S(2)}, u32[]{:S(2)}) collective-permute-start(f32[2,80,80]{2,1,0:T(8,128)S(1)} %collective-permute-done.7.h), channel_id=1, source_target_pairs={{0,16},{32,48},{64,80},{96,112},{16,0},{48,32},{80,64},{112,96},{1... | collective-permute-start | bytes 153608 | tf_op jit(solution)/shard_map/ppermute | solution.py:481
  29.4 4.0 %collective-permute-start.9 = (f32[48,128]{1,0:T(8,128)S(1)}, f32[48,128]{1,0:T(8,128)S(1)}, u32[]{:S(2)}, u32[]{:S(2)}) collective-permute-start(f32[48,128]{1,0:T(8,128)S(1)} %get-tuple-element.77), channel_id=1, source_target_pairs={{0,32},{64,96},{48,80},{112,16},{32,0},{96,64},{80,48},{16,112},{1... | collective-permute-start | bytes 73736 | tf_op jit(solution)/shard_map/ppermute | solution.py:439
  33.4 1.3 %collective-permute-start.10 = (f32[48,128]{1,0:T(8,128)S(1)}, f32[48,128]{1,0:T(8,128)S(1)}, u32[]{:S(2)}, u32[]{:S(2)}) collective-permute-start(f32[48,128]{1,0:T(8,128)S(1)} %collective-permute-done.9.far), channel_id=1, source_target_pairs={{0,16},{32,48},{64,80},{96,112},{16,0},{48,32},{80,64},{112,96},{1... | collective-permute-start | bytes 73736 | tf_op jit(solution)/shard_map/ppermute | solution.py:448
  34.9 3.7 %collective-permute-start.11 = (f32[2,80,80]{2,1,0:T(8,128)S(1)}, f32[2,80,80]{2,1,0:T(8,128)S(1)}, u32[]{:S(2)}, u32[]{:S(2)}) collective-permute-start(f32[2,80,80]{2,1,0:T(8,128)S(1)} %send.6), channel_id=1, source_target_pairs={{0,1},{2,3},{4,5},{6,7},{8,9},{10,11},{12,13},{14,15},{17,18},{19,... | collective-permute-start | bytes 153608 | tf_op jit(solution)/shard_map/ppermute | solution.py:453
  38.6 1.9 %collective-permute-start.12 = (f32[2,80,80]{2,1,0:T(8,128)S(1)}, f32[2,80,80]{2,1,0:T(8,128)S(1)}, u32[]{:S(2)}, u32[]{:S(2)}) collective-permute-start(f32[2,80,80]{2,1,0:T(8,128)S(1)} %collective-permute-done.11.h), channel_id=1, source_target_pairs={{0,16},{32,48},{64,80},{96,112},{16,0},{48,32},{80,64},{112,96},{1... | collective-permute-start | bytes 153608 | tf_op jit(solution)/shard_map/ppermute | solution.py:481
  40.9 4.0 %collective-permute-start.13 = (f32[56,128]{1,0:T(8,128)S(1)}, f32[56,128]{1,0:T(8,128)S(1)}, u32[]{:S(2)}, u32[]{:S(2)}) collective-permute-start(f32[56,128]{1,0:T(8,128)S(1)} %get-tuple-element.88), channel_id=1, source_target_pairs={{0,32},{64,96},{48,80},{112,16},{32,0},{96,64},{80,48},{16,112},{1... | collective-permute-start | bytes 86024 | tf_op jit(solution)/shard_map/ppermute | solution.py:439
  45.0 1.2 %collective-permute-start.14 = (f32[56,128]{1,0:T(8,128)S(1)}, f32[56,128]{1,0:T(8,128)S(1)}, u32[]{:S(2)}, u32[]{:S(2)}) collective-permute-start(f32[56,128]{1,0:T(8,128)S(1)} %collective-permute-done.13.far), channel_id=1, source_target_pairs={{0,16},{32,48},{64,80},{96,112},{16,0},{48,32},{80,64},{112,96},{1... | collective-permute-start | bytes 86024 | tf_op jit(solution)/shard_map/ppermute | solution.py:448
  46.5 5.6 %collective-permute-start.15 = (f32[2,80,80]{2,1,0:T(8,128)S(1)}, f32[2,80,80]{2,1,0:T(8,128)S(1)}, u32[]{:S(2)}, u32[]{:S(2)}) collective-permute-start(f32[2,80,80]{2,1,0:T(8,128)S(1)} %send.7), channel_id=1, source_target_pairs={{0,1},{2,3},{4,5},{6,7},{8,9},{10,11},{12,13},{14,15},{17,18},{19,... | collective-permute-start | bytes 153608 | tf_op jit(solution)/shard_map/ppermute | solution.py:453
  47.7 3.7 %collective-permute-start.16 = (f32[8,128]{1,0:T(8,128)S(1)}, f32[8,128]{1,0:T(8,128)S(1)}, u32[]{:S(2)}, u32[]{:S(2)}) collective-permute-start(f32[8,128]{1,0:T(8,128)S(1)} %slice.3), channel_id=1, source_target_pairs={{0,32},{64,96},{48,80},{112,16},{32,0},{96,64},{80,48},{16,112},{1... | collective-permute-start | bytes 12296 | tf_op jit(solution)/shard_map/ppermute | solution.py:459
  52.0 10.9 %collective-permute-start.17 = (f32[2,80,80]{2,1,0:T(8,128)S(1)}, f32[2,80,80]{2,1,0:T(8,128)S(1)}, u32[]{:S(2)}, u32[]{:S(2)}) collective-permute-start(f32[2,80,80]{2,1,0:T(8,128)S(1)} %collective-permute-done.15.h), channel_id=1, source_target_pairs={{0,16},{32,48},{64,80},{96,112},{16,0},{48,32},{80,64},{112,96},{1... | collective-permute-start | bytes 153608 | tf_op jit(solution)/shard_map/ppermute | solution.py:481
  52.5 18.0 %all-to-all-start = ((f32[16,16,128]{2,1,0:T(8,128)}), f32[16,16,128]{2,1,0:T(8,128)S(1)}, u32[]{:S(2)}, u32[]{:S(2)}) async-start(f32[16,16,128]{2,1,0:T(8,128)} %column.1), calls=%async_computation | async-start | bytes 262144 | tf_op jit(solution)/shard_map/all_to_all | solution.py:465
